TPU v7x, 512 devices: a whole 4x8x8 slice. The times are simulated.
512 devices in a mesh: seq: 128 (over z, y, core), mp: 4 (over x).
Axes of the slice: x: 4, y: 8, z: 8, core: 2. Of those that a mesh axis runs over, the one named last changes fastest.
Arguments:
- tokens: bfloat16 [65536, 768], P('seq'), may hold values from -6 to 6
- slide_tiles: int32 [4], replicated, may hold values from 1 to 49152, 65536 in all
- attn_gain: bfloat16 [768], replicated, may hold values from 0.099609375 to 1.8984375
- w_query: bfloat16 [768, 768], P(None, 'mp'), may hold values from -16 to 16
- w_key: bfloat16 [768, 768], P(None, 'mp'), may hold values from -0.21875 to 0.21875
- w_value: bfloat16 [768, 768], P(None, 'mp'), may hold values from -0.21875 to 0.21875
- w_out: bfloat16 [768, 768], P('mp'), may hold values from -0.21875 to 0.21875
- ffn_gain: bfloat16 [768], replicated, may hold values from 0.099609375 to 1.8984375
- w_up: bfloat16 [768, 3072], P(None, 'mp'), may hold values from -0.21875 to 0.21875
- w_down: bfloat16 [3072, 768], P('mp'), may hold values from -0.109375 to 0.109375
Outputs:
- attended: bfloat16 [65536, 768], P(('seq', 'mp'))
- far_attended: bfloat16 [2048, 768], P('seq', 'mp')
- ffn_out: bfloat16 [65536, 768], P(('seq', 'mp'))
Inputs may be any that keep to these rules, and one draw needn't show every extreme that they name: `slide_tiles`: the tile counts of the slides sum to 65536; the longest slide has 49152 tiles.
All inputs are finite; a program needn't handle non-finite values.
Results may differ from a plain program's by a relative error of at most 0.023.
The roundings to bfloat16 on the way count: a program that leaves them out, or rounds other values in their place, can miss the bound.
Values may be sent and summed in bfloat16 or wider, within the bound.
No kernel may reach another device: no remote copies, remote signals or barrier semaphores. Data moves between devices by JAX's collectives and lax.ppermute only.
A program may use at most 64 MiB of HBM per device.

v0:
```python
import math

import jax
import jax.numpy as jnp
from jax import lax
from jax.sharding import PartitionSpec as P

HEAD_DIM = 64
NEAR_DEVS = 4
MID_DEVS = 8
RATE_MID = 4
RATE_FAR = 32


EPS = 1e-05


def from_partner(value, axis, stride):
    return lax.ppermute(value, axis, [(i, i ^ 1 << stride) for i in range(lax.axis_size(axis))])


def layer_norm(values, norm_gain):
    as_float = values.astype(jnp.float32)
    mean_val = jnp.mean(as_float, -1, keepdims=True)
    centered = as_float - mean_val
    variance = jnp.mean(centered * centered, -1, keepdims=True)
    return (centered * lax.rsqrt(variance + EPS) * norm_gain.astype(jnp.float32)).astype(
        jnp.bfloat16
    )


def slide_of(positions, slide_tiles):
    slide_ends = jnp.cumsum(slide_tiles)
    return jnp.sum((positions[..., None] >= slide_ends).astype(jnp.int32), -1)


def attend(query, keyval, query_slide, key_slide):
    head_width = query.shape[-1]
    key_part = keyval[..., :head_width]
    value_part = keyval[..., head_width:]
    scores = jnp.einsum("qhd,khd->hqk", query, key_part, preferred_element_type=jnp.float32)
    scores = scores * (1.0 / math.sqrt(head_width))
    same_slide = query_slide.T[:, :, None] == key_slide.T[:, None, :]
    scores = jnp.where(same_slide, scores, -1e30)
    peak_score = jnp.max(scores, -1)
    weights = jnp.where(same_slide, jnp.exp(scores - peak_score[..., None]), 0.0)
    totals = jnp.sum(weights, -1)
    partial_out = jnp.einsum(
        "hqk,khd->qhd", weights.astype(jnp.bfloat16), value_part, preferred_element_type=jnp.float32
    )
    return (peak_score.T, totals.T, partial_out)


def pick(values, stride, offsets):
    head_count = offsets.shape[0]
    shaped = values.reshape((values.shape[0] // stride, stride) + values.shape[1:])
    chosen = jnp.arange(stride, dtype=jnp.int32)[:, None] == offsets[None, :]
    chosen = chosen.reshape((1, stride, head_count) + (1,) * (values.ndim - 2))
    kept = jnp.where(chosen, shaped, jnp.zeros((), values.dtype))
    return jnp.sum(kept, axis=1, dtype=values.dtype)


def spread(values, stride, offsets, filler):
    head_count = offsets.shape[0]
    present = jnp.arange(stride, dtype=jnp.int32)[:, None] == offsets[None, :]
    present = present.reshape((1, stride, head_count) + (1,) * (values.ndim - 2))
    widened = jnp.where(present, values[:, None], filler)
    return widened.reshape((values.shape[0] * stride,) + values.shape[1:])


def spread_all(results, stride, offsets):
    return (
        spread(results[0], stride, offsets, -1e30),
        spread(results[1], stride, offsets, 0.0),
        spread(results[2], stride, offsets, 0.0),
    )


def combine(results):
    largest = results[0][0]
    for item in results[1:]:
        largest = jnp.maximum(largest, item[0])
    numerator = jnp.zeros_like(results[0][2])
    denominator = jnp.zeros_like(results[0][1])
    for item in results:
        factor = jnp.exp(item[0] - largest)
        numerator = numerator + factor[..., None] * item[2]
        denominator = denominator + factor * item[1]
    return (numerator / denominator[..., None]).astype(jnp.bfloat16)


def join_pair(mine, partner, seq_place, bit_number):
    lower_half = seq_place // (1 << bit_number) % 2 == 0
    return jnp.where(
        lower_half, jnp.concatenate([mine, partner], 0), jnp.concatenate([partner, mine], 0)
    )


def local(tokens, slide_tiles, attn_gain, w_query, w_key, w_value, w_out, ffn_gain, w_up, w_down):
    row_count = tokens.shape[0]
    head_count = w_query.shape[1] // HEAD_DIM
    mp_count = lax.axis_size("mp")
    seq_place = lax.axis_index("seq")
    mp_place = lax.axis_index("mp")
    near_bits = NEAR_DEVS.bit_length() - 1
    mid_bits = MID_DEVS.bit_length() - 1
    normed = layer_norm(tokens, attn_gain)

    def project(weight):
        product = jnp.dot(normed, weight, preferred_element_type=jnp.float32)
        return product.astype(jnp.bfloat16).reshape(row_count, head_count, HEAD_DIM)

    query = project(w_query)
    keyval = jnp.concatenate([project(w_key), project(w_value)], -1)
    head_ids = mp_place * head_count + jnp.arange(head_count, dtype=jnp.int32)
    positions = seq_place * row_count + jnp.arange(row_count, dtype=jnp.int32)
    own_slides = jnp.broadcast_to(
        slide_of(positions, slide_tiles)[:, None], (row_count, head_count)
    )
    near_kv = keyval
    for bit_number in range(near_bits):
        partner = from_partner(near_kv, "seq", bit_number)
        near_kv = join_pair(near_kv, partner, seq_place, bit_number)
    near_start = seq_place // NEAR_DEVS * NEAR_DEVS * row_count
    near_keys = near_start + jnp.arange(NEAR_DEVS * row_count, dtype=jnp.int32)
    near_slides = jnp.broadcast_to(
        slide_of(near_keys, slide_tiles)[:, None], (near_keys.shape[0], head_count)
    )
    near = attend(query, near_kv, own_slides, near_slides)
    mid_offsets = head_ids % RATE_MID
    mid_query = pick(query, RATE_MID, mid_offsets)
    mid_own = pick(own_slides, RATE_MID, mid_offsets)
    mid_kv = pick(keyval, RATE_MID, mid_offsets)
    for bit_number in range(mid_bits):
        partner = from_partner(mid_kv, "seq", bit_number)
        mid_kv = join_pair(mid_kv, partner, seq_place, bit_number)
    mid_start = seq_place // MID_DEVS * MID_DEVS * row_count
    mid_keys = (
        mid_start
        + jnp.arange(mid_kv.shape[0], dtype=jnp.int32)[:, None] * RATE_MID
        + mid_offsets[None, :]
    )
    middle = spread_all(
        attend(mid_query, mid_kv, mid_own, slide_of(mid_keys, slide_tiles)), RATE_MID, mid_offsets
    )
    far_offsets = head_ids % RATE_FAR
    far_query = pick(query, RATE_FAR, far_offsets)
    far_own = pick(own_slides, RATE_FAR, far_offsets)
    far_kv = lax.all_gather(pick(keyval, RATE_FAR, far_offsets), "seq", axis=0, tiled=True)
    far_keys = (
        jnp.arange(far_kv.shape[0], dtype=jnp.int32)[:, None] * RATE_FAR + far_offsets[None, :]
    )
    far_raw = attend(far_query, far_kv, far_own, slide_of(far_keys, slide_tiles))
    far_attended = (
        (far_raw[2] / far_raw[1][..., None])
        .astype(jnp.bfloat16)
        .reshape(far_query.shape[0], head_count * HEAD_DIM)
    )
    distant = spread_all(far_raw, RATE_FAR, far_offsets)
    mixed = combine([near, middle, distant]).reshape(row_count, head_count * HEAD_DIM)
    share_rows = row_count // mp_count
    share_start = mp_place * share_rows
    summed = lax.psum(
        jnp.dot(mixed, w_out, preferred_element_type=jnp.float32).astype(jnp.bfloat16), "mp"
    )
    attended = lax.dynamic_slice_in_dim(summed, share_start, share_rows, 0)
    normed_ffn = layer_norm(tokens.astype(jnp.float32) + summed.astype(jnp.float32), ffn_gain)
    hidden = jax.nn.gelu(
        jnp.dot(normed_ffn, w_up, preferred_element_type=jnp.float32), approximate=False
    ).astype(jnp.bfloat16)
    ffn_out = lax.psum_scatter(
        jnp.dot(hidden, w_down, preferred_element_type=jnp.float32).astype(jnp.bfloat16),
        "mp",
        scatter_dimension=0,
        tiled=True,
    )
    return (attended, far_attended, ffn_out)


def solution(mesh):
    return jax.shard_map(
        local,
        mesh=mesh,
        in_specs=(
            P("seq", None),
            P(),
            P(),
            P(None, "mp"),
            P(None, "mp"),
            P(None, "mp"),
            P("mp", None),
            P(),
            P(None, "mp"),
            P("mp", None),
        ),
        out_specs=(P(("seq", "mp"), None), P("seq", "mp"), P(("seq", "mp"), None)),
        check_vma=False,
    )
```

profile of v0, /device:TPU:1, one launch (start us, length us, event | category | flops | bytes accessed | tf_op | source)
XLA Modules:
  0.0 230.6 jit_solution(8623931282559549230)
XLA Ops:
  7.3 1.5 convert_reduce_fusion
  8.7 1.5 fusion.8
  11.6 0.8 pad_maximum_fusion
  12.4 8.8 %collective-permute-start = (bf16[512,3,128]{0,2,1:T(8,128)(2,1)}, bf16[512,3,128]{0,2,1:T(8,128)(2,1)}, u32[]{:S(2)}, u32[]{:S(2)}) collective-permute-start(bf16[512,3,128]{0,2,1:T(8,128)(2,1)} %pad_maximum_fusion), channel_id=1, source_target_pairs={{0,4},{4,0},{8,12},{12,8},{16,20},{20,16},{24,28},{28,24},{32,36},... | collective-permute-start | bytes 1179656 | tf_op jit(solution)/shard_map/ppermute | solution.py:19
  21.3 0.8 copy.49
  22.2 2.1 concatenate.62
  24.3 1.0 concatenate.61
  25.3 2.1 fusion.94
  28.0 2.1 concatenate.53
  30.1 1.0 concatenate.52
  31.1 2.2 fusion.93
  33.4 1.9 collective-permute-start.2
  36.0 0.8 convert_reduce_fusion.1
  36.9 1.4 convolution_convert_fusion.4
  39.0 1.1 maximum_select_fusion.6
  40.1 1.9 collective-permute-start.3
  42.0 1.3 convert_reduce_fusion.3
  43.3 1.3 copy.54
  44.7 1.3 broadcast_in_dim.295
  46.1 0.9 reshape_reshape.7
  49.2 0.8 broadcast_in_dim.281
  50.0 2.1 select_reduce_fusion
  52.0 1.1 maximum_select_fusion.5
  53.1 1.9 collective-permute-start.4
  55.1 0.8 select_reduce_fusion.3
  55.9 1.3 select_reduce_fusion.1
  57.2 2.3 maximum_select_fusion.1
  59.5 3.5 %collective-permute-start.1 = (bf16[1024,3,128]{0,2,1:T(8,128)(2,1)}, bf16[1024,3,128]{0,2,1:T(8,128)(2,1)}, u32[]{:S(2)}, u32[]{:S(2)}) collective-permute-start(bf16[1024,3,128]{0,2,1:T(8,128)(2,1)} %maximum_select_fusion.1), channel_id=1, source_target_pairs={{0,8},{4,12},{8,0},{12,4},{16,24},{20,28},{24,16},{28,20},{32,40},... | collective-permute-start | bytes 2359304 | tf_op jit(solution)/shard_map/ppermute | solution.py:19
  63.0 11.8 %collective-permute-done.4 = bf16[512,3,128]{0,2,1:T(8,128)(2,1)S(1)} collective-permute-done((bf16[512,3,128]{0,2,1:T(8,128)(2,1)S(1)}, bf16[512,3,128]{0,2,1:T(8,128)(2,1)S(1)}, u32[]{:S(2)}, u32[]{:S(2)}) %collective-permute-start.4) | collective-permute-done | bytes 393248 | tf_op jit(solution)/shard_map/ppermute | solution.py:19
  75.4 1.2 copy-done.4
  77.4 0.8 broadcast_in_dim.291
  78.1 1.9 fusion.29
  81.0 1.0 copy.62
  82.0 5.5 %collective-permute-done.1 = bf16[1024,3,128]{0,2,1:T(8,128)(2,1)} collective-permute-done((bf16[1024,3,128]{0,2,1:T(8,128)(2,1)}, bf16[1024,3,128]{0,2,1:T(8,128)(2,1)}, u32[]{:S(2)}, u32[]{:S(2)}) %collective-permute-start.1) | collective-permute-done | bytes 786464 | tf_op jit(solution)/shard_map/ppermute | solution.py:19
  87.5 2.5 %maximum_select_fusion = bf16[2048,3,128]{0,2,1:T(8,128)(2,1)S(1)} fusion(bf16[1024,3,128]{0,2,1:T(8,128)(2,1)} %collective-permute-done.1, bf16[1024,3,128]{0,2,1:T(8,128)(2,1)} %maximum_select_fusion.1, pred[]{:T(512)S(6)} %eq.64), kind=kLoop, calls=%fused_computation.25 | loop fusion | flops 7077888 | bytes 3145729 | tf_op jit(solution)/shard_map/jit(_where)/select_n | solution.py:94
  90.0 2.4 %fusion = (f32[3,512]{1,0:T(4,128)S(1)}, f32[3,512,2048]{2,1,0:T(8,128)S(1)}) fusion(s32[2048]{0:T(1024)S(1)} %copy-done.14, s32[512]{0:T(512)S(1)} %copy-done.16, bf16[512,3,64]{0,2,1:T(8,128)(2,1)S(1)} %bitcast.83, bf16[2048,3,128]{0,2,1:T(8,128)(2,1)S(1)} %maximum_select_fusion), kind=kOutput, calls=%fused_computation.2 | convolution fusion | flops 415234560 | bytes 13582336 | tf_op jit(solution)/shard_map/qhd,khd->hqk/dot_general | solution.py:41
  92.4 4.6 %copy-done.2 = f32[3,512,2048]{2,1,0:T(8,128)} copy-done((f32[3,512,2048]{2,1,0:T(8,128)}, f32[3,512,2048]{2,1,0:T(8,128)S(1)}, u32[]{:S(2)}) %copy-start.2) | copy-done | bytes 12582936
  97.0 4.3 %fusion.1 = f32[3,512]{1,0:T(4,128)} fusion(f32[3,512,2048]{2,1,0:T(8,128)S(1)} %get-tuple-element.8, f32[3,512]{1,0:T(4,128)S(1)} %get-tuple-element.7, s32[2048]{0:T(1024)S(1)} %copy-done.14, s32[512]{0:T(512)S(1)} %copy-done.16), kind=kLoop, calls=%fused_computation.3 | loop fusion | flops 18872832 | bytes 12605440 | tf_op jit(solution)/shard_map/reduce_sum | solution.py:47
  101.3 19.4 %all-gather.2.cloned.1.call-done = bf16[2048,3,128]{2,0,1:T(8,128)(2,1)} async-done(((bf16[16,3,128]{2,0,1:T(8,128)(2,1)}), bf16[2048,3,128]{2,0,1:T(8,128)(2,1)}) %all-gather.2.cloned.1.call-update) | async-done | bytes 1572880 | tf_op jit(solution)/shard_map/all_gather | solution.py:149
  120.6 2.0 fusion.146
  124.4 2.6 %divide_convert_fusion = (bf16[16,3,64]{2,0,1:T(8,128)(2,1)}, f32[16,3,64]{2,0,1:T(8,128)S(1)}) fusion(f32[16,3]{0,1:T(4,128)S(1)} %bitcast.105, bf16[2048,3,128]{2,0,1:T(8,128)(2,1)} %all-gather.2.cloned.1.call-done, f32[3,16,2048]{2,1,0:T(8,128)S(1)} %get-tuple-element.10, f32[3,16]{1,0:T(4,128)S(1)} %get-tuple-element.9, s32[3,2048]{1,0:T(4,128)S(1)} %bitcast.86, ...), kind=kOutput, calls=%fused_computation.125 | convolution fusion | flops 12982272 | bytes 2009664 | tf_op jit(solution)/shard_map/hqk,khd->qhd/dot_general | solution.py:48
  127.4 0.8 fusion.107
  128.2 7.4 %fusion.46 = bf16[512,3,64]{0,2,1:T(8,128)(2,1)S(1)} fusion(f32[3,512,2048]{2,1,0:T(8,128)} %copy-done.2, f32[3,512]{1,0:T(4,128)S(1)} %get-tuple-element.7, s32[2048]{0:T(1024)S(1)} %copy-done.14, s32[512]{0:T(512)} %copy-done.15, bf16[2048,3,128]{0,2,1:T(8,128)(2,1)} %copy-done.5, f32[512,3,64]{0,2,1:T(8,128)S(1)} %copy.64, ...), kind=kOutput, calls=%fused_computation.59 | convolution fusion | flops 422412288 | bytes 14397440 | tf_op jit(solution)/shard_map/hqk,khd->qhd/dot_general | solution.py:48
  135.6 1.3 convolution_convert_fusion.1
  137.2 48.6 %all-reduce.2.cloned.1.call-done = bf16[512,768]{1,0:T(8,128)(2,1)} async-done(((bf16[512,768]{1,0:T(8,128)(2,1)}), bf16[512,768]{1,0:T(8,128)(2,1)}) %all-reduce.2.cloned.1.call-update) | async-done | bytes 786448 | tf_op jit(solution)/shard_map/psum | solution.py:163
  185.8 1.5 fusion.25
  187.7 6.8 %convolution_convert_fusion = bf16[512,768]{1,0:T(8,128)(2,1)} fusion(bf16[768,768]{1,0:T(8,128)(2,1)S(1)} %copy-done, bf16[768,768]{1,0:T(8,128)(2,1)} %param.18, bf16[512,768]{1,0:T(8,128)(2,1)S(1)} %copy-done.3, bf16[512,768]{1,0:T(8,128)(2,1)S(1)} %copy-done.1, f32[768]{0:T(1024)S(1)} %convert_element_type.81, f32[512]{0:T(512)S(1)} %add_rsqrt_fusion, ...), kind=kOutput, calls=%fused_computation.45 | convolution fusion | flops 1236664320 | bytes 4725760 | tf_op jit(solution)/shard_map/dot_general | solution.py:172
  195.9 28.1 %reduce-scatter.2.cloned.1.call-done = bf16[128,768]{1,0:T(8,128)(2,1)} async-done(((bf16[512,768]{1,0:T(8,128)(2,1)}), bf16[128,768]{1,0:T(8,128)(2,1)}) %reduce-scatter.2.cloned.1.call-update) | async-done | bytes 196624 | tf_op jit(solution)/shard_map/reduce_scatter | solution.py:171
  (108 shorter events, 12.7 us)
Async XLA Ops:
  7.2 180.5 %copy-start = (bf16[768,768]{1,0:T(8,128)(2,1)S(1)}, bf16[768,768]{1,0:T(8,128)(2,1)}, u32[]{:S(2)}) copy-start(bf16[768,768]{1,0:T(8,128)(2,1)} %param.19) | copy-start | bytes 3538948
  7.2 3.1 %copy-start.1 = (bf16[512,768]{1,0:T(8,128)(2,1)S(1)}, bf16[512,768]{1,0:T(8,128)(2,1)}, u32[]{:S(2)}) copy-start(bf16[512,768]{1,0:T(8,128)(2,1)} %param.10) | copy-start | bytes 2359300
  7.2 3.0 %copy-start.21 = (bf16[768]{0:T(1024)(128)(2,1)S(1)}, bf16[768]{0:T(1024)(128)(2,1)}, u32[]{:S(2)}) copy-start(bf16[768]{0:T(1024)(128)(2,1)} %param.12) | copy-start | bytes 4612
  7.2 3.4 %copy-start.9 = (bf16[768,192]{0,1:T(8,128)(2,1)S(1)}, bf16[768,192]{0,1:T(8,128)(2,1)}, u32[]{:S(2)}) copy-start(bf16[768,192]{0,1:T(8,128)(2,1)} %param.15) | copy-start | bytes 884740
  7.2 113.4 %all-gather.2.cloned.1.call-start = ((), (), s32[]{:S(2)}) async-start(), calls=%async_computation.1 | async-start | bytes 1585152 | tf_op jit(solution)/shard_map/all_gather | solution.py:149
  10.2 1.0 copy-start.10
  12.4 44.8 %collective-permute-start = (bf16[512,3,128]{0,2,1:T(8,128)(2,1)}, bf16[512,3,128]{0,2,1:T(8,128)(2,1)}, u32[]{:S(2)}, u32[]{:S(2)}) collective-permute-start(bf16[512,3,128]{0,2,1:T(8,128)(2,1)} %pad_maximum_fusion), channel_id=1, source_target_pairs={{0,4},{4,0},{8,12},{12,8},{16,20},{20,16},{24,28},{28,24},{32,36},... | collective-permute-start | bytes 1179656 | tf_op jit(solution)/shard_map/ppermute | solution.py:19
  22.2 7.9 %copy-start.12 = (pred[32,3]{1,0:T(8,128)(4,1)}, pred[32,3]{1,0:T(8,128)(4,1)S(1)}, u32[]{:S(2)}) copy-start(pred[32,3]{1,0:T(8,128)(4,1)S(1)} %iota_compare_fusion) | copy-start | bytes 292
  27.3 8.1 %copy-start.24 = (s32[4]{0:T(128)S(1)}, s32[4]{0:T(128)}, u32[]{:S(2)}) copy-start(s32[4]{0:T(128)} %param.11) | copy-start | bytes 52
  28.0 157.8 %all-reduce.2.cloned.1.call-start = ((), (), s32[]{:S(2)}) async-start(), calls=%async_computation.2 | async-start | bytes 1572864 | tf_op jit(solution)/shard_map/psum | solution.py:163
  31.1 5.7 %copy-start.23 = (pred[4,3]{1,0:T(4,128)(4,1)}, pred[4,3]{1,0:T(4,128)(4,1)S(1)}, u32[]{:S(2)}) copy-start(pred[4,3]{1,0:T(4,128)(4,1)S(1)} %iota_compare_fusion.1) | copy-start | bytes 40
  33.4 5.6 %copy-start.6 = (bf16[128,3,128]{0,2,1:T(8,128)(2,1)}, bf16[128,3,128]{0,2,1:T(8,128)(2,1)S(1)}, u32[]{:S(2)}) copy-start(bf16[128,3,128]{0,2,1:T(8,128)(2,1)S(1)} %copy.51) | copy-start | bytes 294916
  33.4 5.6 %collective-permute-start.2 = (bf16[128,3,128]{0,2,1:T(8,128)(2,1)S(1)}, bf16[128,3,128]{0,2,1:T(8,128)(2,1)}, u32[]{:S(2)}, u32[]{:S(2)}) collective-permute-start(bf16[128,3,128]{0,2,1:T(8,128)(2,1)S(1)} %copy.51), channel_id=1, source_target_pairs={{0,4},{4,0},{8,12},{12,8},{16,20},{20,16},{24,28},{28,24},{32,36},... | collective-permute-start | bytes 294920 | tf_op jit(solution)/shard_map/ppermute | solution.py:19
  35.4 3.5 %copy-start.20 = (pred[4,3]{0,1:T(4,128)(4,1)}, pred[4,3]{0,1:T(4,128)(4,1)S(1)}, u32[]{:S(2)}) copy-start(pred[4,3]{0,1:T(4,128)(4,1)S(1)} %copy.46) | copy-start | bytes 40
  35.7 3.3 %copy-start.19 = (s32[4,1]{0,1:T(1,128)}, s32[4,1]{0,1:T(1,128)S(1)}, u32[]{:S(2)}) copy-start(s32[4,1]{0,1:T(1,128)S(1)} %reduce-window.8) | copy-start | bytes 52
  35.8 3.1 %copy-start.15 = (s32[512]{0:T(512)}, s32[512]{0:T(512)S(1)}, u32[]{:S(2)}) copy-start(s32[512]{0:T(512)S(1)} %convert_reduce_fusion.4) | copy-start | bytes 6148
  40.1 11.9 %collective-permute-start.3 = (bf16[256,3,128]{0,2,1:T(8,128)(2,1)S(1)}, bf16[256,3,128]{0,2,1:T(8,128)(2,1)}, u32[]{:S(2)}, u32[]{:S(2)}) collective-permute-start(bf16[256,3,128]{0,2,1:T(8,128)(2,1)S(1)} %maximum_select_fusion.6), channel_id=1, source_target_pairs={{0,8},{4,12},{8,0},{12,4},{16,24},{20,28},{24,16},{28,20},{32,40},... | collective-permute-start | bytes 589832 | tf_op jit(solution)/shard_map/ppermute | solution.py:19
  53.1 21.6 %collective-permute-start.4 = (bf16[512,3,128]{0,2,1:T(8,128)(2,1)S(1)}, bf16[512,3,128]{0,2,1:T(8,128)(2,1)S(1)}, u32[]{:S(2)}, u32[]{:S(2)}) collective-permute-start(bf16[512,3,128]{0,2,1:T(8,128)(2,1)S(1)} %maximum_select_fusion.5), channel_id=1, source_target_pairs={{0,16},{4,20},{8,24},{12,28},{16,0},{20,4},{24,8},{28,12},{32,48},... | collective-permute-start | bytes 1179656 | tf_op jit(solution)/shard_map/ppermute | solution.py:19
  57.2 17.8 %copy-start.18 = (s32[128,3]{0,1:T(4,128)S(1)}, s32[128,3]{0,1:T(4,128)}, u32[]{:S(2)}) copy-start(s32[128,3]{0,1:T(4,128)} %select_reduce_fusion.2) | copy-start | bytes 4612
  59.5 28.1 %collective-permute-start.1 = (bf16[1024,3,128]{0,2,1:T(8,128)(2,1)}, bf16[1024,3,128]{0,2,1:T(8,128)(2,1)}, u32[]{:S(2)}, u32[]{:S(2)}) collective-permute-start(bf16[1024,3,128]{0,2,1:T(8,128)(2,1)} %maximum_select_fusion.1), channel_id=1, source_target_pairs={{0,8},{4,12},{8,0},{12,4},{16,24},{20,28},{24,16},{28,20},{32,40},... | collective-permute-start | bytes 2359304 | tf_op jit(solution)/shard_map/ppermute | solution.py:19
  75.4 1.2 copy-start.4
  82.0 8.0 %copy-start.14 = (s32[2048]{0:T(1024)S(1)}, s32[2048]{0:T(1024)}, u32[]{:S(2)}) copy-start(s32[2048]{0:T(1024)} %convert_reduce_fusion.3) | copy-start | bytes 24580
  82.0 8.0 %copy-start.16 = (s32[512]{0:T(512)S(1)}, s32[512]{0:T(512)}, u32[]{:S(2)}) copy-start(s32[512]{0:T(512)} %copy-done.15) | copy-start | bytes 6148
  90.0 2.4 %copy-start.5 = (bf16[2048,3,128]{0,2,1:T(8,128)(2,1)}, bf16[2048,3,128]{0,2,1:T(8,128)(2,1)S(1)}, u32[]{:S(2)}) copy-start(bf16[2048,3,128]{0,2,1:T(8,128)(2,1)S(1)} %maximum_select_fusion) | copy-start | bytes 4718596
  92.4 4.6 %copy-start.2 = (f32[3,512,2048]{2,1,0:T(8,128)}, f32[3,512,2048]{2,1,0:T(8,128)S(1)}, u32[]{:S(2)}) copy-start(f32[3,512,2048]{2,1,0:T(8,128)S(1)} %get-tuple-element.8) | copy-start | bytes 37748740
  97.0 23.6 %copy-start.8 = (s32[2048,3]{0,1:T(4,128)S(1)}, s32[2048,3]{0,1:T(4,128)}, u32[]{:S(2)}) copy-start(s32[2048,3]{0,1:T(4,128)} %convert_reduce_fusion.1) | copy-start | bytes 73732
  97.0 23.6 %copy-start.13 = (bf16[16,3,64]{2,1,0:T(4,128)(2,1)S(1)}, bf16[16,3,64]{2,1,0:T(4,128)(2,1)}, u32[]{:S(2)}) copy-start(bf16[16,3,64]{2,1,0:T(4,128)(2,1)} %select_reduce_fusion) | copy-start | bytes 18436
  127.1 1.1 copy-start.7
  128.2 7.4 %copy-start.11 = (bf16[192,768]{1,0:T(8,128)(2,1)S(1)}, bf16[192,768]{1,0:T(8,128)(2,1)}, u32[]{:S(2)}) copy-start(bf16[192,768]{1,0:T(8,128)(2,1)} %param.16) | copy-start | bytes 884740
  135.6 1.6 copy-start.22
  136.9 87.1 %reduce-scatter.2.cloned.1.call-start = ((), (), s32[]{:S(2)}) async-start(), calls=%async_computation.3 | async-start | bytes 983040 | tf_op jit(solution)/shard_map/reduce_scatter | solution.py:171
  185.8 1.5 copy-start.3
  187.7 6.8 %copy-start.17 = (bf16[16,3,64]{2,0,1:T(8,128)(2,1)S(1)}, bf16[16,3,64]{2,0,1:T(8,128)(2,1)}, u32[]{:S(2)}) copy-start(bf16[16,3,64]{2,0,1:T(8,128)(2,1)} %get-tuple-element.13) | copy-start | bytes 18436
Sparse Core Ops, SparseCore 0:
  28.1 92.4 all-gather.1
  137.1 48.6 all-reduce.1
  194.6 29.3 reduce-scatter.1
where the time goes:
time: 232 us; the launch traced here: 231 us
  waiting for transfers between devices  113 us (49%)
  other arithmetic  32 us (14%)
  local copies, waits for them, and re-layouts  26.9 us (12%)
  matrix products  25.6 us (11%)
  starting transfers between devices  18.4 us (8%)
  between operations  14.3 us (6%)
    psum x1, waiting for transfers between devices, local(): lax.psum(jnp.dot(mixed, w_out, preferred_element_type=jnp.float32).astype...  48.6 us
    reduce_scatter x1, waiting for transfers between devices, local(): lax.psum_scatter(jnp.dot(hidden, w_down, preferred_element_type=jnp.float...  28.1 us
    all_gather x1, waiting for transfers between devices, local(): lax.all_gather(pick(keyval, RATE_FAR, far_offsets), 'seq', axis=0, tiled=...  19.4 us
    ppermute x5, starting transfers between devices, from_partner(): lax.ppermute(value, axis, [(i, i ^ 1 << stride) for i in range(lax.axis_s...  18.1 us
    ppermute x5, waiting for transfers between devices, from_partner(): lax.ppermute(value, axis, [(i, i ^ 1 << stride) for i in range(lax.axis_s...  17.3 us
    dot_general x3, matrix products, attend(): jnp.einsum('hqk,khd->qhd', weights.astype(jnp.bfloat16), value_part, pref...  10.5 us
    reduce_sum x6, other arithmetic, pick(): return jnp.sum(kept, axis=1, dtype=values.dtype)  9.06 us
    broadcast_in_dim x16, local copies, waits for them, and re-layouts, spread(): widened = jnp.where(present, values[:, None], filler)  7.45 us
  transfers between devices with their start and end apart: 8, of which 5 were waited for; matrix products, arithmetic and copies ran while one was open for 21% of the time, Pallas kernels for 0%

commit v1 on v0

v1 whole, which is shorter than its diff:
```python
import functools

import jax
import jax.numpy as jnp
from jax import lax
from jax.experimental import pallas as pl
from jax.experimental.pallas import tpu as pltpu
from jax.sharding import PartitionSpec as P

HEAD_DIM = 64
LOCAL_HEADS = 3
RATE_MID = 4
RATE_FAR = 32
ROWS = 512
CLASS_ROWS = ROWS // RATE_MID
FAR_ROWS = ROWS // RATE_FAR
LANES = 128
SLIDES = 4
EPS = 1e-05
HIDDEN_SCORE = -1e30
VMEM = 56 * 1024 * 1024

KEY_TILE = (0, 0, 2)
VALUE_TILE = (1, 1, 2)
QUERY_TILE = (0, 0, 1)


def iota(shape, dim):
    return lax.broadcasted_iota(jnp.int32, shape, dim)


def place_of(row):
    return (row & 3) * CLASS_ROWS + ((row >> 2) & 7) * FAR_ROWS + (row >> 5)


def row_at(place):
    return (place & 15) * RATE_FAR + ((place >> 4) & 7) * RATE_MID + (place >> 7)


def layer_norm(as_float, gain):
    mean_val = jnp.mean(as_float, -1, keepdims=True)
    centered = as_float - mean_val
    variance = jnp.mean(centered * centered, -1, keepdims=True)
    return (centered * lax.rsqrt(variance + EPS) * gain.astype(jnp.float32)).astype(jnp.bfloat16)


def matmul(left, right):
    return jnp.dot(left, right, preferred_element_type=jnp.float32)


def slide_of(positions, ends):
    index = (positions >= ends[0]).astype(jnp.int32)
    for end in ends[1:]:
        index = index + (positions >= end).astype(jnp.int32)
    return index


def slide_ends(tiles_ref):
    ends = [tiles_ref[0]]
    for slide in range(1, SLIDES - 1):
        ends.append(ends[-1] + tiles_ref[slide])
    return ends


def query_marks(positions, ends):
    rows = positions.shape[0]
    lane = iota((rows, LANES), 1)
    return (lane == slide_of(positions, ends)).astype(jnp.bfloat16)


def key_marks(positions, ends):
    rows = positions.shape[0]
    lane = iota((rows, LANES), 1)
    hide = (lane < SLIDES) & (lane != slide_of(positions, ends))
    marks = jnp.where(hide, HIDDEN_SCORE, jnp.where(lane == SLIDES, 1.0, 0.0))
    return marks.astype(jnp.bfloat16)


def head_lanes(value, head):
    lane = iota(value.shape, 1)
    keep = lane < HEAD_DIM if head != 1 else lane >= HEAD_DIM
    return jnp.where(keep, value, jnp.zeros_like(value))


def tile(index):
    return slice(index * LANES, (index + 1) * LANES)


def project_kernel(tokens, gain, w_query, w_key, w_value, place, query, keyval, mid, far):
    normed = layer_norm(tokens[...].astype(jnp.float32), gain[...])
    order = iota((ROWS, ROWS), 0) == place_of(iota((ROWS, ROWS), 1))
    normed = matmul(order.astype(jnp.bfloat16), normed).astype(jnp.bfloat16)
    scaled = (matmul(normed, w_query[...]) * (1.0 / 8.0)).astype(jnp.bfloat16)
    query[:, :192] = scaled
    query[:, 192:] = jnp.zeros((ROWS, 64), jnp.bfloat16)
    key = matmul(normed, w_key[...]).astype(jnp.bfloat16)
    value = matmul(normed, w_value[...]).astype(jnp.bfloat16)
    keyval[:, tile(0)] = key[:, :128]
    keyval[:, tile(1)] = value[:, :128]
    keyval[:, tile(2)] = jnp.concatenate([key[:, 128:], value[:, 128:]], 1)
    for source, rows, target in (("mid", CLASS_ROWS, mid), ("far", FAR_ROWS, far)):
        picked = []
        for head in range(LOCAL_HEADS):
            number = place[1] * LOCAL_HEADS + head
            start = (number & 3) * CLASS_ROWS
            if source == "far":
                start = start + (number >> 2) * FAR_ROWS
            picked.append(pl.ds(pl.multiple_of(start, rows), rows))
        for index in range(2):
            low, high = keyval[picked[0], tile(index)], keyval[picked[1], tile(index)]
            lane = iota(low.shape, 1)
            target[:, tile(index)] = jnp.where(lane < HEAD_DIM, low, high)
        target[:, tile(2)] = keyval[picked[2], tile(2)]


def scores_of(query, keys):
    return lax.dot_general(
        query, keys, (((1,), (1,)), ((), ())), preferred_element_type=jnp.float32
    )


def attend(query, keys, values):
    scores = scores_of(query, keys)
    peak = jnp.max(scores, -1, keepdims=True)
    weights = jnp.exp(scores - peak).astype(jnp.bfloat16)
    return peak, matmul(weights, values)


def near_kernel(tiles, place, query, own, other, peaks, sums):
    ends = slide_ends(tiles)
    base = place[0] * ROWS
    rows = row_at(iota((ROWS, LANES), 0))
    marks = query_marks(rows + base, ends)
    keys_marks = jnp.concatenate(
        [key_marks(rows + base, ends), key_marks(rows + (place[0] ^ 1) * ROWS, ends)], 0
    )
    for head in range(LOCAL_HEADS):
        asked = head_lanes(query[:, tile(QUERY_TILE[head])], head)
        asked = jnp.concatenate([asked, marks], 1)
        keys = jnp.concatenate(
            [own[:, tile(KEY_TILE[head])], other[:, tile(KEY_TILE[head])]], 0
        )
        values = jnp.concatenate(
            [own[:, tile(VALUE_TILE[head])], other[:, tile(VALUE_TILE[head])]], 0
        )
        peak, total = attend(
            asked,
            jnp.concatenate([keys, keys_marks], 1),
            jnp.concatenate([values, keys_marks], 1),
        )
        peaks[head] = jnp.broadcast_to(peak, (ROWS, LANES))
        sums[head] = total


def join(peaks, sums, head, rows, peak, total):
    held = peaks[head, rows, :][:, :1]
    largest = jnp.maximum(held, peak)
    sums[head, rows, :] = sums[head, rows, :] * jnp.exp(held - largest) + total * jnp.exp(
        peak - largest
    )
    peaks[head, rows, :] = jnp.broadcast_to(largest, (largest.shape[0], LANES))


def rest_kernel(
    tiles, place, query, own, core, side, corner, mid, far, peaks_in, sums_in,
    mixed, far_out, peaks, sums,
):
    ends = slide_ends(tiles)
    seq, mp = place[0], place[1]
    rows = row_at(iota((ROWS, LANES), 0))
    marks = query_marks(rows + seq * ROWS, ends)
    far_parts = []
    near = (own, core, side, corner)
    near_marks = [key_marks(rows + (seq ^ step) * ROWS, ends) for step in range(4)]
    side_marks = jnp.concatenate(near_marks[2:], 0)
    peaks[...] = peaks_in[...]
    sums[...] = sums_in[...]
    for head in range(LOCAL_HEADS):
        key_tile, value_tile = tile(KEY_TILE[head]), tile(VALUE_TILE[head])
        asked = head_lanes(query[:, tile(QUERY_TILE[head])], head)
        keys = jnp.concatenate([side[:, key_tile], corner[:, key_tile]], 0)
        values = jnp.concatenate([side[:, value_tile], corner[:, value_tile]], 0)
        peak, total = attend(
            jnp.concatenate([asked, marks], 1),
            jnp.concatenate([keys, side_marks], 1),
            jnp.concatenate([values, side_marks], 1),
        )
        join(peaks, sums, head, slice(None), peak, total)

        number = mp * LOCAL_HEADS + head
        offset = number & 3
        picked = pl.ds(pl.multiple_of(offset * CLASS_ROWS, CLASS_ROWS), CLASS_ROWS)
        class_rows = offset + RATE_MID * (
            (iota((CLASS_ROWS, LANES), 0) >> 4) + ((iota((CLASS_ROWS, LANES), 0) & 15) << 3)
        )
        class_marks = jnp.concatenate(
            [key_marks(class_rows + (seq ^ step) * ROWS, ends) for step in range(8)], 0
        )
        asked = head_lanes(query[picked, tile(QUERY_TILE[head])], head)
        asked = jnp.concatenate([asked, query_marks(class_rows + seq * ROWS, ends)], 1)
        keys = jnp.concatenate([ref[picked, key_tile] for ref in near] + [mid[:, key_tile]], 0)
        values = jnp.concatenate(
            [ref[picked, value_tile] for ref in near] + [mid[:, value_tile]], 0
        )
        peak, total = attend(
            asked,
            jnp.concatenate([keys, class_marks], 1),
            jnp.concatenate([values, class_marks], 1),
        )
        join(peaks, sums, head, picked, peak, total)

        start = pl.multiple_of(
            offset * CLASS_ROWS + (number >> 2) * FAR_ROWS, FAR_ROWS
        )
        picked = pl.ds(start, FAR_ROWS)
        asked = head_lanes(query[picked, tile(QUERY_TILE[head])], head)
        scores = scores_of(asked, far[:, key_tile])
        own_slide = slide_of(
            seq * ROWS + number + RATE_FAR * iota(scores.shape, 0), ends
        )
        same = slide_of(number + RATE_FAR * iota(scores.shape, 1), ends) == own_slide
        scores = jnp.where(same, scores, HIDDEN_SCORE)
        peak = jnp.max(scores, -1, keepdims=True)
        weights = jnp.exp(scores - peak)
        total = jnp.sum(weights, -1, keepdims=True)
        part = matmul(weights.astype(jnp.bfloat16), far[:, value_tile])
        far_parts.append(part / total)
        lane = iota((FAR_ROWS, LANES), 1)
        stats = jnp.where(lane == SLIDES, total, 0.0)
        join(peaks, sums, head, picked, peak, jnp.concatenate([part, stats], 1))

    def packed(parts, out):
        lane = iota(parts[0].shape, 1)
        out[:, :128] = jnp.where(lane < HEAD_DIM, parts[0], parts[1]).astype(jnp.bfloat16)
        out[:, 128:] = parts[2][:, HEAD_DIM:].astype(jnp.bfloat16)

    packed(far_parts, far_out)
    back = (place_of(iota((ROWS, ROWS), 0)) == iota((ROWS, ROWS), 1)).astype(jnp.bfloat16)
    parts = []
    for head in range(LOCAL_HEADS):
        part = sums[head, :, :LANES] / sums[head, :, LANES + SLIDES : LANES + SLIDES + 1]
        parts.append(matmul(back, part.astype(jnp.bfloat16)))
    packed(parts, mixed)


def ffn_kernel(tokens, mixed, w_out, gain, w_up, w_down, place, attended, partial):
    summed = matmul(mixed[0], w_out[:192, :])
    for group in range(1, 4):
        summed = summed + matmul(mixed[group], w_out[192 * group : 192 * (group + 1), :])
    summed = summed.astype(jnp.bfloat16)
    partial[...] = summed
    attended[...] = partial[pl.ds(pl.multiple_of(place[1] * 128, 128), 128), :]
    normed = layer_norm(tokens[...].astype(jnp.float32) + summed.astype(jnp.float32), gain[...])
    raised = matmul(normed, w_up[...])
    hidden = (0.5 * raised * (1.0 + lax.erf(raised * 0.7071067811865476))).astype(jnp.bfloat16)
    partial[...] = matmul(hidden, w_down[...]).astype(jnp.bfloat16)


def call(kernel, outs, ins, scratch=()):
    places = {"smem": pltpu.SMEM, "vmem": pltpu.VMEM}
    return pl.pallas_call(
        kernel,
        out_shape=[jax.ShapeDtypeStruct(*out) for out in outs],
        in_specs=[pl.BlockSpec(memory_space=places[where]) for _, where in ins],
        out_specs=[pl.BlockSpec(memory_space=pltpu.VMEM) for _ in outs],
        scratch_shapes=list(scratch),
        compiler_params=pltpu.CompilerParams(vmem_limit_bytes=VMEM),
    )(*[array for array, _ in ins])


def swap(value, step):
    return lax.ppermute(value, "seq", [(i, i ^ step) for i in range(lax.axis_size("seq"))])


def local(tokens, slide_tiles, attn_gain, w_query, w_key, w_value, w_out, ffn_gain, w_up, w_down):
    bf16 = jnp.bfloat16
    place = jnp.stack([lax.axis_index("seq"), lax.axis_index("mp")]).astype(jnp.int32)
    attn_gain, ffn_gain = attn_gain.reshape(1, -1), ffn_gain.reshape(1, -1)
    v, s = "vmem", "smem"
    query, own, mid, far = call(
        project_kernel,
        [((ROWS, 256), bf16), ((ROWS, 384), bf16), ((CLASS_ROWS, 384), bf16), ((FAR_ROWS, 384), bf16)],
        [(tokens, v), (attn_gain, v), (w_query, v), (w_key, v), (w_value, v), (place, s)],
    )
    side = swap(own, 2)
    core = swap(own, 1)
    corner = swap(side, 1)
    mids = [swap(mid, step) for step in (4, 5, 6, 7)]
    far_all = lax.all_gather(far, "seq", axis=0, tiled=True)
    w_out_all = lax.all_gather(w_out, "mp", axis=0, tiled=True)
    state = [((LOCAL_HEADS, ROWS, LANES), jnp.float32), ((LOCAL_HEADS, ROWS, 256), jnp.float32)]
    peaks, sums = call(
        near_kernel,
        state,
        [(slide_tiles, s), (place, s), (query, v), (own, v), (core, v)],
    )
    mixed, far_attended = call(
        rest_kernel,
        [((ROWS, 192), bf16), ((FAR_ROWS, 192), bf16)],
        [
            (slide_tiles, s), (place, s), (query, v), (own, v), (core, v), (side, v), (corner, v),
            (jnp.concatenate(mids, 0), v), (far_all, v), (peaks, v), (sums, v),
        ],
        [pltpu.VMEM(*shape) for shape in state],
    )
    mixed_all = lax.all_gather(mixed, "mp", axis=0)
    attended, partial = call(
        ffn_kernel,
        [((ROWS // 4, 768), bf16), ((ROWS, 768), bf16)],
        [(tokens, v), (mixed_all, v), (w_out_all, v), (ffn_gain, v), (w_up, v), (w_down, v), (place, s)],
    )
    ffn_out = lax.psum_scatter(partial, "mp", scatter_dimension=0, tiled=True)
    return (attended, far_attended, ffn_out)


def solution(mesh):
    return jax.shard_map(
        local,
        mesh=mesh,
        in_specs=(
            P("seq", None),
            P(),
            P(),
            P(None, "mp"),
            P(None, "mp"),
            P(None, "mp"),
            P("mp", None),
            P(),
            P(None, "mp"),
            P("mp", None),
        ),
        out_specs=(P(("seq", "mp"), None), P("seq", "mp"), P(("seq", "mp"), None)),
        check_vma=False,
    )
```

time: 232 us -> 181 us (0.78)
  waiting for transfers between devices: 113 us -> 81.9 us
  other arithmetic: 32 us -> 1.46 us
  matrix products: 25.6 us -> 0 us
  Pallas kernels: 0 us -> 25.4 us
  blocking collectives: 0 us -> 20.8 us
  local copies, waits for them, and re-layouts: 26.9 us -> 6.71 us
  starting transfers between devices: 18.4 us -> 30.2 us
    psum x1 -> x0, waiting for transfers between devices: 48.6 us -> none  [local(): lax.psum(jnp.dot(mixed, w_out, preferred_element_type=jnp.float32).astype...]
    all_gather x1 -> x2, waiting for transfers between devices: 19.4 us -> 48.6 us  [the longest x1 44.8 us: local(): far_all = lax.all_gather(far, 'seq', axis=0, tiled=True)]
    dot_general x11 -> x0, matrix products: 25.6 us -> none  [the longest x3 10.5 us: attend(): jnp.einsum('hqk,khd->qhd', weights.astype(jnp.bfloat16), value_part, pref...]
    pallas_call x0 -> x4, Pallas kernels: none -> 25.4 us  [call(): pl.pallas_call(kernel, out_shape=[jax.ShapeDtypeStruct(*out) for out in o...]
    reduce_sum x17 -> x0, other arithmetic: 22.5 us -> none  [the longest x6 9.06 us: pick(): return jnp.sum(kept, axis=1, dtype=values.dtype)]
    all_gather x0 -> x1, blocking collectives: none -> 20.8 us  [local(): mixed_all = lax.all_gather(mixed, 'mp', axis=0)]
    ppermute x5 -> x7, starting transfers between devices: 18.1 us -> 30.1 us  [swap(): lax.ppermute(value, 'seq', [(i, i ^ step) for i in range(lax.axis_size('s...]
    broadcast_in_dim x18 -> x0, local copies, waits for them, and re-layouts: 8.84 us -> none  [the longest x16 7.45 us: spread(): widened = jnp.where(present, values[:, None], filler)]
  transfers between devices with their start and end apart: 8 -> 10, of which waited for: 5 -> 6; matrix products, arithmetic and copies ran while one was open for 21% -> 1% of each run, Pallas kernels for 0% -> 8%
where the time goes in v1:
time: 181 us; the launch traced here: 180 us
  waiting for transfers between devices  81.9 us (45%)
  starting transfers between devices  30.2 us (17%)
  Pallas kernels  25.4 us (14%)
  blocking collectives  20.8 us (11%)
  between operations  13.9 us (8%)
  local copies, waits for them, and re-layouts  6.71 us (4%)
    all_gather x1, waiting for transfers between devices, local(): far_all = lax.all_gather(far, 'seq', axis=0, tiled=True)  44.8 us
    ppermute x7, starting transfers between devices, swap(): lax.ppermute(value, 'seq', [(i, i ^ step) for i in range(lax.axis_size('s...  30.1 us
    pallas_call x4, Pallas kernels, call(): pl.pallas_call(kernel, out_shape=[jax.ShapeDtypeStruct(*out) for out in o...  25.4 us
    reduce_scatter x1, waiting for transfers between devices, local(): ffn_out = lax.psum_scatter(partial, 'mp', scatter_dimension=0, tiled=True)  24 us
    all_gather x1, blocking collectives, local(): mixed_all = lax.all_gather(mixed, 'mp', axis=0)  20.8 us
    ppermute x7, waiting for transfers between devices, swap(): lax.ppermute(value, 'seq', [(i, i ^ step) for i in range(lax.axis_size('s...  8.5 us
    unnamed x15, local copies, waits for them, and re-layouts  5.53 us
    all_gather x1, waiting for transfers between devices, local(): w_out_all = lax.all_gather(w_out, 'mp', axis=0, tiled=True)  3.82 us
  transfers between devices with their start and end apart: 10, of which 6 were waited for; matrix products, arithmetic and copies ran while one was open for 1% of the time, Pallas kernels for 8%

profile of v1, /device:TPU:1, one launch (start us, length us, event | category | flops | bytes accessed | tf_op | source)
XLA Modules:
  0.0 180.3 jit_solution(10131829662670410731)
XLA Ops:
  7.2 0.0 copy-start.3
  7.2 0.0 copy-start.4
  7.2 0.0 all-gather.4.cloned.1.call-start
  7.2 1.9 %copy.13.w_query = bf16[768,192]{1,0:T(8,128)(2,1)} copy(bf16[768,192]{0,1:T(8,128)(2,1)} %param.13) | data formatting | bytes 589824 | tf_op args[3]
  9.2 1.9 %copy.14.w_key = bf16[768,192]{1,0:T(8,128)(2,1)} copy(bf16[768,192]{0,1:T(8,128)(2,1)} %param.14) | data formatting | bytes 589824 | tf_op args[4]
  11.0 0.0 copy-done.3
  11.0 0.9 copy.15.w_value
  12.0 0.0 copy-done.4
  12.0 0.0 copy-start.5
  12.0 0.6 reshape.12.gain
  12.6 0.7 pad_add_fusion.place
  13.2 4.1 %shard_map.121 = (bf16[512,256]{1,0:T(8,128)(2,1)}, bf16[512,384]{1,0:T(8,128)(2,1)}, bf16[128,384]{1,0:T(8,128)(2,1)}, bf16[16,384]{1,0:T(8,128)(2,1)}) custom-call(bf16[512,768]{1,0:T(8,128)(2,1)} %tokens.3, bf16[1,768]{1,0:T(2,128)(2,1)} %reshape.12.gain, bf16[768,192]{1,0:T(8,128)(2,1)} %copy.13.w_query, bf16[768,192]{1,0:T(8,128)(2,1)} %copy.14.w_key, ...), custom_call_target="tpu_custom_call" | custom-call | tf_op jit(solution)/shard_map/pallas_call | solution.py:261
  17.3 0.0 all-gather.4.cloned.1.call-update
  17.3 0.0 all-gather.6.cloned.1.call-start
  17.4 0.7 all-gather.6.cloned.1.call-update
  18.1 0.0 reduce-scatter.2.cloned.1.call-start
  18.1 4.0 %collective-permute-start.1 = (bf16[512,384]{1,0:T(8,128)(2,1)}, bf16[512,384]{1,0:T(8,128)(2,1)S(1)}, u32[]{:S(2)}, u32[]{:S(2)}) collective-permute-start(bf16[512,384]{1,0:T(8,128)(2,1)} %get-tuple-element.14.own), channel_id=1, source_target_pairs={{0,8},{4,12},{8,0},{12,4},{16,24},{20,28},{24,16},{28,20},{32,40},... | collective-permute-start | bytes 1179656 | tf_op jit(solution)/shard_map/ppermute | solution.py:272
  22.2 6.7 %collective-permute-start = (bf16[512,384]{1,0:T(8,128)(2,1)}, bf16[512,384]{1,0:T(8,128)(2,1)S(1)}, u32[]{:S(2)}, u32[]{:S(2)}) collective-permute-start(bf16[512,384]{1,0:T(8,128)(2,1)} %get-tuple-element.14.own), channel_id=1, source_target_pairs={{0,4},{4,0},{8,12},{12,8},{16,20},{20,16},{24,28},{28,24},{32,36},... | collective-permute-start | bytes 1179656 | tf_op jit(solution)/shard_map/ppermute | solution.py:272
  28.8 0.0 collective-permute-done.1.side
  28.9 0.0 copy-start.1
  28.9 7.9 %collective-permute-start.2 = (bf16[512,384]{1,0:T(8,128)(2,1)S(1)}, bf16[512,384]{1,0:T(8,128)(2,1)S(1)}, u32[]{:S(2)}, u32[]{:S(2)}) collective-permute-start(bf16[512,384]{1,0:T(8,128)(2,1)S(1)} %collective-permute-done.1.side), channel_id=1, source_target_pairs={{0,4},{4,0},{8,12},{12,8},{16,20},{20,16},{24,28},{28,24},{32,36},... | collective-permute-start | bytes 1179656 | tf_op jit(solution)/shard_map/ppermute | solution.py:272
  36.8 1.9 %collective-permute-start.3 = (bf16[128,384]{1,0:T(8,128)(2,1)}, bf16[128,384]{1,0:T(8,128)(2,1)S(1)}, u32[]{:S(2)}, u32[]{:S(2)}) collective-permute-start(bf16[128,384]{1,0:T(8,128)(2,1)} %get-tuple-element.15), channel_id=1, source_target_pairs={{0,16},{4,20},{8,24},{12,28},{16,0},{20,4},{24,8},{28,12},{32,48},... | collective-permute-start | bytes 294920 | tf_op jit(solution)/shard_map/ppermute | solution.py:272
  38.7 4.4 %collective-permute-start.4 = (bf16[128,384]{1,0:T(8,128)(2,1)}, bf16[128,384]{1,0:T(8,128)(2,1)S(1)}, u32[]{:S(2)}, u32[]{:S(2)}) collective-permute-start(bf16[128,384]{1,0:T(8,128)(2,1)} %get-tuple-element.15), channel_id=1, source_target_pairs={{0,20},{4,16},{8,28},{12,24},{16,4},{20,0},{24,12},{28,8},{32,52},... | collective-permute-start | bytes 294920 | tf_op jit(solution)/shard_map/ppermute | solution.py:272
  43.2 2.9 %collective-permute-start.5 = (bf16[128,384]{1,0:T(8,128)(2,1)}, bf16[128,384]{1,0:T(8,128)(2,1)S(1)}, u32[]{:S(2)}, u32[]{:S(2)}) collective-permute-start(bf16[128,384]{1,0:T(8,128)(2,1)} %get-tuple-element.15), channel_id=1, source_target_pairs={{0,24},{4,28},{8,16},{12,20},{16,8},{20,12},{24,0},{28,4},{32,56},... | collective-permute-start | bytes 294920 | tf_op jit(solution)/shard_map/ppermute | solution.py:272
  46.1 2.4 %collective-permute-done.3 = bf16[128,384]{1,0:T(8,128)(2,1)S(1)} collective-permute-done((bf16[128,384]{1,0:T(8,128)(2,1)}, bf16[128,384]{1,0:T(8,128)(2,1)S(1)}, u32[]{:S(2)}, u32[]{:S(2)}) %collective-permute-start.3) | collective-permute-done | bytes 98336 | tf_op jit(solution)/shard_map/ppermute | solution.py:272
  48.5 2.2 %collective-permute-start.6 = (bf16[128,384]{1,0:T(8,128)(2,1)}, bf16[128,384]{1,0:T(8,128)(2,1)S(1)}, u32[]{:S(2)}, u32[]{:S(2)}) collective-permute-start(bf16[128,384]{1,0:T(8,128)(2,1)} %get-tuple-element.15), channel_id=1, source_target_pairs={{0,28},{4,24},{8,20},{12,16},{16,12},{20,8},{24,4},{28,0},{32,60},... | collective-permute-start | bytes 294920 | tf_op jit(solution)/shard_map/ppermute | solution.py:272
  50.6 0.0 copy-done.5
  50.7 0.6 reshape.13.gain
  51.3 1.4 collective-permute-done.4
  52.7 0.0 collective-permute-done.5
  52.7 4.7 %collective-permute-done.6 = bf16[128,384]{1,0:T(8,128)(2,1)S(1)} collective-permute-done((bf16[128,384]{1,0:T(8,128)(2,1)}, bf16[128,384]{1,0:T(8,128)(2,1)S(1)}, u32[]{:S(2)}, u32[]{:S(2)}) %collective-permute-start.6) | collective-permute-done | bytes 98336 | tf_op jit(solution)/shard_map/ppermute | solution.py:272
  57.4 0.8 pad_maximum_fusion.mid
  58.2 0.0 collective-permute-done.other.core
  58.2 0.0 copy-start
  58.2 0.8 copy-done
  59.0 4.9 %shard_map.122 = (f32[3,512,128]{2,1,0:T(8,128)}, f32[3,512,256]{2,1,0:T(8,128)}) custom-call(s32[4]{0:T(128)} %tiles.3, s32[2]{0:T(128)} %pad_add_fusion.place, bf16[512,256]{1,0:T(8,128)(2,1)} %get-tuple-element.13.query, bf16[512,384]{1,0:T(8,128)(2,1)} %get-tuple-element.14.own, bf16[512,384]{1,0:T(8,128)(2,1)} %copy-done), custom_call_target="tpu_custom_call" | custom-call | tf_op jit(solution)/shard_map/pallas_call | solution.py:261
  63.9 0.0 collective-permute-done.2.corner
  63.9 0.0 copy-start.2
  63.9 44.8 %all-gather.4.cloned.1.call-done.far = bf16[2048,384]{1,0:T(8,128)(2,1)} async-done(((bf16[16,384]{1,0:T(8,128)(2,1)}), bf16[2048,384]{1,0:T(8,128)(2,1)}) %all-gather.4.cloned.1.call-update) | async-done | bytes 1572880 | tf_op jit(solution)/shard_map/all_gather | solution.py:289
  108.6 0.0 copy-done.1
  108.6 0.0 copy-done.2
  108.6 9.6 %shard_map.123 = (bf16[512,192]{1,0:T(8,128)(2,1)}, bf16[16,192]{1,0:T(8,128)(2,1)}) custom-call(s32[4]{0:T(128)} %tiles.3, s32[2]{0:T(128)} %pad_add_fusion.place, bf16[512,256]{1,0:T(8,128)(2,1)} %get-tuple-element.13.query, bf16[512,384]{1,0:T(8,128)(2,1)} %get-tuple-element.14.own, bf16[512,384]{1,0:T(8,128)(2,1)} %copy-done, ...), custom_call_target="tpu_custom_call" | custom-call | tf_op jit(solution)/shard_map/pallas_call | solution.py:261
  118.2 20.8 %all-gather = bf16[2048,192]{1,0:T(8,128)(2,1)} all-gather(bf16[512,192]{1,0:T(8,128)(2,1)} %get-tuple-element.19), channel_id=2, replica_groups=mesh['seq'=128,'mp'=4] {'mp'}, dimensions={0}, use_global_device_ids=true | all-gather | bytes 983040 | tf_op jit(solution)/shard_map/all_gather | solution.py:306
  139.0 3.8 %all-gather.6.cloned.1.call-done.w_out = bf16[768,768]{1,0:T(8,128)(2,1)} async-done(((bf16[192,768]{1,0:T(8,128)(2,1)}), bf16[768,768]{1,0:T(8,128)(2,1)}) %all-gather.6.cloned.1.call-update) | async-done | bytes 1179664 | tf_op jit(solution)/shard_map/all_gather | solution.py:290
  142.8 6.8 %shard_map.124 = (bf16[128,768]{1,0:T(8,128)(2,1)}, bf16[512,768]{1,0:T(8,128)(2,1)}) custom-call(bf16[512,768]{1,0:T(8,128)(2,1)} %tokens.3, bf16[4,512,192]{2,1,0:T(8,128)(2,1)} %bitcast.3, bf16[768,768]{1,0:T(8,128)(2,1)} %all-gather.6.cloned.1.call-done.w_out, bf16[1,768]{1,0:T(2,128)(2,1)} %reshape.13.gain, bf16[768,768]{1,0:T(8,128)(2,1)} %w_up.1, ...), custom_call_target="tpu_custom_call" | custom-call | tf_op jit(solution)/shard_map/pallas_call | solution.py:261
  149.7 0.0 reduce-scatter.2.cloned.1.call-update
  149.7 24.0 %reduce-scatter.2.cloned.1.call-done = bf16[128,768]{1,0:T(8,128)(2,1)} async-done(((bf16[512,768]{1,0:T(8,128)(2,1)}), bf16[128,768]{1,0:T(8,128)(2,1)}) %reduce-scatter.2.cloned.1.call-update) | async-done | bytes 196624 | tf_op jit(solution)/shard_map/reduce_scatter | solution.py:312
Async XLA Ops:
  7.2 3.9 %copy-start.3 = (bf16[768,192]{0,1:T(8,128)(2,1)S(1)}, bf16[768,192]{0,1:T(8,128)(2,1)}, u32[]{:S(2)}) copy-start(bf16[768,192]{0,1:T(8,128)(2,1)} %param.15) | copy-start | bytes 884740
  7.2 4.8 %copy-start.4 = (bf16[768]{0:T(1024)(128)(2,1)S(1)}, bf16[768]{0:T(1024)(128)(2,1)}, u32[]{:S(2)}) copy-start(bf16[768]{0:T(1024)(128)(2,1)} %param.12) | copy-start | bytes 4612
  7.2 101.5 %all-gather.4.cloned.1.call-start = ((), (), s32[]{:S(2)}) async-start(), calls=%async_computation.1 | async-start | bytes 1585152 | tf_op jit(solution)/shard_map/all_gather | solution.py:289
  12.0 38.7 %copy-start.5 = (bf16[768]{0:T(1024)(128)(2,1)S(1)}, bf16[768]{0:T(1024)(128)(2,1)}, u32[]{:S(2)}) copy-start(bf16[768]{0:T(1024)(128)(2,1)} %param.17) | copy-start | bytes 4612
  17.3 125.5 %all-gather.6.cloned.1.call-start = ((), (), s32[]{:S(2)}) async-start(), calls=%async_computation.2 | async-start | bytes 1474560 | tf_op jit(solution)/shard_map/all_gather | solution.py:290
  18.1 155.7 %reduce-scatter.2.cloned.1.call-start = ((), (), s32[]{:S(2)}) async-start(), calls=%async_computation.3 | async-start | bytes 983040 | tf_op jit(solution)/shard_map/reduce_scatter | solution.py:312
  18.1 10.7 %collective-permute-start.1 = (bf16[512,384]{1,0:T(8,128)(2,1)}, bf16[512,384]{1,0:T(8,128)(2,1)S(1)}, u32[]{:S(2)}, u32[]{:S(2)}) collective-permute-start(bf16[512,384]{1,0:T(8,128)(2,1)} %get-tuple-element.14.own), channel_id=1, source_target_pairs={{0,8},{4,12},{8,0},{12,4},{16,24},{20,28},{24,16},{28,20},{32,40},... | collective-permute-start | bytes 1179656 | tf_op jit(solution)/shard_map/ppermute | solution.py:272
  22.2 36.0 %collective-permute-start = (bf16[512,384]{1,0:T(8,128)(2,1)}, bf16[512,384]{1,0:T(8,128)(2,1)S(1)}, u32[]{:S(2)}, u32[]{:S(2)}) collective-permute-start(bf16[512,384]{1,0:T(8,128)(2,1)} %get-tuple-element.14.own), channel_id=1, source_target_pairs={{0,4},{4,0},{8,12},{12,8},{16,20},{20,16},{24,28},{28,24},{32,36},... | collective-permute-start | bytes 1179656 | tf_op jit(solution)/shard_map/ppermute | solution.py:272
  28.9 79.8 %copy-start.1 = (bf16[512,384]{1,0:T(8,128)(2,1)}, bf16[512,384]{1,0:T(8,128)(2,1)S(1)}, u32[]{:S(2)}) copy-start(bf16[512,384]{1,0:T(8,128)(2,1)S(1)} %collective-permute-done.1.side) | copy-start | bytes 1179652
  28.9 35.0 %collective-permute-start.2 = (bf16[512,384]{1,0:T(8,128)(2,1)S(1)}, bf16[512,384]{1,0:T(8,128)(2,1)S(1)}, u32[]{:S(2)}, u32[]{:S(2)}) collective-permute-start(bf16[512,384]{1,0:T(8,128)(2,1)S(1)} %collective-permute-done.1.side), channel_id=1, source_target_pairs={{0,4},{4,0},{8,12},{12,8},{16,20},{20,16},{24,28},{28,24},{32,36},... | collective-permute-start | bytes 1179656 | tf_op jit(solution)/shard_map/ppermute | solution.py:272
  36.8 11.7 %collective-permute-start.3 = (bf16[128,384]{1,0:T(8,128)(2,1)}, bf16[128,384]{1,0:T(8,128)(2,1)S(1)}, u32[]{:S(2)}, u32[]{:S(2)}) collective-permute-start(bf16[128,384]{1,0:T(8,128)(2,1)} %get-tuple-element.15), channel_id=1, source_target_pairs={{0,16},{4,20},{8,24},{12,28},{16,0},{20,4},{24,8},{28,12},{32,48},... | collective-permute-start | bytes 294920 | tf_op jit(solution)/shard_map/ppermute | solution.py:272
  38.7 13.9 %collective-permute-start.4 = (bf16[128,384]{1,0:T(8,128)(2,1)}, bf16[128,384]{1,0:T(8,128)(2,1)S(1)}, u32[]{:S(2)}, u32[]{:S(2)}) collective-permute-start(bf16[128,384]{1,0:T(8,128)(2,1)} %get-tuple-element.15), channel_id=1, source_target_pairs={{0,20},{4,16},{8,28},{12,24},{16,4},{20,0},{24,12},{28,8},{32,52},... | collective-permute-start | bytes 294920 | tf_op jit(solution)/shard_map/ppermute | solution.py:272
  43.2 9.5 %collective-permute-start.5 = (bf16[128,384]{1,0:T(8,128)(2,1)}, bf16[128,384]{1,0:T(8,128)(2,1)S(1)}, u32[]{:S(2)}, u32[]{:S(2)}) collective-permute-start(bf16[128,384]{1,0:T(8,128)(2,1)} %get-tuple-element.15), channel_id=1, source_target_pairs={{0,24},{4,28},{8,16},{12,20},{16,8},{20,12},{24,0},{28,4},{32,56},... | collective-permute-start | bytes 294920 | tf_op jit(solution)/shard_map/ppermute | solution.py:272
  48.5 8.9 %collective-permute-start.6 = (bf16[128,384]{1,0:T(8,128)(2,1)}, bf16[128,384]{1,0:T(8,128)(2,1)S(1)}, u32[]{:S(2)}, u32[]{:S(2)}) collective-permute-start(bf16[128,384]{1,0:T(8,128)(2,1)} %get-tuple-element.15), channel_id=1, source_target_pairs={{0,28},{4,24},{8,20},{12,16},{16,12},{20,8},{24,4},{28,0},{32,60},... | collective-permute-start | bytes 294920 | tf_op jit(solution)/shard_map/ppermute | solution.py:272
  58.2 0.8 copy-start
  63.9 44.8 %copy-start.2 = (bf16[512,384]{1,0:T(8,128)(2,1)}, bf16[512,384]{1,0:T(8,128)(2,1)S(1)}, u32[]{:S(2)}) copy-start(bf16[512,384]{1,0:T(8,128)(2,1)S(1)} %collective-permute-done.2.corner) | copy-start | bytes 1179652
Sparse Core Ops, SparseCore 0:
  17.4 91.1 all-gather.3
  110.7 32.0 all-gather.5
  149.8 23.8 reduce-scatter.1

commit v2 on v1

v2 whole, which is shorter than its diff:
```python
import functools

import jax
import jax.numpy as jnp
from jax import lax
from jax.experimental import pallas as pl
from jax.experimental.pallas import tpu as pltpu
from jax.sharding import PartitionSpec as P

HEAD_DIM = 64
LOCAL_HEADS = 3
RATE_MID = 4
RATE_FAR = 32
ROWS = 512
CLASS_ROWS = ROWS // RATE_MID
FAR_ROWS = ROWS // RATE_FAR
LANES = 128
SLIDES = 4
EPS = 1e-05
HIDDEN_SCORE = -1e30
VMEM = 56 * 1024 * 1024

KEY_TILE = (0, 0, 2)
VALUE_TILE = (1, 1, 2)
QUERY_TILE = (0, 0, 1)
SPARE = (64, 0, 0)
FAR_GROUP = 8


def iota(shape, dim):
    return lax.broadcasted_iota(jnp.int32, shape, dim)


def place_of(row):
    return (row & 3) * CLASS_ROWS + ((row >> 2) & 7) * FAR_ROWS + (row >> 5)


def row_at(place):
    return (place & 15) * RATE_FAR + ((place >> 4) & 7) * RATE_MID + (place >> 7)


def layer_norm(as_float, gain):
    mean_val = jnp.mean(as_float, -1, keepdims=True)
    centered = as_float - mean_val
    variance = jnp.mean(centered * centered, -1, keepdims=True)
    return (centered * lax.rsqrt(variance + EPS) * gain.astype(jnp.float32)).astype(jnp.bfloat16)


def matmul(left, right):
    return jnp.dot(left, right, preferred_element_type=jnp.float32)


def matmul_t(left, right):
    return lax.dot_general(
        left, right, (((1,), (1,)), ((), ())), preferred_element_type=jnp.float32
    )


def slide_of(positions, ends):
    index = (positions >= ends[0]).astype(jnp.int32)
    for end in ends[1:]:
        index = index + (positions >= end).astype(jnp.int32)
    return index


def slide_ends(tiles_ref):
    ends = [tiles_ref[0]]
    for slide in range(1, SLIDES - 1):
        ends.append(ends[-1] + tiles_ref[slide])
    return ends


def query_marks(positions, ends):
    rows = positions.shape[0]
    lane = iota((rows, LANES), 1)
    return (lane == slide_of(positions, ends)).astype(jnp.bfloat16)


def key_marks(positions, ends):
    rows = positions.shape[0]
    lane = iota((rows, LANES), 1)
    hide = (lane < SLIDES) & (lane != slide_of(positions, ends))
    marks = jnp.where(hide, HIDDEN_SCORE, jnp.where(lane == SLIDES, 1.0, 0.0))
    return marks.astype(jnp.bfloat16)


def head_lanes(value, head):
    lane = iota(value.shape, 1)
    keep = lane < HEAD_DIM if head != 1 else lane >= HEAD_DIM
    return jnp.where(keep, value, jnp.zeros_like(value))


def tile(index):
    return slice(index * LANES, (index + 1) * LANES)


def project_kernel(tokens, gain, w_query, w_key, w_value, query, keyval, mid, far):
    mp = lax.axis_index("mp")
    normed = layer_norm(tokens[...].astype(jnp.float32), gain[...])
    order = iota((ROWS, ROWS), 0) == place_of(iota((ROWS, ROWS), 1))
    normed = matmul(order.astype(jnp.bfloat16), normed).astype(jnp.bfloat16)
    scaled = (matmul_t(normed, w_query[...]) * (1.0 / 8.0)).astype(jnp.bfloat16)
    query[:, :192] = scaled
    query[:, 192:] = jnp.zeros((ROWS, 64), jnp.bfloat16)
    key = matmul_t(normed, w_key[...]).astype(jnp.bfloat16)
    value = matmul_t(normed, w_value[...]).astype(jnp.bfloat16)
    keyval[:, tile(0)] = key[:, :128]
    keyval[:, tile(1)] = value[:, :128]
    keyval[:, tile(2)] = jnp.concatenate([key[:, 128:], value[:, 128:]], 1)

    def pick(source, index, rows):
        starts = []
        for head in range(LOCAL_HEADS):
            number = mp * LOCAL_HEADS + head
            start = (number & 3) * CLASS_ROWS
            if rows == FAR_ROWS:
                start = start + (number >> 2) * FAR_ROWS
            starts.append(pl.ds(pl.multiple_of(start, rows), rows))
        if index == KEY_TILE[2] and source is keyval or index == QUERY_TILE[2] and source is query:
            return source[starts[2], tile(index)]
        low, high = source[starts[0], tile(index)], source[starts[1], tile(index)]
        return jnp.where(iota(low.shape, 1) < HEAD_DIM, low, high)

    for index in range(3):
        mid[:, tile(index)] = pick(keyval, index, CLASS_ROWS)
    picked = [pick(query, index, FAR_ROWS) for index in range(2)]
    picked += [pick(keyval, index, FAR_ROWS) for index in range(3)]
    for index in range(5):
        for copy in range(FAR_GROUP):
            far[copy, :, tile(index)] = picked[index]


def attend(query, keys, values):
    scores = matmul_t(query, keys)
    peak = jnp.max(scores, -1, keepdims=True)
    weights = jnp.exp(scores - peak).astype(jnp.bfloat16)
    return peak, matmul(weights, values)


def marks_near(seq, ends, steps):
    rows = row_at(iota((ROWS, LANES), 0))
    return jnp.concatenate([key_marks(rows + (seq ^ step) * ROWS, ends) for step in steps], 0)


def near_kernel(tiles, query, own, side, peaks, sums):
    ends = slide_ends(tiles)
    seq = lax.axis_index("seq")
    marks = query_marks(row_at(iota((ROWS, LANES), 0)) + seq * ROWS, ends)
    keys_marks = marks_near(seq, ends, (0, 2))
    for head in range(LOCAL_HEADS):
        key_tile, value_tile = tile(KEY_TILE[head]), tile(VALUE_TILE[head])
        asked = head_lanes(query[:, tile(QUERY_TILE[head])], head)
        keys = jnp.concatenate([own[:, key_tile], side[:, key_tile]], 0)
        values = jnp.concatenate([own[:, value_tile], side[:, value_tile]], 0)
        peak, total = attend(
            jnp.concatenate([asked, marks], 1),
            jnp.concatenate([keys, keys_marks], 1),
            jnp.concatenate([values, keys_marks], 1),
        )
        peaks[head] = jnp.broadcast_to(peak, (ROWS, LANES))
        sums[head] = total


def join(peaks, sums, head, rows, peak, total):
    held = peaks[head, rows, :][:, :1]
    largest = jnp.maximum(held, peak)
    sums[head, rows, :] = sums[head, rows, :] * jnp.exp(held - largest) + total * jnp.exp(
        peak - largest
    )
    peaks[head, rows, :] = jnp.broadcast_to(largest, (largest.shape[0], LANES))


def rest_kernel(tiles, query, own, side, mid_a, mid_b, swapped, peaks_in, sums_in, peaks, sums):
    ends = slide_ends(tiles)
    seq, mp = lax.axis_index("seq"), lax.axis_index("mp")
    marks = query_marks(row_at(iota((ROWS, LANES), 0)) + seq * ROWS, ends)
    near_marks = marks_near(seq, ends, (1, 3))
    peaks[...] = peaks_in[...]
    sums[...] = sums_in[...]
    for head in range(LOCAL_HEADS):
        key_tile, value_tile = tile(KEY_TILE[head]), tile(VALUE_TILE[head])
        asked = head_lanes(query[:, tile(QUERY_TILE[head])], head)
        peak, total = attend(
            jnp.concatenate([asked, marks], 1),
            jnp.concatenate([swapped[: 2 * ROWS, key_tile], near_marks], 1),
            jnp.concatenate([swapped[: 2 * ROWS, value_tile], near_marks], 1),
        )
        join(peaks, sums, head, slice(None), peak, total)

        offset = (mp * LOCAL_HEADS + head) & 3
        start = pl.multiple_of(offset * CLASS_ROWS, CLASS_ROWS)
        picked = pl.ds(start, CLASS_ROWS)
        place = iota((CLASS_ROWS, LANES), 0)
        class_rows = offset + RATE_MID * ((place >> 4) + ((place & 15) << 3))
        class_marks = jnp.concatenate(
            [key_marks(class_rows + (seq ^ step) * ROWS, ends) for step in (0, 2, 1, 3, 4, 6, 5, 7)],
            0,
        )
        asked = head_lanes(query[picked, tile(QUERY_TILE[head])], head)
        asked = jnp.concatenate([asked, query_marks(class_rows + seq * ROWS, ends)], 1)

        def gathered(lanes):
            return jnp.concatenate(
                [
                    own[picked, lanes],
                    side[picked, lanes],
                    swapped[picked, lanes],
                    swapped[pl.ds(start + ROWS, CLASS_ROWS), lanes],
                    mid_a[:, lanes],
                    mid_b[:, lanes],
                    swapped[2 * ROWS :, lanes],
                ],
                0,
            )

        peak, total = attend(
            asked,
            jnp.concatenate([gathered(key_tile), class_marks], 1),
            jnp.concatenate([gathered(value_tile), class_marks], 1),
        )
        join(peaks, sums, head, picked, peak, total)


def far_kernel(tiles, rows, here, other, parts):
    ends = slide_ends(tiles)
    seq, mp = lax.axis_index("seq"), lax.axis_index("mp")
    column = seq & 15
    beside = column ^ ((seq >> 4) << 1)
    count = FAR_GROUP * FAR_ROWS
    shape = (count, 2 * count)

    def position(place, holder):
        return ((place >> 4) * 16 + holder) * ROWS + (place & 15) * RATE_FAR

    at = iota(shape, 1)
    holder = jnp.where(at < count, beside, beside ^ 1)
    key_at = position(at & (count - 1), holder)
    query_at = position(iota(shape, 0), column)
    lane = iota((count, LANES), 1)
    for head in range(LOCAL_HEADS):
        number = mp * LOCAL_HEADS + head
        key_tile, value_tile = tile(KEY_TILE[head]), tile(VALUE_TILE[head])
        asked = rows[:, :, tile(QUERY_TILE[head])].reshape(count, LANES)
        asked = head_lanes(asked, head)
        scores = matmul_t(asked, jnp.concatenate([here[:, key_tile], other[:, key_tile]], 0))
        same = slide_of(query_at + number, ends) == slide_of(key_at + number, ends)
        scores = jnp.where(same, scores, HIDDEN_SCORE)
        peak = jnp.max(scores, -1, keepdims=True)
        weights = jnp.exp(scores - peak)
        total = jnp.sum(weights, -1, keepdims=True)
        values = jnp.concatenate([here[:, value_tile], other[:, value_tile]], 0)
        part = matmul(weights.astype(jnp.bfloat16), values)
        spare = SPARE[head]
        part = jnp.where(lane == spare, peak, jnp.where(lane == spare + 1, total, part))
        parts[:, :, tile(head)] = part.reshape(FAR_GROUP, FAR_ROWS, LANES)


def finish_kernel(parts, peaks_in, sums_in, mixed, far_out, peaks, sums):
    mp = lax.axis_index("mp")
    peaks[...] = peaks_in[...]
    sums[...] = sums_in[...]
    lane = iota((FAR_ROWS, LANES), 1)
    far_parts = []
    for head in range(LOCAL_HEADS):
        spare = SPARE[head]
        pieces = [parts[index, :, tile(head)] for index in range(FAR_GROUP)]
        tops = [piece[:, spare : spare + 1] for piece in pieces]
        peak = functools.reduce(jnp.maximum, tops)
        total = jnp.zeros((FAR_ROWS, LANES), jnp.float32)
        for piece, top in zip(pieces, tops):
            total = total + piece * jnp.exp(top - peak)
        weight = total[:, spare + 1 : spare + 2]
        far_parts.append(total / weight)
        number = mp * LOCAL_HEADS + head
        start = (number & 3) * CLASS_ROWS + (number >> 2) * FAR_ROWS
        picked = pl.ds(pl.multiple_of(start, FAR_ROWS), FAR_ROWS)
        stats = jnp.where(lane == SLIDES, weight, 0.0)
        join(peaks, sums, head, picked, peak, jnp.concatenate([total, stats], 1))

    def packed(values):
        first = jnp.where(iota(values[0].shape, 1) < HEAD_DIM, values[0], values[1])
        return first.astype(jnp.bfloat16), values[2].astype(jnp.bfloat16)

    first, last = packed(far_parts)
    far_out[:, :128] = first
    far_out[:, 128:] = last[:, HEAD_DIM:]
    back = (place_of(iota((ROWS, ROWS), 0)) == iota((ROWS, ROWS), 1)).astype(jnp.bfloat16)
    first, last = packed(
        [
            sums[head, :, :LANES] / sums[head, :, LANES + SLIDES : LANES + SLIDES + 1]
            for head in range(LOCAL_HEADS)
        ]
    )
    first = matmul(back, first).astype(jnp.bfloat16)
    last = matmul(back, last).astype(jnp.bfloat16)
    half = ROWS // 2
    last = jnp.concatenate([last[:half, HEAD_DIM:], last[half:, HEAD_DIM:]], 1)
    for copy in range(4):
        mixed[copy, :ROWS, :] = first
        mixed[copy, ROWS:, :] = last


def ffn_kernel(tokens, mixed, w_out, gain, w_up, w_down, attended, partial, held):
    half = ROWS // 2
    low = iota((half, LANES), 1) < HEAD_DIM
    none = jnp.zeros((half, LANES), jnp.bfloat16)
    summed = jnp.zeros((ROWS, 768), jnp.float32)
    for group in range(4):
        start = 192 * group
        summed = summed + matmul(mixed[group, :ROWS, :], w_out[start : start + 128, :])
        last = mixed[group, ROWS:, :]
        spread = jnp.concatenate([jnp.where(low, last, none), jnp.where(low, none, last)], 0)
        weight = w_out[start + 128 : start + 192, :]
        summed = summed + matmul(spread, jnp.concatenate([weight, weight], 0))
    summed = summed.astype(jnp.bfloat16)
    held[...] = summed
    attended[...] = held[pl.ds(pl.multiple_of(lax.axis_index("mp") * 128, 128), 128), :]
    normed = layer_norm(tokens[...].astype(jnp.float32) + summed.astype(jnp.float32), gain[...])
    raised = matmul(normed, w_up[...])
    hidden = (0.5 * raised * (1.0 + lax.erf(raised * 0.7071067811865476))).astype(jnp.bfloat16)
    partial[...] = matmul(hidden, w_down[...]).astype(jnp.bfloat16).reshape(4, 128, 768)


def call(kernel, micros, outs, ins, scratch=()):
    places = {"smem": pltpu.SMEM, "vmem": pltpu.VMEM}
    return pl.pallas_call(
        kernel,
        out_shape=[jax.ShapeDtypeStruct(*out) for out in outs],
        in_specs=[pl.BlockSpec(memory_space=places[where]) for _, where in ins],
        out_specs=[pl.BlockSpec(memory_space=pltpu.VMEM) for _ in outs],
        scratch_shapes=list(scratch),
        cost_estimate=pl.CostEstimate(
            flops=int(micros * 1.1e9), bytes_accessed=int(micros * 1e6), transcendentals=0
        ),
        compiler_params=pltpu.CompilerParams(vmem_limit_bytes=VMEM),
    )(*[array for array, _ in ins])


def swap(value, step):
    return lax.ppermute(value, "seq", [(i, i ^ step) for i in range(lax.axis_size("seq"))])


def local(tokens, slide_tiles, attn_gain, w_query, w_key, w_value, w_out, ffn_gain, w_up, w_down):
    bf16, f32 = jnp.bfloat16, jnp.float32
    v, s = "vmem", "smem"
    columns = [[16 * z + place for z in range(FAR_GROUP)] for place in range(16)]
    across = [
        (16 * z + (place ^ (2 * z)), 16 * z + place) for z in range(FAR_GROUP) for place in range(16)
    ]
    query, own, mid, far = call(
        project_kernel,
        4,
        [
            ((ROWS, 256), bf16), ((ROWS, 384), bf16), ((CLASS_ROWS, 384), bf16),
            ((FAR_GROUP, FAR_ROWS, 640), bf16),
        ],
        [(tokens, v), (attn_gain, v), (w_query.T, v), (w_key.T, v), (w_value.T, v)],
    )
    side = swap(own, 2)
    mid_a, mid_b = swap(mid, 4), swap(mid, 6)
    w_out_all = lax.all_gather(w_out, "mp", axis=0, tiled=True)
    far_rows = lax.all_to_all(
        far, "seq", split_axis=0, concat_axis=0, tiled=True, axis_index_groups=columns
    )
    far_here = lax.ppermute(far_rows[:, :, 256:].reshape(128, 384), "seq", across)
    swapped = swap(jnp.concatenate([own, side, mid_a, mid_b], 0), 1)
    far_other = swap(far_here, 1)
    state = [((LOCAL_HEADS, ROWS, LANES), f32), ((LOCAL_HEADS, ROWS, 256), f32)]
    held = [pltpu.VMEM(*shape) for shape in state]
    peaks, sums = call(
        near_kernel, 5, state, [(slide_tiles, s), (query, v), (own, v), (side, v)]
    )
    (parts,) = call(
        far_kernel,
        2,
        [((FAR_GROUP, FAR_ROWS, 384), f32)],
        [(slide_tiles, s), (far_rows, v), (far_here, v), (far_other, v)],
    )
    peaks, sums = call(
        rest_kernel,
        7,
        state,
        [
            (slide_tiles, s), (query, v), (own, v), (side, v), (mid_a, v), (mid_b, v), (swapped, v),
            (peaks, v), (sums, v),
        ],
    )
    parts = lax.all_to_all(
        parts, "seq", split_axis=0, concat_axis=0, tiled=True, axis_index_groups=columns
    )
    mixed, far_attended = call(
        finish_kernel,
        2,
        [((4, 768, LANES), bf16), ((FAR_ROWS, 192), bf16)],
        [(parts, v), (peaks, v), (sums, v)],
        held,
    )
    mixed = lax.all_to_all(mixed, "mp", split_axis=0, concat_axis=0, tiled=True)
    attended, partial = call(
        ffn_kernel,
        6,
        [((ROWS // 4, 768), bf16), ((4, 128, 768), bf16)],
        [(tokens, v), (mixed, v), (w_out_all, v), (ffn_gain, v), (w_up, v), (w_down, v)],
        [pltpu.VMEM((ROWS, 768), bf16)],
    )
    terms = lax.all_to_all(partial, "mp", split_axis=0, concat_axis=0, tiled=True)
    ffn_out = jnp.sum(terms.astype(f32), 0).astype(bf16)
    return (attended, far_attended, ffn_out)


def solution(mesh):
    return jax.shard_map(
        local,
        mesh=mesh,
        in_specs=(
            P("seq", None),
            P(),
            P(),
            P(None, "mp"),
            P(None, "mp"),
            P(None, "mp"),
            P("mp", None),
            P(),
            P(None, "mp"),
            P("mp", None),
        ),
        out_specs=(P(("seq", "mp"), None), P("seq", "mp"), P(("seq", "mp"), None)),
        check_vma=False,
    )
```

time: 181 us -> 130 us (0.72)
  waiting for transfers between devices: 81.9 us -> 17.2 us
  starting transfers between devices: 30.2 us -> 48.2 us
  blocking collectives: 20.8 us -> 14 us
  Pallas kernels: 25.4 us -> 30 us
  local copies, waits for them, and re-layouts: 6.71 us -> 3.21 us
    all_gather x1 -> x0, waiting for transfers between devices: 44.8 us -> none  [local(): far_all = lax.all_gather(far, 'seq', axis=0, tiled=True)]
    all_to_all x0 -> x3, starting transfers between devices: none -> 29 us  [the longest x1 14.9 us: local(): lax.all_to_all(parts, 'seq', split_axis=0, concat_axis=0, tiled=True, axi...]
    reduce_scatter x1 -> x0, waiting for transfers between devices: 24 us -> none  [local(): ffn_out = lax.psum_scatter(partial, 'mp', scatter_dimension=0, tiled=True)]
    all_gather x1 -> x0, blocking collectives: 20.8 us -> none  [local(): mixed_all = lax.all_gather(mixed, 'mp', axis=0)]
    all_to_all x0 -> x3, waiting for transfers between devices: none -> 17.1 us  [the longest x1 11.4 us: local(): mixed = lax.all_to_all(mixed, 'mp', split_axis=0, concat_axis=0, tiled=True)]
    all_to_all x0 -> x1, blocking collectives: none -> 14 us  [local(): lax.all_to_all(partial, 'mp', split_axis=0, concat_axis=0, tiled=True)]
    ppermute x7 -> x5, starting transfers between devices: 30.1 us -> 18.5 us  [swap(): lax.ppermute(value, 'seq', [(i, i ^ step) for i in range(lax.axis_size('s...]
    ppermute x7 -> x5, waiting for transfers between devices: 8.5 us -> 0.01 us  [swap(): lax.ppermute(value, 'seq', [(i, i ^ step) for i in range(lax.axis_size('s...]
  transfers between devices with their start and end apart: 10 -> 10, of which waited for: 6 -> 3; matrix products, arithmetic and copies ran while one was open for 1% -> 1% of each run, Pallas kernels for 8% -> 14%
where the time goes in v2:
time: 130 us; the launch traced here: 129 us
  starting transfers between devices  48.2 us (37%)
  Pallas kernels  30 us (23%)
  waiting for transfers between devices  17.2 us (13%)
  between operations  14.2 us (11%)
  blocking collectives  14 us (11%)
  local copies, waits for them, and re-layouts  3.21 us (2%)
  other arithmetic  2.1 us (2%)
    pallas_call x6, Pallas kernels, call(): pl.pallas_call(kernel, out_shape=[jax.ShapeDtypeStruct(*out) for out in o...  30 us
    ppermute x5, starting transfers between devices, swap(): lax.ppermute(value, 'seq', [(i, i ^ step) for i in range(lax.axis_size('s...  18.5 us
    all_to_all x1, starting transfers between devices, local(): lax.all_to_all(parts, 'seq', split_axis=0, concat_axis=0, tiled=True, axi...  14.9 us
    all_to_all x1, blocking collectives, local(): lax.all_to_all(partial, 'mp', split_axis=0, concat_axis=0, tiled=True)  14 us
    all_to_all x1, waiting for transfers between devices, local(): mixed = lax.all_to_all(mixed, 'mp', split_axis=0, concat_axis=0, tiled=True)  11.4 us
    all_to_all x1, starting transfers between devices, local(): lax.all_to_all(far, 'seq', split_axis=0, concat_axis=0, tiled=True, axis_...  10 us
    all_to_all x1, starting transfers between devices, local(): mixed = lax.all_to_all(mixed, 'mp', split_axis=0, concat_axis=0, tiled=True)  4.01 us
    all_to_all x1, waiting for transfers between devices, local(): lax.all_to_all(far, 'seq', split_axis=0, concat_axis=0, tiled=True, axis_...  3.35 us
  transfers between devices with their start and end apart: 10, of which 3 were waited for; matrix products, arithmetic and copies ran while one was open for 1% of the time, Pallas kernels for 14%

profile of v2, /device:TPU:1, one launch (start us, length us, event | category | flops | bytes accessed | tf_op | source)
XLA Modules:
  0.0 128.8 jit_solution(2377820061701149029)
XLA Ops:
  7.2 4.0 %shard_map.121 = (bf16[512,256]{1,0:T(8,128)(2,1)}, bf16[512,384]{1,0:T(8,128)(2,1)}, bf16[128,384]{1,0:T(8,128)(2,1)}, bf16[8,16,640]{2,1,0:T(8,128)(2,1)}) custom-call(bf16[512,768]{1,0:T(8,128)(2,1)} %tokens.3, bf16[768]{0:T(1024)(128)(2,1)} %gain.2, bf16[192,768]{1,0:T(8,128)(2,1)} %bitcast.5, bf16[192,768]{1,0:T(8,128)(2,1)} %bitcast.6, ...), custom_call_target="tpu_custom_call" | custom-call | flops 4400000000 | bytes 4000000 | tf_op jit(solution)/shard_map/pallas_call | solution.py:326
  11.2 4.0 %collective-permute-start.2 = (bf16[512,384]{1,0:T(8,128)(2,1)}, bf16[512,384]{1,0:T(8,128)(2,1)S(1)}, u32[]{:S(2)}, u32[]{:S(2)}) collective-permute-start(bf16[512,384]{1,0:T(8,128)(2,1)} %get-tuple-element.17.own), channel_id=1, source_target_pairs={{0,8},{4,12},{8,0},{12,4},{16,24},{20,28},{24,16},{28,20},{32,40},... | collective-permute-start | bytes 1179656 | tf_op jit(solution)/shard_map/ppermute | solution.py:340
  15.2 4.2 %collective-permute-start.3 = (bf16[128,384]{1,0:T(8,128)(2,1)}, bf16[128,384]{1,0:T(8,128)(2,1)S(1)}, u32[]{:S(2)}, u32[]{:S(2)}) collective-permute-start(bf16[128,384]{1,0:T(8,128)(2,1)} %get-tuple-element.18), channel_id=1, source_target_pairs={{0,16},{4,20},{8,24},{12,28},{16,0},{20,4},{24,8},{28,12},{32,48},... | collective-permute-start | bytes 294920 | tf_op jit(solution)/shard_map/ppermute | solution.py:340
  19.4 1.9 %collective-permute-start.4 = (bf16[128,384]{1,0:T(8,128)(2,1)}, bf16[128,384]{1,0:T(8,128)(2,1)S(1)}, u32[]{:S(2)}, u32[]{:S(2)}) collective-permute-start(bf16[128,384]{1,0:T(8,128)(2,1)} %get-tuple-element.18), channel_id=1, source_target_pairs={{0,24},{4,28},{8,16},{12,20},{16,8},{20,12},{24,0},{28,4},{32,56},... | collective-permute-start | bytes 294920 | tf_op jit(solution)/shard_map/ppermute | solution.py:340
  21.4 10.0 %all-to-all-start = ((bf16[8,16,640]{2,1,0:T(8,128)(2,1)}), bf16[8,16,640]{2,1,0:T(8,128)(2,1)S(1)}, u32[]{:S(2)}, u32[]{:S(2)}) async-start(bf16[8,16,640]{2,1,0:T(8,128)(2,1)} %get-tuple-element.15), calls=%async_computation | async-start | bytes 327680 | tf_op jit(solution)/shard_map/all_to_all | solution.py:362
  31.4 0.0 all-gather.2.cloned.1.call-start
  31.5 0.0 collective-permute-done.3.mid_a
  31.5 0.0 copy-start.4
  31.5 0.0 collective-permute-done.4.mid_b
  31.5 0.0 copy-start.5
  31.5 0.0 collective-permute-done.2.side
  31.5 0.0 copy-start.2
  31.5 1.3 pad_maximum_fusion
  32.8 3.6 %collective-permute-start.5 = (bf16[1280,384]{1,0:T(8,128)(2,1)S(1)}, bf16[1280,384]{1,0:T(8,128)(2,1)S(1)}, u32[]{:S(2)}, u32[]{:S(2)}) collective-permute-start(bf16[1280,384]{1,0:T(8,128)(2,1)S(1)} %pad_maximum_fusion), channel_id=1, source_target_pairs={{0,4},{4,0},{8,12},{12,8},{16,20},{20,16},{24,28},{28,24},{32,36},... | collective-permute-start | bytes 2949128 | tf_op jit(solution)/shard_map/ppermute | solution.py:340
  36.4 3.4 %all-to-all-done.rows = bf16[8,16,640]{2,1,0:T(8,128)(2,1)S(1)} async-done(((bf16[8,16,640]{2,1,0:T(8,128)(2,1)}), bf16[8,16,640]{2,1,0:T(8,128)(2,1)S(1)}, u32[]{:S(2)}, u32[]{:S(2)}) %all-to-all-start) | async-done | bytes 163872 | tf_op jit(solution)/shard_map/all_to_all | solution.py:362
  39.8 0.0 copy-start.1
  39.8 0.7 collective-permute-start
  40.5 0.0 all-gather.2.cloned.1.call-update
  40.5 0.0 collective-permute-done.here
  40.5 0.0 copy-start.7
  40.5 4.7 %collective-permute-start.1 = (bf16[128,384]{1,0:T(8,128)(2,1)S(1)}, bf16[128,384]{1,0:T(8,128)(2,1)S(1)}, u32[]{:S(2)}, u32[]{:S(2)}) collective-permute-start(bf16[128,384]{1,0:T(8,128)(2,1)S(1)} %collective-permute-done.here), channel_id=1, source_target_pairs={{0,4},{4,0},{8,12},{12,8},{16,20},{20,16},{24,28},{28,24},{32,36},... | collective-permute-start | bytes 294920 | tf_op jit(solution)/shard_map/ppermute | solution.py:340
  45.2 0.0 copy-done.2
  45.2 4.9 %shard_map.123 = (f32[3,512,128]{2,1,0:T(8,128)}, f32[3,512,256]{2,1,0:T(8,128)}) custom-call(s32[4]{0:T(128)} %tiles.5, bf16[512,256]{1,0:T(8,128)(2,1)} %get-tuple-element.16.query, bf16[512,384]{1,0:T(8,128)(2,1)} %get-tuple-element.17.own, bf16[512,384]{1,0:T(8,128)(2,1)} %copy-done.2), custom_call_target="tpu_custom_call" | custom-call | flops 5500000256 | bytes 5000000 | tf_op jit(solution)/shard_map/pallas_call | solution.py:326
  50.2 0.0 copy-done.4
  50.2 0.0 copy-done.5
  50.2 0.0 copy-done.1
  50.2 0.0 copy-done.7
  50.2 0.0 collective-permute-done.1.other
  50.2 0.0 copy-start.8
  50.2 0.6 copy-done.8
  50.9 2.4 %shard_map.122 = f32[8,16,384]{2,1,0:T(8,128)} custom-call(s32[4]{0:T(128)} %tiles.5, bf16[8,16,640]{2,1,0:T(8,128)(2,1)} %copy-done.1, bf16[128,384]{1,0:T(8,128)(2,1)} %copy-done.7, bf16[128,384]{1,0:T(8,128)(2,1)} %copy-done.8), custom_call_target="tpu_custom_call" | custom-call | flops 2200000000 | bytes 2000000 | tf_op jit(solution)/shard_map/pallas_call | solution.py:326
  53.2 14.9 %all-to-all-start.1 = ((f32[8,16,384]{2,1,0:T(8,128)}), f32[8,16,384]{2,1,0:T(8,128)S(1)}, u32[]{:S(2)}, u32[]{:S(2)}) async-start(f32[8,16,384]{2,1,0:T(8,128)} %shard_map.122), calls=%async_computation.1 | async-start | bytes 393216 | tf_op jit(solution)/shard_map/all_to_all | solution.py:388
  68.1 0.0 collective-permute-done.5.swapped
  68.1 0.0 copy-start.6
  68.2 1.0 copy-done.6
  69.1 7.5 %shard_map.124 = (f32[3,512,128]{2,1,0:T(8,128)}, f32[3,512,256]{2,1,0:T(8,128)}) custom-call(s32[4]{0:T(128)} %tiles.5, bf16[512,256]{1,0:T(8,128)(2,1)} %get-tuple-element.16.query, bf16[512,384]{1,0:T(8,128)(2,1)} %get-tuple-element.17.own, bf16[512,384]{1,0:T(8,128)(2,1)} %copy-done.2, bf16[128,384]{1,0:T(8,128)(2,1)} %copy-done.4, ...), custom_call_target="tpu_custom_call" | custom-call | flops 7699999744 | bytes 7000000 | tf_op jit(solution)/shard_map/pallas_call | solution.py:326
  76.6 2.4 %all-to-all-done.1.parts = f32[8,16,384]{2,1,0:T(8,128)S(1)} async-done(((f32[8,16,384]{2,1,0:T(8,128)}), f32[8,16,384]{2,1,0:T(8,128)S(1)}, u32[]{:S(2)}, u32[]{:S(2)}) %all-to-all-start.1) | async-done | bytes 196640 | tf_op jit(solution)/shard_map/all_to_all | solution.py:388
  78.9 0.0 copy-start.3
  78.9 0.7 copy-done.3
  79.6 3.5 %shard_map.125 = (bf16[4,768,128]{2,1,0:T(8,128)(2,1)}, bf16[16,192]{1,0:T(8,128)(2,1)}) custom-call(f32[8,16,384]{2,1,0:T(8,128)} %copy-done.3, f32[3,512,128]{2,1,0:T(8,128)} %get-tuple-element.21.peaks_in, f32[3,512,256]{2,1,0:T(8,128)} %get-tuple-element.22.sums_in), custom_call_target="tpu_custom_call" | custom-call | flops 2200000000 | bytes 2000000 | tf_op jit(solution)/shard_map/pallas_call | solution.py:326
  83.1 4.0 %all-to-all-start.2 = ((bf16[4,768,128]{2,1,0:T(8,128)(2,1)}), bf16[4,768,128]{2,1,0:T(8,128)(2,1)S(1)}, u32[]{:S(2)}, u32[]{:S(2)}) async-start(bf16[4,768,128]{2,1,0:T(8,128)(2,1)} %get-tuple-element.23), calls=%async_computation.2 | async-start | bytes 1572864 | tf_op jit(solution)/shard_map/all_to_all | solution.py:398
  87.1 0.0 all-gather.2.cloned.1.call-done.w_out
  87.1 11.4 %all-to-all-done.2.mixed = bf16[4,768,128]{2,1,0:T(8,128)(2,1)S(1)} async-done(((bf16[4,768,128]{2,1,0:T(8,128)(2,1)}), bf16[4,768,128]{2,1,0:T(8,128)(2,1)S(1)}, u32[]{:S(2)}, u32[]{:S(2)}) %all-to-all-start.2) | async-done | bytes 786464 | tf_op jit(solution)/shard_map/all_to_all | solution.py:398
  98.6 0.0 copy-start
  98.6 0.9 copy-done
  99.5 7.7 %shard_map.126 = (bf16[128,768]{1,0:T(8,128)(2,1)}, bf16[4,128,768]{2,1,0:T(8,128)(2,1)}) custom-call(bf16[512,768]{1,0:T(8,128)(2,1)} %tokens.3, bf16[4,768,128]{2,1,0:T(8,128)(2,1)} %copy-done, bf16[768,768]{1,0:T(8,128)(2,1)} %all-gather.2.cloned.1.call-done.w_out, bf16[768]{0:T(1024)(128)(2,1)} %gain.3, bf16[768,768]{1,0:T(8,128)(2,1)} %w_up.1, ...), custom_call_target="tpu_custom_call" | custom-call | flops 6600000000 | bytes 6000000 | tf_op jit(solution)/shard_map/pallas_call | solution.py:326
  107.2 14.0 %all_to_all.20 = bf16[4,128,768]{2,1,0:T(8,128)(2,1)S(1)} all-to-all(bf16[4,128,768]{2,1,0:T(8,128)(2,1)} %get-tuple-element.26), channel_id=1, replica_groups=mesh['seq'=128,'mp'=4] {'mp'}, dimensions={0} | all-to-all | bytes 1572864 | tf_op jit(solution)/shard_map/all_to_all | solution.py:406
  121.1 0.8 reduce_sum.12
  (1 shorter events, 0.0 us)
Async XLA Ops:
  11.2 20.3 %collective-permute-start.2 = (bf16[512,384]{1,0:T(8,128)(2,1)}, bf16[512,384]{1,0:T(8,128)(2,1)S(1)}, u32[]{:S(2)}, u32[]{:S(2)}) collective-permute-start(bf16[512,384]{1,0:T(8,128)(2,1)} %get-tuple-element.17.own), channel_id=1, source_target_pairs={{0,8},{4,12},{8,0},{12,4},{16,24},{20,28},{24,16},{28,20},{32,40},... | collective-permute-start | bytes 1179656 | tf_op jit(solution)/shard_map/ppermute | solution.py:340
  15.2 16.2 %collective-permute-start.3 = (bf16[128,384]{1,0:T(8,128)(2,1)}, bf16[128,384]{1,0:T(8,128)(2,1)S(1)}, u32[]{:S(2)}, u32[]{:S(2)}) collective-permute-start(bf16[128,384]{1,0:T(8,128)(2,1)} %get-tuple-element.18), channel_id=1, source_target_pairs={{0,16},{4,20},{8,24},{12,28},{16,0},{20,4},{24,8},{28,12},{32,48},... | collective-permute-start | bytes 294920 | tf_op jit(solution)/shard_map/ppermute | solution.py:340
  19.4 12.0 %collective-permute-start.4 = (bf16[128,384]{1,0:T(8,128)(2,1)}, bf16[128,384]{1,0:T(8,128)(2,1)S(1)}, u32[]{:S(2)}, u32[]{:S(2)}) collective-permute-start(bf16[128,384]{1,0:T(8,128)(2,1)} %get-tuple-element.18), channel_id=1, source_target_pairs={{0,24},{4,28},{8,16},{12,20},{16,8},{20,12},{24,0},{28,4},{32,56},... | collective-permute-start | bytes 294920 | tf_op jit(solution)/shard_map/ppermute | solution.py:340
  21.4 18.4 %all-to-all-start = ((bf16[8,16,640]{2,1,0:T(8,128)(2,1)}), bf16[8,16,640]{2,1,0:T(8,128)(2,1)S(1)}, u32[]{:S(2)}, u32[]{:S(2)}) async-start(bf16[8,16,640]{2,1,0:T(8,128)(2,1)} %get-tuple-element.15), calls=%async_computation | async-start | bytes 327680 | tf_op jit(solution)/shard_map/all_to_all | solution.py:362
  31.4 55.7 %all-gather.2.cloned.1.call-start = ((), (), s32[]{:S(2)}) async-start(), calls=%async_computation.4 | async-start | bytes 1474560 | tf_op jit(solution)/shard_map/all_gather | solution.py:361
  31.5 18.7 %copy-start.4 = (bf16[128,384]{1,0:T(8,128)(2,1)}, bf16[128,384]{1,0:T(8,128)(2,1)S(1)}, u32[]{:S(2)}) copy-start(bf16[128,384]{1,0:T(8,128)(2,1)S(1)} %collective-permute-done.3.mid_a) | copy-start | bytes 294916
  31.5 18.7 %copy-start.5 = (bf16[128,384]{1,0:T(8,128)(2,1)}, bf16[128,384]{1,0:T(8,128)(2,1)S(1)}, u32[]{:S(2)}) copy-start(bf16[128,384]{1,0:T(8,128)(2,1)S(1)} %collective-permute-done.4.mid_b) | copy-start | bytes 294916
  31.5 13.7 %copy-start.2 = (bf16[512,384]{1,0:T(8,128)(2,1)}, bf16[512,384]{1,0:T(8,128)(2,1)S(1)}, u32[]{:S(2)}) copy-start(bf16[512,384]{1,0:T(8,128)(2,1)S(1)} %collective-permute-done.2.side) | copy-start | bytes 1179652
  32.8 35.3 %collective-permute-start.5 = (bf16[1280,384]{1,0:T(8,128)(2,1)S(1)}, bf16[1280,384]{1,0:T(8,128)(2,1)S(1)}, u32[]{:S(2)}, u32[]{:S(2)}) collective-permute-start(bf16[1280,384]{1,0:T(8,128)(2,1)S(1)} %pad_maximum_fusion), channel_id=1, source_target_pairs={{0,4},{4,0},{8,12},{12,8},{16,20},{20,16},{24,28},{28,24},{32,36},... | collective-permute-start | bytes 2949128 | tf_op jit(solution)/shard_map/ppermute | solution.py:340
  39.8 10.4 %copy-start.1 = (bf16[8,16,640]{2,1,0:T(8,128)(2,1)}, bf16[8,16,640]{2,1,0:T(8,128)(2,1)S(1)}, u32[]{:S(2)}) copy-start(bf16[8,16,640]{2,1,0:T(8,128)(2,1)S(1)} %all-to-all-done.rows) | copy-start | bytes 491524
  39.8 0.7 collective-permute-start
  40.5 9.7 %copy-start.7 = (bf16[128,384]{1,0:T(8,128)(2,1)}, bf16[128,384]{1,0:T(8,128)(2,1)S(1)}, u32[]{:S(2)}) copy-start(bf16[128,384]{1,0:T(8,128)(2,1)S(1)} %collective-permute-done.here) | copy-start | bytes 294916
  40.5 9.7 %collective-permute-start.1 = (bf16[128,384]{1,0:T(8,128)(2,1)S(1)}, bf16[128,384]{1,0:T(8,128)(2,1)S(1)}, u32[]{:S(2)}, u32[]{:S(2)}) collective-permute-start(bf16[128,384]{1,0:T(8,128)(2,1)S(1)} %collective-permute-done.here), channel_id=1, source_target_pairs={{0,4},{4,0},{8,12},{12,8},{16,20},{20,16},{24,28},{28,24},{32,36},... | collective-permute-start | bytes 294920 | tf_op jit(solution)/shard_map/ppermute | solution.py:340
  50.2 0.6 copy-start.8
  53.2 25.7 %all-to-all-start.1 = ((f32[8,16,384]{2,1,0:T(8,128)}), f32[8,16,384]{2,1,0:T(8,128)S(1)}, u32[]{:S(2)}, u32[]{:S(2)}) async-start(f32[8,16,384]{2,1,0:T(8,128)} %shard_map.122), calls=%async_computation.1 | async-start | bytes 393216 | tf_op jit(solution)/shard_map/all_to_all | solution.py:388
  68.1 1.0 copy-start.6
  78.9 0.7 copy-start.3
  83.1 15.4 %all-to-all-start.2 = ((bf16[4,768,128]{2,1,0:T(8,128)(2,1)}), bf16[4,768,128]{2,1,0:T(8,128)(2,1)S(1)}, u32[]{:S(2)}, u32[]{:S(2)}) async-start(bf16[4,768,128]{2,1,0:T(8,128)(2,1)} %get-tuple-element.23), calls=%async_computation.2 | async-start | bytes 1572864 | tf_op jit(solution)/shard_map/all_to_all | solution.py:398
  98.6 0.9 copy-start
Sparse Core Ops, SparseCore 0:
  40.6 29.7 all-gather.1

commit v3 on v2

--- a/solution.py
+++ b/solution.py
@@ -16,9 +16,12 @@
 FAR_ROWS = ROWS // RATE_FAR
 LANES = 128
 SLIDES = 4
+WIDTH = 768
+HALF = WIDTH // 2
+BLOCK = 128
 EPS = 1e-05
 HIDDEN_SCORE = -1e30
-VMEM = 56 * 1024 * 1024
+VMEM = 24 * 1024 * 1024
 
 KEY_TILE = (0, 0, 2)
 VALUE_TILE = (1, 1, 2)
@@ -130,11 +133,28 @@
             far[copy, :, tile(index)] = picked[index]
 
 
-def attend(query, keys, values):
+def attend(query, keys, values, head):
     scores = matmul_t(query, keys)
     peak = jnp.max(scores, -1, keepdims=True)
     weights = jnp.exp(scores - peak).astype(jnp.bfloat16)
-    return peak, matmul(weights, values)
+    sums = matmul(weights, values)
+    lane = iota((sums.shape[0], LANES), 1)
+    total = sums[:, LANES + SLIDES : LANES + SLIDES + 1]
+    return peak, pack(sums[:, :LANES], peak, total, head, lane)
+
+
+def pack(sums, peak, total, head, lane):
+    return jnp.where(
+        lane == SPARE[head], peak, jnp.where(lane == SPARE[head] + 1, total, sums)
+    )
+
+
+def join(held, more, peak, head):
+    spare = SPARE[head]
+    before = held[:, spare : spare + 1]
+    largest = jnp.maximum(before, peak)
+    both = held * jnp.exp(before - largest) + more * jnp.exp(peak - largest)
+    return jnp.where(iota(both.shape, 1) == spare, largest, both)
 
 
 def marks_near(seq, ends, steps):
@@ -142,7 +162,7 @@
     return jnp.concatenate([key_marks(rows + (seq ^ step) * ROWS, ends) for step in steps], 0)
 
 
-def near_kernel(tiles, query, own, side, peaks, sums):
+def near_kernel(tiles, query, own, side, state):
     ends = slide_ends(tiles)
     seq = lax.axis_index("seq")
     marks = query_marks(row_at(iota((ROWS, LANES), 0)) + seq * ROWS, ends)
@@ -152,40 +172,29 @@
         asked = head_lanes(query[:, tile(QUERY_TILE[head])], head)
         keys = jnp.concatenate([own[:, key_tile], side[:, key_tile]], 0)
         values = jnp.concatenate([own[:, value_tile], side[:, value_tile]], 0)
-        peak, total = attend(
+        _, state[head] = attend(
             jnp.concatenate([asked, marks], 1),
             jnp.concatenate([keys, keys_marks], 1),
             jnp.concatenate([values, keys_marks], 1),
-        )
-        peaks[head] = jnp.broadcast_to(peak, (ROWS, LANES))
-        sums[head] = total
-
-
-def join(peaks, sums, head, rows, peak, total):
-    held = peaks[head, rows, :][:, :1]
-    largest = jnp.maximum(held, peak)
-    sums[head, rows, :] = sums[head, rows, :] * jnp.exp(held - largest) + total * jnp.exp(
-        peak - largest
-    )
-    peaks[head, rows, :] = jnp.broadcast_to(largest, (largest.shape[0], LANES))
-
-
-def rest_kernel(tiles, query, own, side, mid_a, mid_b, swapped, peaks_in, sums_in, peaks, sums):
+            head,
+        )
+
+
+def rest_kernel(tiles, query, own, side, mid_a, mid_b, swapped, held, state):
     ends = slide_ends(tiles)
     seq, mp = lax.axis_index("seq"), lax.axis_index("mp")
     marks = query_marks(row_at(iota((ROWS, LANES), 0)) + seq * ROWS, ends)
     near_marks = marks_near(seq, ends, (1, 3))
-    peaks[...] = peaks_in[...]
-    sums[...] = sums_in[...]
     for head in range(LOCAL_HEADS):
         key_tile, value_tile = tile(KEY_TILE[head]), tile(VALUE_TILE[head])
         asked = head_lanes(query[:, tile(QUERY_TILE[head])], head)
-        peak, total = attend(
+        peak, more = attend(
             jnp.concatenate([asked, marks], 1),
             jnp.concatenate([swapped[: 2 * ROWS, key_tile], near_marks], 1),
             jnp.concatenate([swapped[: 2 * ROWS, value_tile], near_marks], 1),
-        )
-        join(peaks, sums, head, slice(None), peak, total)
+            head,
+        )
+        state[head] = join(held[head], more, peak, head)
 
         offset = (mp * LOCAL_HEADS + head) & 3
         start = pl.multiple_of(offset * CLASS_ROWS, CLASS_ROWS)
@@ -213,12 +222,13 @@
                 0,
             )
 
-        peak, total = attend(
+        peak, more = attend(
             asked,
             jnp.concatenate([gathered(key_tile), class_marks], 1),
             jnp.concatenate([gathered(value_tile), class_marks], 1),
-        )
-        join(peaks, sums, head, picked, peak, total)
+            head,
+        )
+        state[head, picked, :] = join(state[head, picked, :], more, peak, head)
 
 
 def far_kernel(tiles, rows, here, other, parts):
@@ -250,16 +260,13 @@
         total = jnp.sum(weights, -1, keepdims=True)
         values = jnp.concatenate([here[:, value_tile], other[:, value_tile]], 0)
         part = matmul(weights.astype(jnp.bfloat16), values)
-        spare = SPARE[head]
-        part = jnp.where(lane == spare, peak, jnp.where(lane == spare + 1, total, part))
+        part = pack(part, peak, total, head, lane)
         parts[:, :, tile(head)] = part.reshape(FAR_GROUP, FAR_ROWS, LANES)
 
 
-def finish_kernel(parts, peaks_in, sums_in, mixed, far_out, peaks, sums):
+def finish_kernel(parts, held, w_out, terms, far_out, state):
     mp = lax.axis_index("mp")
-    peaks[...] = peaks_in[...]
-    sums[...] = sums_in[...]
-    lane = iota((FAR_ROWS, LANES), 1)
+    state[...] = held[...]
     far_parts = []
     for head in range(LOCAL_HEADS):
         spare = SPARE[head]
@@ -269,13 +276,11 @@
         total = jnp.zeros((FAR_ROWS, LANES), jnp.float32)
         for piece, top in zip(pieces, tops):
             total = total + piece * jnp.exp(top - peak)
-        weight = total[:, spare + 1 : spare + 2]
-        far_parts.append(total / weight)
+        far_parts.append(total / total[:, spare + 1 : spare + 2])
         number = mp * LOCAL_HEADS + head
         start = (number & 3) * CLASS_ROWS + (number >> 2) * FAR_ROWS
         picked = pl.ds(pl.multiple_of(start, FAR_ROWS), FAR_ROWS)
-        stats = jnp.where(lane == SLIDES, weight, 0.0)
-        join(peaks, sums, head, picked, peak, jnp.concatenate([total, stats], 1))
+        state[head, picked, :] = join(state[head, picked, :], total, peak, head)
 
     def packed(values):
         first = jnp.where(iota(values[0].shape, 1) < HEAD_DIM, values[0], values[1])
@@ -287,38 +292,91 @@
     back = (place_of(iota((ROWS, ROWS), 0)) == iota((ROWS, ROWS), 1)).astype(jnp.bfloat16)
     first, last = packed(
         [
-            sums[head, :, :LANES] / sums[head, :, LANES + SLIDES : LANES + SLIDES + 1]
+            state[head] / state[head, :, SPARE[head] + 1 : SPARE[head] + 2]
             for head in range(LOCAL_HEADS)
         ]
     )
-    first = matmul(back, first).astype(jnp.bfloat16)
-    last = matmul(back, last).astype(jnp.bfloat16)
-    half = ROWS // 2
-    last = jnp.concatenate([last[:half, HEAD_DIM:], last[half:, HEAD_DIM:]], 1)
-    for copy in range(4):
-        mixed[copy, :ROWS, :] = first
-        mixed[copy, ROWS:, :] = last
-
-
-def ffn_kernel(tokens, mixed, w_out, gain, w_up, w_down, attended, partial, held):
-    half = ROWS // 2
-    low = iota((half, LANES), 1) < HEAD_DIM
-    none = jnp.zeros((half, LANES), jnp.bfloat16)
-    summed = jnp.zeros((ROWS, 768), jnp.float32)
-    for group in range(4):
-        start = 192 * group
-        summed = summed + matmul(mixed[group, :ROWS, :], w_out[start : start + 128, :])
-        last = mixed[group, ROWS:, :]
-        spread = jnp.concatenate([jnp.where(low, last, none), jnp.where(low, none, last)], 0)
-        weight = w_out[start + 128 : start + 192, :]
-        summed = summed + matmul(spread, jnp.concatenate([weight, weight], 0))
-    summed = summed.astype(jnp.bfloat16)
-    held[...] = summed
-    attended[...] = held[pl.ds(pl.multiple_of(lax.axis_index("mp") * 128, 128), 128), :]
-    normed = layer_norm(tokens[...].astype(jnp.float32) + summed.astype(jnp.float32), gain[...])
-    raised = matmul(normed, w_up[...])
+    mixed = jnp.concatenate([first, last[:, HEAD_DIM:]], 1)
+    mixed = matmul(back, mixed).astype(jnp.bfloat16)
+    terms[...] = matmul(mixed, w_out[...]).astype(jnp.bfloat16).reshape(4, BLOCK, WIDTH)
+
+
+def weights_kernel(w_up, w_down, out, sems):
+    start = pl.multiple_of((lax.axis_index("seq") & 1) * HALF, HALF)
+    copies = [
+        pltpu.make_async_copy(
+            w_up.at[pl.ds(block * HALF, HALF), pl.ds(start, HALF)],
+            out.at[pl.ds(0, HALF), pl.ds(block * HALF, HALF)],
+            sems.at[block],
+        )
+        for block in range(2)
+    ]
+    copies.append(
+        pltpu.make_async_copy(
+            w_down.at[pl.ds(start, HALF), :], out.at[pl.ds(HALF, HALF), :], sems.at[2]
+        )
+    )
+    for copy in copies:
+        copy.start()
+    for copy in copies:
+        copy.wait()
+
+
+def hidden_part(normed, weights):
+    raised = matmul(normed[:, :HALF], weights[0, :HALF, :HALF])
+    raised = raised + matmul(normed[:, HALF:], weights[0, :HALF, HALF:])
     hidden = (0.5 * raised * (1.0 + lax.erf(raised * 0.7071067811865476))).astype(jnp.bfloat16)
-    partial[...] = matmul(hidden, w_down[...]).astype(jnp.bfloat16).reshape(4, 128, 768)
+    return matmul(hidden, weights[0, HALF:, :])
+
+
+def first_kernel(tokens, terms, gain, weights, attended, normed, total):
+    @pl.when(pl.program_id(0) == 0)
+    def _():
+        summed = terms[0].astype(jnp.float32)
+        for group in range(1, 4):
+            summed = summed + terms[group].astype(jnp.float32)
+        summed = summed.astype(jnp.bfloat16)
+        attended[...] = summed
+        start = pl.multiple_of(lax.axis_index("mp") * BLOCK, BLOCK)
+        own = tokens[pl.ds(start, BLOCK), :].astype(jnp.float32)
+        normed[...] = layer_norm(own + summed.astype(jnp.float32), gain[...])
+        total[...] = jnp.zeros_like(total)
+
+    total[...] += hidden_part(normed[...], weights)
+
+
+def second_kernel(normed, before, weights, out, total):
+    step = pl.program_id(0)
+
+    @pl.when(step == 0)
+    def _():
+        total[...] = before[...]
+
+    total[...] += hidden_part(normed[...], weights)
+
+    @pl.when(step == pl.num_programs(0) - 1)
+    def _():
+        out[...] = total[...].astype(jnp.bfloat16)
+
+
+def whole(shape):
+    return pl.BlockSpec(shape, lambda step: (0,) * len(shape))
+
+
+def ffn(kernel, arrays, weights, outs, scratch=()):
+    return pl.pallas_call(
+        kernel,
+        grid=(4,),
+        out_shape=[jax.ShapeDtypeStruct(*out) for out in outs],
+        in_specs=[whole(array.shape) for array in arrays]
+        + [pl.BlockSpec((1, 2 * HALF, WIDTH), lambda step: (step, 0, 0))],
+        out_specs=[whole(out[0]) for out in outs],
+        scratch_shapes=list(scratch),
+        cost_estimate=pl.CostEstimate(
+            flops=int(3e9), bytes_accessed=int(5e6), transcendentals=0
+        ),
+        compiler_params=pltpu.CompilerParams(vmem_limit_bytes=24 * 1024 * 1024),
+    )(*arrays, weights)
 
 
 def call(kernel, micros, outs, ins, scratch=()):
@@ -347,6 +405,15 @@
     across = [
         (16 * z + (place ^ (2 * z)), 16 * z + place) for z in range(FAR_GROUP) for place in range(16)
     ]
+    packed = pl.pallas_call(
+        weights_kernel,
+        out_shape=jax.ShapeDtypeStruct((2 * HALF, WIDTH), bf16),
+        in_specs=[pl.BlockSpec(memory_space=pl.ANY)] * 2,
+        out_specs=pl.BlockSpec(memory_space=pl.ANY),
+        scratch_shapes=[pltpu.SemaphoreType.DMA((3,))],
+    )(w_up, w_down)
+    mine = lax.all_gather(packed, "mp", axis=0)
+    theirs = swap(mine, 1)
     query, own, mid, far = call(
         project_kernel,
         4,
@@ -358,17 +425,15 @@
     )
     side = swap(own, 2)
     mid_a, mid_b = swap(mid, 4), swap(mid, 6)
-    w_out_all = lax.all_gather(w_out, "mp", axis=0, tiled=True)
     far_rows = lax.all_to_all(
         far, "seq", split_axis=0, concat_axis=0, tiled=True, axis_index_groups=columns
     )
     far_here = lax.ppermute(far_rows[:, :, 256:].reshape(128, 384), "seq", across)
     swapped = swap(jnp.concatenate([own, side, mid_a, mid_b], 0), 1)
     far_other = swap(far_here, 1)
-    state = [((LOCAL_HEADS, ROWS, LANES), f32), ((LOCAL_HEADS, ROWS, 256), f32)]
-    held = [pltpu.VMEM(*shape) for shape in state]
-    peaks, sums = call(
-        near_kernel, 5, state, [(slide_tiles, s), (query, v), (own, v), (side, v)]
+    state = ((LOCAL_HEADS, ROWS, LANES), f32)
+    (near,) = call(
+        near_kernel, 5, [state], [(slide_tiles, s), (query, v), (own, v), (side, v)]
     )
     (parts,) = call(
         far_kernel,
@@ -376,35 +441,39 @@
         [((FAR_GROUP, FAR_ROWS, 384), f32)],
         [(slide_tiles, s), (far_rows, v), (far_here, v), (far_other, v)],
     )
-    peaks, sums = call(
+    (both,) = call(
         rest_kernel,
         7,
-        state,
+        [state],
         [
             (slide_tiles, s), (query, v), (own, v), (side, v), (mid_a, v), (mid_b, v), (swapped, v),
-            (peaks, v), (sums, v),
+            (near, v),
         ],
     )
     parts = lax.all_to_all(
         parts, "seq", split_axis=0, concat_axis=0, tiled=True, axis_index_groups=columns
     )
-    mixed, far_attended = call(
+    terms, far_attended = call(
         finish_kernel,
-        2,
-        [((4, 768, LANES), bf16), ((FAR_ROWS, 192), bf16)],
-        [(parts, v), (peaks, v), (sums, v)],
-        held,
-    )
-    mixed = lax.all_to_all(mixed, "mp", split_axis=0, concat_axis=0, tiled=True)
-    attended, partial = call(
-        ffn_kernel,
-        6,
-        [((ROWS // 4, 768), bf16), ((4, 128, 768), bf16)],
-        [(tokens, v), (mixed, v), (w_out_all, v), (ffn_gain, v), (w_up, v), (w_down, v)],
-        [pltpu.VMEM((ROWS, 768), bf16)],
-    )
-    terms = lax.all_to_all(partial, "mp", split_axis=0, concat_axis=0, tiled=True)
-    ffn_out = jnp.sum(terms.astype(f32), 0).astype(bf16)
+        3,
+        [((4, BLOCK, WIDTH), bf16), ((FAR_ROWS, 192), bf16)],
+        [(parts, v), (both, v), (w_out, v)],
+        [pltpu.VMEM(*state)],
+    )
+    terms = lax.all_to_all(terms, "mp", split_axis=0, concat_axis=0, tiled=True)
+    attended, normed, total = ffn(
+        first_kernel,
+        [tokens, terms, ffn_gain],
+        mine,
+        [((BLOCK, WIDTH), bf16), ((BLOCK, WIDTH), bf16), ((BLOCK, WIDTH), f32)],
+    )
+    (ffn_out,) = ffn(
+        second_kernel,
+        [normed, total],
+        theirs,
+        [((BLOCK, WIDTH), bf16)],
+        [pltpu.VMEM((BLOCK, WIDTH), f32)],
+    )
     return (attended, far_attended, ffn_out)
 
 

time: 130 us -> 209 us (1.61); the launches traced: 129 us -> 205 us
  waiting for transfers between devices: 17.2 us -> 72.1 us
  Pallas kernels: 30 us -> 58.5 us
  starting transfers between devices: 48.2 us -> 38.3 us
  local copies, waits for them, and re-layouts: 3.21 us -> 6.44 us
    all_gather x1, waiting for transfers between devices: 0.01 us -> 63.6 us  [local(): mine = lax.all_gather(packed, 'mp', axis=0)]
    pallas_call x0 -> x3, Pallas kernels: none -> 44.9 us  [the longest x1 36.9 us: local(): pl.pallas_call(weights_kernel, out_shape=jax.ShapeDtypeStruct((2 * HALF,...]
    pallas_call x6 -> x5, Pallas kernels: 30 us -> 13.6 us  [call(): pl.pallas_call(kernel, out_shape=[jax.ShapeDtypeStruct(*out) for out in o...]
    all_to_all x1 -> x0, waiting for transfers between devices: 11.4 us -> none  [local(): mixed = lax.all_to_all(mixed, 'mp', split_axis=0, concat_axis=0, tiled=True)]
    all_to_all x1 -> x0, starting transfers between devices: 4.01 us -> none  [local(): mixed = lax.all_to_all(mixed, 'mp', split_axis=0, concat_axis=0, tiled=True)]
    all_to_all x1, starting transfers between devices: 14.9 us -> 11.3 us  [local(): lax.all_to_all(parts, 'seq', split_axis=0, concat_axis=0, tiled=True, axi...]
    unnamed x18 -> x26, local copies, waits for them, and re-layouts: 3.2 us -> 6.43 us
    all_to_all x1, starting transfers between devices: 10 us -> 7.11 us  [local(): lax.all_to_all(far, 'seq', split_axis=0, concat_axis=0, tiled=True, axis_...]
  transfers between devices with their start and end apart: 10 -> 10, of which waited for: 3 -> 4; matrix products, arithmetic and copies ran while one was open for 1% -> 1% of each run, Pallas kernels for 14% -> 8%
where the time goes in v3:
time: 209 us; the launch traced here: 205 us
  waiting for transfers between devices  72.1 us (34%)
  Pallas kernels  58.5 us (28%)
  starting transfers between devices  38.3 us (18%)
  blocking collectives  14.3 us (7%)
  between operations  14.3 us (7%)
  local copies, waits for them, and re-layouts  6.44 us (3%)
    all_gather x1, waiting for transfers between devices, local(): mine = lax.all_gather(packed, 'mp', axis=0)  63.6 us
    pallas_call x1, Pallas kernels, local(): pl.pallas_call(weights_kernel, out_shape=jax.ShapeDtypeStruct((2 * HALF,...  36.9 us
    ppermute x6, starting transfers between devices, swap(): lax.ppermute(value, 'seq', [(i, i ^ step) for i in range(lax.axis_size('s...  19.2 us
    all_to_all x1, blocking collectives, local(): terms = lax.all_to_all(terms, 'mp', split_axis=0, concat_axis=0, tiled=True)  14.3 us
    pallas_call x5, Pallas kernels, call(): pl.pallas_call(kernel, out_shape=[jax.ShapeDtypeStruct(*out) for out in o...  13.6 us
    all_to_all x1, starting transfers between devices, local(): lax.all_to_all(parts, 'seq', split_axis=0, concat_axis=0, tiled=True, axi...  11.3 us
    pallas_call x2, Pallas kernels, ffn(): pl.pallas_call(kernel, grid=(4,), out_shape=[jax.ShapeDtypeStruct(*out) f...  8.02 us
    all_to_all x1, starting transfers between devices, local(): lax.all_to_all(far, 'seq', split_axis=0, concat_axis=0, tiled=True, axis_...  7.11 us
  transfers between devices with their start and end apart: 10, of which 4 were waited for; matrix products, arithmetic and copies ran while one was open for 1% of the time, Pallas kernels for 8%

profile of v3, /device:TPU:1, one launch (start us, length us, event | category | flops | bytes accessed | tf_op | source)
XLA Modules:
  0.0 205.0 jit_solution(3183492129605397175)
XLA Ops:
  7.2 0.0 copy-start.1
  7.2 0.0 copy-start.4
  7.2 0.0 copy-start.3
  7.2 0.0 copy-start.2
  7.2 0.0 copy-start.6
  7.2 0.0 all-gather.3.cloned.1.call-start
  7.3 36.9 %shard_map.126 = bf16[768,768]{1,0:T(8,128)(2,1)} custom-call(bf16[768,768]{1,0:T(8,128)(2,1)} %w_up.1, bf16[768,768]{1,0:T(8,128)(2,1)} %w_down.1), custom_call_target="tpu_custom_call" | custom-call | tf_op jit(solution)/shard_map/pallas_call | solution.py:408
  44.1 0.0 all-gather.3.cloned.1.call-update
  44.2 63.6 %all-gather.3.cloned.1.call-done = bf16[3072,768]{1,0:T(8,128)(2,1)} async-done(((bf16[768,768]{1,0:T(8,128)(2,1)}), bf16[3072,768]{1,0:T(8,128)(2,1)}) %all-gather.3.cloned.1.call-update) | async-done | bytes 4718608 | tf_op jit(solution)/shard_map/all_gather | solution.py:415
  107.8 2.6 %collective-permute-start.6 = (bf16[4,768,768]{2,1,0:T(8,128)(2,1)}, bf16[4,768,768]{2,1,0:T(8,128)(2,1)}, u32[]{:S(2)}, u32[]{:S(2)}) collective-permute-start(bf16[4,768,768]{2,1,0:T(8,128)(2,1)} %bitcast.5), channel_id=1, source_target_pairs={{0,4},{4,0},{8,12},{12,8},{16,20},{20,16},{24,28},{28,24},{32,36},... | collective-permute-start | bytes 14155784 | tf_op jit(solution)/shard_map/ppermute | solution.py:398
  110.3 0.0 copy-done.1
  110.3 0.0 copy-done.4
  110.4 0.0 copy-done.3
  110.4 0.0 copy-done.2
  110.4 0.0 copy-done.6
  110.4 2.5 %shard_map.121 = (bf16[512,256]{1,0:T(8,128)(2,1)S(1)}, bf16[512,384]{1,0:T(8,128)(2,1)S(1)}, bf16[128,384]{1,0:T(8,128)(2,1)S(1)}, bf16[8,16,640]{2,1,0:T(8,128)(2,1)}) custom-call(bf16[512,768]{1,0:T(8,128)(2,1)S(1)} %copy-done.1, bf16[768]{0:T(1024)(128)(2,1)S(1)} %copy-done.6, bf16[192,768]{1,0:T(8,128)(2,1)S(1)} %bitcast.7, ...), custom_call_target="tpu_custom_call" | custom-call | flops 4400000000 | bytes 4000000 | tf_op jit(solution)/shard_map/pallas_call | solution.py:384
  112.9 3.2 %collective-permute-start.2 = (bf16[512,384]{1,0:T(8,128)(2,1)S(1)}, bf16[512,384]{1,0:T(8,128)(2,1)S(1)}, u32[]{:S(2)}, u32[]{:S(2)}) collective-permute-start(bf16[512,384]{1,0:T(8,128)(2,1)S(1)} %get-tuple-element.14.own), channel_id=1, source_target_pairs={{0,8},{4,12},{8,0},{12,4},{16,24},{20,28},{24,16},{28,20},{32,40},... | collective-permute-start | bytes 1179656 | tf_op jit(solution)/shard_map/ppermute | solution.py:398
  116.1 4.0 %collective-permute-start.4 = (bf16[128,384]{1,0:T(8,128)(2,1)S(1)}, bf16[128,384]{1,0:T(8,128)(2,1)S(1)}, u32[]{:S(2)}, u32[]{:S(2)}) collective-permute-start(bf16[128,384]{1,0:T(8,128)(2,1)S(1)} %get-tuple-element.15), channel_id=1, source_target_pairs={{0,24},{4,28},{8,16},{12,20},{16,8},{20,12},{24,0},{28,4},{32,56},... | collective-permute-start | bytes 294920 | tf_op jit(solution)/shard_map/ppermute | solution.py:398
  120.1 1.9 collective-permute-start.3
  122.1 7.1 %all-to-all-start = ((bf16[8,16,640]{2,1,0:T(8,128)(2,1)}), bf16[8,16,640]{2,1,0:T(8,128)(2,1)S(1)}, u32[]{:S(2)}, u32[]{:S(2)}) async-start(bf16[8,16,640]{2,1,0:T(8,128)(2,1)} %get-tuple-element.12), calls=%async_computation | async-start | bytes 327680 | tf_op jit(solution)/shard_map/all_to_all | solution.py:428
  129.2 0.4 collective-permute-done.4.mid_b
  129.6 0.0 collective-permute-done.3.mid_a
  129.6 0.0 collective-permute-done.2.side
  129.6 1.1 pad_maximum_fusion
  130.6 3.1 %collective-permute-start.5 = (bf16[1280,384]{1,0:T(8,128)(2,1)}, bf16[1280,384]{1,0:T(8,128)(2,1)S(1)}, u32[]{:S(2)}, u32[]{:S(2)}) collective-permute-start(bf16[1280,384]{1,0:T(8,128)(2,1)} %pad_maximum_fusion), channel_id=1, source_target_pairs={{0,4},{4,0},{8,12},{12,8},{16,20},{20,16},{24,28},{28,24},{32,36},... | collective-permute-start | bytes 2949128 | tf_op jit(solution)/shard_map/ppermute | solution.py:398
  133.7 3.8 %all-to-all-done.rows = bf16[8,16,640]{2,1,0:T(8,128)(2,1)S(1)} async-done(((bf16[8,16,640]{2,1,0:T(8,128)(2,1)}), bf16[8,16,640]{2,1,0:T(8,128)(2,1)S(1)}, u32[]{:S(2)}, u32[]{:S(2)}) %all-to-all-start) | async-done | bytes 163872 | tf_op jit(solution)/shard_map/all_to_all | solution.py:428
  137.5 0.7 collective-permute-start
  138.2 0.0 collective-permute-done.here
  138.2 4.3 %collective-permute-start.1 = (bf16[128,384]{1,0:T(8,128)(2,1)S(1)}, bf16[128,384]{1,0:T(8,128)(2,1)S(1)}, u32[]{:S(2)}, u32[]{:S(2)}) collective-permute-start(bf16[128,384]{1,0:T(8,128)(2,1)S(1)} %collective-permute-done.here), channel_id=1, source_target_pairs={{0,4},{4,0},{8,12},{12,8},{16,20},{20,16},{24,28},{28,24},{32,36},... | collective-permute-start | bytes 294920 | tf_op jit(solution)/shard_map/ppermute | solution.py:398
  142.5 0.0 copy-done.8
  142.6 3.2 %shard_map.123.held = f32[3,512,128]{2,1,0:T(8,128)S(1)} custom-call(s32[4]{0:T(128)S(1)} %copy-done.8, bf16[512,256]{1,0:T(8,128)(2,1)S(1)} %get-tuple-element.13.query, bf16[512,384]{1,0:T(8,128)(2,1)S(1)} %get-tuple-element.14.own, bf16[512,384]{1,0:T(8,128)(2,1)S(1)} %collective-permute-done.2.side), custom_call_target="tpu_custom_call" | custom-call | flops 5500000256 | bytes 5000000 | tf_op jit(solution)/shard_map/pallas_call | solution.py:384
  145.8 0.9 copy-done.11
  146.7 0.0 collective-permute-done.1.other
  146.7 1.9 shard_map.122
  148.5 11.3 %all-to-all-start.1 = ((f32[8,16,384]{2,1,0:T(8,128)}), f32[8,16,384]{2,1,0:T(8,128)S(1)}, u32[]{:S(2)}, u32[]{:S(2)}) async-start(f32[8,16,384]{2,1,0:T(8,128)} %shard_map.122), calls=%async_computation.1 | async-start | bytes 393216 | tf_op jit(solution)/shard_map/all_to_all | solution.py:453
  159.9 0.0 collective-permute-done.5.swapped
  159.9 0.0 copy-start.12
  159.9 1.2 copy-done.12
  161.1 4.4 %shard_map.124.held = f32[3,512,128]{2,1,0:T(8,128)S(1)} custom-call(s32[4]{0:T(128)S(1)} %copy-done.8, bf16[512,256]{1,0:T(8,128)(2,1)S(1)} %get-tuple-element.13.query, bf16[512,384]{1,0:T(8,128)(2,1)S(1)} %get-tuple-element.14.own, bf16[512,384]{1,0:T(8,128)(2,1)S(1)} %collective-permute-done.2.side, bf16[128,384]{1,0:T(8,128)(2,1)S(1)} %collective-permute-done.3.mid_a, ...), custom_call_target="tpu_custom_call" | custom-call | flops 7699999744 | bytes 7000000 | tf_op jit(solution)/shard_map/pallas_call | solution.py:384
  165.5 0.9 copy-done.9
  166.4 4.3 %all-to-all-done.1.parts = f32[8,16,384]{2,1,0:T(8,128)S(1)} async-done(((f32[8,16,384]{2,1,0:T(8,128)}), f32[8,16,384]{2,1,0:T(8,128)S(1)}, u32[]{:S(2)}, u32[]{:S(2)}) %all-to-all-start.1) | async-done | bytes 196640 | tf_op jit(solution)/shard_map/all_to_all | solution.py:453
  170.7 1.1 copy-done.10
  171.8 1.6 shard_map.125
  173.4 14.3 %all_to_all.15.terms = bf16[4,128,768]{2,1,0:T(8,128)(2,1)S(1)} all-to-all(bf16[4,128,768]{2,1,0:T(8,128)(2,1)S(1)} %get-tuple-element.16), channel_id=1, replica_groups=mesh['seq'=128,'mp'=4] {'mp'}, dimensions={0} | all-to-all | bytes 1572864 | tf_op jit(solution)/shard_map/all_to_all | solution.py:463
  187.8 2.3 %copy-done = bf16[3072,768]{1,0:T(8,128)(2,1)S(1)} copy-done((bf16[3072,768]{1,0:T(8,128)(2,1)S(1)}, bf16[3072,768]{1,0:T(8,128)(2,1)}, u32[]{:S(2)}) %copy-start) | copy-done | bytes 4718616
  190.1 3.0 %shard_map.127 = (bf16[128,768]{1,0:T(8,128)(2,1)}, bf16[128,768]{1,0:T(8,128)(2,1)S(1)}, f32[128,768]{1,0:T(8,128)S(1)}) custom-call(bf16[512,768]{1,0:T(8,128)(2,1)S(1)} %copy-done.1, bf16[4,128,768]{2,1,0:T(8,128)(2,1)S(1)} %all_to_all.15.terms, bf16[768]{0:T(1024)(128)(2,1)S(1)} %copy-done.7, bf16[4,768,768]{2,1,0:T(8,128)(2,1)S(1)} %bitcast.6), custom_call_target="tpu_custom_call" | custom-call | flops 3000000000 | bytes 5000000 | tf_op jit(solution)/shard_map/pallas_call | solution.py:367
  193.1 0.0 collective-permute-done.6.weights
  193.1 5.0 %shard_map.128 = bf16[128,768]{1,0:T(8,128)(2,1)} custom-call(bf16[128,768]{1,0:T(8,128)(2,1)S(1)} %get-tuple-element.19.normed, f32[128,768]{1,0:T(8,128)S(1)} %get-tuple-element.20.before, bf16[4,768,768]{2,1,0:T(8,128)(2,1)} %collective-permute-done.6.weights), custom_call_target="tpu_custom_call" | custom-call | flops 3000000000 | bytes 5000000 | tf_op jit(solution)/shard_map/pallas_call | solution.py:367
  (10 shorter events, 0.0 us)
Async XLA Ops:
  7.2 103.2 %copy-start.1 = (bf16[512,768]{1,0:T(8,128)(2,1)S(1)}, bf16[512,768]{1,0:T(8,128)(2,1)}, u32[]{:S(2)}) copy-start(bf16[512,768]{1,0:T(8,128)(2,1)} %tokens.3) | copy-start | bytes 2359300
  7.2 103.2 %copy-start.4 = (bf16[768,192]{0,1:T(8,128)(2,1)S(1)}, bf16[768,192]{0,1:T(8,128)(2,1)}, u32[]{:S(2)}) copy-start(bf16[768,192]{0,1:T(8,128)(2,1)} %param.15) | copy-start | bytes 884740
  7.2 103.2 %copy-start.3 = (bf16[768,192]{0,1:T(8,128)(2,1)S(1)}, bf16[768,192]{0,1:T(8,128)(2,1)}, u32[]{:S(2)}) copy-start(bf16[768,192]{0,1:T(8,128)(2,1)} %param.14) | copy-start | bytes 884740
  7.2 103.2 %copy-start.2 = (bf16[768,192]{0,1:T(8,128)(2,1)S(1)}, bf16[768,192]{0,1:T(8,128)(2,1)}, u32[]{:S(2)}) copy-start(bf16[768,192]{0,1:T(8,128)(2,1)} %param.13) | copy-start | bytes 884740
  7.2 103.2 %copy-start.6 = (bf16[768]{0:T(1024)(128)(2,1)S(1)}, bf16[768]{0:T(1024)(128)(2,1)}, u32[]{:S(2)}) copy-start(bf16[768]{0:T(1024)(128)(2,1)} %gain.2) | copy-start | bytes 4612
  7.2 100.5 %all-gather.3.cloned.1.call-start = ((), (), s32[]{:S(2)}) async-start(), calls=%async_computation.3 | async-start | bytes 5898240 | tf_op jit(solution)/shard_map/all_gather | solution.py:415
  107.8 85.4 %collective-permute-start.6 = (bf16[4,768,768]{2,1,0:T(8,128)(2,1)}, bf16[4,768,768]{2,1,0:T(8,128)(2,1)}, u32[]{:S(2)}, u32[]{:S(2)}) collective-permute-start(bf16[4,768,768]{2,1,0:T(8,128)(2,1)} %bitcast.5), channel_id=1, source_target_pairs={{0,4},{4,0},{8,12},{12,8},{16,20},{20,16},{24,28},{28,24},{32,36},... | collective-permute-start | bytes 14155784 | tf_op jit(solution)/shard_map/ppermute | solution.py:398
  112.9 29.7 %copy-start.8 = (s32[4]{0:T(128)S(1)}, s32[4]{0:T(128)}, u32[]{:S(2)}) copy-start(s32[4]{0:T(128)} %tiles.5) | copy-start | bytes 52
  112.9 16.7 %collective-permute-start.2 = (bf16[512,384]{1,0:T(8,128)(2,1)S(1)}, bf16[512,384]{1,0:T(8,128)(2,1)S(1)}, u32[]{:S(2)}, u32[]{:S(2)}) collective-permute-start(bf16[512,384]{1,0:T(8,128)(2,1)S(1)} %get-tuple-element.14.own), channel_id=1, source_target_pairs={{0,8},{4,12},{8,0},{12,4},{16,24},{20,28},{24,16},{28,20},{32,40},... | collective-permute-start | bytes 1179656 | tf_op jit(solution)/shard_map/ppermute | solution.py:398
  116.1 13.5 %collective-permute-start.4 = (bf16[128,384]{1,0:T(8,128)(2,1)S(1)}, bf16[128,384]{1,0:T(8,128)(2,1)S(1)}, u32[]{:S(2)}, u32[]{:S(2)}) collective-permute-start(bf16[128,384]{1,0:T(8,128)(2,1)S(1)} %get-tuple-element.15), channel_id=1, source_target_pairs={{0,24},{4,28},{8,16},{12,20},{16,8},{20,12},{24,0},{28,4},{32,56},... | collective-permute-start | bytes 294920 | tf_op jit(solution)/shard_map/ppermute | solution.py:398
  120.1 9.4 %collective-permute-start.3 = (bf16[128,384]{1,0:T(8,128)(2,1)S(1)}, bf16[128,384]{1,0:T(8,128)(2,1)S(1)}, u32[]{:S(2)}, u32[]{:S(2)}) collective-permute-start(bf16[128,384]{1,0:T(8,128)(2,1)S(1)} %get-tuple-element.15), channel_id=1, source_target_pairs={{0,16},{4,20},{8,24},{12,28},{16,0},{20,4},{24,8},{28,12},{32,48},... | collective-permute-start | bytes 294920 | tf_op jit(solution)/shard_map/ppermute | solution.py:398
  122.1 15.4 %all-to-all-start = ((bf16[8,16,640]{2,1,0:T(8,128)(2,1)}), bf16[8,16,640]{2,1,0:T(8,128)(2,1)S(1)}, u32[]{:S(2)}, u32[]{:S(2)}) async-start(bf16[8,16,640]{2,1,0:T(8,128)(2,1)} %get-tuple-element.12), calls=%async_computation | async-start | bytes 327680 | tf_op jit(solution)/shard_map/all_to_all | solution.py:428
  130.6 29.2 %collective-permute-start.5 = (bf16[1280,384]{1,0:T(8,128)(2,1)}, bf16[1280,384]{1,0:T(8,128)(2,1)S(1)}, u32[]{:S(2)}, u32[]{:S(2)}) collective-permute-start(bf16[1280,384]{1,0:T(8,128)(2,1)} %pad_maximum_fusion), channel_id=1, source_target_pairs={{0,4},{4,0},{8,12},{12,8},{16,20},{20,16},{24,28},{28,24},{32,36},... | collective-permute-start | bytes 2949128 | tf_op jit(solution)/shard_map/ppermute | solution.py:398
  137.5 0.7 collective-permute-start
  138.2 8.4 %collective-permute-start.1 = (bf16[128,384]{1,0:T(8,128)(2,1)S(1)}, bf16[128,384]{1,0:T(8,128)(2,1)S(1)}, u32[]{:S(2)}, u32[]{:S(2)}) collective-permute-start(bf16[128,384]{1,0:T(8,128)(2,1)S(1)} %collective-permute-done.here), channel_id=1, source_target_pairs={{0,4},{4,0},{8,12},{12,8},{16,20},{20,16},{24,28},{28,24},{32,36},... | collective-permute-start | bytes 294920 | tf_op jit(solution)/shard_map/ppermute | solution.py:398
  145.8 0.9 copy-start.11
  148.5 22.1 %all-to-all-start.1 = ((f32[8,16,384]{2,1,0:T(8,128)}), f32[8,16,384]{2,1,0:T(8,128)S(1)}, u32[]{:S(2)}, u32[]{:S(2)}) async-start(f32[8,16,384]{2,1,0:T(8,128)} %shard_map.122), calls=%async_computation.1 | async-start | bytes 393216 | tf_op jit(solution)/shard_map/all_to_all | solution.py:453
  159.9 10.8 %copy-start.5 = (bf16[192,768]{1,0:T(8,128)(2,1)S(1)}, bf16[192,768]{1,0:T(8,128)(2,1)}, u32[]{:S(2)}) copy-start(bf16[192,768]{1,0:T(8,128)(2,1)} %w_out.1) | copy-start | bytes 884740
  159.9 1.2 copy-start.12
  165.5 0.9 copy-start.9
  166.4 21.4 %copy-start.7 = (bf16[768]{0:T(1024)(128)(2,1)S(1)}, bf16[768]{0:T(1024)(128)(2,1)}, u32[]{:S(2)}) copy-start(bf16[768]{0:T(1024)(128)(2,1)} %gain.3) | copy-start | bytes 4612
  170.7 1.1 copy-start.10
  187.8 2.3 %copy-start = (bf16[3072,768]{1,0:T(8,128)(2,1)S(1)}, bf16[3072,768]{1,0:T(8,128)(2,1)}, u32[]{:S(2)}) copy-start(bf16[3072,768]{1,0:T(8,128)(2,1)} %all-gather.3.cloned.1.call-done) | copy-start | bytes 14155780
Sparse Core Ops, SparseCore 0:
  44.3 63.4 all-gather.2

commit v4 on v3

--- a/solution.py
+++ b/solution.py
@@ -21,7 +21,7 @@
 BLOCK = 128
 EPS = 1e-05
 HIDDEN_SCORE = -1e30
-VMEM = 24 * 1024 * 1024
+VMEM = 16 * 1024 * 1024
 
 KEY_TILE = (0, 0, 2)
 VALUE_TILE = (1, 1, 2)
@@ -97,40 +97,51 @@
     return slice(index * LANES, (index + 1) * LANES)
 
 
-def project_kernel(tokens, gain, w_query, w_key, w_value, query, keyval, mid, far):
+def project(normed, w_query, w_key, w_value):
+    asked = (matmul_t(normed, w_query[...]) * (1.0 / 8.0)).astype(jnp.bfloat16)
+    key = matmul_t(normed, w_key[...]).astype(jnp.bfloat16)
+    value = matmul_t(normed, w_value[...]).astype(jnp.bfloat16)
+    none = jnp.zeros_like(asked[:, 128:])
+    queries = [asked[:, :128], jnp.concatenate([asked[:, 128:], none], 1)]
+    keyvals = [key[:, :128], value[:, :128]]
+    return queries, keyvals + [jnp.concatenate([key[:, 128:], value[:, 128:]], 1)]
+
+
+def far_rows_kernel(tokens, gain, w_query, w_key, w_value, far):
+    first = lax.axis_index("mp") * LOCAL_HEADS
+    shape = (LOCAL_HEADS * FAR_ROWS, ROWS)
+    place = iota(shape, 0)
+    wanted = (place & 15) * RATE_FAR + (place >> 4) + first
+    rows = matmul((iota(shape, 1) == wanted).astype(jnp.bfloat16), tokens[...])
+    queries, keyvals = project(layer_norm(rows, gain[...]), w_query, w_key, w_value)
+    low = iota((FAR_ROWS, LANES), 1) < HEAD_DIM
+    for index, value in enumerate(queries + keyvals):
+        parts = [value[FAR_ROWS * head : FAR_ROWS * (head + 1)] for head in range(LOCAL_HEADS)]
+        chosen = parts[2] if index in (1, 4) else jnp.where(low, parts[0], parts[1])
+        for copy in range(FAR_GROUP):
+            far[copy, :, tile(index)] = chosen
+
+
+def project_kernel(tokens, gain, w_query, w_key, w_value, query, keyval, mid):
     mp = lax.axis_index("mp")
     normed = layer_norm(tokens[...].astype(jnp.float32), gain[...])
     order = iota((ROWS, ROWS), 0) == place_of(iota((ROWS, ROWS), 1))
     normed = matmul(order.astype(jnp.bfloat16), normed).astype(jnp.bfloat16)
-    scaled = (matmul_t(normed, w_query[...]) * (1.0 / 8.0)).astype(jnp.bfloat16)
-    query[:, :192] = scaled
-    query[:, 192:] = jnp.zeros((ROWS, 64), jnp.bfloat16)
-    key = matmul_t(normed, w_key[...]).astype(jnp.bfloat16)
-    value = matmul_t(normed, w_value[...]).astype(jnp.bfloat16)
-    keyval[:, tile(0)] = key[:, :128]
-    keyval[:, tile(1)] = value[:, :128]
-    keyval[:, tile(2)] = jnp.concatenate([key[:, 128:], value[:, 128:]], 1)
-
-    def pick(source, index, rows):
-        starts = []
-        for head in range(LOCAL_HEADS):
-            number = mp * LOCAL_HEADS + head
-            start = (number & 3) * CLASS_ROWS
-            if rows == FAR_ROWS:
-                start = start + (number >> 2) * FAR_ROWS
-            starts.append(pl.ds(pl.multiple_of(start, rows), rows))
-        if index == KEY_TILE[2] and source is keyval or index == QUERY_TILE[2] and source is query:
-            return source[starts[2], tile(index)]
-        low, high = source[starts[0], tile(index)], source[starts[1], tile(index)]
-        return jnp.where(iota(low.shape, 1) < HEAD_DIM, low, high)
-
-    for index in range(3):
-        mid[:, tile(index)] = pick(keyval, index, CLASS_ROWS)
-    picked = [pick(query, index, FAR_ROWS) for index in range(2)]
-    picked += [pick(keyval, index, FAR_ROWS) for index in range(3)]
-    for index in range(5):
-        for copy in range(FAR_GROUP):
-            far[copy, :, tile(index)] = picked[index]
+    queries, keyvals = project(normed, w_query, w_key, w_value)
+    for index, value in enumerate(queries):
+        query[:, tile(index)] = value
+    for index, value in enumerate(keyvals):
+        keyval[:, tile(index)] = value
+    starts = []
+    for head in range(LOCAL_HEADS):
+        start = ((mp * LOCAL_HEADS + head) & 3) * CLASS_ROWS
+        starts.append(pl.ds(pl.multiple_of(start, CLASS_ROWS), CLASS_ROWS))
+    low = iota((CLASS_ROWS, LANES), 1) < HEAD_DIM
+    for index in range(2):
+        mid[:, tile(index)] = jnp.where(
+            low, keyval[starts[0], tile(index)], keyval[starts[1], tile(index)]
+        )
+    mid[:, tile(2)] = keyval[starts[2], tile(2)]
 
 
 def attend(query, keys, values, head):
@@ -301,25 +312,11 @@
     terms[...] = matmul(mixed, w_out[...]).astype(jnp.bfloat16).reshape(4, BLOCK, WIDTH)
 
 
-def weights_kernel(w_up, w_down, out, sems):
+def weights_kernel(w_up, w_down, out):
     start = pl.multiple_of((lax.axis_index("seq") & 1) * HALF, HALF)
-    copies = [
-        pltpu.make_async_copy(
-            w_up.at[pl.ds(block * HALF, HALF), pl.ds(start, HALF)],
-            out.at[pl.ds(0, HALF), pl.ds(block * HALF, HALF)],
-            sems.at[block],
-        )
-        for block in range(2)
-    ]
-    copies.append(
-        pltpu.make_async_copy(
-            w_down.at[pl.ds(start, HALF), :], out.at[pl.ds(HALF, HALF), :], sems.at[2]
-        )
-    )
-    for copy in copies:
-        copy.start()
-    for copy in copies:
-        copy.wait()
+    out[:HALF, :HALF] = w_up[:HALF, pl.ds(start, HALF)]
+    out[:HALF, HALF:] = w_up[HALF:, pl.ds(start, HALF)]
+    out[HALF:, :] = w_down[pl.ds(start, HALF), :]
 
 
 def hidden_part(normed, weights):
@@ -405,23 +402,20 @@
     across = [
         (16 * z + (place ^ (2 * z)), 16 * z + place) for z in range(FAR_GROUP) for place in range(16)
     ]
-    packed = pl.pallas_call(
-        weights_kernel,
-        out_shape=jax.ShapeDtypeStruct((2 * HALF, WIDTH), bf16),
-        in_specs=[pl.BlockSpec(memory_space=pl.ANY)] * 2,
-        out_specs=pl.BlockSpec(memory_space=pl.ANY),
-        scratch_shapes=[pltpu.SemaphoreType.DMA((3,))],
-    )(w_up, w_down)
+    (packed,) = call(weights_kernel, 2, [((2 * HALF, WIDTH), bf16)], [(w_up, v), (w_down, v)])
     mine = lax.all_gather(packed, "mp", axis=0)
-    theirs = swap(mine, 1)
-    query, own, mid, far = call(
+    w_query, w_key, w_value = w_query.T, w_key.T, w_value.T
+    (far,) = call(
+        far_rows_kernel,
+        2,
+        [((FAR_GROUP, FAR_ROWS, 640), bf16)],
+        [(tokens, v), (attn_gain, v), (w_query, v), (w_key, v), (w_value, v)],
+    )
+    query, own, mid = call(
         project_kernel,
-        4,
-        [
-            ((ROWS, 256), bf16), ((ROWS, 384), bf16), ((CLASS_ROWS, 384), bf16),
-            ((FAR_GROUP, FAR_ROWS, 640), bf16),
-        ],
-        [(tokens, v), (attn_gain, v), (w_query.T, v), (w_key.T, v), (w_value.T, v)],
+        3,
+        [((ROWS, 256), bf16), ((ROWS, 384), bf16), ((CLASS_ROWS, 384), bf16)],
+        [(tokens, v), (attn_gain, v), (w_query, v), (w_key, v), (w_value, v)],
     )
     side = swap(own, 2)
     mid_a, mid_b = swap(mid, 4), swap(mid, 6)
@@ -450,6 +444,8 @@
             (near, v),
         ],
     )
+    late, _ = lax.optimization_barrier((mine, both))
+    theirs = swap(late, 1)
     parts = lax.all_to_all(
         parts, "seq", split_axis=0, concat_axis=0, tiled=True, axis_index_groups=columns
     )

time: 209 us -> 153 us (0.73)
  the two profiles are of different devices: /device:TPU:1 before, /device:TPU:8 now
where the time goes in v4:
time: 153 us; the launch traced here: 152 us
  blocking collectives  56.3 us (37%)
  waiting for transfers between devices  37.7 us (25%)
  starting transfers between devices  20.5 us (13%)
  Pallas kernels  20.4 us (13%)
  between operations  14.2 us (9%)
  local copies, waits for them, and re-layouts  3.19 us (2%)
    all_gather x1, waiting for transfers between devices, local(): mine = lax.all_gather(packed, 'mp', axis=0)  32.2 us
    all_to_all x1, blocking collectives, local(): lax.all_to_all(parts, 'seq', split_axis=0, concat_axis=0, tiled=True, axi...  24.5 us
    ppermute x6, starting transfers between devices, swap(): lax.ppermute(value, 'seq', [(i, i ^ step) for i in range(lax.axis_size('s...  19.7 us
    all_to_all x1, blocking collectives, local(): lax.all_to_all(far, 'seq', split_axis=0, concat_axis=0, tiled=True, axis_...  17.6 us
    pallas_call x7, Pallas kernels, call(): pl.pallas_call(kernel, out_shape=[jax.ShapeDtypeStruct(*out) for out in o...  14.5 us
    all_to_all x1, blocking collectives, local(): terms = lax.all_to_all(terms, 'mp', split_axis=0, concat_axis=0, tiled=True)  14.2 us
    pallas_call x2, Pallas kernels, ffn(): pl.pallas_call(kernel, grid=(4,), out_shape=[jax.ShapeDtypeStruct(*out) f...  5.94 us
    ppermute x6, waiting for transfers between devices, swap(): lax.ppermute(value, 'seq', [(i, i ^ step) for i in range(lax.axis_size('s...  5.5 us
  transfers between devices with their start and end apart: 8, of which 3 were waited for; matrix products, arithmetic and copies ran while one was open for 0% of the time, Pallas kernels for 11%

profile of v4, /device:TPU:8, one launch (start us, length us, event | category | flops | bytes accessed | tf_op | source)
XLA Modules:
  0.0 152.5 jit_solution(18244157854889819136)
XLA Ops:
  7.2 0.0 all-gather.3.cloned.1.call-start
  7.2 0.0 copy-start
  7.2 1.3 copy-done
  8.5 0.0 copy-start.1
  8.5 1.3 copy-done.1
  9.8 0.0 copy-start.2
  9.8 0.0 copy-start.7
  9.8 1.1 shard_map.127
  10.9 0.0 all-gather.3.cloned.1.call-update
  10.9 0.2 copy-done.2
  11.1 0.3 copy-done.3
  11.4 0.1 copy-done.4
  11.5 0.1 copy-done.5
  11.6 0.0 copy-done.7
  11.6 1.8 %shard_map.123 = (bf16[512,256]{1,0:T(8,128)(2,1)S(1)}, bf16[512,384]{1,0:T(8,128)(2,1)S(1)}, bf16[128,384]{1,0:T(8,128)(2,1)S(1)}) custom-call(bf16[512,768]{1,0:T(8,128)(2,1)S(1)} %copy-done.2, bf16[768]{0:T(1024)(128)(2,1)S(1)} %copy-done.7, bf16[192,768]{1,0:T(8,128)(2,1)S(1)} %bitcast.9, bf16[192,768]{1,0:T(8,128)(2,1)S(1)} %bitcast.11, ...), custom_call_target="tpu_custom_call" | custom-call | flops 3300000000 | bytes 3000000 | tf_op jit(solution)/shard_map/pallas_call | solution.py:381
  13.4 7.7 %collective-permute-start.2 = (bf16[512,384]{1,0:T(8,128)(2,1)S(1)}, bf16[512,384]{1,0:T(8,128)(2,1)S(1)}, u32[]{:S(2)}, u32[]{:S(2)}) collective-permute-start(bf16[512,384]{1,0:T(8,128)(2,1)S(1)} %get-tuple-element.13.own), channel_id=1, source_target_pairs={{0,8},{4,12},{8,0},{12,4},{16,24},{20,28},{24,16},{28,20},{32,40},... | collective-permute-start | bytes 1179656 | tf_op jit(solution)/shard_map/ppermute | solution.py:395
  21.1 1.9 %collective-permute-start.4 = (bf16[128,384]{1,0:T(8,128)(2,1)S(1)}, bf16[128,384]{1,0:T(8,128)(2,1)S(1)}, u32[]{:S(2)}, u32[]{:S(2)}) collective-permute-start(bf16[128,384]{1,0:T(8,128)(2,1)S(1)} %get-tuple-element.14), channel_id=1, source_target_pairs={{0,24},{4,28},{8,16},{12,20},{16,8},{20,12},{24,0},{28,4},{32,56},... | collective-permute-start | bytes 294920 | tf_op jit(solution)/shard_map/ppermute | solution.py:395
  23.0 4.3 %collective-permute-start.3 = (bf16[128,384]{1,0:T(8,128)(2,1)S(1)}, bf16[128,384]{1,0:T(8,128)(2,1)S(1)}, u32[]{:S(2)}, u32[]{:S(2)}) collective-permute-start(bf16[128,384]{1,0:T(8,128)(2,1)S(1)} %get-tuple-element.14), channel_id=1, source_target_pairs={{0,16},{4,20},{8,24},{12,28},{16,0},{20,4},{24,8},{28,12},{32,48},... | collective-permute-start | bytes 294920 | tf_op jit(solution)/shard_map/ppermute | solution.py:395
  27.3 4.2 %collective-permute-done.4.mid_b = bf16[128,384]{1,0:T(8,128)(2,1)S(1)} collective-permute-done((bf16[128,384]{1,0:T(8,128)(2,1)S(1)}, bf16[128,384]{1,0:T(8,128)(2,1)S(1)}, u32[]{:S(2)}, u32[]{:S(2)}) %collective-permute-start.4) | collective-permute-done | bytes 98336 | tf_op jit(solution)/shard_map/ppermute | solution.py:395
  31.5 0.0 collective-permute-done.3.mid_a
  31.5 0.0 collective-permute-done.2.side
  31.6 0.1 pad_maximum_fusion
  31.7 1.9 %collective-permute-start.5 = (bf16[1280,384]{1,0:T(8,128)(2,1)S(1)}, bf16[1280,384]{1,0:T(8,128)(2,1)S(1)}, u32[]{:S(2)}, u32[]{:S(2)}) collective-permute-start(bf16[1280,384]{1,0:T(8,128)(2,1)S(1)} %pad_maximum_fusion), channel_id=1, source_target_pairs={{0,4},{4,0},{8,12},{12,8},{16,20},{20,16},{24,28},{28,24},{32,36},... | collective-permute-start | bytes 2949128 | tf_op jit(solution)/shard_map/ppermute | solution.py:395
  33.6 0.0 copy-done.9
  33.6 3.2 %shard_map.124.held = f32[3,512,128]{2,1,0:T(8,128)S(1)} custom-call(s32[4]{0:T(128)S(1)} %copy-done.9, bf16[512,256]{1,0:T(8,128)(2,1)S(1)} %get-tuple-element.12.query, bf16[512,384]{1,0:T(8,128)(2,1)S(1)} %get-tuple-element.13.own, bf16[512,384]{1,0:T(8,128)(2,1)S(1)} %collective-permute-done.2.side), custom_call_target="tpu_custom_call" | custom-call | flops 5500000256 | bytes 5000000 | tf_op jit(solution)/shard_map/pallas_call | solution.py:381
  36.8 0.0 collective-permute-done.5.swapped
  36.9 4.6 %shard_map.125.held = f32[3,512,128]{2,1,0:T(8,128)S(1)} custom-call(s32[4]{0:T(128)S(1)} %copy-done.9, bf16[512,256]{1,0:T(8,128)(2,1)S(1)} %get-tuple-element.12.query, bf16[512,384]{1,0:T(8,128)(2,1)S(1)} %get-tuple-element.13.own, bf16[512,384]{1,0:T(8,128)(2,1)S(1)} %collective-permute-done.2.side, bf16[128,384]{1,0:T(8,128)(2,1)S(1)} %collective-permute-done.3.mid_a, ...), custom_call_target="tpu_custom_call" | custom-call | flops 7699999744 | bytes 7000000 | tf_op jit(solution)/shard_map/pallas_call | solution.py:381
  41.4 32.2 %all-gather.3.cloned.1.call-done = bf16[3072,768]{1,0:T(8,128)(2,1)} async-done(((bf16[768,768]{1,0:T(8,128)(2,1)}), bf16[3072,768]{1,0:T(8,128)(2,1)}) %all-gather.3.cloned.1.call-update) | async-done | bytes 4718608 | tf_op jit(solution)/shard_map/all_gather | solution.py:406
  73.6 1.9 %collective-permute-start.6 = (bf16[4,768,768]{2,1,0:T(8,128)(2,1)}, bf16[4,768,768]{2,1,0:T(8,128)(2,1)S(1)}, u32[]{:S(2)}, u32[]{:S(2)}) collective-permute-start(bf16[4,768,768]{2,1,0:T(8,128)(2,1)} %bitcast.5), channel_id=1, source_target_pairs={{0,4},{4,0},{8,12},{12,8},{16,20},{20,16},{24,28},{28,24},{32,36},... | collective-permute-start | bytes 14155784 | tf_op jit(solution)/shard_map/ppermute | solution.py:395
  75.5 0.9 shard_map.121
  76.4 17.6 %all_to_all.15.rows = bf16[8,16,640]{2,1,0:T(8,128)(2,1)S(1)} all-to-all(bf16[8,16,640]{2,1,0:T(8,128)(2,1)S(1)} %shard_map.121), channel_id=1, replica_groups={{0,64,128,192,256,320,384,448},{4,68,132,196,260,324,388,452},{8,72,136..., dimensions={0} | all-to-all | bytes 327680 | tf_op jit(solution)/shard_map/all_to_all | solution.py:422
  94.1 0.0 copy-start.6
  94.1 0.8 collective-permute-start
  94.9 0.0 collective-permute-done.here
  94.9 1.9 %collective-permute-start.1 = (bf16[128,384]{1,0:T(8,128)(2,1)S(1)}, bf16[128,384]{1,0:T(8,128)(2,1)S(1)}, u32[]{:S(2)}, u32[]{:S(2)}) collective-permute-start(bf16[128,384]{1,0:T(8,128)(2,1)S(1)} %collective-permute-done.here), channel_id=1, source_target_pairs={{0,4},{4,0},{8,12},{12,8},{16,20},{20,16},{24,28},{28,24},{32,36},... | collective-permute-start | bytes 294920 | tf_op jit(solution)/shard_map/ppermute | solution.py:395
  96.8 1.3 collective-permute-done.1.other
  98.1 1.2 shard_map.122
  99.3 0.0 slice-start
  99.3 24.5 %all_to_all.16.parts = f32[8,16,384]{2,1,0:T(8,128)S(1)} all-to-all(f32[8,16,384]{2,1,0:T(8,128)S(1)} %shard_map.122), channel_id=1, replica_groups={{0,64,128,192,256,320,384,448},{4,68,132,196,260,324,388,452},{8,72,136..., dimensions={0} | all-to-all | bytes 393216 | tf_op jit(solution)/shard_map/all_to_all | solution.py:449
  123.8 0.0 copy-done.6
  123.8 1.6 %shard_map.126 = (bf16[4,128,768]{2,1,0:T(8,128)(2,1)S(1)}, bf16[16,192]{1,0:T(8,128)(2,1)}) custom-call(f32[8,16,384]{2,1,0:T(8,128)S(1)} %all_to_all.16.parts, f32[3,512,128]{2,1,0:T(8,128)S(1)} %shard_map.125.held, bf16[192,768]{1,0:T(8,128)(2,1)S(1)} %copy-done.6), custom_call_target="tpu_custom_call" | custom-call | flops 3300000000 | bytes 3000000 | tf_op jit(solution)/shard_map/pallas_call | solution.py:381
  125.5 14.2 %all_to_all.17.terms = bf16[4,128,768]{2,1,0:T(8,128)(2,1)S(1)} all-to-all(bf16[4,128,768]{2,1,0:T(8,128)(2,1)S(1)} %get-tuple-element.15), channel_id=1, replica_groups=mesh['seq'=128,'mp'=4] {'mp'}, dimensions={0} | all-to-all | bytes 1572864 | tf_op jit(solution)/shard_map/all_to_all | solution.py:459
  139.7 0.0 slice-done
  139.7 0.0 slice-done.1
  139.7 0.0 copy-done.8
  139.7 3.0 %shard_map.128 = (bf16[128,768]{1,0:T(8,128)(2,1)}, bf16[128,768]{1,0:T(8,128)(2,1)S(1)}, f32[128,768]{1,0:T(8,128)S(1)}) custom-call(bf16[512,768]{1,0:T(8,128)(2,1)S(1)} %copy-done.2, bf16[4,128,768]{2,1,0:T(8,128)(2,1)S(1)} %all_to_all.17.terms, bf16[768]{0:T(1024)(128)(2,1)S(1)} %copy-done.8, bf16[4,768,768]{2,1,0:T(8,128)(2,1)S(1)} %bitcast.8), custom_call_target="tpu_custom_call" | custom-call | flops 3000000000 | bytes 5000000 | tf_op jit(solution)/shard_map/pallas_call | solution.py:364
  142.7 0.0 collective-permute-done.6.weights
  142.7 2.9 %shard_map.129 = bf16[128,768]{1,0:T(8,128)(2,1)} custom-call(bf16[128,768]{1,0:T(8,128)(2,1)S(1)} %get-tuple-element.18.normed, f32[128,768]{1,0:T(8,128)S(1)} %get-tuple-element.19.before, bf16[4,768,768]{2,1,0:T(8,128)(2,1)S(1)} %collective-permute-done.6.weights), custom_call_target="tpu_custom_call" | custom-call | flops 3000000000 | bytes 5000000 | tf_op jit(solution)/shard_map/pallas_call | solution.py:364
  (8 shorter events, 0.0 us)
Async XLA Ops:
  7.2 66.4 %all-gather.3.cloned.1.call-start = ((), (), s32[]{:S(2)}) async-start(), calls=%async_computation.3 | async-start | bytes 5898240 | tf_op jit(solution)/shard_map/all_gather | solution.py:406
  7.2 1.3 copy-start
  8.5 1.3 copy-start.1
  9.8 1.4 copy-start.2
  9.8 1.6 %copy-start.3 = (bf16[768,192]{0,1:T(8,128)(2,1)S(1)}, bf16[768,192]{0,1:T(8,128)(2,1)}, u32[]{:S(2)}) copy-start(bf16[768,192]{0,1:T(8,128)(2,1)} %param.13) | copy-start | bytes 884740
  9.8 1.7 %copy-start.4 = (bf16[768,192]{0,1:T(8,128)(2,1)S(1)}, bf16[768,192]{0,1:T(8,128)(2,1)}, u32[]{:S(2)}) copy-start(bf16[768,192]{0,1:T(8,128)(2,1)} %param.14) | copy-start | bytes 884740
  9.8 1.8 %copy-start.5 = (bf16[768,192]{0,1:T(8,128)(2,1)S(1)}, bf16[768,192]{0,1:T(8,128)(2,1)}, u32[]{:S(2)}) copy-start(bf16[768,192]{0,1:T(8,128)(2,1)} %param.15) | copy-start | bytes 884740
  9.8 1.8 %copy-start.7 = (bf16[768]{0:T(1024)(128)(2,1)S(1)}, bf16[768]{0:T(1024)(128)(2,1)}, u32[]{:S(2)}) copy-start(bf16[768]{0:T(1024)(128)(2,1)} %gain.4) | copy-start | bytes 4612
  13.4 20.2 %copy-start.9 = (s32[4]{0:T(128)S(1)}, s32[4]{0:T(128)}, u32[]{:S(2)}) copy-start(s32[4]{0:T(128)} %tiles.5) | copy-start | bytes 52
  13.4 18.2 %collective-permute-start.2 = (bf16[512,384]{1,0:T(8,128)(2,1)S(1)}, bf16[512,384]{1,0:T(8,128)(2,1)S(1)}, u32[]{:S(2)}, u32[]{:S(2)}) collective-permute-start(bf16[512,384]{1,0:T(8,128)(2,1)S(1)} %get-tuple-element.13.own), channel_id=1, source_target_pairs={{0,8},{4,12},{8,0},{12,4},{16,24},{20,28},{24,16},{28,20},{32,40},... | collective-permute-start | bytes 1179656 | tf_op jit(solution)/shard_map/ppermute | solution.py:395
  21.1 10.4 %collective-permute-start.4 = (bf16[128,384]{1,0:T(8,128)(2,1)S(1)}, bf16[128,384]{1,0:T(8,128)(2,1)S(1)}, u32[]{:S(2)}, u32[]{:S(2)}) collective-permute-start(bf16[128,384]{1,0:T(8,128)(2,1)S(1)} %get-tuple-element.14), channel_id=1, source_target_pairs={{0,24},{4,28},{8,16},{12,20},{16,8},{20,12},{24,0},{28,4},{32,56},... | collective-permute-start | bytes 294920 | tf_op jit(solution)/shard_map/ppermute | solution.py:395
  23.0 8.5 %collective-permute-start.3 = (bf16[128,384]{1,0:T(8,128)(2,1)S(1)}, bf16[128,384]{1,0:T(8,128)(2,1)S(1)}, u32[]{:S(2)}, u32[]{:S(2)}) collective-permute-start(bf16[128,384]{1,0:T(8,128)(2,1)S(1)} %get-tuple-element.14), channel_id=1, source_target_pairs={{0,16},{4,20},{8,24},{12,28},{16,0},{20,4},{24,8},{28,12},{32,48},... | collective-permute-start | bytes 294920 | tf_op jit(solution)/shard_map/ppermute | solution.py:395
  31.7 5.2 %collective-permute-start.5 = (bf16[1280,384]{1,0:T(8,128)(2,1)S(1)}, bf16[1280,384]{1,0:T(8,128)(2,1)S(1)}, u32[]{:S(2)}, u32[]{:S(2)}) collective-permute-start(bf16[1280,384]{1,0:T(8,128)(2,1)S(1)} %pad_maximum_fusion), channel_id=1, source_target_pairs={{0,4},{4,0},{8,12},{12,8},{16,20},{20,16},{24,28},{28,24},{32,36},... | collective-permute-start | bytes 2949128 | tf_op jit(solution)/shard_map/ppermute | solution.py:395
  73.6 69.1 %collective-permute-start.6 = (bf16[4,768,768]{2,1,0:T(8,128)(2,1)}, bf16[4,768,768]{2,1,0:T(8,128)(2,1)S(1)}, u32[]{:S(2)}, u32[]{:S(2)}) collective-permute-start(bf16[4,768,768]{2,1,0:T(8,128)(2,1)} %bitcast.5), channel_id=1, source_target_pairs={{0,4},{4,0},{8,12},{12,8},{16,20},{20,16},{24,28},{28,24},{32,36},... | collective-permute-start | bytes 14155784 | tf_op jit(solution)/shard_map/ppermute | solution.py:395
  94.1 29.8 %copy-start.6 = (bf16[192,768]{1,0:T(8,128)(2,1)S(1)}, bf16[192,768]{1,0:T(8,128)(2,1)}, u32[]{:S(2)}) copy-start(bf16[192,768]{1,0:T(8,128)(2,1)} %w_out.1) | copy-start | bytes 884740
  94.1 0.8 collective-permute-start
  94.9 3.2 %collective-permute-start.1 = (bf16[128,384]{1,0:T(8,128)(2,1)S(1)}, bf16[128,384]{1,0:T(8,128)(2,1)S(1)}, u32[]{:S(2)}, u32[]{:S(2)}) collective-permute-start(bf16[128,384]{1,0:T(8,128)(2,1)S(1)} %collective-permute-done.here), channel_id=1, source_target_pairs={{0,4},{4,0},{8,12},{12,8},{16,20},{20,16},{24,28},{28,24},{32,36},... | collective-permute-start | bytes 294920 | tf_op jit(solution)/shard_map/ppermute | solution.py:395
  99.3 40.4 %slice-start = ((s8[4718592]{0:T(1024)(128)(4,1)}), s8[4194304]{0:T(1024)(128)(4,1)S(1)}, s32[]{:S(2)}) async-start(s8[4718592]{0:T(1024)(128)(4,1)} %bitcast.6), calls=%async_computation.4 | async-start | bytes 8388608
  123.8 15.8 %slice-start.1 = ((s8[4718592]{0:T(1024)(128)(4,1)}), s8[524288]{0:T(1024)(128)(4,1)S(1)}, s32[]{:S(2)}) async-start(s8[4718592]{0:T(1024)(128)(4,1)} %bitcast.6), calls=%async_computation.5 | async-start | bytes 1048576
  123.8 15.8 %copy-start.8 = (bf16[768]{0:T(1024)(128)(2,1)S(1)}, bf16[768]{0:T(1024)(128)(2,1)}, u32[]{:S(2)}) copy-start(bf16[768]{0:T(1024)(128)(2,1)} %gain.5) | copy-start | bytes 4612
Sparse Core Ops, SparseCore 0:
  11.1 62.5 all-gather.2

commit v5 on v4

--- a/solution.py
+++ b/solution.py
@@ -326,54 +326,56 @@
     return matmul(hidden, weights[0, HALF:, :])
 
 
-def first_kernel(tokens, terms, gain, weights, attended, normed, total):
-    @pl.when(pl.program_id(0) == 0)
-    def _():
-        summed = terms[0].astype(jnp.float32)
-        for group in range(1, 4):
-            summed = summed + terms[group].astype(jnp.float32)
-        summed = summed.astype(jnp.bfloat16)
-        attended[...] = summed
-        start = pl.multiple_of(lax.axis_index("mp") * BLOCK, BLOCK)
-        own = tokens[pl.ds(start, BLOCK), :].astype(jnp.float32)
-        normed[...] = layer_norm(own + summed.astype(jnp.float32), gain[...])
-        total[...] = jnp.zeros_like(total)
-
-    total[...] += hidden_part(normed[...], weights)
-
-
-def second_kernel(normed, before, weights, out, total):
+def norm_kernel(tokens, terms, gain, attended, normed):
+    summed = terms[0].astype(jnp.float32)
+    for group in range(1, 4):
+        summed = summed + terms[group].astype(jnp.float32)
+    summed = summed.astype(jnp.bfloat16)
+    attended[...] = summed
+    start = pl.multiple_of(lax.axis_index("mp") * BLOCK, BLOCK)
+    own = tokens[pl.ds(start, BLOCK), :].astype(jnp.float32)
+    normed[...] = layer_norm(own + summed.astype(jnp.float32), gain[...])
+
+
+def ffn_kernel(own, other, weights, kept, sent, rows, total):
     step = pl.program_id(0)
 
     @pl.when(step == 0)
     def _():
-        total[...] = before[...]
-
-    total[...] += hidden_part(normed[...], weights)
+        rows[:BLOCK, :] = own[...]
+        rows[BLOCK:, :] = other[...]
+        total[...] = jnp.zeros_like(total)
+
+    total[...] += hidden_part(rows[...], weights)
 
     @pl.when(step == pl.num_programs(0) - 1)
     def _():
-        out[...] = total[...].astype(jnp.bfloat16)
+        kept[...] = total[:BLOCK, :]
+        sent[...] = total[BLOCK:, :].astype(jnp.bfloat16)
 
 
 def whole(shape):
     return pl.BlockSpec(shape, lambda step: (0,) * len(shape))
 
 
-def ffn(kernel, arrays, weights, outs, scratch=()):
+def ffn(own, other, weights):
+    outs = [((BLOCK, WIDTH), jnp.float32), ((BLOCK, WIDTH), jnp.bfloat16)]
     return pl.pallas_call(
-        kernel,
+        ffn_kernel,
         grid=(4,),
         out_shape=[jax.ShapeDtypeStruct(*out) for out in outs],
-        in_specs=[whole(array.shape) for array in arrays]
+        in_specs=[whole(own.shape), whole(other.shape)]
         + [pl.BlockSpec((1, 2 * HALF, WIDTH), lambda step: (step, 0, 0))],
         out_specs=[whole(out[0]) for out in outs],
-        scratch_shapes=list(scratch),
+        scratch_shapes=[
+            pltpu.VMEM((2 * BLOCK, WIDTH), jnp.bfloat16),
+            pltpu.VMEM((2 * BLOCK, WIDTH), jnp.float32),
+        ],
         cost_estimate=pl.CostEstimate(
-            flops=int(3e9), bytes_accessed=int(5e6), transcendentals=0
+            flops=int(4e9), bytes_accessed=int(5e6), transcendentals=0
         ),
-        compiler_params=pltpu.CompilerParams(vmem_limit_bytes=24 * 1024 * 1024),
-    )(*arrays, weights)
+        compiler_params=pltpu.CompilerParams(vmem_limit_bytes=VMEM),
+    )(own, other, weights)
 
 
 def call(kernel, micros, outs, ins, scratch=()):
@@ -411,44 +413,49 @@
         [((FAR_GROUP, FAR_ROWS, 640), bf16)],
         [(tokens, v), (attn_gain, v), (w_query, v), (w_key, v), (w_value, v)],
     )
+    ordered, _ = lax.optimization_barrier((tokens, far))
     query, own, mid = call(
         project_kernel,
         3,
         [((ROWS, 256), bf16), ((ROWS, 384), bf16), ((CLASS_ROWS, 384), bf16)],
-        [(tokens, v), (attn_gain, v), (w_query, v), (w_key, v), (w_value, v)],
+        [(ordered, v), (attn_gain, v), (w_query, v), (w_key, v), (w_value, v)],
     )
     side = swap(own, 2)
     mid_a, mid_b = swap(mid, 4), swap(mid, 6)
     far_rows = lax.all_to_all(
         far, "seq", split_axis=0, concat_axis=0, tiled=True, axis_index_groups=columns
     )
-    far_here = lax.ppermute(far_rows[:, :, 256:].reshape(128, 384), "seq", across)
+    far_keys = far_rows[:, :, 256:].reshape(128, 384)
+    side, mid_a, mid_b, _ = lax.optimization_barrier((side, mid_a, mid_b, far_keys))
+    far_here = lax.ppermute(far_keys, "seq", across)
     swapped = swap(jnp.concatenate([own, side, mid_a, mid_b], 0), 1)
+    state = ((LOCAL_HEADS, ROWS, LANES), f32)
+    asked, _ = lax.optimization_barrier((query, far_rows))
+    (near,) = call(
+        near_kernel, 3, [state], [(slide_tiles, s), (asked, v), (own, v), (side, v)]
+    )
+    far_here, _ = lax.optimization_barrier((far_here, near))
     far_other = swap(far_here, 1)
-    state = ((LOCAL_HEADS, ROWS, LANES), f32)
-    (near,) = call(
-        near_kernel, 5, [state], [(slide_tiles, s), (query, v), (own, v), (side, v)]
-    )
     (parts,) = call(
         far_kernel,
         2,
         [((FAR_GROUP, FAR_ROWS, 384), f32)],
         [(slide_tiles, s), (far_rows, v), (far_here, v), (far_other, v)],
     )
+    near, _ = lax.optimization_barrier((near, parts))
     (both,) = call(
         rest_kernel,
-        7,
+        5,
         [state],
         [
             (slide_tiles, s), (query, v), (own, v), (side, v), (mid_a, v), (mid_b, v), (swapped, v),
             (near, v),
         ],
     )
-    late, _ = lax.optimization_barrier((mine, both))
-    theirs = swap(late, 1)
     parts = lax.all_to_all(
         parts, "seq", split_axis=0, concat_axis=0, tiled=True, axis_index_groups=columns
     )
+    mine, _ = lax.optimization_barrier((mine, parts))
     terms, far_attended = call(
         finish_kernel,
         3,
@@ -457,19 +464,14 @@
         [pltpu.VMEM(*state)],
     )
     terms = lax.all_to_all(terms, "mp", split_axis=0, concat_axis=0, tiled=True)
-    attended, normed, total = ffn(
-        first_kernel,
-        [tokens, terms, ffn_gain],
-        mine,
-        [((BLOCK, WIDTH), bf16), ((BLOCK, WIDTH), bf16), ((BLOCK, WIDTH), f32)],
-    )
-    (ffn_out,) = ffn(
-        second_kernel,
-        [normed, total],
-        theirs,
-        [((BLOCK, WIDTH), bf16)],
-        [pltpu.VMEM((BLOCK, WIDTH), f32)],
-    )
+    attended, normed = call(
+        norm_kernel,
+        1,
+        [((BLOCK, WIDTH), bf16), ((BLOCK, WIDTH), bf16)],
+        [(tokens, v), (terms, v), (ffn_gain, v)],
+    )
+    kept, sent = ffn(normed, swap(normed, 1), mine)
+    ffn_out = (kept + swap(sent, 1).astype(f32)).astype(bf16)
     return (attended, far_attended, ffn_out)
 
 

time: 153 us -> 121 us (0.79)
  the two profiles are of different devices: /device:TPU:8 before, /device:TPU:1 now
where the time goes in v5:
time: 121 us
  starting transfers between devices  48.1 us (40%)
  Pallas kernels  19.8 us (16%)
  between operations  14.2 us (12%)
  blocking collectives  13.9 us (11%)
  waiting for transfers between devices  12.1 us (10%)
  local copies, waits for them, and re-layouts  10.5 us (9%)
  other arithmetic  1.8 us (1%)
    ppermute x7, starting transfers between devices, swap(): lax.ppermute(value, 'seq', [(i, i ^ step) for i in range(lax.axis_size('s...  22.6 us
    pallas_call x8, Pallas kernels, call(): pl.pallas_call(kernel, out_shape=[jax.ShapeDtypeStruct(*out) for out in o...  16.6 us
    all_to_all x1, starting transfers between devices, local(): lax.all_to_all(parts, 'seq', split_axis=0, concat_axis=0, tiled=True, axi...  14.7 us
    all_to_all x1, blocking collectives, local(): terms = lax.all_to_all(terms, 'mp', split_axis=0, concat_axis=0, tiled=True)  13.9 us
    unnamed x34, local copies, waits for them, and re-layouts  10.5 us
    all_to_all x1, starting transfers between devices, local(): lax.all_to_all(far, 'seq', split_axis=0, concat_axis=0, tiled=True, axis_...  10 us
    ppermute x7, waiting for transfers between devices, swap(): lax.ppermute(value, 'seq', [(i, i ^ step) for i in range(lax.axis_size('s...  8.29 us
    pallas_call x1, Pallas kernels, ffn(): pl.pallas_call(ffn_kernel, grid=(4,), out_shape=[jax.ShapeDtypeStruct(*ou...  3.21 us
  transfers between devices with their start and end apart: 11, of which 6 were waited for; matrix products, arithmetic and copies ran while one was open for 1% of the time, Pallas kernels for 13%

profile of v5, /device:TPU:1, one launch (start us, length us, event | category | flops | bytes accessed | tf_op | source)
XLA Modules:
  0.0 120.5 jit_solution(11980302118484834312)
XLA Ops:
  7.2 0.0 all-gather.3.cloned.1.call-start
  7.2 1.3 %copy-done.1 = bf16[768,768]{1,0:T(8,128)(2,1)S(1)} copy-done((bf16[768,768]{1,0:T(8,128)(2,1)S(1)}, bf16[768,768]{1,0:T(8,128)(2,1)}, u32[]{:S(2)}) %copy-start.1) | copy-done | bytes 1179672
  8.5 1.3 %copy-done.2 = bf16[768,768]{1,0:T(8,128)(2,1)S(1)} copy-done((bf16[768,768]{1,0:T(8,128)(2,1)S(1)}, bf16[768,768]{1,0:T(8,128)(2,1)}, u32[]{:S(2)}) %copy-start.2) | copy-done | bytes 1179672
  9.8 1.1 shard_map.128
  10.9 0.0 all-gather.3.cloned.1.call-update
  10.9 0.2 copy-done.3
  11.1 0.3 copy-done.4
  11.4 0.1 copy-done.5
  11.5 0.1 copy-done.6
  11.6 1.6 %shard_map.121 = bf16[8,16,640]{2,1,0:T(8,128)(2,1)} custom-call(bf16[512,768]{1,0:T(8,128)(2,1)S(1)} %copy-done.3, bf16[768]{0:T(1024)(128)(2,1)S(1)} %copy-done.8, bf16[192,768]{1,0:T(8,128)(2,1)S(1)} %bitcast.6, bf16[192,768]{1,0:T(8,128)(2,1)S(1)} %bitcast.8, bf16[192,768]{1,0:T(8,128)(2,1)S(1)} %bitcast.10), custom_call_target="tpu_custom_call" | custom-call | flops 2200000000 | bytes 2000000 | tf_op jit(solution)/shard_map/pallas_call | solution.py:383
  13.2 1.8 %shard_map.122 = (bf16[512,256]{1,0:T(8,128)(2,1)S(1)}, bf16[512,384]{1,0:T(8,128)(2,1)S(1)}, bf16[128,384]{1,0:T(8,128)(2,1)S(1)}) custom-call(bf16[512,768]{1,0:T(8,128)(2,1)S(1)} %copy-done.3, bf16[768]{0:T(1024)(128)(2,1)S(1)} %copy-done.8, bf16[192,768]{1,0:T(8,128)(2,1)S(1)} %bitcast.7, bf16[192,768]{1,0:T(8,128)(2,1)S(1)} %bitcast.9, ...), custom_call_target="tpu_custom_call" | custom-call | flops 3300000000 | bytes 3000000 | tf_op jit(solution)/shard_map/pallas_call | solution.py:383
  15.0 0.0 copy-start.10
  15.0 4.0 %collective-permute-start.1 = (bf16[512,384]{1,0:T(8,128)(2,1)S(1)}, bf16[512,384]{1,0:T(8,128)(2,1)S(1)}, u32[]{:S(2)}, u32[]{:S(2)}) collective-permute-start(bf16[512,384]{1,0:T(8,128)(2,1)S(1)} %get-tuple-element.23.own), channel_id=1, source_target_pairs={{0,8},{4,12},{8,0},{12,4},{16,24},{20,28},{24,16},{28,20},{32,40},... | collective-permute-start | bytes 1179656 | tf_op jit(solution)/shard_map/ppermute | solution.py:397
  19.0 10.0 %all-to-all-start = ((bf16[8,16,640]{2,1,0:T(8,128)(2,1)}), bf16[8,16,640]{2,1,0:T(8,128)(2,1)S(1)}, u32[]{:S(2)}, u32[]{:S(2)}) async-start(bf16[8,16,640]{2,1,0:T(8,128)(2,1)} %shard_map.121), calls=%async_computation | async-start | bytes 327680 | tf_op jit(solution)/shard_map/all_to_all | solution.py:425
  29.1 4.1 %collective-permute-start.3 = (bf16[128,384]{1,0:T(8,128)(2,1)S(1)}, bf16[128,384]{1,0:T(8,128)(2,1)S(1)}, u32[]{:S(2)}, u32[]{:S(2)}) collective-permute-start(bf16[128,384]{1,0:T(8,128)(2,1)S(1)} %get-tuple-element.24), channel_id=1, source_target_pairs={{0,24},{4,28},{8,16},{12,20},{16,8},{20,12},{24,0},{28,4},{32,56},... | collective-permute-start | bytes 294920 | tf_op jit(solution)/shard_map/ppermute | solution.py:397
  33.2 2.0 %collective-permute-start.2 = (bf16[128,384]{1,0:T(8,128)(2,1)S(1)}, bf16[128,384]{1,0:T(8,128)(2,1)S(1)}, u32[]{:S(2)}, u32[]{:S(2)}) collective-permute-start(bf16[128,384]{1,0:T(8,128)(2,1)S(1)} %get-tuple-element.24), channel_id=1, source_target_pairs={{0,16},{4,20},{8,24},{12,28},{16,0},{20,4},{24,8},{28,12},{32,48},... | collective-permute-start | bytes 294920 | tf_op jit(solution)/shard_map/ppermute | solution.py:397
  35.2 1.9 %all-to-all-done.rows = bf16[8,16,640]{2,1,0:T(8,128)(2,1)S(1)} async-done(((bf16[8,16,640]{2,1,0:T(8,128)(2,1)}), bf16[8,16,640]{2,1,0:T(8,128)(2,1)S(1)}, u32[]{:S(2)}, u32[]{:S(2)}) %all-to-all-start) | async-done | bytes 163872 | tf_op jit(solution)/shard_map/all_to_all | solution.py:425
  37.2 0.0 collective-permute-done.3.mid_b
  37.2 5.0 %collective-permute-done.2.mid_a = bf16[128,384]{1,0:T(8,128)(2,1)S(1)} collective-permute-done((bf16[128,384]{1,0:T(8,128)(2,1)S(1)}, bf16[128,384]{1,0:T(8,128)(2,1)S(1)}, u32[]{:S(2)}, u32[]{:S(2)}) %collective-permute-start.2) | collective-permute-done | bytes 98336 | tf_op jit(solution)/shard_map/ppermute | solution.py:397
  42.1 0.0 collective-permute-done.1.side
  42.1 1.1 pad_maximum_fusion
  43.2 3.1 %collective-permute-start.5 = (bf16[1280,384]{1,0:T(8,128)(2,1)}, bf16[1280,384]{1,0:T(8,128)(2,1)S(1)}, u32[]{:S(2)}, u32[]{:S(2)}) collective-permute-start(bf16[1280,384]{1,0:T(8,128)(2,1)} %pad_maximum_fusion), channel_id=1, source_target_pairs={{0,4},{4,0},{8,12},{12,8},{16,20},{20,16},{24,28},{28,24},{32,36},... | collective-permute-start | bytes 2949128 | tf_op jit(solution)/shard_map/ppermute | solution.py:397
  46.3 0.7 collective-permute-start
  47.0 3.2 %shard_map.123.held = f32[3,512,128]{2,1,0:T(8,128)S(1)} custom-call(s32[4]{0:T(128)S(1)} %copy-done.10, bf16[512,256]{1,0:T(8,128)(2,1)S(1)} %get-tuple-element.22.query, bf16[512,384]{1,0:T(8,128)(2,1)S(1)} %get-tuple-element.23.own, bf16[512,384]{1,0:T(8,128)(2,1)S(1)} %collective-permute-done.1.side), custom_call_target="tpu_custom_call" | custom-call | flops 3300000000 | bytes 3000000 | tf_op jit(solution)/shard_map/pallas_call | solution.py:383
  50.2 0.9 copy-done.11
  51.1 0.0 collective-permute-done.here
  51.1 1.9 %collective-permute-start.4 = (bf16[128,384]{1,0:T(8,128)(2,1)S(1)}, bf16[128,384]{1,0:T(8,128)(2,1)S(1)}, u32[]{:S(2)}, u32[]{:S(2)}) collective-permute-start(bf16[128,384]{1,0:T(8,128)(2,1)S(1)} %collective-permute-done.here), channel_id=1, source_target_pairs={{0,4},{4,0},{8,12},{12,8},{16,20},{20,16},{24,28},{28,24},{32,36},... | collective-permute-start | bytes 294920 | tf_op jit(solution)/shard_map/ppermute | solution.py:397
  53.0 1.3 %collective-permute-done.4.other = bf16[128,384]{1,0:T(8,128)(2,1)S(1)} collective-permute-done((bf16[128,384]{1,0:T(8,128)(2,1)S(1)}, bf16[128,384]{1,0:T(8,128)(2,1)S(1)}, u32[]{:S(2)}, u32[]{:S(2)}) %collective-permute-start.4) | collective-permute-done | bytes 98336 | tf_op jit(solution)/shard_map/ppermute | solution.py:397
  54.3 1.9 %shard_map.124 = f32[8,16,384]{2,1,0:T(8,128)} custom-call(s32[4]{0:T(128)S(1)} %copy-done.10, bf16[8,16,640]{2,1,0:T(8,128)(2,1)S(1)} %all-to-all-done.rows, bf16[128,384]{1,0:T(8,128)(2,1)S(1)} %collective-permute-done.here, bf16[128,384]{1,0:T(8,128)(2,1)S(1)} %collective-permute-done.4.other), custom_call_target="tpu_custom_call" | custom-call | flops 2200000000 | bytes 2000000 | tf_op jit(solution)/shard_map/pallas_call | solution.py:383
  56.2 14.7 %all-to-all-start.1 = ((f32[8,16,384]{2,1,0:T(8,128)}), f32[8,16,384]{2,1,0:T(8,128)S(1)}, u32[]{:S(2)}, u32[]{:S(2)}) async-start(f32[8,16,384]{2,1,0:T(8,128)} %shard_map.124), calls=%async_computation.1 | async-start | bytes 393216 | tf_op jit(solution)/shard_map/all_to_all | solution.py:455
  70.9 0.0 collective-permute-done.5.swapped
  70.9 1.2 copy-done.12
  72.1 0.9 copy-done.16
  73.0 4.5 %shard_map.125.held = f32[3,512,128]{2,1,0:T(8,128)S(1)} custom-call(s32[4]{0:T(128)S(1)} %copy-done.10, bf16[512,256]{1,0:T(8,128)(2,1)S(1)} %copy-done.16, bf16[512,384]{1,0:T(8,128)(2,1)S(1)} %get-tuple-element.23.own, bf16[512,384]{1,0:T(8,128)(2,1)S(1)} %collective-permute-done.1.side, bf16[128,384]{1,0:T(8,128)(2,1)S(1)} %collective-permute-done.2.mid_a, ...), custom_call_target="tpu_custom_call" | custom-call | flops 5500000256 | bytes 5000000 | tf_op jit(solution)/shard_map/pallas_call | solution.py:383
  77.6 0.9 copy-done.13
  78.5 1.9 %all-to-all-done.1.parts = f32[8,16,384]{2,1,0:T(8,128)S(1)} async-done(((f32[8,16,384]{2,1,0:T(8,128)}), f32[8,16,384]{2,1,0:T(8,128)S(1)}, u32[]{:S(2)}, u32[]{:S(2)}) %all-to-all-start.1) | async-done | bytes 196640 | tf_op jit(solution)/shard_map/all_to_all | solution.py:455
  80.3 1.1 copy-done.14
  81.5 1.6 %shard_map.126 = (bf16[4,128,768]{2,1,0:T(8,128)(2,1)S(1)}, bf16[16,192]{1,0:T(8,128)(2,1)}) custom-call(f32[8,16,384]{2,1,0:T(8,128)S(1)} %all-to-all-done.1.parts, f32[3,512,128]{2,1,0:T(8,128)S(1)} %copy-done.14, bf16[192,768]{1,0:T(8,128)(2,1)S(1)} %copy-done.7), custom_call_target="tpu_custom_call" | custom-call | flops 3300000000 | bytes 3000000 | tf_op jit(solution)/shard_map/pallas_call | solution.py:383
  83.1 13.9 %all_to_all.15.terms = bf16[4,128,768]{2,1,0:T(8,128)(2,1)S(1)} all-to-all(bf16[4,128,768]{2,1,0:T(8,128)(2,1)S(1)} %get-tuple-element.30), channel_id=1, replica_groups=mesh['seq'=128,'mp'=4] {'mp'}, dimensions={0} | all-to-all | bytes 1572864 | tf_op jit(solution)/shard_map/all_to_all | solution.py:466
  97.0 0.8 shard_map.127
  97.9 5.1 %collective-permute-start.6 = (bf16[128,768]{1,0:T(8,128)(2,1)S(1)}, bf16[128,768]{1,0:T(8,128)(2,1)S(1)}, u32[]{:S(2)}, u32[]{:S(2)}) collective-permute-start(bf16[128,768]{1,0:T(8,128)(2,1)S(1)} %get-tuple-element.33.own), channel_id=1, source_target_pairs={{0,4},{4,0},{8,12},{12,8},{16,20},{20,16},{24,28},{28,24},{32,36},... | collective-permute-start | bytes 589832 | tf_op jit(solution)/shard_map/ppermute | solution.py:397
  103.0 0.0 all-gather.3.cloned.1.call-done
  103.0 1.0 collective-permute-done.6.other
  104.1 2.3 %copy-done = bf16[3072,768]{1,0:T(8,128)(2,1)S(1)} copy-done((bf16[3072,768]{1,0:T(8,128)(2,1)S(1)}, bf16[3072,768]{1,0:T(8,128)(2,1)}, u32[]{:S(2)}) %copy-start) | copy-done | bytes 4718616
  106.4 3.2 %shard_map.129 = (f32[128,768]{1,0:T(8,128)S(1)}, bf16[128,768]{1,0:T(8,128)(2,1)S(1)}) custom-call(bf16[128,768]{1,0:T(8,128)(2,1)S(1)} %get-tuple-element.33.own, bf16[128,768]{1,0:T(8,128)(2,1)S(1)} %collective-permute-done.6.other, bf16[4,768,768]{2,1,0:T(8,128)(2,1)S(1)} %bitcast.5), custom_call_target="tpu_custom_call" | custom-call | flops 4000000000 | bytes 5000000 | tf_op jit(solution)/shard_map/pallas_call | solution.py:363
  109.6 2.3 %collective-permute-start.7 = (bf16[128,768]{1,0:T(8,128)(2,1)S(1)}, bf16[128,768]{1,0:T(8,128)(2,1)S(1)}, u32[]{:S(2)}, u32[]{:S(2)}) collective-permute-start(bf16[128,768]{1,0:T(8,128)(2,1)S(1)} %get-tuple-element.36), channel_id=1, source_target_pairs={{0,4},{4,0},{8,12},{12,8},{16,20},{20,16},{24,28},{28,24},{32,36},... | collective-permute-start | bytes 589832 | tf_op jit(solution)/shard_map/ppermute | solution.py:397
  111.9 1.0 collective-permute-done.7
  112.9 0.7 add_convert_fusion
  (22 shorter events, 0.0 us)
Async XLA Ops:
  7.2 95.9 %all-gather.3.cloned.1.call-start = ((), (), s32[]{:S(2)}) async-start(), calls=%async_computation.3 | async-start | bytes 5898240 | tf_op jit(solution)/shard_map/all_gather | solution.py:408
  7.2 1.3 %copy-start.1 = (bf16[768,768]{1,0:T(8,128)(2,1)S(1)}, bf16[768,768]{1,0:T(8,128)(2,1)}, u32[]{:S(2)}) copy-start(bf16[768,768]{1,0:T(8,128)(2,1)} %w_up.1) | copy-start | bytes 3538948
  8.5 1.3 %copy-start.2 = (bf16[768,768]{1,0:T(8,128)(2,1)S(1)}, bf16[768,768]{1,0:T(8,128)(2,1)}, u32[]{:S(2)}) copy-start(bf16[768,768]{1,0:T(8,128)(2,1)} %w_down.1) | copy-start | bytes 3538948
  9.8 1.4 %copy-start.3 = (bf16[512,768]{1,0:T(8,128)(2,1)S(1)}, bf16[512,768]{1,0:T(8,128)(2,1)}, u32[]{:S(2)}) copy-start(bf16[512,768]{1,0:T(8,128)(2,1)} %tokens.4) | copy-start | bytes 2359300
  9.8 1.6 %copy-start.4 = (bf16[768,192]{0,1:T(8,128)(2,1)S(1)}, bf16[768,192]{0,1:T(8,128)(2,1)}, u32[]{:S(2)}) copy-start(bf16[768,192]{0,1:T(8,128)(2,1)} %param.13) | copy-start | bytes 884740
  9.8 1.7 %copy-start.5 = (bf16[768,192]{0,1:T(8,128)(2,1)S(1)}, bf16[768,192]{0,1:T(8,128)(2,1)}, u32[]{:S(2)}) copy-start(bf16[768,192]{0,1:T(8,128)(2,1)} %param.14) | copy-start | bytes 884740
  9.8 1.8 %copy-start.6 = (bf16[768,192]{0,1:T(8,128)(2,1)S(1)}, bf16[768,192]{0,1:T(8,128)(2,1)}, u32[]{:S(2)}) copy-start(bf16[768,192]{0,1:T(8,128)(2,1)} %param.15) | copy-start | bytes 884740
  9.8 1.8 %copy-start.8 = (bf16[768]{0:T(1024)(128)(2,1)S(1)}, bf16[768]{0:T(1024)(128)(2,1)}, u32[]{:S(2)}) copy-start(bf16[768]{0:T(1024)(128)(2,1)} %gain.4) | copy-start | bytes 4612
  15.0 35.2 %copy-start.15 = (bf16[512,256]{1,0:T(8,128)(2,1)}, bf16[512,256]{1,0:T(8,128)(2,1)S(1)}, u32[]{:S(2)}) copy-start(bf16[512,256]{1,0:T(8,128)(2,1)S(1)} %get-tuple-element.22.query) | copy-start | bytes 786436
  15.0 32.0 %copy-start.10 = (s32[4]{0:T(128)S(1)}, s32[4]{0:T(128)}, u32[]{:S(2)}) copy-start(s32[4]{0:T(128)} %tiles.5) | copy-start | bytes 52
  15.0 27.1 %collective-permute-start.1 = (bf16[512,384]{1,0:T(8,128)(2,1)S(1)}, bf16[512,384]{1,0:T(8,128)(2,1)S(1)}, u32[]{:S(2)}, u32[]{:S(2)}) collective-permute-start(bf16[512,384]{1,0:T(8,128)(2,1)S(1)} %get-tuple-element.23.own), channel_id=1, source_target_pairs={{0,8},{4,12},{8,0},{12,4},{16,24},{20,28},{24,16},{28,20},{32,40},... | collective-permute-start | bytes 1179656 | tf_op jit(solution)/shard_map/ppermute | solution.py:397
  19.0 18.1 %all-to-all-start = ((bf16[8,16,640]{2,1,0:T(8,128)(2,1)}), bf16[8,16,640]{2,1,0:T(8,128)(2,1)S(1)}, u32[]{:S(2)}, u32[]{:S(2)}) async-start(bf16[8,16,640]{2,1,0:T(8,128)(2,1)} %shard_map.121), calls=%async_computation | async-start | bytes 327680 | tf_op jit(solution)/shard_map/all_to_all | solution.py:425
  29.1 8.1 %collective-permute-start.3 = (bf16[128,384]{1,0:T(8,128)(2,1)S(1)}, bf16[128,384]{1,0:T(8,128)(2,1)S(1)}, u32[]{:S(2)}, u32[]{:S(2)}) collective-permute-start(bf16[128,384]{1,0:T(8,128)(2,1)S(1)} %get-tuple-element.24), channel_id=1, source_target_pairs={{0,24},{4,28},{8,16},{12,20},{16,8},{20,12},{24,0},{28,4},{32,56},... | collective-permute-start | bytes 294920 | tf_op jit(solution)/shard_map/ppermute | solution.py:397
  33.2 8.9 %collective-permute-start.2 = (bf16[128,384]{1,0:T(8,128)(2,1)S(1)}, bf16[128,384]{1,0:T(8,128)(2,1)S(1)}, u32[]{:S(2)}, u32[]{:S(2)}) collective-permute-start(bf16[128,384]{1,0:T(8,128)(2,1)S(1)} %get-tuple-element.24), channel_id=1, source_target_pairs={{0,16},{4,20},{8,24},{12,28},{16,0},{20,4},{24,8},{28,12},{32,48},... | collective-permute-start | bytes 294920 | tf_op jit(solution)/shard_map/ppermute | solution.py:397
  43.2 27.7 %collective-permute-start.5 = (bf16[1280,384]{1,0:T(8,128)(2,1)}, bf16[1280,384]{1,0:T(8,128)(2,1)S(1)}, u32[]{:S(2)}, u32[]{:S(2)}) collective-permute-start(bf16[1280,384]{1,0:T(8,128)(2,1)} %pad_maximum_fusion), channel_id=1, source_target_pairs={{0,4},{4,0},{8,12},{12,8},{16,20},{20,16},{24,28},{28,24},{32,36},... | collective-permute-start | bytes 2949128 | tf_op jit(solution)/shard_map/ppermute | solution.py:397
  46.3 4.8 %collective-permute-start = (bf16[128,384]{1,0:T(8,128)(2,1)S(1)}, bf16[128,384]{1,0:T(8,128)(2,1)S(1)}, u32[]{:S(2)}, u32[]{:S(2)}) collective-permute-start(bf16[128,384]{1,0:T(8,128)(2,1)S(1)} %bitcast.12), channel_id=1, source_target_pairs={{0,0},{4,4},{8,8},{12,12},{16,16},{20,20},{24,24},{28,28},{32,32},... | collective-permute-start | bytes 294920 | tf_op jit(solution)/shard_map/ppermute | solution.py:430
  50.2 0.9 copy-start.11
  51.1 3.2 %collective-permute-start.4 = (bf16[128,384]{1,0:T(8,128)(2,1)S(1)}, bf16[128,384]{1,0:T(8,128)(2,1)S(1)}, u32[]{:S(2)}, u32[]{:S(2)}) collective-permute-start(bf16[128,384]{1,0:T(8,128)(2,1)S(1)} %collective-permute-done.here), channel_id=1, source_target_pairs={{0,4},{4,0},{8,12},{12,8},{16,20},{20,16},{24,28},{28,24},{32,36},... | collective-permute-start | bytes 294920 | tf_op jit(solution)/shard_map/ppermute | solution.py:397
  56.2 24.2 %all-to-all-start.1 = ((f32[8,16,384]{2,1,0:T(8,128)}), f32[8,16,384]{2,1,0:T(8,128)S(1)}, u32[]{:S(2)}, u32[]{:S(2)}) async-start(f32[8,16,384]{2,1,0:T(8,128)} %shard_map.124), calls=%async_computation.1 | async-start | bytes 393216 | tf_op jit(solution)/shard_map/all_to_all | solution.py:455
  70.9 9.5 %copy-start.7 = (bf16[192,768]{1,0:T(8,128)(2,1)S(1)}, bf16[192,768]{1,0:T(8,128)(2,1)}, u32[]{:S(2)}) copy-start(bf16[192,768]{1,0:T(8,128)(2,1)} %w_out.1) | copy-start | bytes 884740
  70.9 1.2 copy-start.12
  72.1 0.9 copy-start.16
  77.5 0.9 copy-start.13
  78.5 18.6 %copy-start.9 = (bf16[768]{0:T(1024)(128)(2,1)S(1)}, bf16[768]{0:T(1024)(128)(2,1)}, u32[]{:S(2)}) copy-start(bf16[768]{0:T(1024)(128)(2,1)} %gain.5) | copy-start | bytes 4612
  80.3 1.1 copy-start.14
  97.9 6.2 %collective-permute-start.6 = (bf16[128,768]{1,0:T(8,128)(2,1)S(1)}, bf16[128,768]{1,0:T(8,128)(2,1)S(1)}, u32[]{:S(2)}, u32[]{:S(2)}) collective-permute-start(bf16[128,768]{1,0:T(8,128)(2,1)S(1)} %get-tuple-element.33.own), channel_id=1, source_target_pairs={{0,4},{4,0},{8,12},{12,8},{16,20},{20,16},{24,28},{28,24},{32,36},... | collective-permute-start | bytes 589832 | tf_op jit(solution)/shard_map/ppermute | solution.py:397
  104.1 2.3 %copy-start = (bf16[3072,768]{1,0:T(8,128)(2,1)S(1)}, bf16[3072,768]{1,0:T(8,128)(2,1)}, u32[]{:S(2)}) copy-start(bf16[3072,768]{1,0:T(8,128)(2,1)} %all-gather.3.cloned.1.call-done) | copy-start | bytes 14155780
  109.6 3.3 %collective-permute-start.7 = (bf16[128,768]{1,0:T(8,128)(2,1)S(1)}, bf16[128,768]{1,0:T(8,128)(2,1)S(1)}, u32[]{:S(2)}, u32[]{:S(2)}) collective-permute-start(bf16[128,768]{1,0:T(8,128)(2,1)S(1)} %get-tuple-element.36), channel_id=1, source_target_pairs={{0,4},{4,0},{8,12},{12,8},{16,20},{20,16},{24,28},{28,24},{32,36},... | collective-permute-start | bytes 589832 | tf_op jit(solution)/shard_map/ppermute | solution.py:397
Sparse Core Ops, SparseCore 0:
  11.1 63.4 all-gather.2

commit v6 on v5

--- a/solution.py
+++ b/solution.py
@@ -173,7 +173,7 @@
     return jnp.concatenate([key_marks(rows + (seq ^ step) * ROWS, ends) for step in steps], 0)
 
 
-def near_kernel(tiles, query, own, side, state):
+def near_kernel(tiles, query, own, side, *state):
     ends = slide_ends(tiles)
     seq = lax.axis_index("seq")
     marks = query_marks(row_at(iota((ROWS, LANES), 0)) + seq * ROWS, ends)
@@ -183,7 +183,7 @@
         asked = head_lanes(query[:, tile(QUERY_TILE[head])], head)
         keys = jnp.concatenate([own[:, key_tile], side[:, key_tile]], 0)
         values = jnp.concatenate([own[:, value_tile], side[:, value_tile]], 0)
-        _, state[head] = attend(
+        _, state[head][...] = attend(
             jnp.concatenate([asked, marks], 1),
             jnp.concatenate([keys, keys_marks], 1),
             jnp.concatenate([values, keys_marks], 1),
@@ -191,7 +191,8 @@
         )
 
 
-def rest_kernel(tiles, query, own, side, mid_a, mid_b, swapped, held, state):
+def rest_kernel(tiles, query, own, side, mid_a, mid_b, swapped, *refs):
+    held, state = refs[:LOCAL_HEADS], refs[LOCAL_HEADS:]
     ends = slide_ends(tiles)
     seq, mp = lax.axis_index("seq"), lax.axis_index("mp")
     marks = query_marks(row_at(iota((ROWS, LANES), 0)) + seq * ROWS, ends)
@@ -205,7 +206,7 @@
             jnp.concatenate([swapped[: 2 * ROWS, value_tile], near_marks], 1),
             head,
         )
-        state[head] = join(held[head], more, peak, head)
+        state[head][...] = join(held[head][...], more, peak, head)
 
         offset = (mp * LOCAL_HEADS + head) & 3
         start = pl.multiple_of(offset * CLASS_ROWS, CLASS_ROWS)
@@ -239,7 +240,7 @@
             jnp.concatenate([gathered(value_tile), class_marks], 1),
             head,
         )
-        state[head, picked, :] = join(state[head, picked, :], more, peak, head)
+        state[head][picked, :] = join(state[head][picked, :], more, peak, head)
 
 
 def far_kernel(tiles, rows, here, other, parts):
@@ -275,9 +276,9 @@
         parts[:, :, tile(head)] = part.reshape(FAR_GROUP, FAR_ROWS, LANES)
 
 
-def finish_kernel(parts, held, w_out, terms, far_out, state):
+def finish_kernel(parts, w_out, *refs):
+    held, (terms, far_out), state = refs[:LOCAL_HEADS], refs[LOCAL_HEADS:-LOCAL_HEADS], refs[-LOCAL_HEADS:]
     mp = lax.axis_index("mp")
-    state[...] = held[...]
     far_parts = []
     for head in range(LOCAL_HEADS):
         spare = SPARE[head]
@@ -291,7 +292,8 @@
         number = mp * LOCAL_HEADS + head
         start = (number & 3) * CLASS_ROWS + (number >> 2) * FAR_ROWS
         picked = pl.ds(pl.multiple_of(start, FAR_ROWS), FAR_ROWS)
-        state[head, picked, :] = join(state[head, picked, :], total, peak, head)
+        state[head][...] = held[head][...]
+        state[head][picked, :] = join(state[head][picked, :], total, peak, head)
 
     def packed(values):
         first = jnp.where(iota(values[0].shape, 1) < HEAD_DIM, values[0], values[1])
@@ -303,7 +305,7 @@
     back = (place_of(iota((ROWS, ROWS), 0)) == iota((ROWS, ROWS), 1)).astype(jnp.bfloat16)
     first, last = packed(
         [
-            state[head] / state[head, :, SPARE[head] + 1 : SPARE[head] + 2]
+            state[head][...] / state[head][:, SPARE[head] + 1 : SPARE[head] + 2]
             for head in range(LOCAL_HEADS)
         ]
     )
@@ -374,7 +376,7 @@
         cost_estimate=pl.CostEstimate(
             flops=int(4e9), bytes_accessed=int(5e6), transcendentals=0
         ),
-        compiler_params=pltpu.CompilerParams(vmem_limit_bytes=VMEM),
+        compiler_params=pltpu.CompilerParams(vmem_limit_bytes=56 * 1024 * 1024),
     )(own, other, weights)
 
 
@@ -404,8 +406,6 @@
     across = [
         (16 * z + (place ^ (2 * z)), 16 * z + place) for z in range(FAR_GROUP) for place in range(16)
     ]
-    (packed,) = call(weights_kernel, 2, [((2 * HALF, WIDTH), bf16)], [(w_up, v), (w_down, v)])
-    mine = lax.all_gather(packed, "mp", axis=0)
     w_query, w_key, w_value = w_query.T, w_key.T, w_value.T
     (far,) = call(
         far_rows_kernel,
@@ -413,43 +413,45 @@
         [((FAR_GROUP, FAR_ROWS, 640), bf16)],
         [(tokens, v), (attn_gain, v), (w_query, v), (w_key, v), (w_value, v)],
     )
-    ordered, _ = lax.optimization_barrier((tokens, far))
+    far_rows = lax.all_to_all(
+        far, "seq", split_axis=0, concat_axis=0, tiled=True, axis_index_groups=columns
+    )
+    tokens, w_up, w_down, _ = lax.optimization_barrier((tokens, w_up, w_down, far))
     query, own, mid = call(
         project_kernel,
-        3,
+        2,
         [((ROWS, 256), bf16), ((ROWS, 384), bf16), ((CLASS_ROWS, 384), bf16)],
-        [(ordered, v), (attn_gain, v), (w_query, v), (w_key, v), (w_value, v)],
-    )
+        [(tokens, v), (attn_gain, v), (w_query, v), (w_key, v), (w_value, v)],
+    )
+    (packed,) = call(weights_kernel, 2, [((2 * HALF, WIDTH), bf16)], [(w_up, v), (w_down, v)])
+    mine = lax.all_gather(packed, "mp", axis=0)
     side = swap(own, 2)
+
+    far_keys = far_rows[:, :, 256:].reshape(128, 384)
+    far_here = lax.ppermute(far_keys, "seq", across)
+    query, _ = lax.optimization_barrier((query, far_keys))
     mid_a, mid_b = swap(mid, 4), swap(mid, 6)
-    far_rows = lax.all_to_all(
-        far, "seq", split_axis=0, concat_axis=0, tiled=True, axis_index_groups=columns
-    )
-    far_keys = far_rows[:, :, 256:].reshape(128, 384)
-    side, mid_a, mid_b, _ = lax.optimization_barrier((side, mid_a, mid_b, far_keys))
-    far_here = lax.ppermute(far_keys, "seq", across)
+    state = [((ROWS, LANES), f32)] * LOCAL_HEADS
+    near = call(near_kernel, 3, state, [(slide_tiles, s), (query, v), (own, v), (side, v)])
+    side, mid_a, mid_b, far_here, *near = lax.optimization_barrier(
+        (side, mid_a, mid_b, far_here, *near)
+    )
+    far_other = swap(far_here, 1)
     swapped = swap(jnp.concatenate([own, side, mid_a, mid_b], 0), 1)
-    state = ((LOCAL_HEADS, ROWS, LANES), f32)
-    asked, _ = lax.optimization_barrier((query, far_rows))
-    (near,) = call(
-        near_kernel, 3, [state], [(slide_tiles, s), (asked, v), (own, v), (side, v)]
-    )
-    far_here, _ = lax.optimization_barrier((far_here, near))
-    far_other = swap(far_here, 1)
     (parts,) = call(
         far_kernel,
         2,
         [((FAR_GROUP, FAR_ROWS, 384), f32)],
         [(slide_tiles, s), (far_rows, v), (far_here, v), (far_other, v)],
     )
-    near, _ = lax.optimization_barrier((near, parts))
-    (both,) = call(
+    parts, *near = lax.optimization_barrier((parts, *near))
+    both = call(
         rest_kernel,
         5,
-        [state],
+        state,
         [
             (slide_tiles, s), (query, v), (own, v), (side, v), (mid_a, v), (mid_b, v), (swapped, v),
-            (near, v),
+            *[(held, v) for held in near],
         ],
     )
     parts = lax.all_to_all(
@@ -460,8 +462,8 @@
         finish_kernel,
         3,
         [((4, BLOCK, WIDTH), bf16), ((FAR_ROWS, 192), bf16)],
-        [(parts, v), (both, v), (w_out, v)],
-        [pltpu.VMEM(*state)],
+        [(parts, v), (w_out, v), *[(held, v) for held in both]],
+        [pltpu.VMEM(*shape) for shape in state],
     )
     terms = lax.all_to_all(terms, "mp", split_axis=0, concat_axis=0, tiled=True)
     attended, normed = call(

time: 121 us -> 122 us (level)
  waiting for transfers between devices: 12.1 us -> 5.52 us
  local copies, waits for them, and re-layouts: 10.5 us -> 17 us
  starting transfers between devices: 48.1 us -> 44.3 us
  Pallas kernels: 19.8 us -> 22.3 us
    unnamed x34 -> x62, local copies, waits for them, and re-layouts: 10.5 us -> 17 us
    ppermute x7, waiting for transfers between devices: 8.29 us -> 3.56 us  [swap(): lax.ppermute(value, 'seq', [(i, i ^ step) for i in range(lax.axis_size('s...]
    all_to_all x1, starting transfers between devices: 14.7 us -> 10.2 us  [local(): lax.all_to_all(parts, 'seq', split_axis=0, concat_axis=0, tiled=True, axi...]
    pallas_call x1, Pallas kernels: 3.21 us -> 5.98 us  [ffn(): pl.pallas_call(ffn_kernel, grid=(4,), out_shape=[jax.ShapeDtypeStruct(*ou...]
    all_to_all x1, waiting for transfers between devices: 1.88 us -> 0.01 us  [local(): lax.all_to_all(parts, 'seq', split_axis=0, concat_axis=0, tiled=True, axi...]
  transfers between devices with their start and end apart: 11 -> 11, of which waited for: 6 -> 4; matrix products, arithmetic and copies ran while one was open for 1% -> 1% of each run, Pallas kernels for 13% -> 11%
where the time goes in v6:
time: 122 us; the launch traced here: 121 us
  starting transfers between devices  44.3 us (36%)
  Pallas kernels  22.3 us (18%)
  local copies, waits for them, and re-layouts  17 us (14%)
  blocking collectives  14.5 us (12%)
  between operations  14.2 us (12%)
  waiting for transfers between devices  5.52 us (5%)
  other arithmetic  2.76 us (2%)
    ppermute x7, starting transfers between devices, swap(): lax.ppermute(value, 'seq', [(i, i ^ step) for i in range(lax.axis_size('s...  23.3 us
    unnamed x62, local copies, waits for them, and re-layouts  17 us
    pallas_call x8, Pallas kernels, call(): pl.pallas_call(kernel, out_shape=[jax.ShapeDtypeStruct(*out) for out in o...  16.3 us
    all_to_all x1, blocking collectives, local(): terms = lax.all_to_all(terms, 'mp', split_axis=0, concat_axis=0, tiled=True)  14.5 us
    all_to_all x1, starting transfers between devices, local(): lax.all_to_all(parts, 'seq', split_axis=0, concat_axis=0, tiled=True, axi...  10.2 us
    all_to_all x1, starting transfers between devices, local(): lax.all_to_all(far, 'seq', split_axis=0, concat_axis=0, tiled=True, axis_...  10 us
    pallas_call x1, Pallas kernels, ffn(): pl.pallas_call(ffn_kernel, grid=(4,), out_shape=[jax.ShapeDtypeStruct(*ou...  5.98 us
    ppermute x7, waiting for transfers between devices, swap(): lax.ppermute(value, 'seq', [(i, i ^ step) for i in range(lax.axis_size('s...  3.56 us
  transfers between devices with their start and end apart: 11, of which 4 were waited for; matrix products, arithmetic and copies ran while one was open for 1% of the time, Pallas kernels for 11%

profile of v6, /device:TPU:1, one launch (start us, length us, event | category | flops | bytes accessed | tf_op | source)
XLA Modules:
  0.0 120.7 jit_solution(11519908303100600437)
XLA Ops:
  7.2 1.1 copy-done.2
  8.3 1.0 copy-done.4
  9.3 1.0 copy-done.6
  10.3 1.0 copy-done.8
  11.2 0.7 copy-done.12
  11.9 1.6 %shard_map.121 = bf16[8,16,640]{2,1,0:T(8,128)(2,1)} custom-call(bf16[512,768]{1,0:T(8,128)(2,1)S(1)} %copy-done.2, bf16[768]{0:T(1024)(128)(2,1)S(1)} %copy-done.12, bf16[192,768]{1,0:T(8,128)(2,1)S(1)} %bitcast.5, bf16[192,768]{1,0:T(8,128)(2,1)S(1)} %bitcast.7, bf16[192,768]{1,0:T(8,128)(2,1)S(1)} %bitcast.9), custom_call_target="tpu_custom_call" | custom-call | flops 2200000000 | bytes 2000000 | tf_op jit(solution)/shard_map/pallas_call | solution.py:385
  13.6 1.1 shard_map.128
  14.7 0.1 copy-done.3
  14.9 0.3 copy-done.5
  15.2 0.1 copy-done.7
  15.3 1.8 %shard_map.122 = (bf16[512,256]{1,0:T(8,128)(2,1)S(1)}, bf16[512,384]{1,0:T(8,128)(2,1)S(1)}, bf16[128,384]{1,0:T(8,128)(2,1)S(1)}) custom-call(bf16[512,768]{1,0:T(8,128)(2,1)S(1)} %copy-done.3, bf16[768]{0:T(1024)(128)(2,1)S(1)} %copy-done.13, bf16[192,768]{1,0:T(8,128)(2,1)S(1)} %bitcast.6, bf16[192,768]{1,0:T(8,128)(2,1)S(1)} %bitcast.8, ...), custom_call_target="tpu_custom_call" | custom-call | flops 2200000000 | bytes 2000000 | tf_op jit(solution)/shard_map/pallas_call | solution.py:385
  17.2 4.0 %collective-permute-start = (bf16[512,384]{1,0:T(8,128)(2,1)S(1)}, bf16[512,384]{1,0:T(8,128)(2,1)S(1)}, u32[]{:S(2)}, u32[]{:S(2)}) collective-permute-start(bf16[512,384]{1,0:T(8,128)(2,1)S(1)} %get-tuple-element.35.own), channel_id=1, source_target_pairs={{0,8},{4,12},{8,0},{12,4},{16,24},{20,28},{24,16},{28,20},{32,40},... | collective-permute-start | bytes 1179656 | tf_op jit(solution)/shard_map/ppermute | solution.py:399
  21.2 10.0 %all-to-all-start = ((bf16[8,16,640]{2,1,0:T(8,128)(2,1)}), bf16[8,16,640]{2,1,0:T(8,128)(2,1)S(1)}, u32[]{:S(2)}, u32[]{:S(2)}) async-start(bf16[8,16,640]{2,1,0:T(8,128)(2,1)} %shard_map.121), calls=%async_computation | async-start | bytes 327680 | tf_op jit(solution)/shard_map/all_to_all | solution.py:416
  31.2 4.1 %collective-permute-start.2 = (bf16[128,384]{1,0:T(8,128)(2,1)S(1)}, bf16[128,384]{1,0:T(8,128)(2,1)S(1)}, u32[]{:S(2)}, u32[]{:S(2)}) collective-permute-start(bf16[128,384]{1,0:T(8,128)(2,1)S(1)} %get-tuple-element.36), channel_id=1, source_target_pairs={{0,24},{4,28},{8,16},{12,20},{16,8},{20,12},{24,0},{28,4},{32,56},... | collective-permute-start | bytes 294920 | tf_op jit(solution)/shard_map/ppermute | solution.py:399
  35.3 2.0 %collective-permute-start.1 = (bf16[128,384]{1,0:T(8,128)(2,1)S(1)}, bf16[128,384]{1,0:T(8,128)(2,1)S(1)}, u32[]{:S(2)}, u32[]{:S(2)}) collective-permute-start(bf16[128,384]{1,0:T(8,128)(2,1)S(1)} %get-tuple-element.36), channel_id=1, source_target_pairs={{0,16},{4,20},{8,24},{12,28},{16,0},{20,4},{24,8},{28,12},{32,48},... | collective-permute-start | bytes 294920 | tf_op jit(solution)/shard_map/ppermute | solution.py:399
  37.4 1.9 %all-to-all-done.rows = bf16[8,16,640]{2,1,0:T(8,128)(2,1)S(1)} async-done(((bf16[8,16,640]{2,1,0:T(8,128)(2,1)}), bf16[8,16,640]{2,1,0:T(8,128)(2,1)S(1)}, u32[]{:S(2)}, u32[]{:S(2)}) %all-to-all-start) | async-done | bytes 163872 | tf_op jit(solution)/shard_map/all_to_all | solution.py:416
  39.3 0.7 collective-permute-start.3
  40.0 3.2 %shard_map.123 = (f32[512,128]{1,0:T(8,128)S(1)}, f32[512,128]{1,0:T(8,128)S(1)}, f32[512,128]{1,0:T(8,128)S(1)}) custom-call(s32[4]{0:T(128)S(1)} %copy-done.15, bf16[512,256]{1,0:T(8,128)(2,1)S(1)} %get-tuple-element.38.query, bf16[512,384]{1,0:T(8,128)(2,1)S(1)} %get-tuple-element.35.own, bf16[512,384]{1,0:T(8,128)(2,1)S(1)} %collective-permute-done.side), custom_call_target="tpu_custom_call" | custom-call | flops 3300000000 | bytes 3000000 | tf_op jit(solution)/shard_map/pallas_call | solution.py:385
  43.2 0.7 copy-done.24
  43.9 0.7 copy-done.26
  44.7 0.7 copy-done.28
  45.4 1.0 pad_maximum_fusion
  46.5 4.6 %collective-permute-start.5 = (bf16[1280,384]{1,0:T(8,128)(2,1)}, bf16[1280,384]{1,0:T(8,128)(2,1)S(1)}, u32[]{:S(2)}, u32[]{:S(2)}) collective-permute-start(bf16[1280,384]{1,0:T(8,128)(2,1)} %pad_maximum_fusion), channel_id=1, source_target_pairs={{0,4},{4,0},{8,12},{12,8},{16,20},{20,16},{24,28},{28,24},{32,36},... | collective-permute-start | bytes 2949128 | tf_op jit(solution)/shard_map/ppermute | solution.py:399
  51.0 1.9 %collective-permute-start.4 = (bf16[128,384]{1,0:T(8,128)(2,1)S(1)}, bf16[128,384]{1,0:T(8,128)(2,1)S(1)}, u32[]{:S(2)}, u32[]{:S(2)}) collective-permute-start(bf16[128,384]{1,0:T(8,128)(2,1)S(1)} %collective-permute-done.3.here), channel_id=1, source_target_pairs={{0,4},{4,0},{8,12},{12,8},{16,20},{20,16},{24,28},{28,24},{32,36},... | collective-permute-start | bytes 294920 | tf_op jit(solution)/shard_map/ppermute | solution.py:399
  52.9 1.3 %collective-permute-done.4.other = bf16[128,384]{1,0:T(8,128)(2,1)S(1)} collective-permute-done((bf16[128,384]{1,0:T(8,128)(2,1)S(1)}, bf16[128,384]{1,0:T(8,128)(2,1)S(1)}, u32[]{:S(2)}, u32[]{:S(2)}) %collective-permute-start.4) | collective-permute-done | bytes 98336 | tf_op jit(solution)/shard_map/ppermute | solution.py:399
  54.2 1.9 %shard_map.124 = f32[8,16,384]{2,1,0:T(8,128)} custom-call(s32[4]{0:T(128)S(1)} %copy-done.15, bf16[8,16,640]{2,1,0:T(8,128)(2,1)S(1)} %all-to-all-done.rows, bf16[128,384]{1,0:T(8,128)(2,1)S(1)} %collective-permute-done.3.here, bf16[128,384]{1,0:T(8,128)(2,1)S(1)} %collective-permute-done.4.other), custom_call_target="tpu_custom_call" | custom-call | flops 2200000000 | bytes 2000000 | tf_op jit(solution)/shard_map/pallas_call | solution.py:385
  56.1 10.2 %all-to-all-start.1 = ((f32[8,16,384]{2,1,0:T(8,128)}), f32[8,16,384]{2,1,0:T(8,128)S(1)}, u32[]{:S(2)}, u32[]{:S(2)}) async-start(f32[8,16,384]{2,1,0:T(8,128)} %shard_map.124), calls=%async_computation.1 | async-start | bytes 393216 | tf_op jit(solution)/shard_map/all_to_all | solution.py:457
  66.4 1.0 copy-done.17
  67.4 0.9 copy-done.25
  68.3 0.9 copy-done.27
  69.3 0.9 copy-done.29
  70.2 4.4 %shard_map.125 = (f32[512,128]{1,0:T(8,128)S(1)}, f32[512,128]{1,0:T(8,128)S(1)}, f32[512,128]{1,0:T(8,128)S(1)}) custom-call(s32[4]{0:T(128)S(1)} %copy-done.15, bf16[512,256]{1,0:T(8,128)(2,1)S(1)} %copy-done.17, bf16[512,384]{1,0:T(8,128)(2,1)S(1)} %get-tuple-element.35.own, bf16[512,384]{1,0:T(8,128)(2,1)S(1)} %collective-permute-done.side, ...), custom_call_target="tpu_custom_call" | custom-call | flops 5500000256 | bytes 5000000 | tf_op jit(solution)/shard_map/pallas_call | solution.py:385
  74.6 0.7 copy-done.18
  75.3 0.7 copy-done.20
  76.0 0.7 copy-done.22
  76.8 0.9 copy-done.19
  77.7 0.9 copy-done.21
  78.7 0.9 copy-done.23
  79.6 1.5 %shard_map.126 = (bf16[4,128,768]{2,1,0:T(8,128)(2,1)S(1)}, bf16[16,192]{1,0:T(8,128)(2,1)}) custom-call(f32[8,16,384]{2,1,0:T(8,128)S(1)} %all-to-all-done.1.parts, bf16[192,768]{1,0:T(8,128)(2,1)S(1)} %copy-done.10, f32[512,128]{1,0:T(8,128)S(1)} %copy-done.19, f32[512,128]{1,0:T(8,128)S(1)} %copy-done.21, f32[512,128]{1,0:T(8,128)S(1)} %copy-done.23), custom_call_target="tpu_custom_call" | custom-call | flops 3300000000 | bytes 3000000 | tf_op jit(solution)/shard_map/pallas_call | solution.py:385
  81.1 14.5 %all_to_all.15.terms = bf16[4,128,768]{2,1,0:T(8,128)(2,1)S(1)} all-to-all(bf16[4,128,768]{2,1,0:T(8,128)(2,1)S(1)} %get-tuple-element.56), channel_id=1, replica_groups=mesh['seq'=128,'mp'=4] {'mp'}, dimensions={0} | all-to-all | bytes 1572864 | tf_op jit(solution)/shard_map/all_to_all | solution.py:468
  95.6 0.8 shard_map.127
  96.5 4.4 %collective-permute-start.6 = (bf16[128,768]{1,0:T(8,128)(2,1)S(1)}, bf16[128,768]{1,0:T(8,128)(2,1)S(1)}, u32[]{:S(2)}, u32[]{:S(2)}) collective-permute-start(bf16[128,768]{1,0:T(8,128)(2,1)S(1)} %get-tuple-element.59.own), channel_id=1, source_target_pairs={{0,4},{4,0},{8,12},{12,8},{16,20},{20,16},{24,28},{28,24},{32,36},... | collective-permute-start | bytes 589832 | tf_op jit(solution)/shard_map/ppermute | solution.py:399
  100.9 1.0 collective-permute-done.6.other
  101.9 0.7 copy-done.30
  102.6 6.0 %shard_map.129 = (f32[128,768]{1,0:T(8,128)}, bf16[128,768]{1,0:T(8,128)(2,1)}) custom-call(bf16[128,768]{1,0:T(8,128)(2,1)} %copy-done.11, bf16[128,768]{1,0:T(8,128)(2,1)} %copy-done.30, bf16[4,768,768]{2,1,0:T(8,128)(2,1)} %bitcast.12), custom_call_target="tpu_custom_call" | custom-call | flops 4000000000 | bytes 5000000 | tf_op jit(solution)/shard_map/pallas_call | solution.py:365
  108.6 2.3 %collective-permute-start.7 = (bf16[128,768]{1,0:T(8,128)(2,1)}, bf16[128,768]{1,0:T(8,128)(2,1)S(1)}, u32[]{:S(2)}, u32[]{:S(2)}) collective-permute-start(bf16[128,768]{1,0:T(8,128)(2,1)} %get-tuple-element.64), channel_id=1, source_target_pairs={{0,4},{4,0},{8,12},{12,8},{16,20},{20,16},{24,28},{28,24},{32,36},... | collective-permute-start | bytes 589832 | tf_op jit(solution)/shard_map/ppermute | solution.py:399
  110.9 1.3 %collective-permute-done.7 = bf16[128,768]{1,0:T(8,128)(2,1)S(1)} collective-permute-done((bf16[128,768]{1,0:T(8,128)(2,1)}, bf16[128,768]{1,0:T(8,128)(2,1)S(1)}, u32[]{:S(2)}, u32[]{:S(2)}) %collective-permute-start.7) | collective-permute-done | bytes 196640 | tf_op jit(solution)/shard_map/ppermute | solution.py:399
  112.1 1.7 %add_convert_fusion = bf16[128,768]{1,0:T(8,128)(2,1)} fusion(f32[128,768]{1,0:T(8,128)} %get-tuple-element.63, bf16[128,768]{1,0:T(8,128)(2,1)S(1)} %collective-permute-done.7), kind=kLoop, calls=%fused_computation.1 | loop fusion | flops 294912 | bytes 786432 | tf_op jit(solution)/shard_map/convert_element_type | solution.py:476
  (50 shorter events, 0.3 us)
Async XLA Ops:
  7.2 93.7 %all-gather.3.cloned.1.call-start = ((), (), s32[]{:S(2)}) async-start(), calls=%async_computation.3 | async-start | bytes 5898240 | tf_op jit(solution)/shard_map/all_gather | solution.py:427
  7.2 1.1 copy-start.2
  8.3 1.0 copy-start.4
  9.3 1.0 copy-start.6
  10.3 1.0 copy-start.8
  11.2 0.7 copy-start.12
  11.9 1.6 %copy-start = (bf16[768,768]{1,0:T(8,128)(2,1)S(1)}, bf16[768,768]{1,0:T(8,128)(2,1)}, u32[]{:S(2)}) copy-start(bf16[768,768]{1,0:T(8,128)(2,1)} %w_up) | copy-start | bytes 3538948
  11.9 1.6 %copy-start.1 = (bf16[768,768]{1,0:T(8,128)(2,1)S(1)}, bf16[768,768]{1,0:T(8,128)(2,1)}, u32[]{:S(2)}) copy-start(bf16[768,768]{1,0:T(8,128)(2,1)} %w_down) | copy-start | bytes 3538948
  13.5 1.3 %copy-start.3 = (bf16[512,768]{1,0:T(8,128)(2,1)S(1)}, bf16[512,768]{1,0:T(8,128)(2,1)}, u32[]{:S(2)}) copy-start(bf16[512,768]{1,0:T(8,128)(2,1)} %tokens.3) | copy-start | bytes 2359300
  13.5 1.6 %copy-start.5 = (bf16[768,192]{0,1:T(8,128)(2,1)S(1)}, bf16[768,192]{0,1:T(8,128)(2,1)}, u32[]{:S(2)}) copy-start(bf16[768,192]{0,1:T(8,128)(2,1)} %param.13) | copy-start | bytes 884740
  13.5 1.7 %copy-start.7 = (bf16[768,192]{0,1:T(8,128)(2,1)S(1)}, bf16[768,192]{0,1:T(8,128)(2,1)}, u32[]{:S(2)}) copy-start(bf16[768,192]{0,1:T(8,128)(2,1)} %param.14) | copy-start | bytes 884740
  13.6 1.8 %copy-start.9 = (bf16[768,192]{0,1:T(8,128)(2,1)S(1)}, bf16[768,192]{0,1:T(8,128)(2,1)}, u32[]{:S(2)}) copy-start(bf16[768,192]{0,1:T(8,128)(2,1)} %param.15) | copy-start | bytes 884740
  13.6 1.8 %copy-start.13 = (bf16[768]{0:T(1024)(128)(2,1)S(1)}, bf16[768]{0:T(1024)(128)(2,1)}, u32[]{:S(2)}) copy-start(bf16[768]{0:T(1024)(128)(2,1)} %gain.4) | copy-start | bytes 4612
  15.3 24.7 %copy-start.15 = (s32[4]{0:T(128)S(1)}, s32[4]{0:T(128)}, u32[]{:S(2)}) copy-start(s32[4]{0:T(128)} %tiles.5) | copy-start | bytes 52
  17.2 26.1 %copy-start.16 = (bf16[512,256]{1,0:T(8,128)(2,1)}, bf16[512,256]{1,0:T(8,128)(2,1)S(1)}, u32[]{:S(2)}) copy-start(bf16[512,256]{1,0:T(8,128)(2,1)S(1)} %get-tuple-element.38.query) | copy-start | bytes 786436
  17.2 22.8 %collective-permute-start = (bf16[512,384]{1,0:T(8,128)(2,1)S(1)}, bf16[512,384]{1,0:T(8,128)(2,1)S(1)}, u32[]{:S(2)}, u32[]{:S(2)}) collective-permute-start(bf16[512,384]{1,0:T(8,128)(2,1)S(1)} %get-tuple-element.35.own), channel_id=1, source_target_pairs={{0,8},{4,12},{8,0},{12,4},{16,24},{20,28},{24,16},{28,20},{32,40},... | collective-permute-start | bytes 1179656 | tf_op jit(solution)/shard_map/ppermute | solution.py:399
  21.2 18.1 %all-to-all-start = ((bf16[8,16,640]{2,1,0:T(8,128)(2,1)}), bf16[8,16,640]{2,1,0:T(8,128)(2,1)S(1)}, u32[]{:S(2)}, u32[]{:S(2)}) async-start(bf16[8,16,640]{2,1,0:T(8,128)(2,1)} %shard_map.121), calls=%async_computation | async-start | bytes 327680 | tf_op jit(solution)/shard_map/all_to_all | solution.py:416
  31.2 14.1 %collective-permute-start.2 = (bf16[128,384]{1,0:T(8,128)(2,1)S(1)}, bf16[128,384]{1,0:T(8,128)(2,1)S(1)}, u32[]{:S(2)}, u32[]{:S(2)}) collective-permute-start(bf16[128,384]{1,0:T(8,128)(2,1)S(1)} %get-tuple-element.36), channel_id=1, source_target_pairs={{0,24},{4,28},{8,16},{12,20},{16,8},{20,12},{24,0},{28,4},{32,56},... | collective-permute-start | bytes 294920 | tf_op jit(solution)/shard_map/ppermute | solution.py:399
  35.3 10.1 %collective-permute-start.1 = (bf16[128,384]{1,0:T(8,128)(2,1)S(1)}, bf16[128,384]{1,0:T(8,128)(2,1)S(1)}, u32[]{:S(2)}, u32[]{:S(2)}) collective-permute-start(bf16[128,384]{1,0:T(8,128)(2,1)S(1)} %get-tuple-element.36), channel_id=1, source_target_pairs={{0,16},{4,20},{8,24},{12,28},{16,0},{20,4},{24,8},{28,12},{32,48},... | collective-permute-start | bytes 294920 | tf_op jit(solution)/shard_map/ppermute | solution.py:399
  39.3 6.1 %collective-permute-start.3 = (bf16[128,384]{1,0:T(8,128)(2,1)S(1)}, bf16[128,384]{1,0:T(8,128)(2,1)S(1)}, u32[]{:S(2)}, u32[]{:S(2)}) collective-permute-start(bf16[128,384]{1,0:T(8,128)(2,1)S(1)} %bitcast.11), channel_id=1, source_target_pairs={{0,0},{4,4},{8,8},{12,12},{16,16},{20,20},{24,24},{28,28},{32,32},... | collective-permute-start | bytes 294920 | tf_op jit(solution)/shard_map/ppermute | solution.py:431
  43.2 0.7 copy-start.24
  43.9 0.7 copy-start.26
  44.7 0.7 copy-start.28
  46.5 19.9 %collective-permute-start.5 = (bf16[1280,384]{1,0:T(8,128)(2,1)}, bf16[1280,384]{1,0:T(8,128)(2,1)S(1)}, u32[]{:S(2)}, u32[]{:S(2)}) collective-permute-start(bf16[1280,384]{1,0:T(8,128)(2,1)} %pad_maximum_fusion), channel_id=1, source_target_pairs={{0,4},{4,0},{8,12},{12,8},{16,20},{20,16},{24,28},{28,24},{32,36},... | collective-permute-start | bytes 2949128 | tf_op jit(solution)/shard_map/ppermute | solution.py:399
  51.0 3.2 %collective-permute-start.4 = (bf16[128,384]{1,0:T(8,128)(2,1)S(1)}, bf16[128,384]{1,0:T(8,128)(2,1)S(1)}, u32[]{:S(2)}, u32[]{:S(2)}) collective-permute-start(bf16[128,384]{1,0:T(8,128)(2,1)S(1)} %collective-permute-done.3.here), channel_id=1, source_target_pairs={{0,4},{4,0},{8,12},{12,8},{16,20},{20,16},{24,28},{28,24},{32,36},... | collective-permute-start | bytes 294920 | tf_op jit(solution)/shard_map/ppermute | solution.py:399
  56.1 20.7 %all-to-all-start.1 = ((f32[8,16,384]{2,1,0:T(8,128)}), f32[8,16,384]{2,1,0:T(8,128)S(1)}, u32[]{:S(2)}, u32[]{:S(2)}) async-start(f32[8,16,384]{2,1,0:T(8,128)} %shard_map.124), calls=%async_computation.1 | async-start | bytes 393216 | tf_op jit(solution)/shard_map/all_to_all | solution.py:457
  66.3 10.4 %copy-start.10 = (bf16[192,768]{1,0:T(8,128)(2,1)S(1)}, bf16[192,768]{1,0:T(8,128)(2,1)}, u32[]{:S(2)}) copy-start(bf16[192,768]{1,0:T(8,128)(2,1)} %w_out.1) | copy-start | bytes 884740
  66.4 1.0 copy-start.17
  67.4 0.9 copy-start.25
  68.3 0.9 copy-start.27
  69.3 0.9 copy-start.29
  74.6 0.7 copy-start.18
  75.3 0.7 copy-start.20
  76.0 0.7 copy-start.22
  76.8 1.0 copy-start.19
  77.7 0.9 copy-start.21
  78.7 0.9 copy-start.23
  79.6 16.0 %copy-start.14 = (bf16[768]{0:T(1024)(128)(2,1)S(1)}, bf16[768]{0:T(1024)(128)(2,1)}, u32[]{:S(2)}) copy-start(bf16[768]{0:T(1024)(128)(2,1)} %gain.5) | copy-start | bytes 4612
  96.5 5.5 %copy-start.11 = (bf16[128,768]{1,0:T(8,128)(2,1)}, bf16[128,768]{1,0:T(8,128)(2,1)S(1)}, u32[]{:S(2)}) copy-start(bf16[128,768]{1,0:T(8,128)(2,1)S(1)} %get-tuple-element.59.own) | copy-start | bytes 589828
  96.5 5.5 %collective-permute-start.6 = (bf16[128,768]{1,0:T(8,128)(2,1)S(1)}, bf16[128,768]{1,0:T(8,128)(2,1)S(1)}, u32[]{:S(2)}, u32[]{:S(2)}) collective-permute-start(bf16[128,768]{1,0:T(8,128)(2,1)S(1)} %get-tuple-element.59.own), channel_id=1, source_target_pairs={{0,4},{4,0},{8,12},{12,8},{16,20},{20,16},{24,28},{28,24},{32,36},... | collective-permute-start | bytes 589832 | tf_op jit(solution)/shard_map/ppermute | solution.py:399
  101.9 0.7 copy-start.30
  108.6 3.5 %collective-permute-start.7 = (bf16[128,768]{1,0:T(8,128)(2,1)}, bf16[128,768]{1,0:T(8,128)(2,1)S(1)}, u32[]{:S(2)}, u32[]{:S(2)}) collective-permute-start(bf16[128,768]{1,0:T(8,128)(2,1)} %get-tuple-element.64), channel_id=1, source_target_pairs={{0,4},{4,0},{8,12},{12,8},{16,20},{20,16},{24,28},{28,24},{32,36},... | collective-permute-start | bytes 589832 | tf_op jit(solution)/shard_map/ppermute | solution.py:399
Sparse Core Ops, SparseCore 0:
  14.9 63.4 all-gather.2

commit v7 on v6

--- a/solution.py
+++ b/solution.py
@@ -22,6 +22,7 @@
 EPS = 1e-05
 HIDDEN_SCORE = -1e30
 VMEM = 16 * 1024 * 1024
+WHOLE_VMEM = 58 * 1024 * 1024
 
 KEY_TILE = (0, 0, 2)
 VALUE_TILE = (1, 1, 2)
@@ -107,41 +108,51 @@
     return queries, keyvals + [jnp.concatenate([key[:, 128:], value[:, 128:]], 1)]
 
 
-def far_rows_kernel(tokens, gain, w_query, w_key, w_value, far):
-    first = lax.axis_index("mp") * LOCAL_HEADS
-    shape = (LOCAL_HEADS * FAR_ROWS, ROWS)
-    place = iota(shape, 0)
-    wanted = (place & 15) * RATE_FAR + (place >> 4) + first
-    rows = matmul((iota(shape, 1) == wanted).astype(jnp.bfloat16), tokens[...])
-    queries, keyvals = project(layer_norm(rows, gain[...]), w_query, w_key, w_value)
-    low = iota((FAR_ROWS, LANES), 1) < HEAD_DIM
-    for index, value in enumerate(queries + keyvals):
-        parts = [value[FAR_ROWS * head : FAR_ROWS * (head + 1)] for head in range(LOCAL_HEADS)]
-        chosen = parts[2] if index in (1, 4) else jnp.where(low, parts[0], parts[1])
-        for copy in range(FAR_GROUP):
-            far[copy, :, tile(index)] = chosen
-
-
-def project_kernel(tokens, gain, w_query, w_key, w_value, query, keyval, mid):
+def project_kernel(
+    tokens, gain, w_query, w_key, w_value, query, keyval, mid, far, rows, weights, sems
+):
     mp = lax.axis_index("mp")
-    normed = layer_norm(tokens[...].astype(jnp.float32), gain[...])
+    copies = []
+    for index in range(4):
+        part = pl.ds(index * BLOCK, BLOCK)
+        copies.append(pltpu.make_async_copy(tokens.at[part], rows.at[part], sems.at[index]))
+    for index, weight in enumerate((w_query, w_key, w_value)):
+        copies.append(pltpu.make_async_copy(weight, weights.at[index], sems.at[4 + index]))
+    for copy in copies:
+        copy.start()
+    for copy in copies[:4]:
+        copy.wait()
+    normed = layer_norm(rows[...].astype(jnp.float32), gain[...])
     order = iota((ROWS, ROWS), 0) == place_of(iota((ROWS, ROWS), 1))
     normed = matmul(order.astype(jnp.bfloat16), normed).astype(jnp.bfloat16)
-    queries, keyvals = project(normed, w_query, w_key, w_value)
+    for copy in copies[4:]:
+        copy.wait()
+    queries, keyvals = project(normed, *[weights.at[index] for index in range(3)])
     for index, value in enumerate(queries):
         query[:, tile(index)] = value
     for index, value in enumerate(keyvals):
         keyval[:, tile(index)] = value
-    starts = []
-    for head in range(LOCAL_HEADS):
-        start = ((mp * LOCAL_HEADS + head) & 3) * CLASS_ROWS
-        starts.append(pl.ds(pl.multiple_of(start, CLASS_ROWS), CLASS_ROWS))
-    low = iota((CLASS_ROWS, LANES), 1) < HEAD_DIM
-    for index in range(2):
-        mid[:, tile(index)] = jnp.where(
-            low, keyval[starts[0], tile(index)], keyval[starts[1], tile(index)]
-        )
-    mid[:, tile(2)] = keyval[starts[2], tile(2)]
+
+    def pick(source, index, whose, count):
+        starts = []
+        for head in range(LOCAL_HEADS):
+            number = mp * LOCAL_HEADS + head
+            start = (number & 3) * CLASS_ROWS
+            if count == FAR_ROWS:
+                start = start + (number >> 2) * FAR_ROWS
+            starts.append(pl.ds(pl.multiple_of(start, count), count))
+        if whose[2] == index:
+            return source[starts[2], tile(index)]
+        low, high = source[starts[0], tile(index)], source[starts[1], tile(index)]
+        return jnp.where(iota(low.shape, 1) < HEAD_DIM, low, high)
+
+    for index in range(3):
+        mid[:, tile(index)] = pick(keyval, index, KEY_TILE, CLASS_ROWS)
+    picked = [pick(query, index, QUERY_TILE, FAR_ROWS) for index in range(2)]
+    picked += [pick(keyval, index, KEY_TILE, FAR_ROWS) for index in range(3)]
+    for index, value in enumerate(picked):
+        for copy in range(FAR_GROUP):
+            far[copy, :, tile(index)] = value
 
 
 def attend(query, keys, values, head):
@@ -173,7 +184,11 @@
     return jnp.concatenate([key_marks(rows + (seq ^ step) * ROWS, ends) for step in steps], 0)
 
 
-def near_kernel(tiles, query, own, side, *state):
+def near_kernel(tiles, query, own, side, *refs):
+    out, state, sems = refs[:LOCAL_HEADS], refs[LOCAL_HEADS:-1], refs[-1]
+    copies = [
+        pltpu.make_async_copy(state[head], out[head], sems.at[head]) for head in range(LOCAL_HEADS)
+    ]
     ends = slide_ends(tiles)
     seq = lax.axis_index("seq")
     marks = query_marks(row_at(iota((ROWS, LANES), 0)) + seq * ROWS, ends)
@@ -189,10 +204,18 @@
             jnp.concatenate([values, keys_marks], 1),
             head,
         )
+        copies[head].start()
+    for copy in copies:
+        copy.wait()
 
 
 def rest_kernel(tiles, query, own, side, mid_a, mid_b, swapped, *refs):
-    held, state = refs[:LOCAL_HEADS], refs[LOCAL_HEADS:]
+    n = LOCAL_HEADS
+    held_from, out, held, state, sems = refs[:n], refs[n : 2 * n], refs[2 * n : 3 * n], refs[3 * n : -1], refs[-1]
+    fetches = [pltpu.make_async_copy(held_from[i], held[i], sems.at[i]) for i in range(n)]
+    copies = [pltpu.make_async_copy(state[i], out[i], sems.at[n + i]) for i in range(n)]
+    for fetch in fetches:
+        fetch.start()
     ends = slide_ends(tiles)
     seq, mp = lax.axis_index("seq"), lax.axis_index("mp")
     marks = query_marks(row_at(iota((ROWS, LANES), 0)) + seq * ROWS, ends)
@@ -206,6 +229,7 @@
             jnp.concatenate([swapped[: 2 * ROWS, value_tile], near_marks], 1),
             head,
         )
+        fetches[head].wait()
         state[head][...] = join(held[head][...], more, peak, head)
 
         offset = (mp * LOCAL_HEADS + head) & 3
@@ -241,6 +265,9 @@
             head,
         )
         state[head][picked, :] = join(state[head][picked, :], more, peak, head)
+        copies[head].start()
+    for copy in copies:
+        copy.wait()
 
 
 def far_kernel(tiles, rows, here, other, parts):
@@ -277,7 +304,11 @@
 
 
 def finish_kernel(parts, w_out, *refs):
-    held, (terms, far_out), state = refs[:LOCAL_HEADS], refs[LOCAL_HEADS:-LOCAL_HEADS], refs[-LOCAL_HEADS:]
+    n = LOCAL_HEADS
+    held, (terms, far_out), state, sems = refs[:n], refs[n : n + 2], refs[n + 2 : -1], refs[-1]
+    fetches = [pltpu.make_async_copy(held[i], state[i], sems.at[i]) for i in range(n)]
+    for fetch in fetches:
+        fetch.start()
     mp = lax.axis_index("mp")
     far_parts = []
     for head in range(LOCAL_HEADS):
@@ -292,7 +323,7 @@
         number = mp * LOCAL_HEADS + head
         start = (number & 3) * CLASS_ROWS + (number >> 2) * FAR_ROWS
         picked = pl.ds(pl.multiple_of(start, FAR_ROWS), FAR_ROWS)
-        state[head][...] = held[head][...]
+        fetches[head].wait()
         state[head][picked, :] = join(state[head][picked, :], total, peak, head)
 
     def packed(values):
@@ -322,10 +353,10 @@
 
 
 def hidden_part(normed, weights):
-    raised = matmul(normed[:, :HALF], weights[0, :HALF, :HALF])
-    raised = raised + matmul(normed[:, HALF:], weights[0, :HALF, HALF:])
+    raised = matmul(normed[:, :HALF], weights[:HALF, :HALF])
+    raised = raised + matmul(normed[:, HALF:], weights[:HALF, HALF:])
     hidden = (0.5 * raised * (1.0 + lax.erf(raised * 0.7071067811865476))).astype(jnp.bfloat16)
-    return matmul(hidden, weights[0, HALF:, :])
+    return matmul(hidden, weights[HALF:, :])
 
 
 def norm_kernel(tokens, terms, gain, attended, normed):
@@ -339,59 +370,40 @@
     normed[...] = layer_norm(own + summed.astype(jnp.float32), gain[...])
 
 
-def ffn_kernel(own, other, weights, kept, sent, rows, total):
-    step = pl.program_id(0)
-
-    @pl.when(step == 0)
-    def _():
-        rows[:BLOCK, :] = own[...]
-        rows[BLOCK:, :] = other[...]
-        total[...] = jnp.zeros_like(total)
-
-    total[...] += hidden_part(rows[...], weights)
-
-    @pl.when(step == pl.num_programs(0) - 1)
-    def _():
-        kept[...] = total[:BLOCK, :]
-        sent[...] = total[BLOCK:, :].astype(jnp.bfloat16)
-
-
-def whole(shape):
-    return pl.BlockSpec(shape, lambda step: (0,) * len(shape))
-
-
-def ffn(own, other, weights):
-    outs = [((BLOCK, WIDTH), jnp.float32), ((BLOCK, WIDTH), jnp.bfloat16)]
-    return pl.pallas_call(
-        ffn_kernel,
-        grid=(4,),
-        out_shape=[jax.ShapeDtypeStruct(*out) for out in outs],
-        in_specs=[whole(own.shape), whole(other.shape)]
-        + [pl.BlockSpec((1, 2 * HALF, WIDTH), lambda step: (step, 0, 0))],
-        out_specs=[whole(out[0]) for out in outs],
-        scratch_shapes=[
-            pltpu.VMEM((2 * BLOCK, WIDTH), jnp.bfloat16),
-            pltpu.VMEM((2 * BLOCK, WIDTH), jnp.float32),
-        ],
-        cost_estimate=pl.CostEstimate(
-            flops=int(4e9), bytes_accessed=int(5e6), transcendentals=0
-        ),
-        compiler_params=pltpu.CompilerParams(vmem_limit_bytes=56 * 1024 * 1024),
-    )(own, other, weights)
-
-
-def call(kernel, micros, outs, ins, scratch=()):
-    places = {"smem": pltpu.SMEM, "vmem": pltpu.VMEM}
+def ffn_kernel(own, other, weights, kept, sent, held, sems):
+    copies = []
+    for group in range(4):
+        for index in range(4):
+            part = pl.ds(index * 192, 192)
+            copies.append(
+                pltpu.make_async_copy(
+                    weights.at[group, part], held.at[group, part], sems.at[4 * group + index]
+                )
+            )
+    for copy in copies:
+        copy.start()
+    rows = jnp.concatenate([own[...], other[...]], 0)
+    total = jnp.zeros((2 * BLOCK, WIDTH), jnp.float32)
+    for group in range(4):
+        for copy in copies[4 * group : 4 * group + 4]:
+            copy.wait()
+        total = total + hidden_part(rows, held.at[group])
+    kept[...] = total[:BLOCK, :]
+    sent[...] = total[BLOCK:, :].astype(jnp.bfloat16)
+
+
+def call(kernel, micros, outs, ins, scratch=(), kept=pltpu.VMEM, limit=VMEM):
+    places = {"smem": pltpu.SMEM, "vmem": pltpu.VMEM, "hbm": pltpu.HBM}
     return pl.pallas_call(
         kernel,
         out_shape=[jax.ShapeDtypeStruct(*out) for out in outs],
         in_specs=[pl.BlockSpec(memory_space=places[where]) for _, where in ins],
-        out_specs=[pl.BlockSpec(memory_space=pltpu.VMEM) for _ in outs],
+        out_specs=[pl.BlockSpec(memory_space=kept) for _ in outs],
         scratch_shapes=list(scratch),
         cost_estimate=pl.CostEstimate(
             flops=int(micros * 1.1e9), bytes_accessed=int(micros * 1e6), transcendentals=0
         ),
-        compiler_params=pltpu.CompilerParams(vmem_limit_bytes=VMEM),
+        compiler_params=pltpu.CompilerParams(vmem_limit_bytes=limit),
     )(*[array for array, _ in ins])
 
 
@@ -401,28 +413,28 @@
 
 def local(tokens, slide_tiles, attn_gain, w_query, w_key, w_value, w_out, ffn_gain, w_up, w_down):
     bf16, f32 = jnp.bfloat16, jnp.float32
-    v, s = "vmem", "smem"
+    v, s, h = "vmem", "smem", "hbm"
+    dma = pltpu.SemaphoreType.DMA
     columns = [[16 * z + place for z in range(FAR_GROUP)] for place in range(16)]
     across = [
         (16 * z + (place ^ (2 * z)), 16 * z + place) for z in range(FAR_GROUP) for place in range(16)
     ]
     w_query, w_key, w_value = w_query.T, w_key.T, w_value.T
-    (far,) = call(
-        far_rows_kernel,
-        2,
-        [((FAR_GROUP, FAR_ROWS, 640), bf16)],
-        [(tokens, v), (attn_gain, v), (w_query, v), (w_key, v), (w_value, v)],
+    query, own, mid, far = call(
+        project_kernel,
+        3,
+        [
+            ((ROWS, 256), bf16), ((ROWS, 384), bf16), ((CLASS_ROWS, 384), bf16),
+            ((FAR_GROUP, FAR_ROWS, 640), bf16),
+        ],
+        [(tokens, h), (attn_gain, v), (w_query, h), (w_key, h), (w_value, h)],
+        [pltpu.VMEM((ROWS, WIDTH), bf16), pltpu.VMEM((3, 192, WIDTH), bf16), dma((7,))],
+        limit=WHOLE_VMEM,
     )
     far_rows = lax.all_to_all(
         far, "seq", split_axis=0, concat_axis=0, tiled=True, axis_index_groups=columns
     )
-    tokens, w_up, w_down, _ = lax.optimization_barrier((tokens, w_up, w_down, far))
-    query, own, mid = call(
-        project_kernel,
-        2,
-        [((ROWS, 256), bf16), ((ROWS, 384), bf16), ((CLASS_ROWS, 384), bf16)],
-        [(tokens, v), (attn_gain, v), (w_query, v), (w_key, v), (w_value, v)],
-    )
+    w_up, w_down, _ = lax.optimization_barrier((w_up, w_down, far))
     (packed,) = call(weights_kernel, 2, [((2 * HALF, WIDTH), bf16)], [(w_up, v), (w_down, v)])
     mine = lax.all_gather(packed, "mp", axis=0)
     side = swap(own, 2)
@@ -432,7 +444,16 @@
     query, _ = lax.optimization_barrier((query, far_keys))
     mid_a, mid_b = swap(mid, 4), swap(mid, 6)
     state = [((ROWS, LANES), f32)] * LOCAL_HEADS
-    near = call(near_kernel, 3, state, [(slide_tiles, s), (query, v), (own, v), (side, v)])
+    scratch = [pltpu.VMEM(*shape) for shape in state]
+    near = call(
+        near_kernel,
+        3,
+        state,
+        [(slide_tiles, s), (query, v), (own, v), (side, v)],
+        [*scratch, dma((3,))],
+        pltpu.HBM,
+        WHOLE_VMEM,
+    )
     side, mid_a, mid_b, far_here, *near = lax.optimization_barrier(
         (side, mid_a, mid_b, far_here, *near)
     )
@@ -451,8 +472,11 @@
         state,
         [
             (slide_tiles, s), (query, v), (own, v), (side, v), (mid_a, v), (mid_b, v), (swapped, v),
-            *[(held, v) for held in near],
+            *[(held, h) for held in near],
         ],
+        [*scratch, *scratch, dma((6,))],
+        pltpu.HBM,
+        WHOLE_VMEM,
     )
     parts = lax.all_to_all(
         parts, "seq", split_axis=0, concat_axis=0, tiled=True, axis_index_groups=columns
@@ -462,8 +486,9 @@
         finish_kernel,
         3,
         [((4, BLOCK, WIDTH), bf16), ((FAR_ROWS, 192), bf16)],
-        [(parts, v), (w_out, v), *[(held, v) for held in both]],
-        [pltpu.VMEM(*shape) for shape in state],
+        [(parts, v), (w_out, v), *[(held, h) for held in both]],
+        [*scratch, dma((3,))],
+        limit=WHOLE_VMEM,
     )
     terms = lax.all_to_all(terms, "mp", split_axis=0, concat_axis=0, tiled=True)
     attended, normed = call(
@@ -472,7 +497,14 @@
         [((BLOCK, WIDTH), bf16), ((BLOCK, WIDTH), bf16)],
         [(tokens, v), (terms, v), (ffn_gain, v)],
     )
-    kept, sent = ffn(normed, swap(normed, 1), mine)
+    kept, sent = call(
+        ffn_kernel,
+        4,
+        [((BLOCK, WIDTH), f32), ((BLOCK, WIDTH), bf16)],
+        [(normed, v), (swap(normed, 1), v), (mine, h)],
+        [pltpu.VMEM((4, 2 * HALF, WIDTH), bf16), dma((16,))],
+        limit=WHOLE_VMEM,
+    )
     ffn_out = (kept + swap(sent, 1).astype(f32)).astype(bf16)
     return (attended, far_attended, ffn_out)
 

time: 122 us -> 119 us (0.975)
  local copies, waits for them, and re-layouts: 17 us -> 3.11 us
  Pallas kernels: 22.3 us -> 32.8 us
    pallas_call x8, Pallas kernels: 16.3 us -> 32.8 us  [call(): pl.pallas_call(kernel, out_shape=[jax.ShapeDtypeStruct(*out) for out in o...]
    unnamed x62 -> x26, local copies, waits for them, and re-layouts: 17 us -> 3.1 us
    pallas_call x1 -> x0, Pallas kernels: 5.98 us -> none  [ffn(): pl.pallas_call(ffn_kernel, grid=(4,), out_shape=[jax.ShapeDtypeStruct(*ou...]
  transfers between devices with their start and end apart: 11 -> 11, of which waited for: 4 -> 5; matrix products, arithmetic and copies ran while one was open for 1% -> 1% of each run, Pallas kernels for 11% -> 17%
where the time goes in v7:
time: 119 us; the launch traced here: 118 us
  starting transfers between devices  44.6 us (37%)
  Pallas kernels  32.8 us (28%)
  blocking collectives  14.5 us (12%)
  between operations  14.3 us (12%)
  waiting for transfers between devices  6 us (5%)
  local copies, waits for them, and re-layouts  3.11 us (3%)
  other arithmetic  2.97 us (2%)
    pallas_call x8, Pallas kernels, call(): pl.pallas_call(kernel, out_shape=[jax.ShapeDtypeStruct(*out) for out in o...  32.8 us
    ppermute x7, starting transfers between devices, swap(): lax.ppermute(value, 'seq', [(i, i ^ step) for i in range(lax.axis_size('s...  23.6 us
    all_to_all x1, blocking collectives, local(): terms = lax.all_to_all(terms, 'mp', split_axis=0, concat_axis=0, tiled=True)  14.5 us
    all_to_all x1, starting transfers between devices, local(): lax.all_to_all(parts, 'seq', split_axis=0, concat_axis=0, tiled=True, axi...  10.3 us
    all_to_all x1, starting transfers between devices, local(): lax.all_to_all(far, 'seq', split_axis=0, concat_axis=0, tiled=True, axis_...  10 us
    ppermute x7, waiting for transfers between devices, swap(): lax.ppermute(value, 'seq', [(i, i ^ step) for i in range(lax.axis_size('s...  3.56 us
    unnamed x26, local copies, waits for them, and re-layouts  3.1 us
  transfers between devices with their start and end apart: 11, of which 5 were waited for; matrix products, arithmetic and copies ran while one was open for 1% of the time, Pallas kernels for 17%

profile of v7, /device:TPU:1, one launch (start us, length us, event | category | flops | bytes accessed | tf_op | source)
XLA Modules:
  0.0 118.2 jit_solution(10902302458685575974)
XLA Ops:
  7.2 0.0 all-gather.3.cloned.1.call-start
  7.2 0.0 copy-start
  7.2 0.0 copy-start.1
  7.2 5.1 %shard_map.121 = (bf16[512,256]{1,0:T(8,128)(2,1)}, bf16[512,384]{1,0:T(8,128)(2,1)}, bf16[128,384]{1,0:T(8,128)(2,1)}, bf16[8,16,640]{2,1,0:T(8,128)(2,1)}) custom-call(bf16[512,768]{1,0:T(8,128)(2,1)} %tokens.3, bf16[768]{0:T(1024)(128)(2,1)} %gain.2, bf16[192,768]{1,0:T(8,128)(2,1)} %bitcast.7, bf16[192,768]{1,0:T(8,128)(2,1)} %bitcast.8, ...), custom_call_target="tpu_custom_call" | custom-call | flops 3300000000 | bytes 3000000 | tf_op jit(solution)/shard_map/pallas_call | solution.py:397
  12.4 0.0 copy-done
  12.4 0.0 copy-done.1
  12.4 0.0 copy-start.12
  12.4 1.1 shard_map.127
  13.6 0.0 all-gather.3.cloned.1.call-update
  13.6 4.1 %collective-permute-start = (bf16[512,384]{1,0:T(8,128)(2,1)}, bf16[512,384]{1,0:T(8,128)(2,1)S(1)}, u32[]{:S(2)}, u32[]{:S(2)}) collective-permute-start(bf16[512,384]{1,0:T(8,128)(2,1)} %get-tuple-element.35.own), channel_id=1, source_target_pairs={{0,8},{4,12},{8,0},{12,4},{16,24},{20,28},{24,16},{28,20},{32,40},... | collective-permute-start | bytes 1179656 | tf_op jit(solution)/shard_map/ppermute | solution.py:411
  17.6 10.0 %all-to-all-start = ((bf16[8,16,640]{2,1,0:T(8,128)(2,1)}), bf16[8,16,640]{2,1,0:T(8,128)(2,1)S(1)}, u32[]{:S(2)}, u32[]{:S(2)}) async-start(bf16[8,16,640]{2,1,0:T(8,128)(2,1)} %get-tuple-element.34), calls=%async_computation | async-start | bytes 327680 | tf_op jit(solution)/shard_map/all_to_all | solution.py:434
  27.7 4.1 %collective-permute-start.2 = (bf16[128,384]{1,0:T(8,128)(2,1)S(1)}, bf16[128,384]{1,0:T(8,128)(2,1)S(1)}, u32[]{:S(2)}, u32[]{:S(2)}) collective-permute-start(bf16[128,384]{1,0:T(8,128)(2,1)S(1)} %copy-done.12), channel_id=1, source_target_pairs={{0,24},{4,28},{8,16},{12,20},{16,8},{20,12},{24,0},{28,4},{32,56},... | collective-permute-start | bytes 294920 | tf_op jit(solution)/shard_map/ppermute | solution.py:411
  31.8 2.0 %collective-permute-start.1 = (bf16[128,384]{1,0:T(8,128)(2,1)S(1)}, bf16[128,384]{1,0:T(8,128)(2,1)S(1)}, u32[]{:S(2)}, u32[]{:S(2)}) collective-permute-start(bf16[128,384]{1,0:T(8,128)(2,1)S(1)} %copy-done.12), channel_id=1, source_target_pairs={{0,16},{4,20},{8,24},{12,28},{16,0},{20,4},{24,8},{28,12},{32,48},... | collective-permute-start | bytes 294920 | tf_op jit(solution)/shard_map/ppermute | solution.py:411
  33.8 1.9 %all-to-all-done.rows = bf16[8,16,640]{2,1,0:T(8,128)(2,1)S(1)} async-done(((bf16[8,16,640]{2,1,0:T(8,128)(2,1)}), bf16[8,16,640]{2,1,0:T(8,128)(2,1)S(1)}, u32[]{:S(2)}, u32[]{:S(2)}) %all-to-all-start) | async-done | bytes 163872 | tf_op jit(solution)/shard_map/all_to_all | solution.py:434
  35.8 0.7 collective-permute-start.3
  36.4 0.0 collective-permute-done.side
  36.4 0.0 copy-start.6
  36.4 0.7 copy-done.6
  37.2 4.6 %shard_map.122 = (f32[512,128]{1,0:T(8,128)}, f32[512,128]{1,0:T(8,128)}, f32[512,128]{1,0:T(8,128)}) custom-call(s32[4]{0:T(128)} %tiles.5, bf16[512,256]{1,0:T(8,128)(2,1)} %get-tuple-element.38.query, bf16[512,384]{1,0:T(8,128)(2,1)} %get-tuple-element.35.own, bf16[512,384]{1,0:T(8,128)(2,1)} %copy-done.6), custom_call_target="tpu_custom_call" | custom-call | flops 3300000000 | bytes 3000000 | tf_op jit(solution)/shard_map/pallas_call | solution.py:397
  41.8 0.0 copy-start.5
  41.9 0.0 collective-permute-done.2.mid_b
  41.9 0.0 collective-permute-done.1.mid_a
  41.9 0.0 copy-start.9
  41.9 0.0 collective-permute-done.3.here
  41.9 1.3 %pad_maximum_fusion = bf16[1280,384]{1,0:T(8,128)(2,1)S(1)} fusion(bf16[128,384]{1,0:T(8,128)(2,1)S(1)} %collective-permute-done.2.mid_b, bf16[128,384]{1,0:T(8,128)(2,1)S(1)} %collective-permute-done.1.mid_a, bf16[512,384]{1,0:T(8,128)(2,1)} %copy-done.6, bf16[512,384]{1,0:T(8,128)(2,1)} %get-tuple-element.35.own), kind=kLoop, calls=%fused_computation | loop fusion | flops 3932160 | bytes 1966080 | tf_op jit(solution)/shard_map/concatenate | solution.py:461
  43.2 4.5 %collective-permute-start.5 = (bf16[1280,384]{1,0:T(8,128)(2,1)S(1)}, bf16[1280,384]{1,0:T(8,128)(2,1)S(1)}, u32[]{:S(2)}, u32[]{:S(2)}) collective-permute-start(bf16[1280,384]{1,0:T(8,128)(2,1)S(1)} %pad_maximum_fusion), channel_id=1, source_target_pairs={{0,4},{4,0},{8,12},{12,8},{16,20},{20,16},{24,28},{28,24},{32,36},... | collective-permute-start | bytes 2949128 | tf_op jit(solution)/shard_map/ppermute | solution.py:411
  47.7 1.9 %collective-permute-start.4 = (bf16[128,384]{1,0:T(8,128)(2,1)S(1)}, bf16[128,384]{1,0:T(8,128)(2,1)S(1)}, u32[]{:S(2)}, u32[]{:S(2)}) collective-permute-start(bf16[128,384]{1,0:T(8,128)(2,1)S(1)} %collective-permute-done.3.here), channel_id=1, source_target_pairs={{0,4},{4,0},{8,12},{12,8},{16,20},{20,16},{24,28},{28,24},{32,36},... | collective-permute-start | bytes 294920 | tf_op jit(solution)/shard_map/ppermute | solution.py:411
  49.6 1.3 %collective-permute-done.4.other = bf16[128,384]{1,0:T(8,128)(2,1)S(1)} collective-permute-done((bf16[128,384]{1,0:T(8,128)(2,1)S(1)}, bf16[128,384]{1,0:T(8,128)(2,1)S(1)}, u32[]{:S(2)}, u32[]{:S(2)}) %collective-permute-start.4) | collective-permute-done | bytes 98336 | tf_op jit(solution)/shard_map/ppermute | solution.py:411
  50.9 0.0 copy-done.5
  50.9 1.9 %shard_map.123 = f32[8,16,384]{2,1,0:T(8,128)} custom-call(s32[4]{0:T(128)S(1)} %copy-done.5, bf16[8,16,640]{2,1,0:T(8,128)(2,1)S(1)} %all-to-all-done.rows, bf16[128,384]{1,0:T(8,128)(2,1)S(1)} %collective-permute-done.3.here, bf16[128,384]{1,0:T(8,128)(2,1)S(1)} %collective-permute-done.4.other), custom_call_target="tpu_custom_call" | custom-call | flops 2200000000 | bytes 2000000 | tf_op jit(solution)/shard_map/pallas_call | solution.py:397
  52.8 10.3 %all-to-all-start.1 = ((f32[8,16,384]{2,1,0:T(8,128)}), f32[8,16,384]{2,1,0:T(8,128)S(1)}, u32[]{:S(2)}, u32[]{:S(2)}) async-start(f32[8,16,384]{2,1,0:T(8,128)} %shard_map.123), calls=%async_computation.1 | async-start | bytes 393216 | tf_op jit(solution)/shard_map/all_to_all | solution.py:481
  63.0 0.0 collective-permute-done.5.swapped
  63.0 1.0 copy-done.10
  64.0 8.4 %shard_map.124 = (f32[512,128]{1,0:T(8,128)}, f32[512,128]{1,0:T(8,128)}, f32[512,128]{1,0:T(8,128)}) custom-call(s32[4]{0:T(128)} %tiles.5, bf16[512,256]{1,0:T(8,128)(2,1)} %get-tuple-element.38.query, bf16[512,384]{1,0:T(8,128)(2,1)} %get-tuple-element.35.own, bf16[512,384]{1,0:T(8,128)(2,1)} %copy-done.6, bf16[128,384]{1,0:T(8,128)(2,1)} %copy-done.9, ...), custom_call_target="tpu_custom_call" | custom-call | flops 5500000256 | bytes 5000000 | tf_op jit(solution)/shard_map/pallas_call | solution.py:397
  72.4 0.5 all-to-all-done.1.parts
  72.9 0.7 copy-done.7
  73.6 4.5 %shard_map.125 = (bf16[4,128,768]{2,1,0:T(8,128)(2,1)}, bf16[16,192]{1,0:T(8,128)(2,1)}) custom-call(f32[8,16,384]{2,1,0:T(8,128)} %copy-done.7, bf16[192,768]{1,0:T(8,128)(2,1)} %w_out.1, f32[512,128]{1,0:T(8,128)} %get-tuple-element.53.refs_0_, f32[512,128]{1,0:T(8,128)} %get-tuple-element.54.refs_1_, f32[512,128]{1,0:T(8,128)} %get-tuple-element.55.refs_2_), custom_call_target="tpu_custom_call" | custom-call | flops 3300000000 | bytes 3000000 | tf_op jit(solution)/shard_map/pallas_call | solution.py:397
  78.0 14.5 %all_to_all.15.terms = bf16[4,128,768]{2,1,0:T(8,128)(2,1)S(1)} all-to-all(bf16[4,128,768]{2,1,0:T(8,128)(2,1)} %get-tuple-element.56), channel_id=1, replica_groups=mesh['seq'=128,'mp'=4] {'mp'}, dimensions={0} | all-to-all | bytes 1572864 | tf_op jit(solution)/shard_map/all_to_all | solution.py:493
  92.5 0.0 copy-done.2
  92.5 0.8 shard_map.126
  93.4 4.7 %collective-permute-start.6 = (bf16[128,768]{1,0:T(8,128)(2,1)S(1)}, bf16[128,768]{1,0:T(8,128)(2,1)S(1)}, u32[]{:S(2)}, u32[]{:S(2)}) collective-permute-start(bf16[128,768]{1,0:T(8,128)(2,1)S(1)} %get-tuple-element.59.own), channel_id=1, source_target_pairs={{0,4},{4,0},{8,12},{12,8},{16,20},{20,16},{24,28},{28,24},{32,36},... | collective-permute-start | bytes 589832 | tf_op jit(solution)/shard_map/ppermute | solution.py:411
  98.0 0.0 all-gather.3.cloned.1.call-done
  98.1 1.0 collective-permute-done.6.other
  99.1 0.7 copy-done.11
  99.8 6.4 %shard_map.128 = (f32[128,768]{1,0:T(8,128)}, bf16[128,768]{1,0:T(8,128)(2,1)}) custom-call(bf16[128,768]{1,0:T(8,128)(2,1)} %copy-done.3, bf16[128,768]{1,0:T(8,128)(2,1)} %copy-done.11, bf16[4,768,768]{2,1,0:T(8,128)(2,1)} %bitcast.6), custom_call_target="tpu_custom_call" | custom-call | flops 4400000000 | bytes 4000000 | tf_op jit(solution)/shard_map/pallas_call | solution.py:397
  106.1 2.3 %collective-permute-start.7 = (bf16[128,768]{1,0:T(8,128)(2,1)}, bf16[128,768]{1,0:T(8,128)(2,1)S(1)}, u32[]{:S(2)}, u32[]{:S(2)}) collective-permute-start(bf16[128,768]{1,0:T(8,128)(2,1)} %get-tuple-element.64), channel_id=1, source_target_pairs={{0,4},{4,0},{8,12},{12,8},{16,20},{20,16},{24,28},{28,24},{32,36},... | collective-permute-start | bytes 589832 | tf_op jit(solution)/shard_map/ppermute | solution.py:411
  108.4 1.3 %collective-permute-done.7 = bf16[128,768]{1,0:T(8,128)(2,1)S(1)} collective-permute-done((bf16[128,768]{1,0:T(8,128)(2,1)}, bf16[128,768]{1,0:T(8,128)(2,1)S(1)}, u32[]{:S(2)}, u32[]{:S(2)}) %collective-permute-start.7) | collective-permute-done | bytes 196640 | tf_op jit(solution)/shard_map/ppermute | solution.py:411
  109.7 1.7 %add_convert_fusion = bf16[128,768]{1,0:T(8,128)(2,1)} fusion(f32[128,768]{1,0:T(8,128)} %get-tuple-element.63, bf16[128,768]{1,0:T(8,128)(2,1)S(1)} %collective-permute-done.7), kind=kLoop, calls=%fused_computation.1 | loop fusion | flops 294912 | bytes 786432 | tf_op jit(solution)/shard_map/convert_element_type | solution.py:508
  (13 shorter events, 0.0 us)
Async XLA Ops:
  7.2 90.9 %all-gather.3.cloned.1.call-start = ((), (), s32[]{:S(2)}) async-start(), calls=%async_computation.3 | async-start | bytes 5898240 | tf_op jit(solution)/shard_map/all_gather | solution.py:439
  7.2 5.2 %copy-start = (bf16[768,768]{1,0:T(8,128)(2,1)S(1)}, bf16[768,768]{1,0:T(8,128)(2,1)}, u32[]{:S(2)}) copy-start(bf16[768,768]{1,0:T(8,128)(2,1)} %w_up) | copy-start | bytes 3538948
  7.2 5.2 %copy-start.1 = (bf16[768,768]{1,0:T(8,128)(2,1)S(1)}, bf16[768,768]{1,0:T(8,128)(2,1)}, u32[]{:S(2)}) copy-start(bf16[768,768]{1,0:T(8,128)(2,1)} %w_down) | copy-start | bytes 3538948
  12.4 15.3 %copy-start.12 = (bf16[128,384]{1,0:T(8,128)(2,1)S(1)}, bf16[128,384]{1,0:T(8,128)(2,1)}, u32[]{:S(2)}) copy-start(bf16[128,384]{1,0:T(8,128)(2,1)} %get-tuple-element.36) | copy-start | bytes 294916
  13.6 22.8 %collective-permute-start = (bf16[512,384]{1,0:T(8,128)(2,1)}, bf16[512,384]{1,0:T(8,128)(2,1)S(1)}, u32[]{:S(2)}, u32[]{:S(2)}) collective-permute-start(bf16[512,384]{1,0:T(8,128)(2,1)} %get-tuple-element.35.own), channel_id=1, source_target_pairs={{0,8},{4,12},{8,0},{12,4},{16,24},{20,28},{24,16},{28,20},{32,40},... | collective-permute-start | bytes 1179656 | tf_op jit(solution)/shard_map/ppermute | solution.py:411
  17.6 18.1 %all-to-all-start = ((bf16[8,16,640]{2,1,0:T(8,128)(2,1)}), bf16[8,16,640]{2,1,0:T(8,128)(2,1)S(1)}, u32[]{:S(2)}, u32[]{:S(2)}) async-start(bf16[8,16,640]{2,1,0:T(8,128)(2,1)} %get-tuple-element.34), calls=%async_computation | async-start | bytes 327680 | tf_op jit(solution)/shard_map/all_to_all | solution.py:434
  27.7 14.2 %collective-permute-start.2 = (bf16[128,384]{1,0:T(8,128)(2,1)S(1)}, bf16[128,384]{1,0:T(8,128)(2,1)S(1)}, u32[]{:S(2)}, u32[]{:S(2)}) collective-permute-start(bf16[128,384]{1,0:T(8,128)(2,1)S(1)} %copy-done.12), channel_id=1, source_target_pairs={{0,24},{4,28},{8,16},{12,20},{16,8},{20,12},{24,0},{28,4},{32,56},... | collective-permute-start | bytes 294920 | tf_op jit(solution)/shard_map/ppermute | solution.py:411
  31.8 10.1 %collective-permute-start.1 = (bf16[128,384]{1,0:T(8,128)(2,1)S(1)}, bf16[128,384]{1,0:T(8,128)(2,1)S(1)}, u32[]{:S(2)}, u32[]{:S(2)}) collective-permute-start(bf16[128,384]{1,0:T(8,128)(2,1)S(1)} %copy-done.12), channel_id=1, source_target_pairs={{0,16},{4,20},{8,24},{12,28},{16,0},{20,4},{24,8},{28,12},{32,48},... | collective-permute-start | bytes 294920 | tf_op jit(solution)/shard_map/ppermute | solution.py:411
  35.8 6.1 %collective-permute-start.3 = (bf16[128,384]{1,0:T(8,128)(2,1)S(1)}, bf16[128,384]{1,0:T(8,128)(2,1)S(1)}, u32[]{:S(2)}, u32[]{:S(2)}) collective-permute-start(bf16[128,384]{1,0:T(8,128)(2,1)S(1)} %bitcast.5), channel_id=1, source_target_pairs={{0,0},{4,4},{8,8},{12,12},{16,16},{20,20},{24,24},{28,28},{32,32},... | collective-permute-start | bytes 294920 | tf_op jit(solution)/shard_map/ppermute | solution.py:443
  36.4 0.8 copy-start.6
  41.8 9.0 %copy-start.5 = (s32[4]{0:T(128)S(1)}, s32[4]{0:T(128)}, u32[]{:S(2)}) copy-start(s32[4]{0:T(128)} %tiles.5) | copy-start | bytes 52
  41.9 10.9 %copy-start.8 = (bf16[128,384]{1,0:T(8,128)(2,1)}, bf16[128,384]{1,0:T(8,128)(2,1)S(1)}, u32[]{:S(2)}) copy-start(bf16[128,384]{1,0:T(8,128)(2,1)S(1)} %collective-permute-done.2.mid_b) | copy-start | bytes 294916
  41.9 10.9 %copy-start.9 = (bf16[128,384]{1,0:T(8,128)(2,1)}, bf16[128,384]{1,0:T(8,128)(2,1)S(1)}, u32[]{:S(2)}) copy-start(bf16[128,384]{1,0:T(8,128)(2,1)S(1)} %collective-permute-done.1.mid_a) | copy-start | bytes 294916
  43.2 19.9 %collective-permute-start.5 = (bf16[1280,384]{1,0:T(8,128)(2,1)S(1)}, bf16[1280,384]{1,0:T(8,128)(2,1)S(1)}, u32[]{:S(2)}, u32[]{:S(2)}) collective-permute-start(bf16[1280,384]{1,0:T(8,128)(2,1)S(1)} %pad_maximum_fusion), channel_id=1, source_target_pairs={{0,4},{4,0},{8,12},{12,8},{16,20},{20,16},{24,28},{28,24},{32,36},... | collective-permute-start | bytes 2949128 | tf_op jit(solution)/shard_map/ppermute | solution.py:411
  47.7 3.2 %collective-permute-start.4 = (bf16[128,384]{1,0:T(8,128)(2,1)S(1)}, bf16[128,384]{1,0:T(8,128)(2,1)S(1)}, u32[]{:S(2)}, u32[]{:S(2)}) collective-permute-start(bf16[128,384]{1,0:T(8,128)(2,1)S(1)} %collective-permute-done.3.here), channel_id=1, source_target_pairs={{0,4},{4,0},{8,12},{12,8},{16,20},{20,16},{24,28},{28,24},{32,36},... | collective-permute-start | bytes 294920 | tf_op jit(solution)/shard_map/ppermute | solution.py:411
  52.8 20.1 %all-to-all-start.1 = ((f32[8,16,384]{2,1,0:T(8,128)}), f32[8,16,384]{2,1,0:T(8,128)S(1)}, u32[]{:S(2)}, u32[]{:S(2)}) async-start(f32[8,16,384]{2,1,0:T(8,128)} %shard_map.123), calls=%async_computation.1 | async-start | bytes 393216 | tf_op jit(solution)/shard_map/all_to_all | solution.py:481
  63.0 1.0 copy-start.10
  72.9 0.7 copy-start.7
  73.6 19.0 %copy-start.2 = (bf16[512,768]{1,0:T(8,128)(2,1)S(1)}, bf16[512,768]{1,0:T(8,128)(2,1)}, u32[]{:S(2)}) copy-start(bf16[512,768]{1,0:T(8,128)(2,1)} %tokens.3) | copy-start | bytes 2359300
  73.6 19.0 %copy-start.4 = (bf16[768]{0:T(1024)(128)(2,1)S(1)}, bf16[768]{0:T(1024)(128)(2,1)}, u32[]{:S(2)}) copy-start(bf16[768]{0:T(1024)(128)(2,1)} %gain.3) | copy-start | bytes 4612
  93.4 5.7 %copy-start.3 = (bf16[128,768]{1,0:T(8,128)(2,1)}, bf16[128,768]{1,0:T(8,128)(2,1)S(1)}, u32[]{:S(2)}) copy-start(bf16[128,768]{1,0:T(8,128)(2,1)S(1)} %get-tuple-element.59.own) | copy-start | bytes 589828
  93.4 5.7 %collective-permute-start.6 = (bf16[128,768]{1,0:T(8,128)(2,1)S(1)}, bf16[128,768]{1,0:T(8,128)(2,1)S(1)}, u32[]{:S(2)}, u32[]{:S(2)}) collective-permute-start(bf16[128,768]{1,0:T(8,128)(2,1)S(1)} %get-tuple-element.59.own), channel_id=1, source_target_pairs={{0,4},{4,0},{8,12},{12,8},{16,20},{20,16},{24,28},{28,24},{32,36},... | collective-permute-start | bytes 589832 | tf_op jit(solution)/shard_map/ppermute | solution.py:411
  99.1 0.7 copy-start.11
  106.1 3.5 %collective-permute-start.7 = (bf16[128,768]{1,0:T(8,128)(2,1)}, bf16[128,768]{1,0:T(8,128)(2,1)S(1)}, u32[]{:S(2)}, u32[]{:S(2)}) collective-permute-start(bf16[128,768]{1,0:T(8,128)(2,1)} %get-tuple-element.64), channel_id=1, source_target_pairs={{0,4},{4,0},{8,12},{12,8},{16,20},{20,16},{24,28},{28,24},{32,36},... | collective-permute-start | bytes 589832 | tf_op jit(solution)/shard_map/ppermute | solution.py:411
Sparse Core Ops, SparseCore 0:
  13.7 63.4 all-gather.2

commit v8 on v7

--- a/solution.py
+++ b/solution.py
@@ -184,11 +184,7 @@
     return jnp.concatenate([key_marks(rows + (seq ^ step) * ROWS, ends) for step in steps], 0)
 
 
-def near_kernel(tiles, query, own, side, *refs):
-    out, state, sems = refs[:LOCAL_HEADS], refs[LOCAL_HEADS:-1], refs[-1]
-    copies = [
-        pltpu.make_async_copy(state[head], out[head], sems.at[head]) for head in range(LOCAL_HEADS)
-    ]
+def near_kernel(tiles, query, own, side, *state):
     ends = slide_ends(tiles)
     seq = lax.axis_index("seq")
     marks = query_marks(row_at(iota((ROWS, LANES), 0)) + seq * ROWS, ends)
@@ -204,18 +200,11 @@
             jnp.concatenate([values, keys_marks], 1),
             head,
         )
-        copies[head].start()
-    for copy in copies:
-        copy.wait()
-
-
-def rest_kernel(tiles, query, own, side, mid_a, mid_b, swapped, *refs):
+
+
+def rest_kernel(tiles, query, own, side, mid_a, mid_b, swapped, parts, w_out, *refs):
     n = LOCAL_HEADS
-    held_from, out, held, state, sems = refs[:n], refs[n : 2 * n], refs[2 * n : 3 * n], refs[3 * n : -1], refs[-1]
-    fetches = [pltpu.make_async_copy(held_from[i], held[i], sems.at[i]) for i in range(n)]
-    copies = [pltpu.make_async_copy(state[i], out[i], sems.at[n + i]) for i in range(n)]
-    for fetch in fetches:
-        fetch.start()
+    held, (terms, far_out), state = refs[:n], refs[n : n + 2], refs[n + 2 :]
     ends = slide_ends(tiles)
     seq, mp = lax.axis_index("seq"), lax.axis_index("mp")
     marks = query_marks(row_at(iota((ROWS, LANES), 0)) + seq * ROWS, ends)
@@ -229,7 +218,6 @@
             jnp.concatenate([swapped[: 2 * ROWS, value_tile], near_marks], 1),
             head,
         )
-        fetches[head].wait()
         state[head][...] = join(held[head][...], more, peak, head)
 
         offset = (mp * LOCAL_HEADS + head) & 3
@@ -265,9 +253,38 @@
             head,
         )
         state[head][picked, :] = join(state[head][picked, :], more, peak, head)
-        copies[head].start()
-    for copy in copies:
-        copy.wait()
+    far_parts = []
+    for head in range(LOCAL_HEADS):
+        spare = SPARE[head]
+        pieces = [parts[index, :, tile(head)] for index in range(FAR_GROUP)]
+        tops = [piece[:, spare : spare + 1] for piece in pieces]
+        peak = functools.reduce(jnp.maximum, tops)
+        total = jnp.zeros((FAR_ROWS, LANES), jnp.float32)
+        for piece, top in zip(pieces, tops):
+            total = total + piece * jnp.exp(top - peak)
+        far_parts.append(total / total[:, spare + 1 : spare + 2])
+        number = mp * LOCAL_HEADS + head
+        start = (number & 3) * CLASS_ROWS + (number >> 2) * FAR_ROWS
+        picked = pl.ds(pl.multiple_of(start, FAR_ROWS), FAR_ROWS)
+        state[head][picked, :] = join(state[head][picked, :], total, peak, head)
+
+    def packed(values):
+        first = jnp.where(iota(values[0].shape, 1) < HEAD_DIM, values[0], values[1])
+        return first.astype(jnp.bfloat16), values[2].astype(jnp.bfloat16)
+
+    first, last = packed(far_parts)
+    far_out[:, :128] = first
+    far_out[:, 128:] = last[:, HEAD_DIM:]
+    back = (place_of(iota((ROWS, ROWS), 0)) == iota((ROWS, ROWS), 1)).astype(jnp.bfloat16)
+    first, last = packed(
+        [
+            state[head][...] / state[head][:, SPARE[head] + 1 : SPARE[head] + 2]
+            for head in range(LOCAL_HEADS)
+        ]
+    )
+    mixed = jnp.concatenate([first, last[:, HEAD_DIM:]], 1)
+    mixed = matmul(back, mixed).astype(jnp.bfloat16)
+    terms[...] = matmul(mixed, w_out[...]).astype(jnp.bfloat16).reshape(4, BLOCK, WIDTH)
 
 
 def far_kernel(tiles, rows, here, other, parts):
@@ -303,48 +320,6 @@
         parts[:, :, tile(head)] = part.reshape(FAR_GROUP, FAR_ROWS, LANES)
 
 
-def finish_kernel(parts, w_out, *refs):
-    n = LOCAL_HEADS
-    held, (terms, far_out), state, sems = refs[:n], refs[n : n + 2], refs[n + 2 : -1], refs[-1]
-    fetches = [pltpu.make_async_copy(held[i], state[i], sems.at[i]) for i in range(n)]
-    for fetch in fetches:
-        fetch.start()
-    mp = lax.axis_index("mp")
-    far_parts = []
-    for head in range(LOCAL_HEADS):
-        spare = SPARE[head]
-        pieces = [parts[index, :, tile(head)] for index in range(FAR_GROUP)]
-        tops = [piece[:, spare : spare + 1] for piece in pieces]
-        peak = functools.reduce(jnp.maximum, tops)
-        total = jnp.zeros((FAR_ROWS, LANES), jnp.float32)
-        for piece, top in zip(pieces, tops):
-            total = total + piece * jnp.exp(top - peak)
-        far_parts.append(total / total[:, spare + 1 : spare + 2])
-        number = mp * LOCAL_HEADS + head
-        start = (number & 3) * CLASS_ROWS + (number >> 2) * FAR_ROWS
-        picked = pl.ds(pl.multiple_of(start, FAR_ROWS), FAR_ROWS)
-        fetches[head].wait()
-        state[head][picked, :] = join(state[head][picked, :], total, peak, head)
-
-    def packed(values):
-        first = jnp.where(iota(values[0].shape, 1) < HEAD_DIM, values[0], values[1])
-        return first.astype(jnp.bfloat16), values[2].astype(jnp.bfloat16)
-
-    first, last = packed(far_parts)
-    far_out[:, :128] = first
-    far_out[:, 128:] = last[:, HEAD_DIM:]
-    back = (place_of(iota((ROWS, ROWS), 0)) == iota((ROWS, ROWS), 1)).astype(jnp.bfloat16)
-    first, last = packed(
-        [
-            state[head][...] / state[head][:, SPARE[head] + 1 : SPARE[head] + 2]
-            for head in range(LOCAL_HEADS)
-        ]
-    )
-    mixed = jnp.concatenate([first, last[:, HEAD_DIM:]], 1)
-    mixed = matmul(back, mixed).astype(jnp.bfloat16)
-    terms[...] = matmul(mixed, w_out[...]).astype(jnp.bfloat16).reshape(4, BLOCK, WIDTH)
-
-
 def weights_kernel(w_up, w_down, out):
     start = pl.multiple_of((lax.axis_index("seq") & 1) * HALF, HALF)
     out[:HALF, :HALF] = w_up[:HALF, pl.ds(start, HALF)]
@@ -370,35 +345,22 @@
     normed[...] = layer_norm(own + summed.astype(jnp.float32), gain[...])
 
 
-def ffn_kernel(own, other, weights, kept, sent, held, sems):
-    copies = []
-    for group in range(4):
-        for index in range(4):
-            part = pl.ds(index * 192, 192)
-            copies.append(
-                pltpu.make_async_copy(
-                    weights.at[group, part], held.at[group, part], sems.at[4 * group + index]
-                )
-            )
-    for copy in copies:
-        copy.start()
+def ffn_kernel(own, other, weights, kept, sent):
     rows = jnp.concatenate([own[...], other[...]], 0)
     total = jnp.zeros((2 * BLOCK, WIDTH), jnp.float32)
     for group in range(4):
-        for copy in copies[4 * group : 4 * group + 4]:
-            copy.wait()
-        total = total + hidden_part(rows, held.at[group])
+        total = total + hidden_part(rows, weights.at[group])
     kept[...] = total[:BLOCK, :]
     sent[...] = total[BLOCK:, :].astype(jnp.bfloat16)
 
 
-def call(kernel, micros, outs, ins, scratch=(), kept=pltpu.VMEM, limit=VMEM):
+def call(kernel, micros, outs, ins, scratch=(), limit=VMEM):
     places = {"smem": pltpu.SMEM, "vmem": pltpu.VMEM, "hbm": pltpu.HBM}
     return pl.pallas_call(
         kernel,
         out_shape=[jax.ShapeDtypeStruct(*out) for out in outs],
         in_specs=[pl.BlockSpec(memory_space=places[where]) for _, where in ins],
-        out_specs=[pl.BlockSpec(memory_space=kept) for _ in outs],
+        out_specs=[pl.BlockSpec(memory_space=pltpu.VMEM) for _ in outs],
         scratch_shapes=list(scratch),
         cost_estimate=pl.CostEstimate(
             flops=int(micros * 1.1e9), bytes_accessed=int(micros * 1e6), transcendentals=0
@@ -444,16 +406,7 @@
     query, _ = lax.optimization_barrier((query, far_keys))
     mid_a, mid_b = swap(mid, 4), swap(mid, 6)
     state = [((ROWS, LANES), f32)] * LOCAL_HEADS
-    scratch = [pltpu.VMEM(*shape) for shape in state]
-    near = call(
-        near_kernel,
-        3,
-        state,
-        [(slide_tiles, s), (query, v), (own, v), (side, v)],
-        [*scratch, dma((3,))],
-        pltpu.HBM,
-        WHOLE_VMEM,
-    )
+    near = call(near_kernel, 3, state, [(slide_tiles, s), (query, v), (own, v), (side, v)])
     side, mid_a, mid_b, far_here, *near = lax.optimization_barrier(
         (side, mid_a, mid_b, far_here, *near)
     )
@@ -465,32 +418,21 @@
         [((FAR_GROUP, FAR_ROWS, 384), f32)],
         [(slide_tiles, s), (far_rows, v), (far_here, v), (far_other, v)],
     )
-    parts, *near = lax.optimization_barrier((parts, *near))
-    both = call(
+    parts = lax.all_to_all(
+        parts, "seq", split_axis=0, concat_axis=0, tiled=True, axis_index_groups=columns
+    )
+    terms, far_attended = call(
         rest_kernel,
-        5,
-        state,
+        7,
+        [((4, BLOCK, WIDTH), bf16), ((FAR_ROWS, 192), bf16)],
         [
             (slide_tiles, s), (query, v), (own, v), (side, v), (mid_a, v), (mid_b, v), (swapped, v),
-            *[(held, h) for held in near],
+            (parts, v), (w_out, v), *[(held, v) for held in near],
         ],
-        [*scratch, *scratch, dma((6,))],
-        pltpu.HBM,
-        WHOLE_VMEM,
-    )
-    parts = lax.all_to_all(
-        parts, "seq", split_axis=0, concat_axis=0, tiled=True, axis_index_groups=columns
-    )
-    mine, _ = lax.optimization_barrier((mine, parts))
-    terms, far_attended = call(
-        finish_kernel,
-        3,
-        [((4, BLOCK, WIDTH), bf16), ((FAR_ROWS, 192), bf16)],
-        [(parts, v), (w_out, v), *[(held, h) for held in both]],
-        [*scratch, dma((3,))],
-        limit=WHOLE_VMEM,
+        [pltpu.VMEM(*shape) for shape in state],
     )
     terms = lax.all_to_all(terms, "mp", split_axis=0, concat_axis=0, tiled=True)
+    terms, mine = lax.optimization_barrier((terms, mine))
     attended, normed = call(
         norm_kernel,
         1,
@@ -501,9 +443,7 @@
         ffn_kernel,
         4,
         [((BLOCK, WIDTH), f32), ((BLOCK, WIDTH), bf16)],
-        [(normed, v), (swap(normed, 1), v), (mine, h)],
-        [pltpu.VMEM((4, 2 * HALF, WIDTH), bf16), dma((16,))],
-        limit=WHOLE_VMEM,
+        [(normed, v), (swap(normed, 1), v), (mine, v)],
     )
     ffn_out = (kept + swap(sent, 1).astype(f32)).astype(bf16)
     return (attended, far_attended, ffn_out)

time: 119 us -> 114 us (0.958)
  blocking collectives: 14.5 us -> 35 us
  Pallas kernels: 32.8 us -> 20 us
  starting transfers between devices: 44.6 us -> 33.5 us
  other arithmetic: 2.97 us -> 0.82 us
    all_to_all x0 -> x1, blocking collectives: none -> 20.7 us  [local(): lax.all_to_all(parts, 'seq', split_axis=0, concat_axis=0, tiled=True, axi...]
    pallas_call x8 -> x7, Pallas kernels: 32.8 us -> 20 us  [call(): pl.pallas_call(kernel, out_shape=[jax.ShapeDtypeStruct(*out) for out in o...]
    all_to_all x1 -> x0, starting transfers between devices: 10.3 us -> none  [local(): lax.all_to_all(parts, 'seq', split_axis=0, concat_axis=0, tiled=True, axi...]
    unnamed x26 -> x20, local copies, waits for them, and re-layouts: 3.1 us -> 2.38 us
  transfers between devices with their start and end apart: 11 -> 10, of which waited for: 5 -> 5; matrix products, arithmetic and copies ran while one was open for 1% -> 0% of each run, Pallas kernels for 17% -> 9%
where the time goes in v8:
time: 114 us; the launch traced here: 112 us
  blocking collectives  35 us (31%)
  starting transfers between devices  33.5 us (29%)
  Pallas kernels  20 us (18%)
  between operations  14.3 us (13%)
  waiting for transfers between devices  6.36 us (6%)
  local copies, waits for them, and re-layouts  2.39 us (2%)
    ppermute x7, starting transfers between devices, swap(): lax.ppermute(value, 'seq', [(i, i ^ step) for i in range(lax.axis_size('s...  22.7 us
    all_to_all x1, blocking collectives, local(): lax.all_to_all(parts, 'seq', split_axis=0, concat_axis=0, tiled=True, axi...  20.7 us
    pallas_call x7, Pallas kernels, call(): pl.pallas_call(kernel, out_shape=[jax.ShapeDtypeStruct(*out) for out in o...  20 us
    all_to_all x1, blocking collectives, local(): terms = lax.all_to_all(terms, 'mp', split_axis=0, concat_axis=0, tiled=True)  14.3 us
    all_to_all x1, starting transfers between devices, local(): lax.all_to_all(far, 'seq', split_axis=0, concat_axis=0, tiled=True, axis_...  10 us
    ppermute x7, waiting for transfers between devices, swap(): lax.ppermute(value, 'seq', [(i, i ^ step) for i in range(lax.axis_size('s...  4.44 us
    unnamed x20, local copies, waits for them, and re-layouts  2.38 us
  transfers between devices with their start and end apart: 10, of which 5 were waited for; matrix products, arithmetic and copies ran while one was open for 0% of the time, Pallas kernels for 9%

profile of v8, /device:TPU:1, one launch (start us, length us, event | category | flops | bytes accessed | tf_op | source)
XLA Modules:
  0.0 112.3 jit_solution(11370575400130823072)
XLA Ops:
  7.2 0.0 all-gather.3.cloned.1.call-start
  7.2 0.0 copy-start.2
  7.2 0.0 copy-start.3
  7.2 5.1 %shard_map.121 = (bf16[512,256]{1,0:T(8,128)(2,1)}, bf16[512,384]{1,0:T(8,128)(2,1)}, bf16[128,384]{1,0:T(8,128)(2,1)}, bf16[8,16,640]{2,1,0:T(8,128)(2,1)}) custom-call(bf16[512,768]{1,0:T(8,128)(2,1)} %tokens.3, bf16[768]{0:T(1024)(128)(2,1)} %gain.2, bf16[192,768]{1,0:T(8,128)(2,1)} %bitcast.7, bf16[192,768]{1,0:T(8,128)(2,1)} %bitcast.8, ...), custom_call_target="tpu_custom_call" | custom-call | flops 3300000000 | bytes 3000000 | tf_op jit(solution)/shard_map/pallas_call | solution.py:359
  12.4 0.0 copy-done.2
  12.4 0.0 copy-done.3
  12.4 0.0 copy-start
  12.4 0.0 copy-start.9
  12.4 0.0 copy-start.7
  12.4 0.0 copy-start.8
  12.4 1.1 %shard_map.125 = bf16[768,768]{1,0:T(8,128)(2,1)} custom-call(bf16[768,768]{1,0:T(8,128)(2,1)S(1)} %copy-done.2, bf16[768,768]{1,0:T(8,128)(2,1)S(1)} %copy-done.3), custom_call_target="tpu_custom_call" | custom-call | flops 2200000000 | bytes 2000000 | tf_op jit(solution)/shard_map/pallas_call | solution.py:359
  13.6 0.0 all-gather.3.cloned.1.call-update
  13.6 0.0 copy-done
  13.6 4.0 %collective-permute-start = (bf16[512,384]{1,0:T(8,128)(2,1)S(1)}, bf16[512,384]{1,0:T(8,128)(2,1)S(1)}, u32[]{:S(2)}, u32[]{:S(2)}) collective-permute-start(bf16[512,384]{1,0:T(8,128)(2,1)S(1)} %copy-done), channel_id=1, source_target_pairs={{0,8},{4,12},{8,0},{12,4},{16,24},{20,28},{24,16},{28,20},{32,40},... | collective-permute-start | bytes 1179656 | tf_op jit(solution)/shard_map/ppermute | solution.py:373
  17.7 10.0 %all-to-all-start = ((bf16[8,16,640]{2,1,0:T(8,128)(2,1)}), bf16[8,16,640]{2,1,0:T(8,128)(2,1)S(1)}, u32[]{:S(2)}, u32[]{:S(2)}) async-start(bf16[8,16,640]{2,1,0:T(8,128)(2,1)} %get-tuple-element.29), calls=%async_computation | async-start | bytes 327680 | tf_op jit(solution)/shard_map/all_to_all | solution.py:396
  27.7 0.0 copy-done.9
  27.7 4.1 %collective-permute-start.2 = (bf16[128,384]{1,0:T(8,128)(2,1)S(1)}, bf16[128,384]{1,0:T(8,128)(2,1)S(1)}, u32[]{:S(2)}, u32[]{:S(2)}) collective-permute-start(bf16[128,384]{1,0:T(8,128)(2,1)S(1)} %copy-done.9), channel_id=1, source_target_pairs={{0,24},{4,28},{8,16},{12,20},{16,8},{20,12},{24,0},{28,4},{32,56},... | collective-permute-start | bytes 294920 | tf_op jit(solution)/shard_map/ppermute | solution.py:373
  31.8 2.0 %collective-permute-start.1 = (bf16[128,384]{1,0:T(8,128)(2,1)S(1)}, bf16[128,384]{1,0:T(8,128)(2,1)S(1)}, u32[]{:S(2)}, u32[]{:S(2)}) collective-permute-start(bf16[128,384]{1,0:T(8,128)(2,1)S(1)} %copy-done.9), channel_id=1, source_target_pairs={{0,16},{4,20},{8,24},{12,28},{16,0},{20,4},{24,8},{28,12},{32,48},... | collective-permute-start | bytes 294920 | tf_op jit(solution)/shard_map/ppermute | solution.py:373
  33.9 1.9 %all-to-all-done.rows = bf16[8,16,640]{2,1,0:T(8,128)(2,1)S(1)} async-done(((bf16[8,16,640]{2,1,0:T(8,128)(2,1)}), bf16[8,16,640]{2,1,0:T(8,128)(2,1)S(1)}, u32[]{:S(2)}, u32[]{:S(2)}) %all-to-all-start) | async-done | bytes 163872 | tf_op jit(solution)/shard_map/all_to_all | solution.py:396
  35.8 0.7 collective-permute-start.3
  36.5 0.0 collective-permute-done.side
  36.5 0.0 copy-done.7
  36.5 0.0 copy-done.8
  36.5 3.2 %shard_map.122 = (f32[512,128]{1,0:T(8,128)S(1)}, f32[512,128]{1,0:T(8,128)S(1)}, f32[512,128]{1,0:T(8,128)S(1)}) custom-call(s32[4]{0:T(128)S(1)} %copy-done.7, bf16[512,256]{1,0:T(8,128)(2,1)S(1)} %copy-done.8, bf16[512,384]{1,0:T(8,128)(2,1)S(1)} %copy-done, bf16[512,384]{1,0:T(8,128)(2,1)S(1)} %collective-permute-done.side), custom_call_target="tpu_custom_call" | custom-call | flops 3300000000 | bytes 3000000 | tf_op jit(solution)/shard_map/pallas_call | solution.py:359
  39.7 0.0 collective-permute-done.2.mid_b
  39.7 1.1 collective-permute-done.1.mid_a
  40.8 0.0 collective-permute-done.3.here
  40.8 0.1 pad_maximum_fusion
  40.9 0.0 copy-start.5
  40.9 3.7 %collective-permute-start.4 = (bf16[1280,384]{1,0:T(8,128)(2,1)S(1)}, bf16[1280,384]{1,0:T(8,128)(2,1)S(1)}, u32[]{:S(2)}, u32[]{:S(2)}) collective-permute-start(bf16[1280,384]{1,0:T(8,128)(2,1)S(1)} %pad_maximum_fusion), channel_id=1, source_target_pairs={{0,4},{4,0},{8,12},{12,8},{16,20},{20,16},{24,28},{28,24},{32,36},... | collective-permute-start | bytes 2949128 | tf_op jit(solution)/shard_map/ppermute | solution.py:373
  44.6 1.9 %collective-permute-start.5 = (bf16[128,384]{1,0:T(8,128)(2,1)S(1)}, bf16[128,384]{1,0:T(8,128)(2,1)S(1)}, u32[]{:S(2)}, u32[]{:S(2)}) collective-permute-start(bf16[128,384]{1,0:T(8,128)(2,1)S(1)} %collective-permute-done.3.here), channel_id=1, source_target_pairs={{0,4},{4,0},{8,12},{12,8},{16,20},{20,16},{24,28},{28,24},{32,36},... | collective-permute-start | bytes 294920 | tf_op jit(solution)/shard_map/ppermute | solution.py:373
  46.5 1.3 %collective-permute-done.5.other = bf16[128,384]{1,0:T(8,128)(2,1)S(1)} collective-permute-done((bf16[128,384]{1,0:T(8,128)(2,1)S(1)}, bf16[128,384]{1,0:T(8,128)(2,1)S(1)}, u32[]{:S(2)}, u32[]{:S(2)}) %collective-permute-start.5) | collective-permute-done | bytes 98336 | tf_op jit(solution)/shard_map/ppermute | solution.py:373
  47.8 1.2 %shard_map.123 = f32[8,16,384]{2,1,0:T(8,128)S(1)} custom-call(s32[4]{0:T(128)S(1)} %copy-done.7, bf16[8,16,640]{2,1,0:T(8,128)(2,1)S(1)} %all-to-all-done.rows, bf16[128,384]{1,0:T(8,128)(2,1)S(1)} %collective-permute-done.3.here, bf16[128,384]{1,0:T(8,128)(2,1)S(1)} %collective-permute-done.5.other), custom_call_target="tpu_custom_call" | custom-call | flops 2200000000 | bytes 2000000 | tf_op jit(solution)/shard_map/pallas_call | solution.py:359
  49.0 20.7 %all_to_all.15.parts = f32[8,16,384]{2,1,0:T(8,128)S(1)} all-to-all(f32[8,16,384]{2,1,0:T(8,128)S(1)} %shard_map.123), channel_id=1, replica_groups={{0,64,128,192,256,320,384,448},{4,68,132,196,260,324,388,452},{8,72,136..., dimensions={0} | all-to-all | bytes 393216 | tf_op jit(solution)/shard_map/all_to_all | solution.py:421
  69.7 0.0 collective-permute-done.4.swapped
  69.7 0.0 copy-done.5
  69.7 6.3 %shard_map.124 = (bf16[4,128,768]{2,1,0:T(8,128)(2,1)S(1)}, bf16[16,192]{1,0:T(8,128)(2,1)}) custom-call(s32[4]{0:T(128)S(1)} %copy-done.7, bf16[512,256]{1,0:T(8,128)(2,1)S(1)} %copy-done.8, bf16[512,384]{1,0:T(8,128)(2,1)S(1)} %copy-done, bf16[512,384]{1,0:T(8,128)(2,1)S(1)} %collective-permute-done.side, ...), custom_call_target="tpu_custom_call" | custom-call | flops 7699999744 | bytes 7000000 | tf_op jit(solution)/shard_map/pallas_call | solution.py:359
  75.9 14.3 %all_to_all.16.terms = bf16[4,128,768]{2,1,0:T(8,128)(2,1)S(1)} all-to-all(bf16[4,128,768]{2,1,0:T(8,128)(2,1)S(1)} %get-tuple-element.43), channel_id=1, replica_groups=mesh['seq'=128,'mp'=4] {'mp'}, dimensions={0} | all-to-all | bytes 1572864 | tf_op jit(solution)/shard_map/all_to_all | solution.py:434
  90.2 0.0 copy-done.4
  90.2 0.0 copy-done.6
  90.2 0.8 shard_map.126
  91.0 4.7 %collective-permute-start.6 = (bf16[128,768]{1,0:T(8,128)(2,1)S(1)}, bf16[128,768]{1,0:T(8,128)(2,1)S(1)}, u32[]{:S(2)}, u32[]{:S(2)}) collective-permute-start(bf16[128,768]{1,0:T(8,128)(2,1)S(1)} %get-tuple-element.49.own), channel_id=1, source_target_pairs={{0,4},{4,0},{8,12},{12,8},{16,20},{20,16},{24,28},{28,24},{32,36},... | collective-permute-start | bytes 589832 | tf_op jit(solution)/shard_map/ppermute | solution.py:373
  95.7 1.0 collective-permute-done.6.other
  96.8 2.3 %copy-done.1 = bf16[3072,768]{1,0:T(8,128)(2,1)S(1)} copy-done((bf16[3072,768]{1,0:T(8,128)(2,1)S(1)}, bf16[3072,768]{1,0:T(8,128)(2,1)}, u32[]{:S(2)}) %copy-start.1) | copy-done | bytes 4718616
  99.1 2.3 %shard_map.127 = (f32[128,768]{1,0:T(8,128)S(1)}, bf16[128,768]{1,0:T(8,128)(2,1)S(1)}) custom-call(bf16[128,768]{1,0:T(8,128)(2,1)S(1)} %get-tuple-element.49.own, bf16[128,768]{1,0:T(8,128)(2,1)S(1)} %collective-permute-done.6.other, bf16[4,768,768]{2,1,0:T(8,128)(2,1)S(1)} %bitcast.5), custom_call_target="tpu_custom_call" | custom-call | flops 4400000000 | bytes 4000000 | tf_op jit(solution)/shard_map/pallas_call | solution.py:359
  101.4 2.3 %collective-permute-start.7 = (bf16[128,768]{1,0:T(8,128)(2,1)S(1)}, bf16[128,768]{1,0:T(8,128)(2,1)S(1)}, u32[]{:S(2)}, u32[]{:S(2)}) collective-permute-start(bf16[128,768]{1,0:T(8,128)(2,1)S(1)} %get-tuple-element.52), channel_id=1, source_target_pairs={{0,4},{4,0},{8,12},{12,8},{16,20},{20,16},{24,28},{28,24},{32,36},... | collective-permute-start | bytes 589832 | tf_op jit(solution)/shard_map/ppermute | solution.py:373
  103.7 1.0 collective-permute-done.7
  104.7 0.7 add_convert_fusion
  (5 shorter events, 0.0 us)
Async XLA Ops:
  7.2 83.0 %all-gather.3.cloned.1.call-start = ((), (), s32[]{:S(2)}) async-start(), calls=%async_computation.3 | async-start | bytes 5898240 | tf_op jit(solution)/shard_map/all_gather | solution.py:401
  7.2 5.2 %copy-start.2 = (bf16[768,768]{1,0:T(8,128)(2,1)S(1)}, bf16[768,768]{1,0:T(8,128)(2,1)}, u32[]{:S(2)}) copy-start(bf16[768,768]{1,0:T(8,128)(2,1)} %w_up) | copy-start | bytes 3538948
  7.2 5.2 %copy-start.3 = (bf16[768,768]{1,0:T(8,128)(2,1)S(1)}, bf16[768,768]{1,0:T(8,128)(2,1)}, u32[]{:S(2)}) copy-start(bf16[768,768]{1,0:T(8,128)(2,1)} %w_down) | copy-start | bytes 3538948
  12.4 1.2 %copy-start = (bf16[512,384]{1,0:T(8,128)(2,1)S(1)}, bf16[512,384]{1,0:T(8,128)(2,1)}, u32[]{:S(2)}) copy-start(bf16[512,384]{1,0:T(8,128)(2,1)} %get-tuple-element.31.own) | copy-start | bytes 1179652
  12.4 15.3 %copy-start.9 = (bf16[128,384]{1,0:T(8,128)(2,1)S(1)}, bf16[128,384]{1,0:T(8,128)(2,1)}, u32[]{:S(2)}) copy-start(bf16[128,384]{1,0:T(8,128)(2,1)} %get-tuple-element.32) | copy-start | bytes 294916
  12.4 24.1 %copy-start.7 = (s32[4]{0:T(128)S(1)}, s32[4]{0:T(128)}, u32[]{:S(2)}) copy-start(s32[4]{0:T(128)} %tiles.5) | copy-start | bytes 52
  12.4 24.1 %copy-start.8 = (bf16[512,256]{1,0:T(8,128)(2,1)S(1)}, bf16[512,256]{1,0:T(8,128)(2,1)}, u32[]{:S(2)}) copy-start(bf16[512,256]{1,0:T(8,128)(2,1)} %get-tuple-element.30.query) | copy-start | bytes 786436
  13.6 22.8 %collective-permute-start = (bf16[512,384]{1,0:T(8,128)(2,1)S(1)}, bf16[512,384]{1,0:T(8,128)(2,1)S(1)}, u32[]{:S(2)}, u32[]{:S(2)}) collective-permute-start(bf16[512,384]{1,0:T(8,128)(2,1)S(1)} %copy-done), channel_id=1, source_target_pairs={{0,8},{4,12},{8,0},{12,4},{16,24},{20,28},{24,16},{28,20},{32,40},... | collective-permute-start | bytes 1179656 | tf_op jit(solution)/shard_map/ppermute | solution.py:373
  17.7 18.1 %all-to-all-start = ((bf16[8,16,640]{2,1,0:T(8,128)(2,1)}), bf16[8,16,640]{2,1,0:T(8,128)(2,1)S(1)}, u32[]{:S(2)}, u32[]{:S(2)}) async-start(bf16[8,16,640]{2,1,0:T(8,128)(2,1)} %get-tuple-element.29), calls=%async_computation | async-start | bytes 327680 | tf_op jit(solution)/shard_map/all_to_all | solution.py:396
  27.7 12.0 %collective-permute-start.2 = (bf16[128,384]{1,0:T(8,128)(2,1)S(1)}, bf16[128,384]{1,0:T(8,128)(2,1)S(1)}, u32[]{:S(2)}, u32[]{:S(2)}) collective-permute-start(bf16[128,384]{1,0:T(8,128)(2,1)S(1)} %copy-done.9), channel_id=1, source_target_pairs={{0,24},{4,28},{8,16},{12,20},{16,8},{20,12},{24,0},{28,4},{32,56},... | collective-permute-start | bytes 294920 | tf_op jit(solution)/shard_map/ppermute | solution.py:373
  31.8 8.9 %collective-permute-start.1 = (bf16[128,384]{1,0:T(8,128)(2,1)S(1)}, bf16[128,384]{1,0:T(8,128)(2,1)S(1)}, u32[]{:S(2)}, u32[]{:S(2)}) collective-permute-start(bf16[128,384]{1,0:T(8,128)(2,1)S(1)} %copy-done.9), channel_id=1, source_target_pairs={{0,16},{4,20},{8,24},{12,28},{16,0},{20,4},{24,8},{28,12},{32,48},... | collective-permute-start | bytes 294920 | tf_op jit(solution)/shard_map/ppermute | solution.py:373
  35.8 5.0 %collective-permute-start.3 = (bf16[128,384]{1,0:T(8,128)(2,1)S(1)}, bf16[128,384]{1,0:T(8,128)(2,1)S(1)}, u32[]{:S(2)}, u32[]{:S(2)}) collective-permute-start(bf16[128,384]{1,0:T(8,128)(2,1)S(1)} %bitcast.6), channel_id=1, source_target_pairs={{0,0},{4,4},{8,8},{12,12},{16,16},{20,20},{24,24},{28,28},{32,32},... | collective-permute-start | bytes 294920 | tf_op jit(solution)/shard_map/ppermute | solution.py:405
  40.9 28.8 %copy-start.5 = (bf16[192,768]{1,0:T(8,128)(2,1)S(1)}, bf16[192,768]{1,0:T(8,128)(2,1)}, u32[]{:S(2)}) copy-start(bf16[192,768]{1,0:T(8,128)(2,1)} %w_out.1) | copy-start | bytes 884740
  40.9 28.8 %collective-permute-start.4 = (bf16[1280,384]{1,0:T(8,128)(2,1)S(1)}, bf16[1280,384]{1,0:T(8,128)(2,1)S(1)}, u32[]{:S(2)}, u32[]{:S(2)}) collective-permute-start(bf16[1280,384]{1,0:T(8,128)(2,1)S(1)} %pad_maximum_fusion), channel_id=1, source_target_pairs={{0,4},{4,0},{8,12},{12,8},{16,20},{20,16},{24,28},{28,24},{32,36},... | collective-permute-start | bytes 2949128 | tf_op jit(solution)/shard_map/ppermute | solution.py:373
  44.6 3.2 %collective-permute-start.5 = (bf16[128,384]{1,0:T(8,128)(2,1)S(1)}, bf16[128,384]{1,0:T(8,128)(2,1)S(1)}, u32[]{:S(2)}, u32[]{:S(2)}) collective-permute-start(bf16[128,384]{1,0:T(8,128)(2,1)S(1)} %collective-permute-done.3.here), channel_id=1, source_target_pairs={{0,4},{4,0},{8,12},{12,8},{16,20},{20,16},{24,28},{28,24},{32,36},... | collective-permute-start | bytes 294920 | tf_op jit(solution)/shard_map/ppermute | solution.py:373
  69.7 20.5 %copy-start.4 = (bf16[512,768]{1,0:T(8,128)(2,1)S(1)}, bf16[512,768]{1,0:T(8,128)(2,1)}, u32[]{:S(2)}) copy-start(bf16[512,768]{1,0:T(8,128)(2,1)} %tokens.3) | copy-start | bytes 2359300
  69.7 20.5 %copy-start.6 = (bf16[768]{0:T(1024)(128)(2,1)S(1)}, bf16[768]{0:T(1024)(128)(2,1)}, u32[]{:S(2)}) copy-start(bf16[768]{0:T(1024)(128)(2,1)} %gain.3) | copy-start | bytes 4612
  91.0 5.7 %collective-permute-start.6 = (bf16[128,768]{1,0:T(8,128)(2,1)S(1)}, bf16[128,768]{1,0:T(8,128)(2,1)S(1)}, u32[]{:S(2)}, u32[]{:S(2)}) collective-permute-start(bf16[128,768]{1,0:T(8,128)(2,1)S(1)} %get-tuple-element.49.own), channel_id=1, source_target_pairs={{0,4},{4,0},{8,12},{12,8},{16,20},{20,16},{24,28},{28,24},{32,36},... | collective-permute-start | bytes 589832 | tf_op jit(solution)/shard_map/ppermute | solution.py:373
  96.8 2.3 %copy-start.1 = (bf16[3072,768]{1,0:T(8,128)(2,1)S(1)}, bf16[3072,768]{1,0:T(8,128)(2,1)}, u32[]{:S(2)}) copy-start(bf16[3072,768]{1,0:T(8,128)(2,1)} %all-gather.3.cloned.1.call-done) | copy-start | bytes 14155780
  101.4 3.3 %collective-permute-start.7 = (bf16[128,768]{1,0:T(8,128)(2,1)S(1)}, bf16[128,768]{1,0:T(8,128)(2,1)S(1)}, u32[]{:S(2)}, u32[]{:S(2)}) collective-permute-start(bf16[128,768]{1,0:T(8,128)(2,1)S(1)} %get-tuple-element.52), channel_id=1, source_target_pairs={{0,4},{4,0},{8,12},{12,8},{16,20},{20,16},{24,28},{28,24},{32,36},... | collective-permute-start | bytes 589832 | tf_op jit(solution)/shard_map/ppermute | solution.py:373
Sparse Core Ops, SparseCore 0:
  13.7 63.4 all-gather.2

commit v9 on v8

--- a/solution.py
+++ b/solution.py
@@ -109,7 +109,7 @@
 
 
 def project_kernel(
-    tokens, gain, w_query, w_key, w_value, query, keyval, mid, far, rows, weights, sems
+    tokens, gain, w_query, w_key, w_value, query, keyval, mid, far_query, far_keyval, rows, weights, sems
 ):
     mp = lax.axis_index("mp")
     copies = []
@@ -148,11 +148,11 @@
 
     for index in range(3):
         mid[:, tile(index)] = pick(keyval, index, KEY_TILE, CLASS_ROWS)
-    picked = [pick(query, index, QUERY_TILE, FAR_ROWS) for index in range(2)]
-    picked += [pick(keyval, index, KEY_TILE, FAR_ROWS) for index in range(3)]
-    for index, value in enumerate(picked):
-        for copy in range(FAR_GROUP):
-            far[copy, :, tile(index)] = value
+    for source, whose, target in ((query, QUERY_TILE, far_query), (keyval, KEY_TILE, far_keyval)):
+        for index in range(whose[2] + 1):
+            value = pick(source, index, whose, FAR_ROWS)
+            for copy in range(FAR_GROUP):
+                target[copy, :, tile(index)] = value
 
 
 def attend(query, keys, values, head):
@@ -204,7 +204,7 @@
 
 def rest_kernel(tiles, query, own, side, mid_a, mid_b, swapped, parts, w_out, *refs):
     n = LOCAL_HEADS
-    held, (terms, far_out), state = refs[:n], refs[n : n + 2], refs[n + 2 :]
+    held, terms, far_out, state = refs[:n], refs[n : n + 4], refs[n + 4], refs[n + 5 :]
     ends = slide_ends(tiles)
     seq, mp = lax.axis_index("seq"), lax.axis_index("mp")
     marks = query_marks(row_at(iota((ROWS, LANES), 0)) + seq * ROWS, ends)
@@ -275,7 +275,8 @@
     first, last = packed(far_parts)
     far_out[:, :128] = first
     far_out[:, 128:] = last[:, HEAD_DIM:]
-    back = (place_of(iota((ROWS, ROWS), 0)) == iota((ROWS, ROWS), 1)).astype(jnp.bfloat16)
+    row = (iota((ROWS, ROWS), 0) + mp * BLOCK) & (ROWS - 1)
+    back = (place_of(row) == iota((ROWS, ROWS), 1)).astype(jnp.bfloat16)
     first, last = packed(
         [
             state[head][...] / state[head][:, SPARE[head] + 1 : SPARE[head] + 2]
@@ -284,37 +285,42 @@
     )
     mixed = jnp.concatenate([first, last[:, HEAD_DIM:]], 1)
     mixed = matmul(back, mixed).astype(jnp.bfloat16)
-    terms[...] = matmul(mixed, w_out[...]).astype(jnp.bfloat16).reshape(4, BLOCK, WIDTH)
+    for index, term in enumerate(terms):
+        part = mixed[index * BLOCK : (index + 1) * BLOCK]
+        term[...] = matmul(part, w_out[...]).astype(jnp.bfloat16)
 
 
 def far_kernel(tiles, rows, here, other, parts):
     ends = slide_ends(tiles)
     seq, mp = lax.axis_index("seq"), lax.axis_index("mp")
-    column = seq & 15
-    beside = column ^ ((seq >> 4) << 1)
     count = FAR_GROUP * FAR_ROWS
     shape = (count, 2 * count)
 
     def position(place, holder):
-        return ((place >> 4) * 16 + holder) * ROWS + (place & 15) * RATE_FAR
+        return holder * ROWS + (place & 15) * RATE_FAR
 
     at = iota(shape, 1)
-    holder = jnp.where(at < count, beside, beside ^ 1)
-    key_at = position(at & (count - 1), holder)
-    query_at = position(iota(shape, 0), column)
+    core = (seq & 1) ^ (at >> 7)
+    key_at = position(at, (seq & 112) + ((at >> 4) & 7) * 2 + core)
+    at = iota(shape, 0)
+    query_at = position(at, (at >> 4) * 16 + (seq & 15))
     lane = iota((count, LANES), 1)
+
+    def flat(ref, lanes):
+        return ref[:, :, lanes].reshape(count, LANES)
+
     for head in range(LOCAL_HEADS):
         number = mp * LOCAL_HEADS + head
         key_tile, value_tile = tile(KEY_TILE[head]), tile(VALUE_TILE[head])
         asked = rows[:, :, tile(QUERY_TILE[head])].reshape(count, LANES)
         asked = head_lanes(asked, head)
-        scores = matmul_t(asked, jnp.concatenate([here[:, key_tile], other[:, key_tile]], 0))
+        scores = matmul_t(asked, jnp.concatenate([flat(here, key_tile), flat(other, key_tile)], 0))
         same = slide_of(query_at + number, ends) == slide_of(key_at + number, ends)
         scores = jnp.where(same, scores, HIDDEN_SCORE)
         peak = jnp.max(scores, -1, keepdims=True)
         weights = jnp.exp(scores - peak)
         total = jnp.sum(weights, -1, keepdims=True)
-        values = jnp.concatenate([here[:, value_tile], other[:, value_tile]], 0)
+        values = jnp.concatenate([flat(here, value_tile), flat(other, value_tile)], 0)
         part = matmul(weights.astype(jnp.bfloat16), values)
         part = pack(part, peak, total, head, lane)
         parts[:, :, tile(head)] = part.reshape(FAR_GROUP, FAR_ROWS, LANES)
@@ -334,10 +340,11 @@
     return matmul(hidden, weights[HALF:, :])
 
 
-def norm_kernel(tokens, terms, gain, attended, normed):
-    summed = terms[0].astype(jnp.float32)
-    for group in range(1, 4):
-        summed = summed + terms[group].astype(jnp.float32)
+def norm_kernel(tokens, gain, *refs):
+    terms, attended, normed = refs[:4], refs[4], refs[5]
+    summed = terms[0][...].astype(jnp.float32)
+    for term in terms[1:]:
+        summed = summed + term[...].astype(jnp.float32)
     summed = summed.astype(jnp.bfloat16)
     attended[...] = summed
     start = pl.multiple_of(lax.axis_index("mp") * BLOCK, BLOCK)
@@ -378,39 +385,41 @@
     v, s, h = "vmem", "smem", "hbm"
     dma = pltpu.SemaphoreType.DMA
     columns = [[16 * z + place for z in range(FAR_GROUP)] for place in range(16)]
-    across = [
-        (16 * z + (place ^ (2 * z)), 16 * z + place) for z in range(FAR_GROUP) for place in range(16)
+    planes = [
+        [16 * z + 2 * y + core for y in range(FAR_GROUP)] for z in range(FAR_GROUP) for core in range(2)
     ]
+
+    def to_all(value, groups):
+        return lax.all_to_all(
+            value, "seq", split_axis=0, concat_axis=0, tiled=True, axis_index_groups=groups
+        )
+
     w_query, w_key, w_value = w_query.T, w_key.T, w_value.T
-    query, own, mid, far = call(
+    query, own, mid, far_query, far_keyval = call(
         project_kernel,
         3,
         [
             ((ROWS, 256), bf16), ((ROWS, 384), bf16), ((CLASS_ROWS, 384), bf16),
-            ((FAR_GROUP, FAR_ROWS, 640), bf16),
+            ((FAR_GROUP, FAR_ROWS, 256), bf16), ((FAR_GROUP, FAR_ROWS, 384), bf16),
         ],
         [(tokens, h), (attn_gain, v), (w_query, h), (w_key, h), (w_value, h)],
         [pltpu.VMEM((ROWS, WIDTH), bf16), pltpu.VMEM((3, 192, WIDTH), bf16), dma((7,))],
         limit=WHOLE_VMEM,
     )
-    far_rows = lax.all_to_all(
-        far, "seq", split_axis=0, concat_axis=0, tiled=True, axis_index_groups=columns
-    )
-    w_up, w_down, _ = lax.optimization_barrier((w_up, w_down, far))
+    far_here = to_all(far_keyval, planes)
+    far_query, _ = lax.optimization_barrier((far_query, far_here))
+    far_rows = to_all(far_query, columns)
+    w_up, w_down, _ = lax.optimization_barrier((w_up, w_down, far_keyval))
     (packed,) = call(weights_kernel, 2, [((2 * HALF, WIDTH), bf16)], [(w_up, v), (w_down, v)])
     mine = lax.all_gather(packed, "mp", axis=0)
     side = swap(own, 2)
 
-    far_keys = far_rows[:, :, 256:].reshape(128, 384)
-    far_here = lax.ppermute(far_keys, "seq", across)
-    query, _ = lax.optimization_barrier((query, far_keys))
     mid_a, mid_b = swap(mid, 4), swap(mid, 6)
     state = [((ROWS, LANES), f32)] * LOCAL_HEADS
+    query, _, _ = lax.optimization_barrier((query, far_here, far_rows))
     near = call(near_kernel, 3, state, [(slide_tiles, s), (query, v), (own, v), (side, v)])
-    side, mid_a, mid_b, far_here, *near = lax.optimization_barrier(
-        (side, mid_a, mid_b, far_here, *near)
-    )
     far_other = swap(far_here, 1)
+    far_other, *near = lax.optimization_barrier((far_other, *near))
     swapped = swap(jnp.concatenate([own, side, mid_a, mid_b], 0), 1)
     (parts,) = call(
         far_kernel,
@@ -418,26 +427,26 @@
         [((FAR_GROUP, FAR_ROWS, 384), f32)],
         [(slide_tiles, s), (far_rows, v), (far_here, v), (far_other, v)],
     )
-    parts = lax.all_to_all(
-        parts, "seq", split_axis=0, concat_axis=0, tiled=True, axis_index_groups=columns
-    )
-    terms, far_attended = call(
+    parts = to_all(parts, columns)
+    *terms, far_attended = call(
         rest_kernel,
         7,
-        [((4, BLOCK, WIDTH), bf16), ((FAR_ROWS, 192), bf16)],
+        [((BLOCK, WIDTH), bf16)] * 4 + [((FAR_ROWS, 192), bf16)],
         [
             (slide_tiles, s), (query, v), (own, v), (side, v), (mid_a, v), (mid_b, v), (swapped, v),
             (parts, v), (w_out, v), *[(held, v) for held in near],
         ],
         [pltpu.VMEM(*shape) for shape in state],
     )
-    terms = lax.all_to_all(terms, "mp", split_axis=0, concat_axis=0, tiled=True)
-    terms, mine = lax.optimization_barrier((terms, mine))
+    for step in (2, 1, 3):
+        terms[step] = lax.ppermute(terms[step], "mp", [(i, (i + step) % 4) for i in range(4)])
+    terms[2], mine = lax.optimization_barrier((terms[2], mine))
+    terms = lax.optimization_barrier(terms)
     attended, normed = call(
         norm_kernel,
         1,
         [((BLOCK, WIDTH), bf16), ((BLOCK, WIDTH), bf16)],
-        [(tokens, v), (terms, v), (ffn_gain, v)],
+        [(tokens, v), (ffn_gain, v), *[(term, v) for term in terms]],
     )
     kept, sent = call(
         ffn_kernel,

time: 114 us -> 117 us (1.026)
  starting transfers between devices: 33.5 us -> 57.2 us
  blocking collectives: 35 us -> 13.3 us
    all_to_all x2 -> x1, blocking collectives: 35 us -> 13.3 us  [to_all(): lax.all_to_all(value, 'seq', split_axis=0, concat_axis=0, tiled=True, axi...]
    ppermute x1 -> x3, starting transfers between devices: 0.67 us -> 11.1 us  [local(): lax.ppermute(terms[step], 'mp', [(i, (i + step) % 4) for i in range(4)])]
    ppermute x7, starting transfers between devices: 22.7 us -> 31.8 us  [swap(): lax.ppermute(value, 'seq', [(i, i ^ step) for i in range(lax.axis_size('s...]
    all_to_all x1 -> x2, starting transfers between devices: 10 us -> 14.3 us  [to_all(): lax.all_to_all(value, 'seq', split_axis=0, concat_axis=0, tiled=True, axi...]
    ppermute x1 -> x3, waiting for transfers between devices: 0.01 us -> 2.84 us  [local(): lax.ppermute(terms[step], 'mp', [(i, (i + step) % 4) for i in range(4)])]
    ppermute x7, waiting for transfers between devices: 4.44 us -> 2.46 us  [swap(): lax.ppermute(value, 'seq', [(i, i ^ step) for i in range(lax.axis_size('s...]
    unnamed x20 -> x22, local copies, waits for them, and re-layouts: 2.38 us -> 2.38 us
  transfers between devices with their start and end apart: 10 -> 13, of which waited for: 5 -> 5; matrix products, arithmetic and copies ran while one was open for 0% -> 1% of each run, Pallas kernels for 9% -> 9%
where the time goes in v9:
time: 117 us; the launch traced here: 116 us
  starting transfers between devices  57.2 us (49%)
  Pallas kernels  19.9 us (17%)
  between operations  14.3 us (12%)
  blocking collectives  13.3 us (11%)
  waiting for transfers between devices  7.44 us (6%)
  local copies, waits for them, and re-layouts  2.38 us (2%)
  other arithmetic  1.8 us (2%)
    ppermute x7, starting transfers between devices, swap(): lax.ppermute(value, 'seq', [(i, i ^ step) for i in range(lax.axis_size('s...  31.8 us
    pallas_call x7, Pallas kernels, call(): pl.pallas_call(kernel, out_shape=[jax.ShapeDtypeStruct(*out) for out in o...  19.9 us
    all_to_all x2, starting transfers between devices, to_all(): lax.all_to_all(value, 'seq', split_axis=0, concat_axis=0, tiled=True, axi...  14.3 us
    all_to_all x1, blocking collectives, to_all(): lax.all_to_all(value, 'seq', split_axis=0, concat_axis=0, tiled=True, axi...  13.3 us
    ppermute x3, starting transfers between devices, local(): lax.ppermute(terms[step], 'mp', [(i, (i + step) % 4) for i in range(4)])  11.1 us
    ppermute x3, waiting for transfers between devices, local(): lax.ppermute(terms[step], 'mp', [(i, (i + step) % 4) for i in range(4)])  2.84 us
    ppermute x7, waiting for transfers between devices, swap(): lax.ppermute(value, 'seq', [(i, i ^ step) for i in range(lax.axis_size('s...  2.46 us
    unnamed x22, local copies, waits for them, and re-layouts  2.38 us
  transfers between devices with their start and end apart: 13, of which 5 were waited for; matrix products, arithmetic and copies ran while one was open for 1% of the time, Pallas kernels for 9%

profile of v9, /device:TPU:1, one launch (start us, length us, event | category | flops | bytes accessed | tf_op | source)
XLA Modules:
  0.0 116.4 jit_solution(13725417752991538871)
XLA Ops:
  7.2 0.0 all-gather.3.cloned.1.call-start
  7.2 0.0 copy-start.2
  7.2 0.0 copy-start.3
  7.2 5.1 %shard_map.121 = (bf16[512,256]{1,0:T(8,128)(2,1)}, bf16[512,384]{1,0:T(8,128)(2,1)}, bf16[128,384]{1,0:T(8,128)(2,1)}, bf16[8,16,256]{2,1,0:T(8,128)(2,1)}, bf16[8,16,384]{2,1,0:T(8,128)(2,1)}) custom-call(bf16[512,768]{1,0:T(8,128)(2,1)} %tokens.3, bf16[768]{0:T(1024)(128)(2,1)} %gain.2, bf16[192,768]{1,0:T(8,128)(2,1)} %bitcast.5, ...), custom_call_target="tpu_custom_call" | custom-call | flops 3300000000 | bytes 3000000 | tf_op jit(solution)/shard_map/pallas_call | solution.py:366
  12.4 0.0 copy-done.2
  12.4 0.0 copy-done.3
  12.4 0.0 copy-start
  12.4 0.0 copy-start.10
  12.4 1.1 shard_map.125
  13.6 0.0 all-gather.3.cloned.1.call-update
  13.6 4.2 %collective-permute-start = (bf16[512,384]{1,0:T(8,128)(2,1)S(1)}, bf16[512,384]{1,0:T(8,128)(2,1)S(1)}, u32[]{:S(2)}, u32[]{:S(2)}) collective-permute-start(bf16[512,384]{1,0:T(8,128)(2,1)S(1)} %copy-done), channel_id=1, source_target_pairs={{0,8},{4,12},{8,0},{12,4},{16,24},{20,28},{24,16},{28,20},{32,40},... | collective-permute-start | bytes 1179656 | tf_op jit(solution)/shard_map/ppermute | solution.py:380
  17.8 4.1 %collective-permute-start.2 = (bf16[128,384]{1,0:T(8,128)(2,1)S(1)}, bf16[128,384]{1,0:T(8,128)(2,1)S(1)}, u32[]{:S(2)}, u32[]{:S(2)}) collective-permute-start(bf16[128,384]{1,0:T(8,128)(2,1)S(1)} %copy-done.10), channel_id=1, source_target_pairs={{0,24},{4,28},{8,16},{12,20},{16,8},{20,12},{24,0},{28,4},{32,56},... | collective-permute-start | bytes 294920 | tf_op jit(solution)/shard_map/ppermute | solution.py:380
  21.9 2.0 %collective-permute-start.1 = (bf16[128,384]{1,0:T(8,128)(2,1)S(1)}, bf16[128,384]{1,0:T(8,128)(2,1)S(1)}, u32[]{:S(2)}, u32[]{:S(2)}) collective-permute-start(bf16[128,384]{1,0:T(8,128)(2,1)S(1)} %copy-done.10), channel_id=1, source_target_pairs={{0,16},{4,20},{8,24},{12,28},{16,0},{20,4},{24,8},{28,12},{32,48},... | collective-permute-start | bytes 294920 | tf_op jit(solution)/shard_map/ppermute | solution.py:380
  23.9 6.0 %all-to-all-start = ((bf16[8,16,384]{2,1,0:T(8,128)(2,1)}), bf16[8,16,384]{2,1,0:T(8,128)(2,1)S(1)}, u32[]{:S(2)}, u32[]{:S(2)}) async-start(bf16[8,16,384]{2,1,0:T(8,128)(2,1)} %get-tuple-element.35), calls=%async_computation | async-start | bytes 196608 | tf_op jit(solution)/shard_map/all_to_all | solution.py:393
  29.9 0.4 collective-permute-done.2.mid_b
  30.3 0.0 collective-permute-done.1.mid_a
  30.3 0.0 collective-permute-done.side
  30.3 1.1 pad_maximum_fusion
  31.3 7.9 %collective-permute-start.3 = (bf16[1280,384]{1,0:T(8,128)(2,1)}, bf16[1280,384]{1,0:T(8,128)(2,1)S(1)}, u32[]{:S(2)}, u32[]{:S(2)}) collective-permute-start(bf16[1280,384]{1,0:T(8,128)(2,1)} %pad_maximum_fusion), channel_id=1, source_target_pairs={{0,4},{4,0},{8,12},{12,8},{16,20},{20,16},{24,28},{28,24},{32,36},... | collective-permute-start | bytes 2949128 | tf_op jit(solution)/shard_map/ppermute | solution.py:380
  39.2 0.0 all-to-all-done.here
  39.2 8.3 %all-to-all-start.1 = ((bf16[8,16,256]{2,1,0:T(8,128)(2,1)}), bf16[8,16,256]{2,1,0:T(8,128)(2,1)S(1)}, u32[]{:S(2)}, u32[]{:S(2)}) async-start(bf16[8,16,256]{2,1,0:T(8,128)(2,1)} %get-tuple-element.37), calls=%async_computation.1 | async-start | bytes 131072 | tf_op jit(solution)/shard_map/all_to_all | solution.py:393
  47.5 5.1 %collective-permute-start.4 = (bf16[8,16,384]{2,1,0:T(8,128)(2,1)S(1)}, bf16[8,16,384]{2,1,0:T(8,128)(2,1)S(1)}, u32[]{:S(2)}, u32[]{:S(2)}) collective-permute-start(bf16[8,16,384]{2,1,0:T(8,128)(2,1)S(1)} %all-to-all-done.here), channel_id=1, source_target_pairs={{0,4},{4,0},{8,12},{12,8},{16,20},{20,16},{24,28},{28,24},{32,36},... | collective-permute-start | bytes 294920 | tf_op jit(solution)/shard_map/ppermute | solution.py:380
  52.7 2.1 %all-to-all-done.1.rows = bf16[8,16,256]{2,1,0:T(8,128)(2,1)S(1)} async-done(((bf16[8,16,256]{2,1,0:T(8,128)(2,1)}), bf16[8,16,256]{2,1,0:T(8,128)(2,1)S(1)}, u32[]{:S(2)}, u32[]{:S(2)}) %all-to-all-start.1) | async-done | bytes 65568 | tf_op jit(solution)/shard_map/all_to_all | solution.py:393
  54.8 0.0 copy-done.8
  54.8 3.2 %shard_map.122 = (f32[512,128]{1,0:T(8,128)S(1)}, f32[512,128]{1,0:T(8,128)S(1)}, f32[512,128]{1,0:T(8,128)S(1)}) custom-call(s32[4]{0:T(128)S(1)} %copy-done.7, bf16[512,256]{1,0:T(8,128)(2,1)S(1)} %copy-done.8, bf16[512,384]{1,0:T(8,128)(2,1)S(1)} %copy-done, bf16[512,384]{1,0:T(8,128)(2,1)S(1)} %collective-permute-done.side), custom_call_target="tpu_custom_call" | custom-call | flops 3300000000 | bytes 3000000 | tf_op jit(solution)/shard_map/pallas_call | solution.py:366
  57.9 0.0 collective-permute-done.4.other
  58.0 0.0 copy-start.5
  58.0 0.0 copy-start.9
  58.0 1.2 %shard_map.123 = f32[8,16,384]{2,1,0:T(8,128)S(1)} custom-call(s32[4]{0:T(128)S(1)} %copy-done.7, bf16[8,16,256]{2,1,0:T(8,128)(2,1)S(1)} %all-to-all-done.1.rows, bf16[8,16,384]{2,1,0:T(8,128)(2,1)S(1)} %all-to-all-done.here, bf16[8,16,384]{2,1,0:T(8,128)(2,1)S(1)} %collective-permute-done.4.other), custom_call_target="tpu_custom_call" | custom-call | flops 2200000000 | bytes 2000000 | tf_op jit(solution)/shard_map/pallas_call | solution.py:366
  59.2 13.3 %all_to_all.15.parts = f32[8,16,384]{2,1,0:T(8,128)S(1)} all-to-all(f32[8,16,384]{2,1,0:T(8,128)S(1)} %shard_map.123), channel_id=1, replica_groups={{0,64,128,192,256,320,384,448},{4,68,132,196,260,324,388,452},{8,72,136..., dimensions={0} | all-to-all | bytes 393216 | tf_op jit(solution)/shard_map/all_to_all | solution.py:393
  72.5 0.0 collective-permute-done.3.swapped
  72.5 0.0 copy-done.5
  72.5 6.2 %shard_map.124 = (bf16[128,768]{1,0:T(8,128)(2,1)S(1)}, bf16[128,768]{1,0:T(8,128)(2,1)S(1)}, bf16[128,768]{1,0:T(8,128)(2,1)S(1)}, bf16[128,768]{1,0:T(8,128)(2,1)S(1)}, bf16[16,192]{1,0:T(8,128)(2,1)}) custom-call(s32[4]{0:T(128)S(1)} %copy-done.7, bf16[512,256]{1,0:T(8,128)(2,1)S(1)} %copy-done.9, bf16[512,384]{1,0:T(8,128)(2,1)S(1)} %copy-done, ...), custom_call_target="tpu_custom_call" | custom-call | flops 7699999744 | bytes 7000000 | tf_op jit(solution)/shard_map/pallas_call | solution.py:366
  78.7 4.6 %collective-permute-start.6 = (bf16[128,768]{1,0:T(8,128)(2,1)S(1)}, bf16[128,768]{1,0:T(8,128)(2,1)S(1)}, u32[]{:S(2)}, u32[]{:S(2)}) collective-permute-start(bf16[128,768]{1,0:T(8,128)(2,1)S(1)} %get-tuple-element.50), channel_id=1, source_target_pairs={{0,2},{1,3},{2,0},{3,1},{4,6},{5,7},{6,4},{7,5},{8,10},{9,11},{10,... | collective-permute-start | bytes 589832 | tf_op jit(solution)/shard_map/ppermute | solution.py:442
  83.3 2.2 %collective-permute-start.5 = (bf16[128,768]{1,0:T(8,128)(2,1)S(1)}, bf16[128,768]{1,0:T(8,128)(2,1)S(1)}, u32[]{:S(2)}, u32[]{:S(2)}) collective-permute-start(bf16[128,768]{1,0:T(8,128)(2,1)S(1)} %get-tuple-element.49), channel_id=1, source_target_pairs={{0,1},{1,2},{2,3},{3,0},{4,5},{5,6},{6,7},{7,4},{8,9},{9,10},{10,1... | collective-permute-start | bytes 589832 | tf_op jit(solution)/shard_map/ppermute | solution.py:442
  85.6 4.2 %collective-permute-start.7 = (bf16[128,768]{1,0:T(8,128)(2,1)S(1)}, bf16[128,768]{1,0:T(8,128)(2,1)S(1)}, u32[]{:S(2)}, u32[]{:S(2)}) collective-permute-start(bf16[128,768]{1,0:T(8,128)(2,1)S(1)} %get-tuple-element.54), channel_id=1, source_target_pairs={{0,3},{1,0},{2,1},{3,2},{4,7},{5,4},{6,5},{7,6},{8,11},{9,8},{10,9... | collective-permute-start | bytes 589832 | tf_op jit(solution)/shard_map/ppermute | solution.py:442
  89.9 0.0 collective-permute-done.6.refs_2_
  89.9 0.0 all-gather.3.cloned.1.call-done
  89.9 2.8 %collective-permute-done.5.refs_1_ = bf16[128,768]{1,0:T(8,128)(2,1)S(1)} collective-permute-done((bf16[128,768]{1,0:T(8,128)(2,1)S(1)}, bf16[128,768]{1,0:T(8,128)(2,1)S(1)}, u32[]{:S(2)}, u32[]{:S(2)}) %collective-permute-start.5) | collective-permute-done | bytes 196640 | tf_op jit(solution)/shard_map/ppermute | solution.py:442
  92.7 0.0 collective-permute-done.7.refs_3_
  92.7 0.8 shard_map.126
  93.6 6.2 %collective-permute-start.8 = (bf16[128,768]{1,0:T(8,128)(2,1)S(1)}, bf16[128,768]{1,0:T(8,128)(2,1)S(1)}, u32[]{:S(2)}, u32[]{:S(2)}) collective-permute-start(bf16[128,768]{1,0:T(8,128)(2,1)S(1)} %get-tuple-element.61.own), channel_id=1, source_target_pairs={{0,4},{4,0},{8,12},{12,8},{16,20},{20,16},{24,28},{28,24},{32,36},... | collective-permute-start | bytes 589832 | tf_op jit(solution)/shard_map/ppermute | solution.py:380
  99.8 1.0 collective-permute-done.8.other
  100.9 2.3 %copy-done.1 = bf16[3072,768]{1,0:T(8,128)(2,1)S(1)} copy-done((bf16[3072,768]{1,0:T(8,128)(2,1)S(1)}, bf16[3072,768]{1,0:T(8,128)(2,1)}, u32[]{:S(2)}) %copy-start.1) | copy-done | bytes 4718616
  103.2 2.3 %shard_map.127 = (f32[128,768]{1,0:T(8,128)S(1)}, bf16[128,768]{1,0:T(8,128)(2,1)S(1)}) custom-call(bf16[128,768]{1,0:T(8,128)(2,1)S(1)} %get-tuple-element.61.own, bf16[128,768]{1,0:T(8,128)(2,1)S(1)} %collective-permute-done.8.other, bf16[4,768,768]{2,1,0:T(8,128)(2,1)S(1)} %bitcast.4), custom_call_target="tpu_custom_call" | custom-call | flops 4400000000 | bytes 4000000 | tf_op jit(solution)/shard_map/pallas_call | solution.py:366
  105.5 2.3 %collective-permute-start.9 = (bf16[128,768]{1,0:T(8,128)(2,1)S(1)}, bf16[128,768]{1,0:T(8,128)(2,1)S(1)}, u32[]{:S(2)}, u32[]{:S(2)}) collective-permute-start(bf16[128,768]{1,0:T(8,128)(2,1)S(1)} %get-tuple-element.64), channel_id=1, source_target_pairs={{0,4},{4,0},{8,12},{12,8},{16,20},{20,16},{24,28},{28,24},{32,36},... | collective-permute-start | bytes 589832 | tf_op jit(solution)/shard_map/ppermute | solution.py:380
  107.8 1.0 collective-permute-done.9
  108.8 0.7 add_convert_fusion
  (11 shorter events, 0.0 us)
Async XLA Ops:
  7.2 82.7 %all-gather.3.cloned.1.call-start = ((), (), s32[]{:S(2)}) async-start(), calls=%async_computation.3 | async-start | bytes 5898240 | tf_op jit(solution)/shard_map/all_gather | solution.py:414
  7.2 5.2 %copy-start.2 = (bf16[768,768]{1,0:T(8,128)(2,1)S(1)}, bf16[768,768]{1,0:T(8,128)(2,1)}, u32[]{:S(2)}) copy-start(bf16[768,768]{1,0:T(8,128)(2,1)} %w_up) | copy-start | bytes 3538948
  7.2 5.2 %copy-start.3 = (bf16[768,768]{1,0:T(8,128)(2,1)S(1)}, bf16[768,768]{1,0:T(8,128)(2,1)}, u32[]{:S(2)}) copy-start(bf16[768,768]{1,0:T(8,128)(2,1)} %w_down) | copy-start | bytes 3538948
  12.4 1.2 %copy-start = (bf16[512,384]{1,0:T(8,128)(2,1)S(1)}, bf16[512,384]{1,0:T(8,128)(2,1)}, u32[]{:S(2)}) copy-start(bf16[512,384]{1,0:T(8,128)(2,1)} %get-tuple-element.39.own) | copy-start | bytes 1179652
  12.4 5.4 %copy-start.10 = (bf16[128,384]{1,0:T(8,128)(2,1)S(1)}, bf16[128,384]{1,0:T(8,128)(2,1)}, u32[]{:S(2)}) copy-start(bf16[128,384]{1,0:T(8,128)(2,1)} %get-tuple-element.40) | copy-start | bytes 294916
  13.6 41.2 %copy-start.7 = (s32[4]{0:T(128)S(1)}, s32[4]{0:T(128)}, u32[]{:S(2)}) copy-start(s32[4]{0:T(128)} %tiles.5) | copy-start | bytes 52
  13.6 41.2 %copy-start.8 = (bf16[512,256]{1,0:T(8,128)(2,1)S(1)}, bf16[512,256]{1,0:T(8,128)(2,1)}, u32[]{:S(2)}) copy-start(bf16[512,256]{1,0:T(8,128)(2,1)} %get-tuple-element.38.query) | copy-start | bytes 786436
  13.6 16.7 %collective-permute-start = (bf16[512,384]{1,0:T(8,128)(2,1)S(1)}, bf16[512,384]{1,0:T(8,128)(2,1)S(1)}, u32[]{:S(2)}, u32[]{:S(2)}) collective-permute-start(bf16[512,384]{1,0:T(8,128)(2,1)S(1)} %copy-done), channel_id=1, source_target_pairs={{0,8},{4,12},{8,0},{12,4},{16,24},{20,28},{24,16},{28,20},{32,40},... | collective-permute-start | bytes 1179656 | tf_op jit(solution)/shard_map/ppermute | solution.py:380
  17.8 12.5 %collective-permute-start.2 = (bf16[128,384]{1,0:T(8,128)(2,1)S(1)}, bf16[128,384]{1,0:T(8,128)(2,1)S(1)}, u32[]{:S(2)}, u32[]{:S(2)}) collective-permute-start(bf16[128,384]{1,0:T(8,128)(2,1)S(1)} %copy-done.10), channel_id=1, source_target_pairs={{0,24},{4,28},{8,16},{12,20},{16,8},{20,12},{24,0},{28,4},{32,56},... | collective-permute-start | bytes 294920 | tf_op jit(solution)/shard_map/ppermute | solution.py:380
  21.9 8.4 %collective-permute-start.1 = (bf16[128,384]{1,0:T(8,128)(2,1)S(1)}, bf16[128,384]{1,0:T(8,128)(2,1)S(1)}, u32[]{:S(2)}, u32[]{:S(2)}) collective-permute-start(bf16[128,384]{1,0:T(8,128)(2,1)S(1)} %copy-done.10), channel_id=1, source_target_pairs={{0,16},{4,20},{8,24},{12,28},{16,0},{20,4},{24,8},{28,12},{32,48},... | collective-permute-start | bytes 294920 | tf_op jit(solution)/shard_map/ppermute | solution.py:380
  23.9 15.3 %all-to-all-start = ((bf16[8,16,384]{2,1,0:T(8,128)(2,1)}), bf16[8,16,384]{2,1,0:T(8,128)(2,1)S(1)}, u32[]{:S(2)}, u32[]{:S(2)}) async-start(bf16[8,16,384]{2,1,0:T(8,128)(2,1)} %get-tuple-element.35), calls=%async_computation | async-start | bytes 196608 | tf_op jit(solution)/shard_map/all_to_all | solution.py:393
  31.3 41.2 %collective-permute-start.3 = (bf16[1280,384]{1,0:T(8,128)(2,1)}, bf16[1280,384]{1,0:T(8,128)(2,1)S(1)}, u32[]{:S(2)}, u32[]{:S(2)}) collective-permute-start(bf16[1280,384]{1,0:T(8,128)(2,1)} %pad_maximum_fusion), channel_id=1, source_target_pairs={{0,4},{4,0},{8,12},{12,8},{16,20},{20,16},{24,28},{28,24},{32,36},... | collective-permute-start | bytes 2949128 | tf_op jit(solution)/shard_map/ppermute | solution.py:380
  39.2 15.5 %all-to-all-start.1 = ((bf16[8,16,256]{2,1,0:T(8,128)(2,1)}), bf16[8,16,256]{2,1,0:T(8,128)(2,1)S(1)}, u32[]{:S(2)}, u32[]{:S(2)}) async-start(bf16[8,16,256]{2,1,0:T(8,128)(2,1)} %get-tuple-element.37), calls=%async_computation.1 | async-start | bytes 131072 | tf_op jit(solution)/shard_map/all_to_all | solution.py:393
  47.5 10.4 %collective-permute-start.4 = (bf16[8,16,384]{2,1,0:T(8,128)(2,1)S(1)}, bf16[8,16,384]{2,1,0:T(8,128)(2,1)S(1)}, u32[]{:S(2)}, u32[]{:S(2)}) collective-permute-start(bf16[8,16,384]{2,1,0:T(8,128)(2,1)S(1)} %all-to-all-done.here), channel_id=1, source_target_pairs={{0,4},{4,0},{8,12},{12,8},{16,20},{20,16},{24,28},{28,24},{32,36},... | collective-permute-start | bytes 294920 | tf_op jit(solution)/shard_map/ppermute | solution.py:380
  58.0 14.6 %copy-start.5 = (bf16[192,768]{1,0:T(8,128)(2,1)S(1)}, bf16[192,768]{1,0:T(8,128)(2,1)}, u32[]{:S(2)}) copy-start(bf16[192,768]{1,0:T(8,128)(2,1)} %w_out.1) | copy-start | bytes 884740
  58.0 14.6 %copy-start.9 = (bf16[512,256]{1,0:T(8,128)(2,1)S(1)}, bf16[512,256]{1,0:T(8,128)(2,1)}, u32[]{:S(2)}) copy-start(bf16[512,256]{1,0:T(8,128)(2,1)} %get-tuple-element.38.query) | copy-start | bytes 786436
  72.5 20.2 %copy-start.4 = (bf16[512,768]{1,0:T(8,128)(2,1)S(1)}, bf16[512,768]{1,0:T(8,128)(2,1)}, u32[]{:S(2)}) copy-start(bf16[512,768]{1,0:T(8,128)(2,1)} %tokens.3) | copy-start | bytes 2359300
  72.5 20.2 %copy-start.6 = (bf16[768]{0:T(1024)(128)(2,1)S(1)}, bf16[768]{0:T(1024)(128)(2,1)}, u32[]{:S(2)}) copy-start(bf16[768]{0:T(1024)(128)(2,1)} %gain.3) | copy-start | bytes 4612
  78.7 11.1 %collective-permute-start.6 = (bf16[128,768]{1,0:T(8,128)(2,1)S(1)}, bf16[128,768]{1,0:T(8,128)(2,1)S(1)}, u32[]{:S(2)}, u32[]{:S(2)}) collective-permute-start(bf16[128,768]{1,0:T(8,128)(2,1)S(1)} %get-tuple-element.50), channel_id=1, source_target_pairs={{0,2},{1,3},{2,0},{3,1},{4,6},{5,7},{6,4},{7,5},{8,10},{9,11},{10,... | collective-permute-start | bytes 589832 | tf_op jit(solution)/shard_map/ppermute | solution.py:442
  83.3 9.4 %collective-permute-start.5 = (bf16[128,768]{1,0:T(8,128)(2,1)S(1)}, bf16[128,768]{1,0:T(8,128)(2,1)S(1)}, u32[]{:S(2)}, u32[]{:S(2)}) collective-permute-start(bf16[128,768]{1,0:T(8,128)(2,1)S(1)} %get-tuple-element.49), channel_id=1, source_target_pairs={{0,1},{1,2},{2,3},{3,0},{4,5},{5,6},{6,7},{7,4},{8,9},{9,10},{10,1... | collective-permute-start | bytes 589832 | tf_op jit(solution)/shard_map/ppermute | solution.py:442
  85.6 7.1 %collective-permute-start.7 = (bf16[128,768]{1,0:T(8,128)(2,1)S(1)}, bf16[128,768]{1,0:T(8,128)(2,1)S(1)}, u32[]{:S(2)}, u32[]{:S(2)}) collective-permute-start(bf16[128,768]{1,0:T(8,128)(2,1)S(1)} %get-tuple-element.54), channel_id=1, source_target_pairs={{0,3},{1,0},{2,1},{3,2},{4,7},{5,4},{6,5},{7,6},{8,11},{9,8},{10,9... | collective-permute-start | bytes 589832 | tf_op jit(solution)/shard_map/ppermute | solution.py:442
  93.6 7.3 %collective-permute-start.8 = (bf16[128,768]{1,0:T(8,128)(2,1)S(1)}, bf16[128,768]{1,0:T(8,128)(2,1)S(1)}, u32[]{:S(2)}, u32[]{:S(2)}) collective-permute-start(bf16[128,768]{1,0:T(8,128)(2,1)S(1)} %get-tuple-element.61.own), channel_id=1, source_target_pairs={{0,4},{4,0},{8,12},{12,8},{16,20},{20,16},{24,28},{28,24},{32,36},... | collective-permute-start | bytes 589832 | tf_op jit(solution)/shard_map/ppermute | solution.py:380
  100.9 2.3 %copy-start.1 = (bf16[3072,768]{1,0:T(8,128)(2,1)S(1)}, bf16[3072,768]{1,0:T(8,128)(2,1)}, u32[]{:S(2)}) copy-start(bf16[3072,768]{1,0:T(8,128)(2,1)} %all-gather.3.cloned.1.call-done) | copy-start | bytes 14155780
  105.5 3.3 %collective-permute-start.9 = (bf16[128,768]{1,0:T(8,128)(2,1)S(1)}, bf16[128,768]{1,0:T(8,128)(2,1)S(1)}, u32[]{:S(2)}, u32[]{:S(2)}) collective-permute-start(bf16[128,768]{1,0:T(8,128)(2,1)S(1)} %get-tuple-element.64), channel_id=1, source_target_pairs={{0,4},{4,0},{8,12},{12,8},{16,20},{20,16},{24,28},{28,24},{32,36},... | collective-permute-start | bytes 589832 | tf_op jit(solution)/shard_map/ppermute | solution.py:380
Sparse Core Ops, SparseCore 0:
  13.7 63.4 all-gather.2

commit v10 on v9

--- a/solution.py
+++ b/solution.py
@@ -416,7 +416,9 @@
 
     mid_a, mid_b = swap(mid, 4), swap(mid, 6)
     state = [((ROWS, LANES), f32)] * LOCAL_HEADS
-    query, _, _ = lax.optimization_barrier((query, far_here, far_rows))
+    query, side, mid_a, mid_b, _, _ = lax.optimization_barrier(
+        (query, side, mid_a, mid_b, far_here, far_rows)
+    )
     near = call(near_kernel, 3, state, [(slide_tiles, s), (query, v), (own, v), (side, v)])
     far_other = swap(far_here, 1)
     far_other, *near = lax.optimization_barrier((far_other, *near))

time: 117 us -> 125 us (1.068)
  blocking collectives: 13.3 us -> 29.9 us
  starting transfers between devices: 57.2 us -> 44.5 us
  waiting for transfers between devices: 7.44 us -> 12.3 us
    all_to_all x1 -> x2, blocking collectives: 13.3 us -> 29.9 us  [to_all(): lax.all_to_all(value, 'seq', split_axis=0, concat_axis=0, tiled=True, axi...]
    ppermute x7, starting transfers between devices: 31.8 us -> 23.1 us  [swap(): lax.ppermute(value, 'seq', [(i, i ^ step) for i in range(lax.axis_size('s...]
    ppermute x7, waiting for transfers between devices: 2.46 us -> 9.75 us  [swap(): lax.ppermute(value, 'seq', [(i, i ^ step) for i in range(lax.axis_size('s...]
    all_to_all x2 -> x1, starting transfers between devices: 14.3 us -> 10.1 us  [to_all(): lax.all_to_all(value, 'seq', split_axis=0, concat_axis=0, tiled=True, axi...]
    all_to_all x2 -> x1, waiting for transfers between devices: 2.1 us -> 0.01 us  [to_all(): lax.all_to_all(value, 'seq', split_axis=0, concat_axis=0, tiled=True, axi...]
  transfers between devices with their start and end apart: 13 -> 12, of which waited for: 5 -> 6; matrix products, arithmetic and copies ran while one was open for 1% -> 0% of each run, Pallas kernels for 9% -> 9%
where the time goes in v10:
time: 125 us; the launch traced here: 124 us
  starting transfers between devices  44.5 us (36%)
  blocking collectives  29.9 us (24%)
  Pallas kernels  20 us (16%)
  between operations  14.3 us (11%)
  waiting for transfers between devices  12.3 us (10%)
  local copies, waits for them, and re-layouts  2.38 us (2%)
    all_to_all x2, blocking collectives, to_all(): lax.all_to_all(value, 'seq', split_axis=0, concat_axis=0, tiled=True, axi...  29.9 us
    ppermute x7, starting transfers between devices, swap(): lax.ppermute(value, 'seq', [(i, i ^ step) for i in range(lax.axis_size('s...  23.1 us
    pallas_call x7, Pallas kernels, call(): pl.pallas_call(kernel, out_shape=[jax.ShapeDtypeStruct(*out) for out in o...  20 us
    ppermute x3, starting transfers between devices, local(): lax.ppermute(terms[step], 'mp', [(i, (i + step) % 4) for i in range(4)])  11.1 us
    all_to_all x1, starting transfers between devices, to_all(): lax.all_to_all(value, 'seq', split_axis=0, concat_axis=0, tiled=True, axi...  10.1 us
    ppermute x7, waiting for transfers between devices, swap(): lax.ppermute(value, 'seq', [(i, i ^ step) for i in range(lax.axis_size('s...  9.75 us
    ppermute x3, waiting for transfers between devices, local(): lax.ppermute(terms[step], 'mp', [(i, (i + step) % 4) for i in range(4)])  2.56 us
  transfers between devices with their start and end apart: 12, of which 6 were waited for; matrix products, arithmetic and copies ran while one was open for 0% of the time, Pallas kernels for 9%

profile of v10, /device:TPU:1, one launch (start us, length us, event | category | flops | bytes accessed | tf_op | source)
XLA Modules:
  0.0 124.2 jit_solution(6356335065718858109)
XLA Ops:
  7.2 0.0 all-gather.3.cloned.1.call-start
  7.2 0.0 copy-start.2
  7.2 0.0 copy-start.3
  7.2 5.1 %shard_map.121 = (bf16[512,256]{1,0:T(8,128)(2,1)}, bf16[512,384]{1,0:T(8,128)(2,1)}, bf16[128,384]{1,0:T(8,128)(2,1)}, bf16[8,16,256]{2,1,0:T(8,128)(2,1)}, bf16[8,16,384]{2,1,0:T(8,128)(2,1)}) custom-call(bf16[512,768]{1,0:T(8,128)(2,1)} %tokens.3, bf16[768]{0:T(1024)(128)(2,1)} %gain.2, bf16[192,768]{1,0:T(8,128)(2,1)} %bitcast.5, ...), custom_call_target="tpu_custom_call" | custom-call | flops 3300000000 | bytes 3000000 | tf_op jit(solution)/shard_map/pallas_call | solution.py:366
  12.4 0.0 copy-done.2
  12.4 0.0 copy-done.3
  12.4 0.0 copy-start
  12.4 0.0 copy-start.9
  12.4 0.0 copy-start.10
  12.4 1.1 shard_map.125
  13.6 0.0 all-gather.3.cloned.1.call-update
  13.6 0.0 copy-done
  13.6 4.2 %collective-permute-start = (bf16[512,384]{1,0:T(8,128)(2,1)S(1)}, bf16[512,384]{1,0:T(8,128)(2,1)S(1)}, u32[]{:S(2)}, u32[]{:S(2)}) collective-permute-start(bf16[512,384]{1,0:T(8,128)(2,1)S(1)} %copy-done), channel_id=1, source_target_pairs={{0,8},{4,12},{8,0},{12,4},{16,24},{20,28},{24,16},{28,20},{32,40},... | collective-permute-start | bytes 1179656 | tf_op jit(solution)/shard_map/ppermute | solution.py:380
  17.8 0.0 copy-done.9
  17.8 14.3 %all_to_all.15.here = bf16[8,16,384]{2,1,0:T(8,128)(2,1)S(1)} all-to-all(bf16[8,16,384]{2,1,0:T(8,128)(2,1)S(1)} %copy-done.9), channel_id=1, replica_groups={{0,8,16,24,32,40,48,56},{4,12,20,28,36,44,52,60},{64,72,80,88,96,104,11..., dimensions={0} | all-to-all | bytes 196608 | tf_op jit(solution)/shard_map/all_to_all | solution.py:393
  32.0 10.1 %all-to-all-start.1 = ((bf16[8,16,256]{2,1,0:T(8,128)(2,1)}), bf16[8,16,256]{2,1,0:T(8,128)(2,1)S(1)}, u32[]{:S(2)}, u32[]{:S(2)}) async-start(bf16[8,16,256]{2,1,0:T(8,128)(2,1)} %get-tuple-element.42), calls=%async_computation.1 | async-start | bytes 131072 | tf_op jit(solution)/shard_map/all_to_all | solution.py:393
  42.2 3.8 %collective-permute-start.2 = (bf16[128,384]{1,0:T(8,128)(2,1)S(1)}, bf16[128,384]{1,0:T(8,128)(2,1)S(1)}, u32[]{:S(2)}, u32[]{:S(2)}) collective-permute-start(bf16[128,384]{1,0:T(8,128)(2,1)S(1)} %copy-done.10), channel_id=1, source_target_pairs={{0,24},{4,28},{8,16},{12,20},{16,8},{20,12},{24,0},{28,4},{32,56},... | collective-permute-start | bytes 294920 | tf_op jit(solution)/shard_map/ppermute | solution.py:380
  46.0 2.4 %collective-permute-start.1 = (bf16[128,384]{1,0:T(8,128)(2,1)S(1)}, bf16[128,384]{1,0:T(8,128)(2,1)S(1)}, u32[]{:S(2)}, u32[]{:S(2)}) collective-permute-start(bf16[128,384]{1,0:T(8,128)(2,1)S(1)} %copy-done.10), channel_id=1, source_target_pairs={{0,16},{4,20},{8,24},{12,28},{16,0},{20,4},{24,8},{28,12},{32,48},... | collective-permute-start | bytes 294920 | tf_op jit(solution)/shard_map/ppermute | solution.py:380
  48.3 1.3 %collective-permute-done.2.mid_b = bf16[128,384]{1,0:T(8,128)(2,1)S(1)} collective-permute-done((bf16[128,384]{1,0:T(8,128)(2,1)S(1)}, bf16[128,384]{1,0:T(8,128)(2,1)S(1)}, u32[]{:S(2)}, u32[]{:S(2)}) %collective-permute-start.2) | collective-permute-done | bytes 98336 | tf_op jit(solution)/shard_map/ppermute | solution.py:380
  49.6 6.4 %collective-permute-done.1.mid_a = bf16[128,384]{1,0:T(8,128)(2,1)S(1)} collective-permute-done((bf16[128,384]{1,0:T(8,128)(2,1)S(1)}, bf16[128,384]{1,0:T(8,128)(2,1)S(1)}, u32[]{:S(2)}, u32[]{:S(2)}) %collective-permute-start.1) | collective-permute-done | bytes 98336 | tf_op jit(solution)/shard_map/ppermute | solution.py:380
  56.0 0.0 all-to-all-done.1.rows
  56.0 0.0 collective-permute-done.side
  56.0 0.1 pad_maximum_fusion
  56.1 3.1 %collective-permute-start.3 = (bf16[1280,384]{1,0:T(8,128)(2,1)S(1)}, bf16[1280,384]{1,0:T(8,128)(2,1)S(1)}, u32[]{:S(2)}, u32[]{:S(2)}) collective-permute-start(bf16[1280,384]{1,0:T(8,128)(2,1)S(1)} %pad_maximum_fusion), channel_id=1, source_target_pairs={{0,4},{4,0},{8,12},{12,8},{16,20},{20,16},{24,28},{28,24},{32,36},... | collective-permute-start | bytes 2949128 | tf_op jit(solution)/shard_map/ppermute | solution.py:380
  59.2 1.9 %collective-permute-start.4 = (bf16[8,16,384]{2,1,0:T(8,128)(2,1)S(1)}, bf16[8,16,384]{2,1,0:T(8,128)(2,1)S(1)}, u32[]{:S(2)}, u32[]{:S(2)}) collective-permute-start(bf16[8,16,384]{2,1,0:T(8,128)(2,1)S(1)} %all_to_all.15.here), channel_id=1, source_target_pairs={{0,4},{4,0},{8,12},{12,8},{16,20},{20,16},{24,28},{28,24},{32,36},... | collective-permute-start | bytes 294920 | tf_op jit(solution)/shard_map/ppermute | solution.py:380
  61.2 3.2 %shard_map.122 = (f32[512,128]{1,0:T(8,128)S(1)}, f32[512,128]{1,0:T(8,128)S(1)}, f32[512,128]{1,0:T(8,128)S(1)}) custom-call(s32[4]{0:T(128)S(1)} %copy-done.7, bf16[512,256]{1,0:T(8,128)(2,1)S(1)} %copy-done.8, bf16[512,384]{1,0:T(8,128)(2,1)S(1)} %copy-done, bf16[512,384]{1,0:T(8,128)(2,1)S(1)} %collective-permute-done.side), custom_call_target="tpu_custom_call" | custom-call | flops 3300000000 | bytes 3000000 | tf_op jit(solution)/shard_map/pallas_call | solution.py:366
  64.4 0.0 collective-permute-done.4.other
  64.4 0.0 copy-start.5
  64.4 1.2 shard_map.123
  65.6 15.7 %all_to_all.16.parts = f32[8,16,384]{2,1,0:T(8,128)S(1)} all-to-all(f32[8,16,384]{2,1,0:T(8,128)S(1)} %shard_map.123), channel_id=1, replica_groups={{0,64,128,192,256,320,384,448},{4,68,132,196,260,324,388,452},{8,72,136..., dimensions={0} | all-to-all | bytes 393216 | tf_op jit(solution)/shard_map/all_to_all | solution.py:393
  81.3 0.0 collective-permute-done.3.swapped
  81.3 0.0 copy-done.5
  81.3 6.2 %shard_map.124 = (bf16[128,768]{1,0:T(8,128)(2,1)S(1)}, bf16[128,768]{1,0:T(8,128)(2,1)S(1)}, bf16[128,768]{1,0:T(8,128)(2,1)S(1)}, bf16[128,768]{1,0:T(8,128)(2,1)S(1)}, bf16[16,192]{1,0:T(8,128)(2,1)}) custom-call(s32[4]{0:T(128)S(1)} %copy-done.7, bf16[512,256]{1,0:T(8,128)(2,1)S(1)} %copy-done.8, bf16[512,384]{1,0:T(8,128)(2,1)S(1)} %copy-done, ...), custom_call_target="tpu_custom_call" | custom-call | flops 7699999744 | bytes 7000000 | tf_op jit(solution)/shard_map/pallas_call | solution.py:366
  87.5 4.6 %collective-permute-start.6 = (bf16[128,768]{1,0:T(8,128)(2,1)S(1)}, bf16[128,768]{1,0:T(8,128)(2,1)S(1)}, u32[]{:S(2)}, u32[]{:S(2)}) collective-permute-start(bf16[128,768]{1,0:T(8,128)(2,1)S(1)} %get-tuple-element.56), channel_id=1, source_target_pairs={{0,2},{1,3},{2,0},{3,1},{4,6},{5,7},{6,4},{7,5},{8,10},{9,11},{10,... | collective-permute-start | bytes 589832 | tf_op jit(solution)/shard_map/ppermute | solution.py:444
  92.2 2.3 %collective-permute-start.5 = (bf16[128,768]{1,0:T(8,128)(2,1)S(1)}, bf16[128,768]{1,0:T(8,128)(2,1)S(1)}, u32[]{:S(2)}, u32[]{:S(2)}) collective-permute-start(bf16[128,768]{1,0:T(8,128)(2,1)S(1)} %get-tuple-element.55), channel_id=1, source_target_pairs={{0,1},{1,2},{2,3},{3,0},{4,5},{5,6},{6,7},{7,4},{8,9},{9,10},{10,1... | collective-permute-start | bytes 589832 | tf_op jit(solution)/shard_map/ppermute | solution.py:444
  94.4 4.2 %collective-permute-start.7 = (bf16[128,768]{1,0:T(8,128)(2,1)S(1)}, bf16[128,768]{1,0:T(8,128)(2,1)S(1)}, u32[]{:S(2)}, u32[]{:S(2)}) collective-permute-start(bf16[128,768]{1,0:T(8,128)(2,1)S(1)} %get-tuple-element.60), channel_id=1, source_target_pairs={{0,3},{1,0},{2,1},{3,2},{4,7},{5,4},{6,5},{7,6},{8,11},{9,8},{10,9... | collective-permute-start | bytes 589832 | tf_op jit(solution)/shard_map/ppermute | solution.py:444
  98.7 0.0 collective-permute-done.6.refs_2_
  98.7 0.0 all-gather.3.cloned.1.call-done
  98.7 1.8 %collective-permute-done.5.refs_1_ = bf16[128,768]{1,0:T(8,128)(2,1)S(1)} collective-permute-done((bf16[128,768]{1,0:T(8,128)(2,1)S(1)}, bf16[128,768]{1,0:T(8,128)(2,1)S(1)}, u32[]{:S(2)}, u32[]{:S(2)}) %collective-permute-start.5) | collective-permute-done | bytes 196640 | tf_op jit(solution)/shard_map/ppermute | solution.py:444
  100.5 0.8 collective-permute-done.7.refs_3_
  101.3 0.8 shard_map.126
  102.1 5.5 %collective-permute-start.8 = (bf16[128,768]{1,0:T(8,128)(2,1)S(1)}, bf16[128,768]{1,0:T(8,128)(2,1)S(1)}, u32[]{:S(2)}, u32[]{:S(2)}) collective-permute-start(bf16[128,768]{1,0:T(8,128)(2,1)S(1)} %get-tuple-element.67.own), channel_id=1, source_target_pairs={{0,4},{4,0},{8,12},{12,8},{16,20},{20,16},{24,28},{28,24},{32,36},... | collective-permute-start | bytes 589832 | tf_op jit(solution)/shard_map/ppermute | solution.py:380
  107.7 1.0 collective-permute-done.8.other
  108.7 2.3 %copy-done.1 = bf16[3072,768]{1,0:T(8,128)(2,1)S(1)} copy-done((bf16[3072,768]{1,0:T(8,128)(2,1)S(1)}, bf16[3072,768]{1,0:T(8,128)(2,1)}, u32[]{:S(2)}) %copy-start.1) | copy-done | bytes 4718616
  111.0 2.3 %shard_map.127 = (f32[128,768]{1,0:T(8,128)S(1)}, bf16[128,768]{1,0:T(8,128)(2,1)S(1)}) custom-call(bf16[128,768]{1,0:T(8,128)(2,1)S(1)} %get-tuple-element.67.own, bf16[128,768]{1,0:T(8,128)(2,1)S(1)} %collective-permute-done.8.other, bf16[4,768,768]{2,1,0:T(8,128)(2,1)S(1)} %bitcast.4), custom_call_target="tpu_custom_call" | custom-call | flops 4400000000 | bytes 4000000 | tf_op jit(solution)/shard_map/pallas_call | solution.py:366
  113.3 2.3 %collective-permute-start.9 = (bf16[128,768]{1,0:T(8,128)(2,1)S(1)}, bf16[128,768]{1,0:T(8,128)(2,1)S(1)}, u32[]{:S(2)}, u32[]{:S(2)}) collective-permute-start(bf16[128,768]{1,0:T(8,128)(2,1)S(1)} %get-tuple-element.70), channel_id=1, source_target_pairs={{0,4},{4,0},{8,12},{12,8},{16,20},{20,16},{24,28},{28,24},{32,36},... | collective-permute-start | bytes 589832 | tf_op jit(solution)/shard_map/ppermute | solution.py:380
  115.6 1.0 collective-permute-done.9
  116.7 0.7 add_convert_fusion
  (10 shorter events, 0.0 us)
Async XLA Ops:
  7.2 91.6 %all-gather.3.cloned.1.call-start = ((), (), s32[]{:S(2)}) async-start(), calls=%async_computation.3 | async-start | bytes 5898240 | tf_op jit(solution)/shard_map/all_gather | solution.py:414
  7.2 5.2 %copy-start.2 = (bf16[768,768]{1,0:T(8,128)(2,1)S(1)}, bf16[768,768]{1,0:T(8,128)(2,1)}, u32[]{:S(2)}) copy-start(bf16[768,768]{1,0:T(8,128)(2,1)} %w_up) | copy-start | bytes 3538948
  7.2 5.2 %copy-start.3 = (bf16[768,768]{1,0:T(8,128)(2,1)S(1)}, bf16[768,768]{1,0:T(8,128)(2,1)}, u32[]{:S(2)}) copy-start(bf16[768,768]{1,0:T(8,128)(2,1)} %w_down) | copy-start | bytes 3538948
  12.4 1.2 copy-start
  12.4 5.4 %copy-start.9 = (bf16[8,16,384]{2,1,0:T(8,128)(2,1)S(1)}, bf16[8,16,384]{2,1,0:T(8,128)(2,1)}, u32[]{:S(2)}) copy-start(bf16[8,16,384]{2,1,0:T(8,128)(2,1)} %get-tuple-element.40) | copy-start | bytes 294916
  12.4 29.8 %copy-start.10 = (bf16[128,384]{1,0:T(8,128)(2,1)S(1)}, bf16[128,384]{1,0:T(8,128)(2,1)}, u32[]{:S(2)}) copy-start(bf16[128,384]{1,0:T(8,128)(2,1)} %get-tuple-element.39) | copy-start | bytes 294916
  13.6 47.6 %copy-start.7 = (s32[4]{0:T(128)S(1)}, s32[4]{0:T(128)}, u32[]{:S(2)}) copy-start(s32[4]{0:T(128)} %tiles.5) | copy-start | bytes 52
  13.6 47.6 %copy-start.8 = (bf16[512,256]{1,0:T(8,128)(2,1)S(1)}, bf16[512,256]{1,0:T(8,128)(2,1)}, u32[]{:S(2)}) copy-start(bf16[512,256]{1,0:T(8,128)(2,1)} %get-tuple-element.43.query) | copy-start | bytes 786436
  13.6 42.4 %collective-permute-start = (bf16[512,384]{1,0:T(8,128)(2,1)S(1)}, bf16[512,384]{1,0:T(8,128)(2,1)S(1)}, u32[]{:S(2)}, u32[]{:S(2)}) collective-permute-start(bf16[512,384]{1,0:T(8,128)(2,1)S(1)} %copy-done), channel_id=1, source_target_pairs={{0,8},{4,12},{8,0},{12,4},{16,24},{20,28},{24,16},{28,20},{32,40},... | collective-permute-start | bytes 1179656 | tf_op jit(solution)/shard_map/ppermute | solution.py:380
  32.0 23.9 %all-to-all-start.1 = ((bf16[8,16,256]{2,1,0:T(8,128)(2,1)}), bf16[8,16,256]{2,1,0:T(8,128)(2,1)S(1)}, u32[]{:S(2)}, u32[]{:S(2)}) async-start(bf16[8,16,256]{2,1,0:T(8,128)(2,1)} %get-tuple-element.42), calls=%async_computation.1 | async-start | bytes 131072 | tf_op jit(solution)/shard_map/all_to_all | solution.py:393
  42.2 7.4 %collective-permute-start.2 = (bf16[128,384]{1,0:T(8,128)(2,1)S(1)}, bf16[128,384]{1,0:T(8,128)(2,1)S(1)}, u32[]{:S(2)}, u32[]{:S(2)}) collective-permute-start(bf16[128,384]{1,0:T(8,128)(2,1)S(1)} %copy-done.10), channel_id=1, source_target_pairs={{0,24},{4,28},{8,16},{12,20},{16,8},{20,12},{24,0},{28,4},{32,56},... | collective-permute-start | bytes 294920 | tf_op jit(solution)/shard_map/ppermute | solution.py:380
  46.0 10.0 %collective-permute-start.1 = (bf16[128,384]{1,0:T(8,128)(2,1)S(1)}, bf16[128,384]{1,0:T(8,128)(2,1)S(1)}, u32[]{:S(2)}, u32[]{:S(2)}) collective-permute-start(bf16[128,384]{1,0:T(8,128)(2,1)S(1)} %copy-done.10), channel_id=1, source_target_pairs={{0,16},{4,20},{8,24},{12,28},{16,0},{20,4},{24,8},{28,12},{32,48},... | collective-permute-start | bytes 294920 | tf_op jit(solution)/shard_map/ppermute | solution.py:380
  56.1 25.2 %collective-permute-start.3 = (bf16[1280,384]{1,0:T(8,128)(2,1)S(1)}, bf16[1280,384]{1,0:T(8,128)(2,1)S(1)}, u32[]{:S(2)}, u32[]{:S(2)}) collective-permute-start(bf16[1280,384]{1,0:T(8,128)(2,1)S(1)} %pad_maximum_fusion), channel_id=1, source_target_pairs={{0,4},{4,0},{8,12},{12,8},{16,20},{20,16},{24,28},{28,24},{32,36},... | collective-permute-start | bytes 2949128 | tf_op jit(solution)/shard_map/ppermute | solution.py:380
  59.2 5.2 %collective-permute-start.4 = (bf16[8,16,384]{2,1,0:T(8,128)(2,1)S(1)}, bf16[8,16,384]{2,1,0:T(8,128)(2,1)S(1)}, u32[]{:S(2)}, u32[]{:S(2)}) collective-permute-start(bf16[8,16,384]{2,1,0:T(8,128)(2,1)S(1)} %all_to_all.15.here), channel_id=1, source_target_pairs={{0,4},{4,0},{8,12},{12,8},{16,20},{20,16},{24,28},{28,24},{32,36},... | collective-permute-start | bytes 294920 | tf_op jit(solution)/shard_map/ppermute | solution.py:380
  64.4 16.9 %copy-start.5 = (bf16[192,768]{1,0:T(8,128)(2,1)S(1)}, bf16[192,768]{1,0:T(8,128)(2,1)}, u32[]{:S(2)}) copy-start(bf16[192,768]{1,0:T(8,128)(2,1)} %w_out.1) | copy-start | bytes 884740
  81.3 20.0 %copy-start.4 = (bf16[512,768]{1,0:T(8,128)(2,1)S(1)}, bf16[512,768]{1,0:T(8,128)(2,1)}, u32[]{:S(2)}) copy-start(bf16[512,768]{1,0:T(8,128)(2,1)} %tokens.3) | copy-start | bytes 2359300
  81.3 20.0 %copy-start.6 = (bf16[768]{0:T(1024)(128)(2,1)S(1)}, bf16[768]{0:T(1024)(128)(2,1)}, u32[]{:S(2)}) copy-start(bf16[768]{0:T(1024)(128)(2,1)} %gain.3) | copy-start | bytes 4612
  87.5 11.2 %collective-permute-start.6 = (bf16[128,768]{1,0:T(8,128)(2,1)S(1)}, bf16[128,768]{1,0:T(8,128)(2,1)S(1)}, u32[]{:S(2)}, u32[]{:S(2)}) collective-permute-start(bf16[128,768]{1,0:T(8,128)(2,1)S(1)} %get-tuple-element.56), channel_id=1, source_target_pairs={{0,2},{1,3},{2,0},{3,1},{4,6},{5,7},{6,4},{7,5},{8,10},{9,11},{10,... | collective-permute-start | bytes 589832 | tf_op jit(solution)/shard_map/ppermute | solution.py:444
  92.2 8.3 %collective-permute-start.5 = (bf16[128,768]{1,0:T(8,128)(2,1)S(1)}, bf16[128,768]{1,0:T(8,128)(2,1)S(1)}, u32[]{:S(2)}, u32[]{:S(2)}) collective-permute-start(bf16[128,768]{1,0:T(8,128)(2,1)S(1)} %get-tuple-element.55), channel_id=1, source_target_pairs={{0,1},{1,2},{2,3},{3,0},{4,5},{5,6},{6,7},{7,4},{8,9},{9,10},{10,1... | collective-permute-start | bytes 589832 | tf_op jit(solution)/shard_map/ppermute | solution.py:444
  94.4 6.8 %collective-permute-start.7 = (bf16[128,768]{1,0:T(8,128)(2,1)S(1)}, bf16[128,768]{1,0:T(8,128)(2,1)S(1)}, u32[]{:S(2)}, u32[]{:S(2)}) collective-permute-start(bf16[128,768]{1,0:T(8,128)(2,1)S(1)} %get-tuple-element.60), channel_id=1, source_target_pairs={{0,3},{1,0},{2,1},{3,2},{4,7},{5,4},{6,5},{7,6},{8,11},{9,8},{10,9... | collective-permute-start | bytes 589832 | tf_op jit(solution)/shard_map/ppermute | solution.py:444
  102.1 6.6 %collective-permute-start.8 = (bf16[128,768]{1,0:T(8,128)(2,1)S(1)}, bf16[128,768]{1,0:T(8,128)(2,1)S(1)}, u32[]{:S(2)}, u32[]{:S(2)}) collective-permute-start(bf16[128,768]{1,0:T(8,128)(2,1)S(1)} %get-tuple-element.67.own), channel_id=1, source_target_pairs={{0,4},{4,0},{8,12},{12,8},{16,20},{20,16},{24,28},{28,24},{32,36},... | collective-permute-start | bytes 589832 | tf_op jit(solution)/shard_map/ppermute | solution.py:380
  108.7 2.3 %copy-start.1 = (bf16[3072,768]{1,0:T(8,128)(2,1)S(1)}, bf16[3072,768]{1,0:T(8,128)(2,1)}, u32[]{:S(2)}) copy-start(bf16[3072,768]{1,0:T(8,128)(2,1)} %all-gather.3.cloned.1.call-done) | copy-start | bytes 14155780
  113.3 3.3 %collective-permute-start.9 = (bf16[128,768]{1,0:T(8,128)(2,1)S(1)}, bf16[128,768]{1,0:T(8,128)(2,1)S(1)}, u32[]{:S(2)}, u32[]{:S(2)}) collective-permute-start(bf16[128,768]{1,0:T(8,128)(2,1)S(1)} %get-tuple-element.70), channel_id=1, source_target_pairs={{0,4},{4,0},{8,12},{12,8},{16,20},{20,16},{24,28},{28,24},{32,36},... | collective-permute-start | bytes 589832 | tf_op jit(solution)/shard_map/ppermute | solution.py:380
Sparse Core Ops, SparseCore 0:
  13.7 63.4 all-gather.2

commit v11 on v8

--- a/solution.py
+++ b/solution.py
@@ -291,7 +291,7 @@
     ends = slide_ends(tiles)
     seq, mp = lax.axis_index("seq"), lax.axis_index("mp")
     column = seq & 15
-    beside = column ^ ((seq >> 4) << 1)
+    beside = ((((seq >> 4) - (column >> 1)) & 7) << 1) + (column & 1)
     count = FAR_GROUP * FAR_ROWS
     shape = (count, 2 * count)
 
@@ -379,7 +379,10 @@
     dma = pltpu.SemaphoreType.DMA
     columns = [[16 * z + place for z in range(FAR_GROUP)] for place in range(16)]
     across = [
-        (16 * z + (place ^ (2 * z)), 16 * z + place) for z in range(FAR_GROUP) for place in range(16)
+        (16 * z + 2 * ((z - y) % 8) + core, 16 * z + 2 * y + core)
+        for z in range(FAR_GROUP)
+        for y in range(8)
+        for core in range(2)
     ]
     w_query, w_key, w_value = w_query.T, w_key.T, w_value.T
     query, own, mid, far = call(
@@ -407,10 +410,9 @@
     mid_a, mid_b = swap(mid, 4), swap(mid, 6)
     state = [((ROWS, LANES), f32)] * LOCAL_HEADS
     near = call(near_kernel, 3, state, [(slide_tiles, s), (query, v), (own, v), (side, v)])
-    side, mid_a, mid_b, far_here, *near = lax.optimization_barrier(
-        (side, mid_a, mid_b, far_here, *near)
-    )
+    far_here, *near = lax.optimization_barrier((far_here, *near))
     far_other = swap(far_here, 1)
+    side, mid_a, mid_b, far_other = lax.optimization_barrier((side, mid_a, mid_b, far_other))
     swapped = swap(jnp.concatenate([own, side, mid_a, mid_b], 0), 1)
     (parts,) = call(
         far_kernel,

time: 114 us -> 112 us (0.982); the launches traced: 112 us -> 112 us
  waiting for transfers between devices: 6.36 us -> 4.93 us
  starting transfers between devices: 33.5 us -> 34.8 us
    ppermute x7, waiting for transfers between devices: 4.44 us -> 3.01 us  [swap(): lax.ppermute(value, 'seq', [(i, i ^ step) for i in range(lax.axis_size('s...]
    ppermute x7, starting transfers between devices: 22.7 us -> 24.1 us  [swap(): lax.ppermute(value, 'seq', [(i, i ^ step) for i in range(lax.axis_size('s...]
  transfers between devices with their start and end apart: 10 -> 10, of which waited for: 5 -> 4; matrix products, arithmetic and copies ran while one was open for 0% -> 0% of each run, Pallas kernels for 9% -> 10%
where the time goes in v11:
time: 112 us
  starting transfers between devices  34.8 us (31%)
  blocking collectives  34.4 us (31%)
  Pallas kernels  20 us (18%)
  between operations  14.3 us (13%)
  waiting for transfers between devices  4.93 us (4%)
  local copies, waits for them, and re-layouts  2.39 us (2%)
    ppermute x7, starting transfers between devices, swap(): lax.ppermute(value, 'seq', [(i, i ^ step) for i in range(lax.axis_size('s...  24.1 us
    all_to_all x1, blocking collectives, local(): lax.all_to_all(parts, 'seq', split_axis=0, concat_axis=0, tiled=True, axi...  20.1 us
    pallas_call x7, Pallas kernels, call(): pl.pallas_call(kernel, out_shape=[jax.ShapeDtypeStruct(*out) for out in o...  20 us
    all_to_all x1, blocking collectives, local(): terms = lax.all_to_all(terms, 'mp', split_axis=0, concat_axis=0, tiled=True)  14.3 us
    all_to_all x1, starting transfers between devices, local(): lax.all_to_all(far, 'seq', split_axis=0, concat_axis=0, tiled=True, axis_...  10 us
    ppermute x7, waiting for transfers between devices, swap(): lax.ppermute(value, 'seq', [(i, i ^ step) for i in range(lax.axis_size('s...  3.01 us
    unnamed x20, local copies, waits for them, and re-layouts  2.38 us
  transfers between devices with their start and end apart: 10, of which 4 were waited for; matrix products, arithmetic and copies ran while one was open for 0% of the time, Pallas kernels for 10%

profile of v11, /device:TPU:1, one launch (start us, length us, event | category | flops | bytes accessed | tf_op | source)
XLA Modules:
  0.0 111.7 jit_solution(8813201688073565612)
XLA Ops:
  7.2 0.0 all-gather.3.cloned.1.call-start
  7.2 0.0 copy-start.2
  7.2 0.0 copy-start.3
  7.2 5.1 %shard_map.121 = (bf16[512,256]{1,0:T(8,128)(2,1)}, bf16[512,384]{1,0:T(8,128)(2,1)}, bf16[128,384]{1,0:T(8,128)(2,1)}, bf16[8,16,640]{2,1,0:T(8,128)(2,1)}) custom-call(bf16[512,768]{1,0:T(8,128)(2,1)} %tokens.3, bf16[768]{0:T(1024)(128)(2,1)} %gain.2, bf16[192,768]{1,0:T(8,128)(2,1)} %bitcast.7, bf16[192,768]{1,0:T(8,128)(2,1)} %bitcast.8, ...), custom_call_target="tpu_custom_call" | custom-call | flops 3300000000 | bytes 3000000 | tf_op jit(solution)/shard_map/pallas_call | solution.py:359
  12.4 0.0 copy-done.2
  12.4 0.0 copy-done.3
  12.4 0.0 copy-start
  12.4 0.0 copy-start.9
  12.4 0.0 copy-start.7
  12.4 0.0 copy-start.8
  12.4 1.1 %shard_map.125 = bf16[768,768]{1,0:T(8,128)(2,1)} custom-call(bf16[768,768]{1,0:T(8,128)(2,1)S(1)} %copy-done.2, bf16[768,768]{1,0:T(8,128)(2,1)S(1)} %copy-done.3), custom_call_target="tpu_custom_call" | custom-call | flops 2200000000 | bytes 2000000 | tf_op jit(solution)/shard_map/pallas_call | solution.py:359
  13.6 0.0 all-gather.3.cloned.1.call-update
  13.6 0.0 copy-done
  13.6 4.0 %collective-permute-start = (bf16[512,384]{1,0:T(8,128)(2,1)S(1)}, bf16[512,384]{1,0:T(8,128)(2,1)S(1)}, u32[]{:S(2)}, u32[]{:S(2)}) collective-permute-start(bf16[512,384]{1,0:T(8,128)(2,1)S(1)} %copy-done), channel_id=1, source_target_pairs={{0,8},{4,12},{8,0},{12,4},{16,24},{20,28},{24,16},{28,20},{32,40},... | collective-permute-start | bytes 1179656 | tf_op jit(solution)/shard_map/ppermute | solution.py:373
  17.7 10.0 %all-to-all-start = ((bf16[8,16,640]{2,1,0:T(8,128)(2,1)}), bf16[8,16,640]{2,1,0:T(8,128)(2,1)S(1)}, u32[]{:S(2)}, u32[]{:S(2)}) async-start(bf16[8,16,640]{2,1,0:T(8,128)(2,1)} %get-tuple-element.30), calls=%async_computation | async-start | bytes 327680 | tf_op jit(solution)/shard_map/all_to_all | solution.py:399
  27.7 0.0 copy-done.9
  27.7 4.1 %collective-permute-start.2 = (bf16[128,384]{1,0:T(8,128)(2,1)S(1)}, bf16[128,384]{1,0:T(8,128)(2,1)S(1)}, u32[]{:S(2)}, u32[]{:S(2)}) collective-permute-start(bf16[128,384]{1,0:T(8,128)(2,1)S(1)} %copy-done.9), channel_id=1, source_target_pairs={{0,24},{4,28},{8,16},{12,20},{16,8},{20,12},{24,0},{28,4},{32,56},... | collective-permute-start | bytes 294920 | tf_op jit(solution)/shard_map/ppermute | solution.py:373
  31.8 2.0 %collective-permute-start.1 = (bf16[128,384]{1,0:T(8,128)(2,1)S(1)}, bf16[128,384]{1,0:T(8,128)(2,1)S(1)}, u32[]{:S(2)}, u32[]{:S(2)}) collective-permute-start(bf16[128,384]{1,0:T(8,128)(2,1)S(1)} %copy-done.9), channel_id=1, source_target_pairs={{0,16},{4,20},{8,24},{12,28},{16,0},{20,4},{24,8},{28,12},{32,48},... | collective-permute-start | bytes 294920 | tf_op jit(solution)/shard_map/ppermute | solution.py:373
  33.9 1.9 %all-to-all-done.rows = bf16[8,16,640]{2,1,0:T(8,128)(2,1)S(1)} async-done(((bf16[8,16,640]{2,1,0:T(8,128)(2,1)}), bf16[8,16,640]{2,1,0:T(8,128)(2,1)S(1)}, u32[]{:S(2)}, u32[]{:S(2)}) %all-to-all-start) | async-done | bytes 163872 | tf_op jit(solution)/shard_map/all_to_all | solution.py:399
  35.8 0.7 collective-permute-start.3
  36.5 0.0 collective-permute-done.side
  36.5 0.0 copy-done.7
  36.5 0.0 copy-done.8
  36.5 3.2 %shard_map.122 = (f32[512,128]{1,0:T(8,128)S(1)}, f32[512,128]{1,0:T(8,128)S(1)}, f32[512,128]{1,0:T(8,128)S(1)}) custom-call(s32[4]{0:T(128)S(1)} %copy-done.7, bf16[512,256]{1,0:T(8,128)(2,1)S(1)} %copy-done.8, bf16[512,384]{1,0:T(8,128)(2,1)S(1)} %copy-done, bf16[512,384]{1,0:T(8,128)(2,1)S(1)} %collective-permute-done.side), custom_call_target="tpu_custom_call" | custom-call | flops 3300000000 | bytes 3000000 | tf_op jit(solution)/shard_map/pallas_call | solution.py:359
  39.7 0.0 collective-permute-done.3.here
  39.7 4.6 %collective-permute-start.4 = (bf16[128,384]{1,0:T(8,128)(2,1)S(1)}, bf16[128,384]{1,0:T(8,128)(2,1)S(1)}, u32[]{:S(2)}, u32[]{:S(2)}) collective-permute-start(bf16[128,384]{1,0:T(8,128)(2,1)S(1)} %collective-permute-done.3.here), channel_id=1, source_target_pairs={{0,4},{4,0},{8,12},{12,8},{16,20},{20,16},{24,28},{28,24},{32,36},... | collective-permute-start | bytes 294920 | tf_op jit(solution)/shard_map/ppermute | solution.py:373
  44.3 0.0 collective-permute-done.2.mid_b
  44.3 0.0 collective-permute-done.1.mid_a
  44.3 0.9 collective-permute-done.4.other
  45.2 0.1 pad_maximum_fusion
  45.3 0.0 copy-start.5
  45.3 2.4 %collective-permute-start.5 = (bf16[1280,384]{1,0:T(8,128)(2,1)S(1)}, bf16[1280,384]{1,0:T(8,128)(2,1)S(1)}, u32[]{:S(2)}, u32[]{:S(2)}) collective-permute-start(bf16[1280,384]{1,0:T(8,128)(2,1)S(1)} %pad_maximum_fusion), channel_id=1, source_target_pairs={{0,4},{4,0},{8,12},{12,8},{16,20},{20,16},{24,28},{28,24},{32,36},... | collective-permute-start | bytes 2949128 | tf_op jit(solution)/shard_map/ppermute | solution.py:373
  47.7 1.2 %shard_map.123 = f32[8,16,384]{2,1,0:T(8,128)S(1)} custom-call(s32[4]{0:T(128)S(1)} %copy-done.7, bf16[8,16,640]{2,1,0:T(8,128)(2,1)S(1)} %all-to-all-done.rows, bf16[128,384]{1,0:T(8,128)(2,1)S(1)} %collective-permute-done.3.here, bf16[128,384]{1,0:T(8,128)(2,1)S(1)} %collective-permute-done.4.other), custom_call_target="tpu_custom_call" | custom-call | flops 2200000000 | bytes 2000000 | tf_op jit(solution)/shard_map/pallas_call | solution.py:359
  48.9 20.1 %all_to_all.15.parts = f32[8,16,384]{2,1,0:T(8,128)S(1)} all-to-all(f32[8,16,384]{2,1,0:T(8,128)S(1)} %shard_map.123), channel_id=1, replica_groups={{0,64,128,192,256,320,384,448},{4,68,132,196,260,324,388,452},{8,72,136..., dimensions={0} | all-to-all | bytes 393216 | tf_op jit(solution)/shard_map/all_to_all | solution.py:423
  69.1 0.0 collective-permute-done.5.swapped
  69.1 0.0 copy-done.5
  69.1 6.3 %shard_map.124 = (bf16[4,128,768]{2,1,0:T(8,128)(2,1)S(1)}, bf16[16,192]{1,0:T(8,128)(2,1)}) custom-call(s32[4]{0:T(128)S(1)} %copy-done.7, bf16[512,256]{1,0:T(8,128)(2,1)S(1)} %copy-done.8, bf16[512,384]{1,0:T(8,128)(2,1)S(1)} %copy-done, bf16[512,384]{1,0:T(8,128)(2,1)S(1)} %collective-permute-done.side, ...), custom_call_target="tpu_custom_call" | custom-call | flops 7699999744 | bytes 7000000 | tf_op jit(solution)/shard_map/pallas_call | solution.py:359
  75.3 14.3 %all_to_all.16.terms = bf16[4,128,768]{2,1,0:T(8,128)(2,1)S(1)} all-to-all(bf16[4,128,768]{2,1,0:T(8,128)(2,1)S(1)} %get-tuple-element.45), channel_id=1, replica_groups=mesh['seq'=128,'mp'=4] {'mp'}, dimensions={0} | all-to-all | bytes 1572864 | tf_op jit(solution)/shard_map/all_to_all | solution.py:436
  89.6 0.0 copy-done.4
  89.6 0.0 copy-done.6
  89.6 0.8 shard_map.126
  90.4 4.7 %collective-permute-start.6 = (bf16[128,768]{1,0:T(8,128)(2,1)S(1)}, bf16[128,768]{1,0:T(8,128)(2,1)S(1)}, u32[]{:S(2)}, u32[]{:S(2)}) collective-permute-start(bf16[128,768]{1,0:T(8,128)(2,1)S(1)} %get-tuple-element.51.own), channel_id=1, source_target_pairs={{0,4},{4,0},{8,12},{12,8},{16,20},{20,16},{24,28},{28,24},{32,36},... | collective-permute-start | bytes 589832 | tf_op jit(solution)/shard_map/ppermute | solution.py:373
  95.1 1.0 collective-permute-done.6.other
  96.2 2.3 %copy-done.1 = bf16[3072,768]{1,0:T(8,128)(2,1)S(1)} copy-done((bf16[3072,768]{1,0:T(8,128)(2,1)S(1)}, bf16[3072,768]{1,0:T(8,128)(2,1)}, u32[]{:S(2)}) %copy-start.1) | copy-done | bytes 4718616
  98.5 2.3 %shard_map.127 = (f32[128,768]{1,0:T(8,128)S(1)}, bf16[128,768]{1,0:T(8,128)(2,1)S(1)}) custom-call(bf16[128,768]{1,0:T(8,128)(2,1)S(1)} %get-tuple-element.51.own, bf16[128,768]{1,0:T(8,128)(2,1)S(1)} %collective-permute-done.6.other, bf16[4,768,768]{2,1,0:T(8,128)(2,1)S(1)} %bitcast.5), custom_call_target="tpu_custom_call" | custom-call | flops 4400000000 | bytes 4000000 | tf_op jit(solution)/shard_map/pallas_call | solution.py:359
  100.8 2.3 %collective-permute-start.7 = (bf16[128,768]{1,0:T(8,128)(2,1)S(1)}, bf16[128,768]{1,0:T(8,128)(2,1)S(1)}, u32[]{:S(2)}, u32[]{:S(2)}) collective-permute-start(bf16[128,768]{1,0:T(8,128)(2,1)S(1)} %get-tuple-element.54), channel_id=1, source_target_pairs={{0,4},{4,0},{8,12},{12,8},{16,20},{20,16},{24,28},{28,24},{32,36},... | collective-permute-start | bytes 589832 | tf_op jit(solution)/shard_map/ppermute | solution.py:373
  103.1 1.0 collective-permute-done.7
  104.1 0.7 add_convert_fusion
  (5 shorter events, 0.0 us)
Async XLA Ops:
  7.2 82.4 %all-gather.3.cloned.1.call-start = ((), (), s32[]{:S(2)}) async-start(), calls=%async_computation.3 | async-start | bytes 5898240 | tf_op jit(solution)/shard_map/all_gather | solution.py:404
  7.2 5.2 %copy-start.2 = (bf16[768,768]{1,0:T(8,128)(2,1)S(1)}, bf16[768,768]{1,0:T(8,128)(2,1)}, u32[]{:S(2)}) copy-start(bf16[768,768]{1,0:T(8,128)(2,1)} %w_up) | copy-start | bytes 3538948
  7.2 5.2 %copy-start.3 = (bf16[768,768]{1,0:T(8,128)(2,1)S(1)}, bf16[768,768]{1,0:T(8,128)(2,1)}, u32[]{:S(2)}) copy-start(bf16[768,768]{1,0:T(8,128)(2,1)} %w_down) | copy-start | bytes 3538948
  12.4 1.2 %copy-start = (bf16[512,384]{1,0:T(8,128)(2,1)S(1)}, bf16[512,384]{1,0:T(8,128)(2,1)}, u32[]{:S(2)}) copy-start(bf16[512,384]{1,0:T(8,128)(2,1)} %get-tuple-element.32.own) | copy-start | bytes 1179652
  12.4 15.3 %copy-start.9 = (bf16[128,384]{1,0:T(8,128)(2,1)S(1)}, bf16[128,384]{1,0:T(8,128)(2,1)}, u32[]{:S(2)}) copy-start(bf16[128,384]{1,0:T(8,128)(2,1)} %get-tuple-element.33) | copy-start | bytes 294916
  12.4 24.1 %copy-start.7 = (s32[4]{0:T(128)S(1)}, s32[4]{0:T(128)}, u32[]{:S(2)}) copy-start(s32[4]{0:T(128)} %tiles.5) | copy-start | bytes 52
  12.4 24.1 %copy-start.8 = (bf16[512,256]{1,0:T(8,128)(2,1)S(1)}, bf16[512,256]{1,0:T(8,128)(2,1)}, u32[]{:S(2)}) copy-start(bf16[512,256]{1,0:T(8,128)(2,1)} %get-tuple-element.31.query) | copy-start | bytes 786436
  13.6 22.8 %collective-permute-start = (bf16[512,384]{1,0:T(8,128)(2,1)S(1)}, bf16[512,384]{1,0:T(8,128)(2,1)S(1)}, u32[]{:S(2)}, u32[]{:S(2)}) collective-permute-start(bf16[512,384]{1,0:T(8,128)(2,1)S(1)} %copy-done), channel_id=1, source_target_pairs={{0,8},{4,12},{8,0},{12,4},{16,24},{20,28},{24,16},{28,20},{32,40},... | collective-permute-start | bytes 1179656 | tf_op jit(solution)/shard_map/ppermute | solution.py:373
  17.7 18.1 %all-to-all-start = ((bf16[8,16,640]{2,1,0:T(8,128)(2,1)}), bf16[8,16,640]{2,1,0:T(8,128)(2,1)S(1)}, u32[]{:S(2)}, u32[]{:S(2)}) async-start(bf16[8,16,640]{2,1,0:T(8,128)(2,1)} %get-tuple-element.30), calls=%async_computation | async-start | bytes 327680 | tf_op jit(solution)/shard_map/all_to_all | solution.py:399
  27.7 16.6 %collective-permute-start.2 = (bf16[128,384]{1,0:T(8,128)(2,1)S(1)}, bf16[128,384]{1,0:T(8,128)(2,1)S(1)}, u32[]{:S(2)}, u32[]{:S(2)}) collective-permute-start(bf16[128,384]{1,0:T(8,128)(2,1)S(1)} %copy-done.9), channel_id=1, source_target_pairs={{0,24},{4,28},{8,16},{12,20},{16,8},{20,12},{24,0},{28,4},{32,56},... | collective-permute-start | bytes 294920 | tf_op jit(solution)/shard_map/ppermute | solution.py:373
  31.8 12.5 %collective-permute-start.1 = (bf16[128,384]{1,0:T(8,128)(2,1)S(1)}, bf16[128,384]{1,0:T(8,128)(2,1)S(1)}, u32[]{:S(2)}, u32[]{:S(2)}) collective-permute-start(bf16[128,384]{1,0:T(8,128)(2,1)S(1)} %copy-done.9), channel_id=1, source_target_pairs={{0,16},{4,20},{8,24},{12,28},{16,0},{20,4},{24,8},{28,12},{32,48},... | collective-permute-start | bytes 294920 | tf_op jit(solution)/shard_map/ppermute | solution.py:373
  35.8 3.9 %collective-permute-start.3 = (bf16[128,384]{1,0:T(8,128)(2,1)S(1)}, bf16[128,384]{1,0:T(8,128)(2,1)S(1)}, u32[]{:S(2)}, u32[]{:S(2)}) collective-permute-start(bf16[128,384]{1,0:T(8,128)(2,1)S(1)} %bitcast.6), channel_id=1, source_target_pairs={{0,0},{4,4},{56,8},{60,12},{48,16},{52,20},{40,24},{44,28},{32,32}... | collective-permute-start | bytes 294920 | tf_op jit(solution)/shard_map/ppermute | solution.py:408
  39.7 5.5 %collective-permute-start.4 = (bf16[128,384]{1,0:T(8,128)(2,1)S(1)}, bf16[128,384]{1,0:T(8,128)(2,1)S(1)}, u32[]{:S(2)}, u32[]{:S(2)}) collective-permute-start(bf16[128,384]{1,0:T(8,128)(2,1)S(1)} %collective-permute-done.3.here), channel_id=1, source_target_pairs={{0,4},{4,0},{8,12},{12,8},{16,20},{20,16},{24,28},{28,24},{32,36},... | collective-permute-start | bytes 294920 | tf_op jit(solution)/shard_map/ppermute | solution.py:373
  45.3 23.7 %copy-start.5 = (bf16[192,768]{1,0:T(8,128)(2,1)S(1)}, bf16[192,768]{1,0:T(8,128)(2,1)}, u32[]{:S(2)}) copy-start(bf16[192,768]{1,0:T(8,128)(2,1)} %w_out.1) | copy-start | bytes 884740
  45.3 23.7 %collective-permute-start.5 = (bf16[1280,384]{1,0:T(8,128)(2,1)S(1)}, bf16[1280,384]{1,0:T(8,128)(2,1)S(1)}, u32[]{:S(2)}, u32[]{:S(2)}) collective-permute-start(bf16[1280,384]{1,0:T(8,128)(2,1)S(1)} %pad_maximum_fusion), channel_id=1, source_target_pairs={{0,4},{4,0},{8,12},{12,8},{16,20},{20,16},{24,28},{28,24},{32,36},... | collective-permute-start | bytes 2949128 | tf_op jit(solution)/shard_map/ppermute | solution.py:373
  69.0 20.6 %copy-start.4 = (bf16[512,768]{1,0:T(8,128)(2,1)S(1)}, bf16[512,768]{1,0:T(8,128)(2,1)}, u32[]{:S(2)}) copy-start(bf16[512,768]{1,0:T(8,128)(2,1)} %tokens.3) | copy-start | bytes 2359300
  69.1 20.6 %copy-start.6 = (bf16[768]{0:T(1024)(128)(2,1)S(1)}, bf16[768]{0:T(1024)(128)(2,1)}, u32[]{:S(2)}) copy-start(bf16[768]{0:T(1024)(128)(2,1)} %gain.3) | copy-start | bytes 4612
  90.4 5.7 %collective-permute-start.6 = (bf16[128,768]{1,0:T(8,128)(2,1)S(1)}, bf16[128,768]{1,0:T(8,128)(2,1)S(1)}, u32[]{:S(2)}, u32[]{:S(2)}) collective-permute-start(bf16[128,768]{1,0:T(8,128)(2,1)S(1)} %get-tuple-element.51.own), channel_id=1, source_target_pairs={{0,4},{4,0},{8,12},{12,8},{16,20},{20,16},{24,28},{28,24},{32,36},... | collective-permute-start | bytes 589832 | tf_op jit(solution)/shard_map/ppermute | solution.py:373
  96.2 2.3 %copy-start.1 = (bf16[3072,768]{1,0:T(8,128)(2,1)S(1)}, bf16[3072,768]{1,0:T(8,128)(2,1)}, u32[]{:S(2)}) copy-start(bf16[3072,768]{1,0:T(8,128)(2,1)} %all-gather.3.cloned.1.call-done) | copy-start | bytes 14155780
  100.8 3.3 %collective-permute-start.7 = (bf16[128,768]{1,0:T(8,128)(2,1)S(1)}, bf16[128,768]{1,0:T(8,128)(2,1)S(1)}, u32[]{:S(2)}, u32[]{:S(2)}) collective-permute-start(bf16[128,768]{1,0:T(8,128)(2,1)S(1)} %get-tuple-element.54), channel_id=1, source_target_pairs={{0,4},{4,0},{8,12},{12,8},{16,20},{20,16},{24,28},{28,24},{32,36},... | collective-permute-start | bytes 589832 | tf_op jit(solution)/shard_map/ppermute | solution.py:373
Sparse Core Ops, SparseCore 0:
  13.7 63.4 all-gather.2

commit v12 on v11

--- a/solution.py
+++ b/solution.py
@@ -112,22 +112,18 @@
     tokens, gain, w_query, w_key, w_value, query, keyval, mid, far, rows, weights, sems
 ):
     mp = lax.axis_index("mp")
-    copies = []
-    for index in range(4):
-        part = pl.ds(index * BLOCK, BLOCK)
-        copies.append(pltpu.make_async_copy(tokens.at[part], rows.at[part], sems.at[index]))
-    for index, weight in enumerate((w_query, w_key, w_value)):
-        copies.append(pltpu.make_async_copy(weight, weights.at[index], sems.at[4 + index]))
+    copies = [pltpu.make_async_copy(tokens, rows, sems.at[0])]
+    for index, weight in enumerate((w_key, w_value, w_query)):
+        copies.append(pltpu.make_async_copy(weight, weights.at[index], sems.at[1 + index]))
     for copy in copies:
         copy.start()
-    for copy in copies[:4]:
-        copy.wait()
+    copies[0].wait()
     normed = layer_norm(rows[...].astype(jnp.float32), gain[...])
     order = iota((ROWS, ROWS), 0) == place_of(iota((ROWS, ROWS), 1))
     normed = matmul(order.astype(jnp.bfloat16), normed).astype(jnp.bfloat16)
-    for copy in copies[4:]:
+    for copy in copies[1:]:
         copy.wait()
-    queries, keyvals = project(normed, *[weights.at[index] for index in range(3)])
+    queries, keyvals = project(normed, *[weights.at[index] for index in (2, 0, 1)])
     for index, value in enumerate(queries):
         query[:, tile(index)] = value
     for index, value in enumerate(keyvals):
@@ -393,7 +389,7 @@
             ((FAR_GROUP, FAR_ROWS, 640), bf16),
         ],
         [(tokens, h), (attn_gain, v), (w_query, h), (w_key, h), (w_value, h)],
-        [pltpu.VMEM((ROWS, WIDTH), bf16), pltpu.VMEM((3, 192, WIDTH), bf16), dma((7,))],
+        [pltpu.VMEM((ROWS, WIDTH), bf16), pltpu.VMEM((3, 192, WIDTH), bf16), dma((4,))],
         limit=WHOLE_VMEM,
     )
     far_rows = lax.all_to_all(
@@ -412,7 +408,7 @@
     near = call(near_kernel, 3, state, [(slide_tiles, s), (query, v), (own, v), (side, v)])
     far_here, *near = lax.optimization_barrier((far_here, *near))
     far_other = swap(far_here, 1)
-    side, mid_a, mid_b, far_other = lax.optimization_barrier((side, mid_a, mid_b, far_other))
+    side, mid_a, mid_b, _ = lax.optimization_barrier((side, mid_a, mid_b, far_here))
     swapped = swap(jnp.concatenate([own, side, mid_a, mid_b], 0), 1)
     (parts,) = call(
         far_kernel,
@@ -437,7 +433,7 @@
     terms, mine = lax.optimization_barrier((terms, mine))
     attended, normed = call(
         norm_kernel,
-        1,
+        9,
         [((BLOCK, WIDTH), bf16), ((BLOCK, WIDTH), bf16)],
         [(tokens, v), (terms, v), (ffn_gain, v)],
     )

time: 112 us -> 110 us (0.982)
  local copies, waits for them, and re-layouts: 2.39 us -> 0.06 us
  waiting for transfers between devices: 4.93 us -> 6.35 us
  starting transfers between devices: 34.8 us -> 33.6 us
    unnamed x20, local copies, waits for them, and re-layouts: 2.38 us -> 0.05 us
    ppermute x7, waiting for transfers between devices: 3.01 us -> 4.42 us  [swap(): lax.ppermute(value, 'seq', [(i, i ^ step) for i in range(lax.axis_size('s...]
    ppermute x7, starting transfers between devices: 24.1 us -> 22.9 us  [swap(): lax.ppermute(value, 'seq', [(i, i ^ step) for i in range(lax.axis_size('s...]
  transfers between devices with their start and end apart: 10 -> 10, of which waited for: 4 -> 5; matrix products, arithmetic and copies ran while one was open for 0% -> 0% of each run, Pallas kernels for 10% -> 10%
where the time goes in v12:
time: 110 us; the launch traced here: 109 us
  blocking collectives  34.4 us (31%)
  starting transfers between devices  33.6 us (31%)
  Pallas kernels  19.9 us (18%)
  between operations  14.3 us (13%)
  waiting for transfers between devices  6.35 us (6%)
    ppermute x7, starting transfers between devices, swap(): lax.ppermute(value, 'seq', [(i, i ^ step) for i in range(lax.axis_size('s...  22.9 us
    all_to_all x1, blocking collectives, local(): lax.all_to_all(parts, 'seq', split_axis=0, concat_axis=0, tiled=True, axi...  20.1 us
    pallas_call x7, Pallas kernels, call(): pl.pallas_call(kernel, out_shape=[jax.ShapeDtypeStruct(*out) for out in o...  19.9 us
    all_to_all x1, blocking collectives, local(): terms = lax.all_to_all(terms, 'mp', split_axis=0, concat_axis=0, tiled=True)  14.3 us
    all_to_all x1, starting transfers between devices, local(): lax.all_to_all(far, 'seq', split_axis=0, concat_axis=0, tiled=True, axis_...  10 us
    ppermute x7, waiting for transfers between devices, swap(): lax.ppermute(value, 'seq', [(i, i ^ step) for i in range(lax.axis_size('s...  4.42 us
  transfers between devices with their start and end apart: 10, of which 5 were waited for; matrix products, arithmetic and copies ran while one was open for 0% of the time, Pallas kernels for 10%

profile of v12, /device:TPU:1, one launch (start us, length us, event | category | flops | bytes accessed | tf_op | source)
XLA Modules:
  0.0 109.4 jit_solution(9733897770357125378)
XLA Ops:
  7.2 0.0 all-gather.3.cloned.1.call-start
  7.2 0.0 copy-start.2
  7.2 0.0 copy-start.3
  7.2 5.0 %shard_map.121 = (bf16[512,256]{1,0:T(8,128)(2,1)}, bf16[512,384]{1,0:T(8,128)(2,1)}, bf16[128,384]{1,0:T(8,128)(2,1)}, bf16[8,16,640]{2,1,0:T(8,128)(2,1)}) custom-call(bf16[512,768]{1,0:T(8,128)(2,1)} %tokens.3, bf16[768]{0:T(1024)(128)(2,1)} %gain.2, bf16[192,768]{1,0:T(8,128)(2,1)} %bitcast.7, bf16[192,768]{1,0:T(8,128)(2,1)} %bitcast.8, ...), custom_call_target="tpu_custom_call" | custom-call | flops 3300000000 | bytes 3000000 | tf_op jit(solution)/shard_map/pallas_call | solution.py:355
  12.3 0.0 copy-done.2
  12.3 0.0 copy-done.3
  12.3 0.0 copy-start
  12.3 0.0 copy-start.9
  12.3 0.0 copy-start.7
  12.3 0.0 copy-start.8
  12.3 1.1 %shard_map.125 = bf16[768,768]{1,0:T(8,128)(2,1)} custom-call(bf16[768,768]{1,0:T(8,128)(2,1)S(1)} %copy-done.2, bf16[768,768]{1,0:T(8,128)(2,1)S(1)} %copy-done.3), custom_call_target="tpu_custom_call" | custom-call | flops 2200000000 | bytes 2000000 | tf_op jit(solution)/shard_map/pallas_call | solution.py:355
  13.5 0.0 all-gather.3.cloned.1.call-update
  13.5 0.0 copy-done
  13.5 4.0 %collective-permute-start = (bf16[512,384]{1,0:T(8,128)(2,1)S(1)}, bf16[512,384]{1,0:T(8,128)(2,1)S(1)}, u32[]{:S(2)}, u32[]{:S(2)}) collective-permute-start(bf16[512,384]{1,0:T(8,128)(2,1)S(1)} %copy-done), channel_id=1, source_target_pairs={{0,8},{4,12},{8,0},{12,4},{16,24},{20,28},{24,16},{28,20},{32,40},... | collective-permute-start | bytes 1179656 | tf_op jit(solution)/shard_map/ppermute | solution.py:369
  17.6 10.0 %all-to-all-start = ((bf16[8,16,640]{2,1,0:T(8,128)(2,1)}), bf16[8,16,640]{2,1,0:T(8,128)(2,1)S(1)}, u32[]{:S(2)}, u32[]{:S(2)}) async-start(bf16[8,16,640]{2,1,0:T(8,128)(2,1)} %get-tuple-element.29), calls=%async_computation | async-start | bytes 327680 | tf_op jit(solution)/shard_map/all_to_all | solution.py:395
  27.6 0.0 copy-done.9
  27.6 4.1 %collective-permute-start.2 = (bf16[128,384]{1,0:T(8,128)(2,1)S(1)}, bf16[128,384]{1,0:T(8,128)(2,1)S(1)}, u32[]{:S(2)}, u32[]{:S(2)}) collective-permute-start(bf16[128,384]{1,0:T(8,128)(2,1)S(1)} %copy-done.9), channel_id=1, source_target_pairs={{0,24},{4,28},{8,16},{12,20},{16,8},{20,12},{24,0},{28,4},{32,56},... | collective-permute-start | bytes 294920 | tf_op jit(solution)/shard_map/ppermute | solution.py:369
  31.7 2.0 %collective-permute-start.1 = (bf16[128,384]{1,0:T(8,128)(2,1)S(1)}, bf16[128,384]{1,0:T(8,128)(2,1)S(1)}, u32[]{:S(2)}, u32[]{:S(2)}) collective-permute-start(bf16[128,384]{1,0:T(8,128)(2,1)S(1)} %copy-done.9), channel_id=1, source_target_pairs={{0,16},{4,20},{8,24},{12,28},{16,0},{20,4},{24,8},{28,12},{32,48},... | collective-permute-start | bytes 294920 | tf_op jit(solution)/shard_map/ppermute | solution.py:369
  33.8 1.9 %all-to-all-done.rows = bf16[8,16,640]{2,1,0:T(8,128)(2,1)S(1)} async-done(((bf16[8,16,640]{2,1,0:T(8,128)(2,1)}), bf16[8,16,640]{2,1,0:T(8,128)(2,1)S(1)}, u32[]{:S(2)}, u32[]{:S(2)}) %all-to-all-start) | async-done | bytes 163872 | tf_op jit(solution)/shard_map/all_to_all | solution.py:395
  35.7 0.7 collective-permute-start.3
  36.4 0.0 collective-permute-done.side
  36.4 0.0 copy-done.7
  36.4 0.0 copy-done.8
  36.4 3.2 %shard_map.122 = (f32[512,128]{1,0:T(8,128)S(1)}, f32[512,128]{1,0:T(8,128)S(1)}, f32[512,128]{1,0:T(8,128)S(1)}) custom-call(s32[4]{0:T(128)S(1)} %copy-done.7, bf16[512,256]{1,0:T(8,128)(2,1)S(1)} %copy-done.8, bf16[512,384]{1,0:T(8,128)(2,1)S(1)} %copy-done, bf16[512,384]{1,0:T(8,128)(2,1)S(1)} %collective-permute-done.side), custom_call_target="tpu_custom_call" | custom-call | flops 3300000000 | bytes 3000000 | tf_op jit(solution)/shard_map/pallas_call | solution.py:355
  39.6 0.0 collective-permute-done.3.here
  39.6 0.0 collective-permute-done.2.mid_b
  39.6 1.1 collective-permute-done.1.mid_a
  40.7 0.1 pad_maximum_fusion
  40.8 0.0 copy-start.5
  40.8 3.7 %collective-permute-start.4 = (bf16[1280,384]{1,0:T(8,128)(2,1)S(1)}, bf16[1280,384]{1,0:T(8,128)(2,1)S(1)}, u32[]{:S(2)}, u32[]{:S(2)}) collective-permute-start(bf16[1280,384]{1,0:T(8,128)(2,1)S(1)} %pad_maximum_fusion), channel_id=1, source_target_pairs={{0,4},{4,0},{8,12},{12,8},{16,20},{20,16},{24,28},{28,24},{32,36},... | collective-permute-start | bytes 2949128 | tf_op jit(solution)/shard_map/ppermute | solution.py:369
  44.5 1.9 %collective-permute-start.5 = (bf16[128,384]{1,0:T(8,128)(2,1)S(1)}, bf16[128,384]{1,0:T(8,128)(2,1)S(1)}, u32[]{:S(2)}, u32[]{:S(2)}) collective-permute-start(bf16[128,384]{1,0:T(8,128)(2,1)S(1)} %collective-permute-done.3.here), channel_id=1, source_target_pairs={{0,4},{4,0},{8,12},{12,8},{16,20},{20,16},{24,28},{28,24},{32,36},... | collective-permute-start | bytes 294920 | tf_op jit(solution)/shard_map/ppermute | solution.py:369
  46.4 1.3 %collective-permute-done.5.other = bf16[128,384]{1,0:T(8,128)(2,1)S(1)} collective-permute-done((bf16[128,384]{1,0:T(8,128)(2,1)S(1)}, bf16[128,384]{1,0:T(8,128)(2,1)S(1)}, u32[]{:S(2)}, u32[]{:S(2)}) %collective-permute-start.5) | collective-permute-done | bytes 98336 | tf_op jit(solution)/shard_map/ppermute | solution.py:369
  47.7 1.2 %shard_map.123 = f32[8,16,384]{2,1,0:T(8,128)S(1)} custom-call(s32[4]{0:T(128)S(1)} %copy-done.7, bf16[8,16,640]{2,1,0:T(8,128)(2,1)S(1)} %all-to-all-done.rows, bf16[128,384]{1,0:T(8,128)(2,1)S(1)} %collective-permute-done.3.here, bf16[128,384]{1,0:T(8,128)(2,1)S(1)} %collective-permute-done.5.other), custom_call_target="tpu_custom_call" | custom-call | flops 2200000000 | bytes 2000000 | tf_op jit(solution)/shard_map/pallas_call | solution.py:355
  48.9 20.1 %all_to_all.15.parts = f32[8,16,384]{2,1,0:T(8,128)S(1)} all-to-all(f32[8,16,384]{2,1,0:T(8,128)S(1)} %shard_map.123), channel_id=1, replica_groups={{0,64,128,192,256,320,384,448},{4,68,132,196,260,324,388,452},{8,72,136..., dimensions={0} | all-to-all | bytes 393216 | tf_op jit(solution)/shard_map/all_to_all | solution.py:419
  69.0 0.0 collective-permute-done.4.swapped
  69.0 0.0 copy-done.5
  69.0 6.3 %shard_map.124 = (bf16[4,128,768]{2,1,0:T(8,128)(2,1)S(1)}, bf16[16,192]{1,0:T(8,128)(2,1)}) custom-call(s32[4]{0:T(128)S(1)} %copy-done.7, bf16[512,256]{1,0:T(8,128)(2,1)S(1)} %copy-done.8, bf16[512,384]{1,0:T(8,128)(2,1)S(1)} %copy-done, bf16[512,384]{1,0:T(8,128)(2,1)S(1)} %collective-permute-done.side, ...), custom_call_target="tpu_custom_call" | custom-call | flops 7699999744 | bytes 7000000 | tf_op jit(solution)/shard_map/pallas_call | solution.py:355
  75.2 14.3 %all_to_all.16.terms = bf16[4,128,768]{2,1,0:T(8,128)(2,1)S(1)} all-to-all(bf16[4,128,768]{2,1,0:T(8,128)(2,1)S(1)} %get-tuple-element.43), channel_id=1, replica_groups=mesh['seq'=128,'mp'=4] {'mp'}, dimensions={0} | all-to-all | bytes 1572864 | tf_op jit(solution)/shard_map/all_to_all | solution.py:432
  89.5 0.0 copy-done.4
  89.5 0.0 copy-done.6
  89.5 0.8 shard_map.126
  90.3 4.8 %collective-permute-start.6 = (bf16[128,768]{1,0:T(8,128)(2,1)S(1)}, bf16[128,768]{1,0:T(8,128)(2,1)S(1)}, u32[]{:S(2)}, u32[]{:S(2)}) collective-permute-start(bf16[128,768]{1,0:T(8,128)(2,1)S(1)} %get-tuple-element.49.own), channel_id=1, source_target_pairs={{0,4},{4,0},{8,12},{12,8},{16,20},{20,16},{24,28},{28,24},{32,36},... | collective-permute-start | bytes 589832 | tf_op jit(solution)/shard_map/ppermute | solution.py:369
  95.2 1.0 collective-permute-done.6.other
  96.2 0.0 copy-done.1
  96.2 2.3 %shard_map.127 = (f32[128,768]{1,0:T(8,128)S(1)}, bf16[128,768]{1,0:T(8,128)(2,1)S(1)}) custom-call(bf16[128,768]{1,0:T(8,128)(2,1)S(1)} %get-tuple-element.49.own, bf16[128,768]{1,0:T(8,128)(2,1)S(1)} %collective-permute-done.6.other, bf16[4,768,768]{2,1,0:T(8,128)(2,1)S(1)} %bitcast.5), custom_call_target="tpu_custom_call" | custom-call | flops 4400000000 | bytes 4000000 | tf_op jit(solution)/shard_map/pallas_call | solution.py:355
  98.5 2.3 %collective-permute-start.7 = (bf16[128,768]{1,0:T(8,128)(2,1)S(1)}, bf16[128,768]{1,0:T(8,128)(2,1)S(1)}, u32[]{:S(2)}, u32[]{:S(2)}) collective-permute-start(bf16[128,768]{1,0:T(8,128)(2,1)S(1)} %get-tuple-element.52), channel_id=1, source_target_pairs={{0,4},{4,0},{8,12},{12,8},{16,20},{20,16},{24,28},{28,24},{32,36},... | collective-permute-start | bytes 589832 | tf_op jit(solution)/shard_map/ppermute | solution.py:369
  100.8 1.0 collective-permute-done.7
  101.8 0.7 add_convert_fusion
  (5 shorter events, 0.0 us)
Async XLA Ops:
  7.2 82.3 %all-gather.3.cloned.1.call-start = ((), (), s32[]{:S(2)}) async-start(), calls=%async_computation.3 | async-start | bytes 5898240 | tf_op jit(solution)/shard_map/all_gather | solution.py:400
  7.2 5.1 %copy-start.2 = (bf16[768,768]{1,0:T(8,128)(2,1)S(1)}, bf16[768,768]{1,0:T(8,128)(2,1)}, u32[]{:S(2)}) copy-start(bf16[768,768]{1,0:T(8,128)(2,1)} %w_up) | copy-start | bytes 3538948
  7.2 5.1 %copy-start.3 = (bf16[768,768]{1,0:T(8,128)(2,1)S(1)}, bf16[768,768]{1,0:T(8,128)(2,1)}, u32[]{:S(2)}) copy-start(bf16[768,768]{1,0:T(8,128)(2,1)} %w_down) | copy-start | bytes 3538948
  12.3 1.2 %copy-start = (bf16[512,384]{1,0:T(8,128)(2,1)S(1)}, bf16[512,384]{1,0:T(8,128)(2,1)}, u32[]{:S(2)}) copy-start(bf16[512,384]{1,0:T(8,128)(2,1)} %get-tuple-element.31.own) | copy-start | bytes 1179652
  12.3 15.3 %copy-start.9 = (bf16[128,384]{1,0:T(8,128)(2,1)S(1)}, bf16[128,384]{1,0:T(8,128)(2,1)}, u32[]{:S(2)}) copy-start(bf16[128,384]{1,0:T(8,128)(2,1)} %get-tuple-element.32) | copy-start | bytes 294916
  12.3 24.1 %copy-start.7 = (s32[4]{0:T(128)S(1)}, s32[4]{0:T(128)}, u32[]{:S(2)}) copy-start(s32[4]{0:T(128)} %tiles.5) | copy-start | bytes 52
  12.3 24.1 %copy-start.8 = (bf16[512,256]{1,0:T(8,128)(2,1)S(1)}, bf16[512,256]{1,0:T(8,128)(2,1)}, u32[]{:S(2)}) copy-start(bf16[512,256]{1,0:T(8,128)(2,1)} %get-tuple-element.30.query) | copy-start | bytes 786436
  13.5 22.8 %collective-permute-start = (bf16[512,384]{1,0:T(8,128)(2,1)S(1)}, bf16[512,384]{1,0:T(8,128)(2,1)S(1)}, u32[]{:S(2)}, u32[]{:S(2)}) collective-permute-start(bf16[512,384]{1,0:T(8,128)(2,1)S(1)} %copy-done), channel_id=1, source_target_pairs={{0,8},{4,12},{8,0},{12,4},{16,24},{20,28},{24,16},{28,20},{32,40},... | collective-permute-start | bytes 1179656 | tf_op jit(solution)/shard_map/ppermute | solution.py:369
  17.6 18.1 %all-to-all-start = ((bf16[8,16,640]{2,1,0:T(8,128)(2,1)}), bf16[8,16,640]{2,1,0:T(8,128)(2,1)S(1)}, u32[]{:S(2)}, u32[]{:S(2)}) async-start(bf16[8,16,640]{2,1,0:T(8,128)(2,1)} %get-tuple-element.29), calls=%async_computation | async-start | bytes 327680 | tf_op jit(solution)/shard_map/all_to_all | solution.py:395
  27.6 12.0 %collective-permute-start.2 = (bf16[128,384]{1,0:T(8,128)(2,1)S(1)}, bf16[128,384]{1,0:T(8,128)(2,1)S(1)}, u32[]{:S(2)}, u32[]{:S(2)}) collective-permute-start(bf16[128,384]{1,0:T(8,128)(2,1)S(1)} %copy-done.9), channel_id=1, source_target_pairs={{0,24},{4,28},{8,16},{12,20},{16,8},{20,12},{24,0},{28,4},{32,56},... | collective-permute-start | bytes 294920 | tf_op jit(solution)/shard_map/ppermute | solution.py:369
  31.7 8.9 %collective-permute-start.1 = (bf16[128,384]{1,0:T(8,128)(2,1)S(1)}, bf16[128,384]{1,0:T(8,128)(2,1)S(1)}, u32[]{:S(2)}, u32[]{:S(2)}) collective-permute-start(bf16[128,384]{1,0:T(8,128)(2,1)S(1)} %copy-done.9), channel_id=1, source_target_pairs={{0,16},{4,20},{8,24},{12,28},{16,0},{20,4},{24,8},{28,12},{32,48},... | collective-permute-start | bytes 294920 | tf_op jit(solution)/shard_map/ppermute | solution.py:369
  35.7 3.9 %collective-permute-start.3 = (bf16[128,384]{1,0:T(8,128)(2,1)S(1)}, bf16[128,384]{1,0:T(8,128)(2,1)S(1)}, u32[]{:S(2)}, u32[]{:S(2)}) collective-permute-start(bf16[128,384]{1,0:T(8,128)(2,1)S(1)} %bitcast.6), channel_id=1, source_target_pairs={{0,0},{4,4},{56,8},{60,12},{48,16},{52,20},{40,24},{44,28},{32,32}... | collective-permute-start | bytes 294920 | tf_op jit(solution)/shard_map/ppermute | solution.py:404
  40.8 28.2 %copy-start.5 = (bf16[192,768]{1,0:T(8,128)(2,1)S(1)}, bf16[192,768]{1,0:T(8,128)(2,1)}, u32[]{:S(2)}) copy-start(bf16[192,768]{1,0:T(8,128)(2,1)} %w_out.1) | copy-start | bytes 884740
  40.8 28.2 %collective-permute-start.4 = (bf16[1280,384]{1,0:T(8,128)(2,1)S(1)}, bf16[1280,384]{1,0:T(8,128)(2,1)S(1)}, u32[]{:S(2)}, u32[]{:S(2)}) collective-permute-start(bf16[1280,384]{1,0:T(8,128)(2,1)S(1)} %pad_maximum_fusion), channel_id=1, source_target_pairs={{0,4},{4,0},{8,12},{12,8},{16,20},{20,16},{24,28},{28,24},{32,36},... | collective-permute-start | bytes 2949128 | tf_op jit(solution)/shard_map/ppermute | solution.py:369
  44.5 3.2 %collective-permute-start.5 = (bf16[128,384]{1,0:T(8,128)(2,1)S(1)}, bf16[128,384]{1,0:T(8,128)(2,1)S(1)}, u32[]{:S(2)}, u32[]{:S(2)}) collective-permute-start(bf16[128,384]{1,0:T(8,128)(2,1)S(1)} %collective-permute-done.3.here), channel_id=1, source_target_pairs={{0,4},{4,0},{8,12},{12,8},{16,20},{20,16},{24,28},{28,24},{32,36},... | collective-permute-start | bytes 294920 | tf_op jit(solution)/shard_map/ppermute | solution.py:369
  69.0 20.6 %copy-start.4 = (bf16[512,768]{1,0:T(8,128)(2,1)S(1)}, bf16[512,768]{1,0:T(8,128)(2,1)}, u32[]{:S(2)}) copy-start(bf16[512,768]{1,0:T(8,128)(2,1)} %tokens.3) | copy-start | bytes 2359300
  69.0 20.6 %copy-start.6 = (bf16[768]{0:T(1024)(128)(2,1)S(1)}, bf16[768]{0:T(1024)(128)(2,1)}, u32[]{:S(2)}) copy-start(bf16[768]{0:T(1024)(128)(2,1)} %gain.3) | copy-start | bytes 4612
  89.5 6.7 %copy-start.1 = (bf16[3072,768]{1,0:T(8,128)(2,1)S(1)}, bf16[3072,768]{1,0:T(8,128)(2,1)}, u32[]{:S(2)}) copy-start(bf16[3072,768]{1,0:T(8,128)(2,1)} %all-gather.3.cloned.1.call-done) | copy-start | bytes 14155780
  90.3 5.9 %collective-permute-start.6 = (bf16[128,768]{1,0:T(8,128)(2,1)S(1)}, bf16[128,768]{1,0:T(8,128)(2,1)S(1)}, u32[]{:S(2)}, u32[]{:S(2)}) collective-permute-start(bf16[128,768]{1,0:T(8,128)(2,1)S(1)} %get-tuple-element.49.own), channel_id=1, source_target_pairs={{0,4},{4,0},{8,12},{12,8},{16,20},{20,16},{24,28},{28,24},{32,36},... | collective-permute-start | bytes 589832 | tf_op jit(solution)/shard_map/ppermute | solution.py:369
  98.5 3.3 %collective-permute-start.7 = (bf16[128,768]{1,0:T(8,128)(2,1)S(1)}, bf16[128,768]{1,0:T(8,128)(2,1)S(1)}, u32[]{:S(2)}, u32[]{:S(2)}) collective-permute-start(bf16[128,768]{1,0:T(8,128)(2,1)S(1)} %get-tuple-element.52), channel_id=1, source_target_pairs={{0,4},{4,0},{8,12},{12,8},{16,20},{20,16},{24,28},{28,24},{32,36},... | collective-permute-start | bytes 589832 | tf_op jit(solution)/shard_map/ppermute | solution.py:369
Sparse Core Ops, SparseCore 0:
  13.6 63.4 all-gather.2

commit v13 on v12

--- a/solution.py
+++ b/solution.py
@@ -251,14 +251,17 @@
         state[head][picked, :] = join(state[head][picked, :], more, peak, head)
     far_parts = []
     for head in range(LOCAL_HEADS):
-        spare = SPARE[head]
-        pieces = [parts[index, :, tile(head)] for index in range(FAR_GROUP)]
-        tops = [piece[:, spare : spare + 1] for piece in pieces]
-        peak = functools.reduce(jnp.maximum, tops)
+        pieces = [parts[index, :, tile(QUERY_TILE[head])] for index in range(FAR_GROUP)]
+        stats = [parts[index, :, LANES + 2 * head : LANES + 2 * head + 2] for index in range(FAR_GROUP)]
+        peak = functools.reduce(jnp.maximum, [stat[:, :1] for stat in stats])
         total = jnp.zeros((FAR_ROWS, LANES), jnp.float32)
-        for piece, top in zip(pieces, tops):
-            total = total + piece * jnp.exp(top - peak)
-        far_parts.append(total / total[:, spare + 1 : spare + 2])
+        weight = jnp.zeros((FAR_ROWS, 1), jnp.float32)
+        for piece, stat in zip(pieces, stats):
+            factor = jnp.exp(stat[:, :1] - peak)
+            total = total + piece * factor
+            weight = weight + stat[:, 1:] * factor
+        far_parts.append(total / weight)
+        total = pack(total, peak, weight, head, iota((FAR_ROWS, LANES), 1))
         number = mp * LOCAL_HEADS + head
         start = (number & 3) * CLASS_ROWS + (number >> 2) * FAR_ROWS
         picked = pl.ds(pl.multiple_of(start, FAR_ROWS), FAR_ROWS)
@@ -299,6 +302,7 @@
     key_at = position(at & (count - 1), holder)
     query_at = position(iota(shape, 0), column)
     lane = iota((count, LANES), 1)
+    results, stats = [], jnp.zeros((count, LANES), jnp.float32)
     for head in range(LOCAL_HEADS):
         number = mp * LOCAL_HEADS + head
         key_tile, value_tile = tile(KEY_TILE[head]), tile(VALUE_TILE[head])
@@ -312,8 +316,13 @@
         total = jnp.sum(weights, -1, keepdims=True)
         values = jnp.concatenate([here[:, value_tile], other[:, value_tile]], 0)
         part = matmul(weights.astype(jnp.bfloat16), values)
-        part = pack(part, peak, total, head, lane)
-        parts[:, :, tile(head)] = part.reshape(FAR_GROUP, FAR_ROWS, LANES)
+        results.append(part)
+        for step, value in enumerate((peak, total)):
+            stats = jnp.where(lane == 2 * head + step, value, stats)
+    low = lane < HEAD_DIM
+    whole = (FAR_GROUP, FAR_ROWS, LANES)
+    parts[:, :, tile(0)] = jnp.where(low, results[0], results[1]).reshape(whole)
+    parts[:, :, tile(1)] = jnp.where(low, stats, results[2]).reshape(whole)
 
 
 def weights_kernel(w_up, w_down, out):
@@ -413,7 +422,7 @@
     (parts,) = call(
         far_kernel,
         2,
-        [((FAR_GROUP, FAR_ROWS, 384), f32)],
+        [((FAR_GROUP, FAR_ROWS, 256), f32)],
         [(slide_tiles, s), (far_rows, v), (far_here, v), (far_other, v)],
     )
     parts = lax.all_to_all(

time: 110 us -> 108 us (0.982)
  blocking collectives: 34.4 us -> 32.5 us
    all_to_all x1, blocking collectives: 20.1 us -> 18.6 us  [local(): lax.all_to_all(parts, 'seq', split_axis=0, concat_axis=0, tiled=True, axi...]
where the time goes in v13:
time: 108 us
  starting transfers between devices  34 us (31%)
  blocking collectives  32.5 us (30%)
  Pallas kernels  19.6 us (18%)
  between operations  14.3 us (13%)
  waiting for transfers between devices  6.35 us (6%)
    ppermute x7, starting transfers between devices, swap(): lax.ppermute(value, 'seq', [(i, i ^ step) for i in range(lax.axis_size('s...  23.2 us
    pallas_call x7, Pallas kernels, call(): pl.pallas_call(kernel, out_shape=[jax.ShapeDtypeStruct(*out) for out in o...  19.6 us
    all_to_all x1, blocking collectives, local(): lax.all_to_all(parts, 'seq', split_axis=0, concat_axis=0, tiled=True, axi...  18.6 us
    all_to_all x1, blocking collectives, local(): terms = lax.all_to_all(terms, 'mp', split_axis=0, concat_axis=0, tiled=True)  13.9 us
    all_to_all x1, starting transfers between devices, local(): lax.all_to_all(far, 'seq', split_axis=0, concat_axis=0, tiled=True, axis_...  10 us
    ppermute x7, waiting for transfers between devices, swap(): lax.ppermute(value, 'seq', [(i, i ^ step) for i in range(lax.axis_size('s...  4.43 us
  transfers between devices with their start and end apart: 10, of which 5 were waited for; matrix products, arithmetic and copies ran while one was open for 0% of the time, Pallas kernels for 10%

profile of v13, /device:TPU:1, one launch (start us, length us, event | category | flops | bytes accessed | tf_op | source)
XLA Modules:
  0.0 107.6 jit_solution(5103852966528588745)
XLA Ops:
  7.2 0.0 all-gather.3.cloned.1.call-start
  7.2 0.0 copy-start.2
  7.2 0.0 copy-start.3
  7.2 5.0 %shard_map.121 = (bf16[512,256]{1,0:T(8,128)(2,1)}, bf16[512,384]{1,0:T(8,128)(2,1)}, bf16[128,384]{1,0:T(8,128)(2,1)}, bf16[8,16,640]{2,1,0:T(8,128)(2,1)}) custom-call(bf16[512,768]{1,0:T(8,128)(2,1)} %tokens.3, bf16[768]{0:T(1024)(128)(2,1)} %gain.2, bf16[192,768]{1,0:T(8,128)(2,1)} %bitcast.7, bf16[192,768]{1,0:T(8,128)(2,1)} %bitcast.8, ...), custom_call_target="tpu_custom_call" | custom-call | flops 3300000000 | bytes 3000000 | tf_op jit(solution)/shard_map/pallas_call | solution.py:364
  12.3 0.0 copy-done.2
  12.3 0.0 copy-done.3
  12.3 0.0 copy-start
  12.3 0.0 copy-start.9
  12.3 0.0 copy-start.7
  12.3 0.0 copy-start.8
  12.3 1.1 %shard_map.125 = bf16[768,768]{1,0:T(8,128)(2,1)} custom-call(bf16[768,768]{1,0:T(8,128)(2,1)S(1)} %copy-done.2, bf16[768,768]{1,0:T(8,128)(2,1)S(1)} %copy-done.3), custom_call_target="tpu_custom_call" | custom-call | flops 2200000000 | bytes 2000000 | tf_op jit(solution)/shard_map/pallas_call | solution.py:364
  13.5 0.0 all-gather.3.cloned.1.call-update
  13.5 0.0 copy-done
  13.5 4.0 %collective-permute-start = (bf16[512,384]{1,0:T(8,128)(2,1)S(1)}, bf16[512,384]{1,0:T(8,128)(2,1)S(1)}, u32[]{:S(2)}, u32[]{:S(2)}) collective-permute-start(bf16[512,384]{1,0:T(8,128)(2,1)S(1)} %copy-done), channel_id=1, source_target_pairs={{0,8},{4,12},{8,0},{12,4},{16,24},{20,28},{24,16},{28,20},{32,40},... | collective-permute-start | bytes 1179656 | tf_op jit(solution)/shard_map/ppermute | solution.py:378
  17.6 10.0 %all-to-all-start = ((bf16[8,16,640]{2,1,0:T(8,128)(2,1)}), bf16[8,16,640]{2,1,0:T(8,128)(2,1)S(1)}, u32[]{:S(2)}, u32[]{:S(2)}) async-start(bf16[8,16,640]{2,1,0:T(8,128)(2,1)} %get-tuple-element.29), calls=%async_computation | async-start | bytes 327680 | tf_op jit(solution)/shard_map/all_to_all | solution.py:404
  27.6 0.0 copy-done.9
  27.6 4.1 %collective-permute-start.2 = (bf16[128,384]{1,0:T(8,128)(2,1)S(1)}, bf16[128,384]{1,0:T(8,128)(2,1)S(1)}, u32[]{:S(2)}, u32[]{:S(2)}) collective-permute-start(bf16[128,384]{1,0:T(8,128)(2,1)S(1)} %copy-done.9), channel_id=1, source_target_pairs={{0,24},{4,28},{8,16},{12,20},{16,8},{20,12},{24,0},{28,4},{32,56},... | collective-permute-start | bytes 294920 | tf_op jit(solution)/shard_map/ppermute | solution.py:378
  31.7 2.0 %collective-permute-start.1 = (bf16[128,384]{1,0:T(8,128)(2,1)S(1)}, bf16[128,384]{1,0:T(8,128)(2,1)S(1)}, u32[]{:S(2)}, u32[]{:S(2)}) collective-permute-start(bf16[128,384]{1,0:T(8,128)(2,1)S(1)} %copy-done.9), channel_id=1, source_target_pairs={{0,16},{4,20},{8,24},{12,28},{16,0},{20,4},{24,8},{28,12},{32,48},... | collective-permute-start | bytes 294920 | tf_op jit(solution)/shard_map/ppermute | solution.py:378
  33.8 1.9 %all-to-all-done.rows = bf16[8,16,640]{2,1,0:T(8,128)(2,1)S(1)} async-done(((bf16[8,16,640]{2,1,0:T(8,128)(2,1)}), bf16[8,16,640]{2,1,0:T(8,128)(2,1)S(1)}, u32[]{:S(2)}, u32[]{:S(2)}) %all-to-all-start) | async-done | bytes 163872 | tf_op jit(solution)/shard_map/all_to_all | solution.py:404
  35.7 0.7 collective-permute-start.3
  36.4 0.0 collective-permute-done.side
  36.4 0.0 copy-done.7
  36.4 0.0 copy-done.8
  36.4 3.2 %shard_map.122 = (f32[512,128]{1,0:T(8,128)S(1)}, f32[512,128]{1,0:T(8,128)S(1)}, f32[512,128]{1,0:T(8,128)S(1)}) custom-call(s32[4]{0:T(128)S(1)} %copy-done.7, bf16[512,256]{1,0:T(8,128)(2,1)S(1)} %copy-done.8, bf16[512,384]{1,0:T(8,128)(2,1)S(1)} %copy-done, bf16[512,384]{1,0:T(8,128)(2,1)S(1)} %collective-permute-done.side), custom_call_target="tpu_custom_call" | custom-call | flops 3300000000 | bytes 3000000 | tf_op jit(solution)/shard_map/pallas_call | solution.py:364
  39.6 0.0 collective-permute-done.3.here
  39.6 0.0 collective-permute-done.2.mid_b
  39.6 1.1 collective-permute-done.1.mid_a
  40.7 0.1 pad_maximum_fusion
  40.8 0.0 copy-start.5
  40.8 3.7 %collective-permute-start.4 = (bf16[1280,384]{1,0:T(8,128)(2,1)S(1)}, bf16[1280,384]{1,0:T(8,128)(2,1)S(1)}, u32[]{:S(2)}, u32[]{:S(2)}) collective-permute-start(bf16[1280,384]{1,0:T(8,128)(2,1)S(1)} %pad_maximum_fusion), channel_id=1, source_target_pairs={{0,4},{4,0},{8,12},{12,8},{16,20},{20,16},{24,28},{28,24},{32,36},... | collective-permute-start | bytes 2949128 | tf_op jit(solution)/shard_map/ppermute | solution.py:378
  44.5 1.9 %collective-permute-start.5 = (bf16[128,384]{1,0:T(8,128)(2,1)S(1)}, bf16[128,384]{1,0:T(8,128)(2,1)S(1)}, u32[]{:S(2)}, u32[]{:S(2)}) collective-permute-start(bf16[128,384]{1,0:T(8,128)(2,1)S(1)} %collective-permute-done.3.here), channel_id=1, source_target_pairs={{0,4},{4,0},{8,12},{12,8},{16,20},{20,16},{24,28},{28,24},{32,36},... | collective-permute-start | bytes 294920 | tf_op jit(solution)/shard_map/ppermute | solution.py:378
  46.4 1.3 %collective-permute-done.5.other = bf16[128,384]{1,0:T(8,128)(2,1)S(1)} collective-permute-done((bf16[128,384]{1,0:T(8,128)(2,1)S(1)}, bf16[128,384]{1,0:T(8,128)(2,1)S(1)}, u32[]{:S(2)}, u32[]{:S(2)}) %collective-permute-start.5) | collective-permute-done | bytes 98336 | tf_op jit(solution)/shard_map/ppermute | solution.py:378
  47.7 1.2 %shard_map.123 = f32[8,16,256]{2,1,0:T(8,128)S(1)} custom-call(s32[4]{0:T(128)S(1)} %copy-done.7, bf16[8,16,640]{2,1,0:T(8,128)(2,1)S(1)} %all-to-all-done.rows, bf16[128,384]{1,0:T(8,128)(2,1)S(1)} %collective-permute-done.3.here, bf16[128,384]{1,0:T(8,128)(2,1)S(1)} %collective-permute-done.5.other), custom_call_target="tpu_custom_call" | custom-call | flops 2200000000 | bytes 2000000 | tf_op jit(solution)/shard_map/pallas_call | solution.py:364
  48.9 18.6 %all_to_all.15.parts = f32[8,16,256]{2,1,0:T(8,128)S(1)} all-to-all(f32[8,16,256]{2,1,0:T(8,128)S(1)} %shard_map.123), channel_id=1, replica_groups={{0,64,128,192,256,320,384,448},{4,68,132,196,260,324,388,452},{8,72,136..., dimensions={0} | all-to-all | bytes 262144 | tf_op jit(solution)/shard_map/all_to_all | solution.py:428
  67.5 0.0 collective-permute-done.4.swapped
  67.5 0.0 copy-done.5
  67.5 6.0 %shard_map.124 = (bf16[4,128,768]{2,1,0:T(8,128)(2,1)S(1)}, bf16[16,192]{1,0:T(8,128)(2,1)}) custom-call(s32[4]{0:T(128)S(1)} %copy-done.7, bf16[512,256]{1,0:T(8,128)(2,1)S(1)} %copy-done.8, bf16[512,384]{1,0:T(8,128)(2,1)S(1)} %copy-done, bf16[512,384]{1,0:T(8,128)(2,1)S(1)} %collective-permute-done.side, ...), custom_call_target="tpu_custom_call" | custom-call | flops 7699999744 | bytes 7000000 | tf_op jit(solution)/shard_map/pallas_call | solution.py:364
  73.5 13.9 %all_to_all.16.terms = bf16[4,128,768]{2,1,0:T(8,128)(2,1)S(1)} all-to-all(bf16[4,128,768]{2,1,0:T(8,128)(2,1)S(1)} %get-tuple-element.43), channel_id=1, replica_groups=mesh['seq'=128,'mp'=4] {'mp'}, dimensions={0} | all-to-all | bytes 1572864 | tf_op jit(solution)/shard_map/all_to_all | solution.py:441
  87.4 0.0 copy-done.4
  87.4 0.0 copy-done.6
  87.4 0.8 shard_map.126
  88.2 5.2 %collective-permute-start.6 = (bf16[128,768]{1,0:T(8,128)(2,1)S(1)}, bf16[128,768]{1,0:T(8,128)(2,1)S(1)}, u32[]{:S(2)}, u32[]{:S(2)}) collective-permute-start(bf16[128,768]{1,0:T(8,128)(2,1)S(1)} %get-tuple-element.49.own), channel_id=1, source_target_pairs={{0,4},{4,0},{8,12},{12,8},{16,20},{20,16},{24,28},{28,24},{32,36},... | collective-permute-start | bytes 589832 | tf_op jit(solution)/shard_map/ppermute | solution.py:378
  93.4 1.0 collective-permute-done.6.other
  94.4 0.0 copy-done.1
  94.4 2.3 %shard_map.127 = (f32[128,768]{1,0:T(8,128)S(1)}, bf16[128,768]{1,0:T(8,128)(2,1)S(1)}) custom-call(bf16[128,768]{1,0:T(8,128)(2,1)S(1)} %get-tuple-element.49.own, bf16[128,768]{1,0:T(8,128)(2,1)S(1)} %collective-permute-done.6.other, bf16[4,768,768]{2,1,0:T(8,128)(2,1)S(1)} %bitcast.5), custom_call_target="tpu_custom_call" | custom-call | flops 4400000000 | bytes 4000000 | tf_op jit(solution)/shard_map/pallas_call | solution.py:364
  96.7 2.3 %collective-permute-start.7 = (bf16[128,768]{1,0:T(8,128)(2,1)S(1)}, bf16[128,768]{1,0:T(8,128)(2,1)S(1)}, u32[]{:S(2)}, u32[]{:S(2)}) collective-permute-start(bf16[128,768]{1,0:T(8,128)(2,1)S(1)} %get-tuple-element.52), channel_id=1, source_target_pairs={{0,4},{4,0},{8,12},{12,8},{16,20},{20,16},{24,28},{28,24},{32,36},... | collective-permute-start | bytes 589832 | tf_op jit(solution)/shard_map/ppermute | solution.py:378
  99.0 1.0 collective-permute-done.7
  100.0 0.7 add_convert_fusion
  (5 shorter events, 0.0 us)
Async XLA Ops:
  7.2 80.2 %all-gather.3.cloned.1.call-start = ((), (), s32[]{:S(2)}) async-start(), calls=%async_computation.3 | async-start | bytes 5898240 | tf_op jit(solution)/shard_map/all_gather | solution.py:409
  7.2 5.1 %copy-start.2 = (bf16[768,768]{1,0:T(8,128)(2,1)S(1)}, bf16[768,768]{1,0:T(8,128)(2,1)}, u32[]{:S(2)}) copy-start(bf16[768,768]{1,0:T(8,128)(2,1)} %w_up) | copy-start | bytes 3538948
  7.2 5.1 %copy-start.3 = (bf16[768,768]{1,0:T(8,128)(2,1)S(1)}, bf16[768,768]{1,0:T(8,128)(2,1)}, u32[]{:S(2)}) copy-start(bf16[768,768]{1,0:T(8,128)(2,1)} %w_down) | copy-start | bytes 3538948
  12.3 1.2 %copy-start = (bf16[512,384]{1,0:T(8,128)(2,1)S(1)}, bf16[512,384]{1,0:T(8,128)(2,1)}, u32[]{:S(2)}) copy-start(bf16[512,384]{1,0:T(8,128)(2,1)} %get-tuple-element.31.own) | copy-start | bytes 1179652
  12.3 15.3 %copy-start.9 = (bf16[128,384]{1,0:T(8,128)(2,1)S(1)}, bf16[128,384]{1,0:T(8,128)(2,1)}, u32[]{:S(2)}) copy-start(bf16[128,384]{1,0:T(8,128)(2,1)} %get-tuple-element.32) | copy-start | bytes 294916
  12.3 24.1 %copy-start.7 = (s32[4]{0:T(128)S(1)}, s32[4]{0:T(128)}, u32[]{:S(2)}) copy-start(s32[4]{0:T(128)} %tiles.5) | copy-start | bytes 52
  12.3 24.1 %copy-start.8 = (bf16[512,256]{1,0:T(8,128)(2,1)S(1)}, bf16[512,256]{1,0:T(8,128)(2,1)}, u32[]{:S(2)}) copy-start(bf16[512,256]{1,0:T(8,128)(2,1)} %get-tuple-element.30.query) | copy-start | bytes 786436
  13.5 22.8 %collective-permute-start = (bf16[512,384]{1,0:T(8,128)(2,1)S(1)}, bf16[512,384]{1,0:T(8,128)(2,1)S(1)}, u32[]{:S(2)}, u32[]{:S(2)}) collective-permute-start(bf16[512,384]{1,0:T(8,128)(2,1)S(1)} %copy-done), channel_id=1, source_target_pairs={{0,8},{4,12},{8,0},{12,4},{16,24},{20,28},{24,16},{28,20},{32,40},... | collective-permute-start | bytes 1179656 | tf_op jit(solution)/shard_map/ppermute | solution.py:378
  17.6 18.1 %all-to-all-start = ((bf16[8,16,640]{2,1,0:T(8,128)(2,1)}), bf16[8,16,640]{2,1,0:T(8,128)(2,1)S(1)}, u32[]{:S(2)}, u32[]{:S(2)}) async-start(bf16[8,16,640]{2,1,0:T(8,128)(2,1)} %get-tuple-element.29), calls=%async_computation | async-start | bytes 327680 | tf_op jit(solution)/shard_map/all_to_all | solution.py:404
  27.6 12.0 %collective-permute-start.2 = (bf16[128,384]{1,0:T(8,128)(2,1)S(1)}, bf16[128,384]{1,0:T(8,128)(2,1)S(1)}, u32[]{:S(2)}, u32[]{:S(2)}) collective-permute-start(bf16[128,384]{1,0:T(8,128)(2,1)S(1)} %copy-done.9), channel_id=1, source_target_pairs={{0,24},{4,28},{8,16},{12,20},{16,8},{20,12},{24,0},{28,4},{32,56},... | collective-permute-start | bytes 294920 | tf_op jit(solution)/shard_map/ppermute | solution.py:378
  31.7 8.9 %collective-permute-start.1 = (bf16[128,384]{1,0:T(8,128)(2,1)S(1)}, bf16[128,384]{1,0:T(8,128)(2,1)S(1)}, u32[]{:S(2)}, u32[]{:S(2)}) collective-permute-start(bf16[128,384]{1,0:T(8,128)(2,1)S(1)} %copy-done.9), channel_id=1, source_target_pairs={{0,16},{4,20},{8,24},{12,28},{16,0},{20,4},{24,8},{28,12},{32,48},... | collective-permute-start | bytes 294920 | tf_op jit(solution)/shard_map/ppermute | solution.py:378
  35.7 3.9 %collective-permute-start.3 = (bf16[128,384]{1,0:T(8,128)(2,1)S(1)}, bf16[128,384]{1,0:T(8,128)(2,1)S(1)}, u32[]{:S(2)}, u32[]{:S(2)}) collective-permute-start(bf16[128,384]{1,0:T(8,128)(2,1)S(1)} %bitcast.6), channel_id=1, source_target_pairs={{0,0},{4,4},{56,8},{60,12},{48,16},{52,20},{40,24},{44,28},{32,32}... | collective-permute-start | bytes 294920 | tf_op jit(solution)/shard_map/ppermute | solution.py:413
  40.8 26.7 %copy-start.5 = (bf16[192,768]{1,0:T(8,128)(2,1)S(1)}, bf16[192,768]{1,0:T(8,128)(2,1)}, u32[]{:S(2)}) copy-start(bf16[192,768]{1,0:T(8,128)(2,1)} %w_out.1) | copy-start | bytes 884740
  40.8 26.7 %collective-permute-start.4 = (bf16[1280,384]{1,0:T(8,128)(2,1)S(1)}, bf16[1280,384]{1,0:T(8,128)(2,1)S(1)}, u32[]{:S(2)}, u32[]{:S(2)}) collective-permute-start(bf16[1280,384]{1,0:T(8,128)(2,1)S(1)} %pad_maximum_fusion), channel_id=1, source_target_pairs={{0,4},{4,0},{8,12},{12,8},{16,20},{20,16},{24,28},{28,24},{32,36},... | collective-permute-start | bytes 2949128 | tf_op jit(solution)/shard_map/ppermute | solution.py:378
  44.5 3.2 %collective-permute-start.5 = (bf16[128,384]{1,0:T(8,128)(2,1)S(1)}, bf16[128,384]{1,0:T(8,128)(2,1)S(1)}, u32[]{:S(2)}, u32[]{:S(2)}) collective-permute-start(bf16[128,384]{1,0:T(8,128)(2,1)S(1)} %collective-permute-done.3.here), channel_id=1, source_target_pairs={{0,4},{4,0},{8,12},{12,8},{16,20},{20,16},{24,28},{28,24},{32,36},... | collective-permute-start | bytes 294920 | tf_op jit(solution)/shard_map/ppermute | solution.py:378
  67.5 19.9 %copy-start.4 = (bf16[512,768]{1,0:T(8,128)(2,1)S(1)}, bf16[512,768]{1,0:T(8,128)(2,1)}, u32[]{:S(2)}) copy-start(bf16[512,768]{1,0:T(8,128)(2,1)} %tokens.3) | copy-start | bytes 2359300
  67.5 19.9 %copy-start.6 = (bf16[768]{0:T(1024)(128)(2,1)S(1)}, bf16[768]{0:T(1024)(128)(2,1)}, u32[]{:S(2)}) copy-start(bf16[768]{0:T(1024)(128)(2,1)} %gain.3) | copy-start | bytes 4612
  87.4 7.1 %copy-start.1 = (bf16[3072,768]{1,0:T(8,128)(2,1)S(1)}, bf16[3072,768]{1,0:T(8,128)(2,1)}, u32[]{:S(2)}) copy-start(bf16[3072,768]{1,0:T(8,128)(2,1)} %all-gather.3.cloned.1.call-done) | copy-start | bytes 14155780
  88.2 6.2 %collective-permute-start.6 = (bf16[128,768]{1,0:T(8,128)(2,1)S(1)}, bf16[128,768]{1,0:T(8,128)(2,1)S(1)}, u32[]{:S(2)}, u32[]{:S(2)}) collective-permute-start(bf16[128,768]{1,0:T(8,128)(2,1)S(1)} %get-tuple-element.49.own), channel_id=1, source_target_pairs={{0,4},{4,0},{8,12},{12,8},{16,20},{20,16},{24,28},{28,24},{32,36},... | collective-permute-start | bytes 589832 | tf_op jit(solution)/shard_map/ppermute | solution.py:378
  96.7 3.3 %collective-permute-start.7 = (bf16[128,768]{1,0:T(8,128)(2,1)S(1)}, bf16[128,768]{1,0:T(8,128)(2,1)S(1)}, u32[]{:S(2)}, u32[]{:S(2)}) collective-permute-start(bf16[128,768]{1,0:T(8,128)(2,1)S(1)} %get-tuple-element.52), channel_id=1, source_target_pairs={{0,4},{4,0},{8,12},{12,8},{16,20},{20,16},{24,28},{28,24},{32,36},... | collective-permute-start | bytes 589832 | tf_op jit(solution)/shard_map/ppermute | solution.py:378
Sparse Core Ops, SparseCore 0:
  13.6 63.4 all-gather.2

commit v14 on v13

--- a/solution.py
+++ b/solution.py
@@ -251,15 +251,20 @@
         state[head][picked, :] = join(state[head][picked, :], more, peak, head)
     far_parts = []
     for head in range(LOCAL_HEADS):
-        pieces = [parts[index, :, tile(QUERY_TILE[head])] for index in range(FAR_GROUP)]
-        stats = [parts[index, :, LANES + 2 * head : LANES + 2 * head + 2] for index in range(FAR_GROUP)]
-        peak = functools.reduce(jnp.maximum, [stat[:, :1] for stat in stats])
+        pieces, tops, weights = [], [], []
+        for index in range(FAR_GROUP):
+            pieces.append(parts[index, :, tile(QUERY_TILE[head])].astype(jnp.float32))
+            stats = parts[index, :, tile(1)].astype(jnp.float32)
+            thirds_of = [stats[:, 6 * head + step : 6 * head + step + 1] for step in range(6)]
+            tops.append(thirds_of[0] + thirds_of[1] + thirds_of[2])
+            weights.append(thirds_of[3] + thirds_of[4] + thirds_of[5])
+        peak = functools.reduce(jnp.maximum, tops)
         total = jnp.zeros((FAR_ROWS, LANES), jnp.float32)
         weight = jnp.zeros((FAR_ROWS, 1), jnp.float32)
-        for piece, stat in zip(pieces, stats):
-            factor = jnp.exp(stat[:, :1] - peak)
+        for piece, top, held_weight in zip(pieces, tops, weights):
+            factor = held_weight * jnp.exp(top - peak)
             total = total + piece * factor
-            weight = weight + stat[:, 1:] * factor
+            weight = weight + factor
         far_parts.append(total / weight)
         total = pack(total, peak, weight, head, iota((FAR_ROWS, LANES), 1))
         number = mp * LOCAL_HEADS + head
@@ -284,6 +289,14 @@
     mixed = jnp.concatenate([first, last[:, HEAD_DIM:]], 1)
     mixed = matmul(back, mixed).astype(jnp.bfloat16)
     terms[...] = matmul(mixed, w_out[...]).astype(jnp.bfloat16).reshape(4, BLOCK, WIDTH)
+
+
+def thirds(value):
+    parts = []
+    for _ in range(3):
+        parts.append(value.astype(jnp.bfloat16).astype(jnp.float32))
+        value = value - parts[-1]
+    return parts
 
 
 def far_kernel(tiles, rows, here, other, parts):
@@ -316,13 +329,15 @@
         total = jnp.sum(weights, -1, keepdims=True)
         values = jnp.concatenate([here[:, value_tile], other[:, value_tile]], 0)
         part = matmul(weights.astype(jnp.bfloat16), values)
-        results.append(part)
-        for step, value in enumerate((peak, total)):
-            stats = jnp.where(lane == 2 * head + step, value, stats)
+        results.append(part / total)
+        for step, value in enumerate(thirds(peak) + thirds(total)):
+            stats = jnp.where(lane == 6 * head + step, value, stats)
     low = lane < HEAD_DIM
-    whole = (FAR_GROUP, FAR_ROWS, LANES)
-    parts[:, :, tile(0)] = jnp.where(low, results[0], results[1]).reshape(whole)
-    parts[:, :, tile(1)] = jnp.where(low, stats, results[2]).reshape(whole)
+    for index, value in enumerate(
+        (jnp.where(low, results[0], results[1]), jnp.where(low, stats, results[2]))
+    ):
+        shaped = value.reshape(FAR_GROUP, FAR_ROWS, LANES)
+        parts[:, :, tile(index)] = shaped.astype(jnp.bfloat16)
 
 
 def weights_kernel(w_up, w_down, out):
@@ -422,7 +437,7 @@
     (parts,) = call(
         far_kernel,
         2,
-        [((FAR_GROUP, FAR_ROWS, 256), f32)],
+        [((FAR_GROUP, FAR_ROWS, 256), bf16)],
         [(slide_tiles, s), (far_rows, v), (far_here, v), (far_other, v)],
     )
     parts = lax.all_to_all(

time: 108 us -> 107 us (level)
  blocking collectives: 32.5 us -> 31.3 us
    all_to_all x1, blocking collectives: 18.6 us -> 17.4 us  [local(): lax.all_to_all(parts, 'seq', split_axis=0, concat_axis=0, tiled=True, axi...]
where the time goes in v14:
time: 107 us; the launch traced here: 106 us
  starting transfers between devices  34 us (32%)
  blocking collectives  31.3 us (29%)
  Pallas kernels  19.7 us (18%)
  between operations  14.3 us (13%)
  waiting for transfers between devices  6.35 us (6%)
    ppermute x7, starting transfers between devices, swap(): lax.ppermute(value, 'seq', [(i, i ^ step) for i in range(lax.axis_size('s...  23.2 us
    pallas_call x7, Pallas kernels, call(): pl.pallas_call(kernel, out_shape=[jax.ShapeDtypeStruct(*out) for out in o...  19.7 us
    all_to_all x1, blocking collectives, local(): lax.all_to_all(parts, 'seq', split_axis=0, concat_axis=0, tiled=True, axi...  17.4 us
    all_to_all x1, blocking collectives, local(): terms = lax.all_to_all(terms, 'mp', split_axis=0, concat_axis=0, tiled=True)  13.9 us
    all_to_all x1, starting transfers between devices, local(): lax.all_to_all(far, 'seq', split_axis=0, concat_axis=0, tiled=True, axis_...  10 us
    ppermute x7, waiting for transfers between devices, swap(): lax.ppermute(value, 'seq', [(i, i ^ step) for i in range(lax.axis_size('s...  4.42 us
  transfers between devices with their start and end apart: 10, of which 5 were waited for; matrix products, arithmetic and copies ran while one was open for 0% of the time, Pallas kernels for 10%

profile of v14, /device:TPU:1, one launch (start us, length us, event | category | flops | bytes accessed | tf_op | source)
XLA Modules:
  0.0 106.4 jit_solution(8369452164373857916)
XLA Ops:
  7.2 0.0 all-gather.3.cloned.1.call-start
  7.2 0.0 copy-start.2
  7.2 0.0 copy-start.3
  7.2 5.0 %shard_map.121 = (bf16[512,256]{1,0:T(8,128)(2,1)}, bf16[512,384]{1,0:T(8,128)(2,1)}, bf16[128,384]{1,0:T(8,128)(2,1)}, bf16[8,16,640]{2,1,0:T(8,128)(2,1)}) custom-call(bf16[512,768]{1,0:T(8,128)(2,1)} %tokens.3, bf16[768]{0:T(1024)(128)(2,1)} %gain.2, bf16[192,768]{1,0:T(8,128)(2,1)} %bitcast.7, bf16[192,768]{1,0:T(8,128)(2,1)} %bitcast.8, ...), custom_call_target="tpu_custom_call" | custom-call | flops 3300000000 | bytes 3000000 | tf_op jit(solution)/shard_map/pallas_call | solution.py:379
  12.3 0.0 copy-done.2
  12.3 0.0 copy-done.3
  12.3 0.0 copy-start
  12.3 0.0 copy-start.9
  12.3 0.0 copy-start.7
  12.3 0.0 copy-start.8
  12.3 1.1 %shard_map.125 = bf16[768,768]{1,0:T(8,128)(2,1)} custom-call(bf16[768,768]{1,0:T(8,128)(2,1)S(1)} %copy-done.2, bf16[768,768]{1,0:T(8,128)(2,1)S(1)} %copy-done.3), custom_call_target="tpu_custom_call" | custom-call | flops 2200000000 | bytes 2000000 | tf_op jit(solution)/shard_map/pallas_call | solution.py:379
  13.5 0.0 all-gather.3.cloned.1.call-update
  13.5 0.0 copy-done
  13.5 4.0 %collective-permute-start = (bf16[512,384]{1,0:T(8,128)(2,1)S(1)}, bf16[512,384]{1,0:T(8,128)(2,1)S(1)}, u32[]{:S(2)}, u32[]{:S(2)}) collective-permute-start(bf16[512,384]{1,0:T(8,128)(2,1)S(1)} %copy-done), channel_id=1, source_target_pairs={{0,8},{4,12},{8,0},{12,4},{16,24},{20,28},{24,16},{28,20},{32,40},... | collective-permute-start | bytes 1179656 | tf_op jit(solution)/shard_map/ppermute | solution.py:393
  17.6 10.0 %all-to-all-start = ((bf16[8,16,640]{2,1,0:T(8,128)(2,1)}), bf16[8,16,640]{2,1,0:T(8,128)(2,1)S(1)}, u32[]{:S(2)}, u32[]{:S(2)}) async-start(bf16[8,16,640]{2,1,0:T(8,128)(2,1)} %get-tuple-element.29), calls=%async_computation | async-start | bytes 327680 | tf_op jit(solution)/shard_map/all_to_all | solution.py:419
  27.6 0.0 copy-done.9
  27.6 4.1 %collective-permute-start.2 = (bf16[128,384]{1,0:T(8,128)(2,1)S(1)}, bf16[128,384]{1,0:T(8,128)(2,1)S(1)}, u32[]{:S(2)}, u32[]{:S(2)}) collective-permute-start(bf16[128,384]{1,0:T(8,128)(2,1)S(1)} %copy-done.9), channel_id=1, source_target_pairs={{0,24},{4,28},{8,16},{12,20},{16,8},{20,12},{24,0},{28,4},{32,56},... | collective-permute-start | bytes 294920 | tf_op jit(solution)/shard_map/ppermute | solution.py:393
  31.7 2.0 %collective-permute-start.1 = (bf16[128,384]{1,0:T(8,128)(2,1)S(1)}, bf16[128,384]{1,0:T(8,128)(2,1)S(1)}, u32[]{:S(2)}, u32[]{:S(2)}) collective-permute-start(bf16[128,384]{1,0:T(8,128)(2,1)S(1)} %copy-done.9), channel_id=1, source_target_pairs={{0,16},{4,20},{8,24},{12,28},{16,0},{20,4},{24,8},{28,12},{32,48},... | collective-permute-start | bytes 294920 | tf_op jit(solution)/shard_map/ppermute | solution.py:393
  33.8 1.9 %all-to-all-done.rows = bf16[8,16,640]{2,1,0:T(8,128)(2,1)S(1)} async-done(((bf16[8,16,640]{2,1,0:T(8,128)(2,1)}), bf16[8,16,640]{2,1,0:T(8,128)(2,1)S(1)}, u32[]{:S(2)}, u32[]{:S(2)}) %all-to-all-start) | async-done | bytes 163872 | tf_op jit(solution)/shard_map/all_to_all | solution.py:419
  35.7 0.7 collective-permute-start.3
  36.4 0.0 collective-permute-done.side
  36.4 0.0 copy-done.7
  36.4 0.0 copy-done.8
  36.4 3.2 %shard_map.122 = (f32[512,128]{1,0:T(8,128)S(1)}, f32[512,128]{1,0:T(8,128)S(1)}, f32[512,128]{1,0:T(8,128)S(1)}) custom-call(s32[4]{0:T(128)S(1)} %copy-done.7, bf16[512,256]{1,0:T(8,128)(2,1)S(1)} %copy-done.8, bf16[512,384]{1,0:T(8,128)(2,1)S(1)} %copy-done, bf16[512,384]{1,0:T(8,128)(2,1)S(1)} %collective-permute-done.side), custom_call_target="tpu_custom_call" | custom-call | flops 3300000000 | bytes 3000000 | tf_op jit(solution)/shard_map/pallas_call | solution.py:379
  39.6 0.0 collective-permute-done.3.here
  39.6 0.0 collective-permute-done.2.mid_b
  39.6 1.1 collective-permute-done.1.mid_a
  40.7 0.1 pad_maximum_fusion
  40.8 0.0 copy-start.5
  40.8 3.7 %collective-permute-start.4 = (bf16[1280,384]{1,0:T(8,128)(2,1)S(1)}, bf16[1280,384]{1,0:T(8,128)(2,1)S(1)}, u32[]{:S(2)}, u32[]{:S(2)}) collective-permute-start(bf16[1280,384]{1,0:T(8,128)(2,1)S(1)} %pad_maximum_fusion), channel_id=1, source_target_pairs={{0,4},{4,0},{8,12},{12,8},{16,20},{20,16},{24,28},{28,24},{32,36},... | collective-permute-start | bytes 2949128 | tf_op jit(solution)/shard_map/ppermute | solution.py:393
  44.5 1.9 %collective-permute-start.5 = (bf16[128,384]{1,0:T(8,128)(2,1)S(1)}, bf16[128,384]{1,0:T(8,128)(2,1)S(1)}, u32[]{:S(2)}, u32[]{:S(2)}) collective-permute-start(bf16[128,384]{1,0:T(8,128)(2,1)S(1)} %collective-permute-done.3.here), channel_id=1, source_target_pairs={{0,4},{4,0},{8,12},{12,8},{16,20},{20,16},{24,28},{28,24},{32,36},... | collective-permute-start | bytes 294920 | tf_op jit(solution)/shard_map/ppermute | solution.py:393
  46.4 1.3 %collective-permute-done.5.other = bf16[128,384]{1,0:T(8,128)(2,1)S(1)} collective-permute-done((bf16[128,384]{1,0:T(8,128)(2,1)S(1)}, bf16[128,384]{1,0:T(8,128)(2,1)S(1)}, u32[]{:S(2)}, u32[]{:S(2)}) %collective-permute-start.5) | collective-permute-done | bytes 98336 | tf_op jit(solution)/shard_map/ppermute | solution.py:393
  47.7 1.2 %shard_map.123 = bf16[8,16,256]{2,1,0:T(8,128)(2,1)S(1)} custom-call(s32[4]{0:T(128)S(1)} %copy-done.7, bf16[8,16,640]{2,1,0:T(8,128)(2,1)S(1)} %all-to-all-done.rows, bf16[128,384]{1,0:T(8,128)(2,1)S(1)} %collective-permute-done.3.here, bf16[128,384]{1,0:T(8,128)(2,1)S(1)} %collective-permute-done.5.other), custom_call_target="tpu_custom_call" | custom-call | flops 2200000000 | bytes 2000000 | tf_op jit(solution)/shard_map/pallas_call | solution.py:379
  48.9 17.4 %all_to_all.15.parts = bf16[8,16,256]{2,1,0:T(8,128)(2,1)S(1)} all-to-all(bf16[8,16,256]{2,1,0:T(8,128)(2,1)S(1)} %shard_map.123), channel_id=1, replica_groups={{0,64,128,192,256,320,384,448},{4,68,132,196,260,324,388,452},{8,72,136..., dimensions={0} | all-to-all | bytes 131072 | tf_op jit(solution)/shard_map/all_to_all | solution.py:443
  66.3 0.0 collective-permute-done.4.swapped
  66.3 0.0 copy-done.5
  66.3 6.0 %shard_map.124 = (bf16[4,128,768]{2,1,0:T(8,128)(2,1)S(1)}, bf16[16,192]{1,0:T(8,128)(2,1)}) custom-call(s32[4]{0:T(128)S(1)} %copy-done.7, bf16[512,256]{1,0:T(8,128)(2,1)S(1)} %copy-done.8, bf16[512,384]{1,0:T(8,128)(2,1)S(1)} %copy-done, bf16[512,384]{1,0:T(8,128)(2,1)S(1)} %collective-permute-done.side, ...), custom_call_target="tpu_custom_call" | custom-call | flops 7699999744 | bytes 7000000 | tf_op jit(solution)/shard_map/pallas_call | solution.py:379
  72.3 13.9 %all_to_all.16.terms = bf16[4,128,768]{2,1,0:T(8,128)(2,1)S(1)} all-to-all(bf16[4,128,768]{2,1,0:T(8,128)(2,1)S(1)} %get-tuple-element.43), channel_id=1, replica_groups=mesh['seq'=128,'mp'=4] {'mp'}, dimensions={0} | all-to-all | bytes 1572864 | tf_op jit(solution)/shard_map/all_to_all | solution.py:456
  86.2 0.0 copy-done.4
  86.2 0.0 copy-done.6
  86.2 0.8 shard_map.126
  87.0 5.2 %collective-permute-start.6 = (bf16[128,768]{1,0:T(8,128)(2,1)S(1)}, bf16[128,768]{1,0:T(8,128)(2,1)S(1)}, u32[]{:S(2)}, u32[]{:S(2)}) collective-permute-start(bf16[128,768]{1,0:T(8,128)(2,1)S(1)} %get-tuple-element.49.own), channel_id=1, source_target_pairs={{0,4},{4,0},{8,12},{12,8},{16,20},{20,16},{24,28},{28,24},{32,36},... | collective-permute-start | bytes 589832 | tf_op jit(solution)/shard_map/ppermute | solution.py:393
  92.2 1.0 collective-permute-done.6.other
  93.3 0.0 copy-done.1
  93.3 2.3 %shard_map.127 = (f32[128,768]{1,0:T(8,128)S(1)}, bf16[128,768]{1,0:T(8,128)(2,1)S(1)}) custom-call(bf16[128,768]{1,0:T(8,128)(2,1)S(1)} %get-tuple-element.49.own, bf16[128,768]{1,0:T(8,128)(2,1)S(1)} %collective-permute-done.6.other, bf16[4,768,768]{2,1,0:T(8,128)(2,1)S(1)} %bitcast.5), custom_call_target="tpu_custom_call" | custom-call | flops 4400000000 | bytes 4000000 | tf_op jit(solution)/shard_map/pallas_call | solution.py:379
  95.5 2.3 %collective-permute-start.7 = (bf16[128,768]{1,0:T(8,128)(2,1)S(1)}, bf16[128,768]{1,0:T(8,128)(2,1)S(1)}, u32[]{:S(2)}, u32[]{:S(2)}) collective-permute-start(bf16[128,768]{1,0:T(8,128)(2,1)S(1)} %get-tuple-element.52), channel_id=1, source_target_pairs={{0,4},{4,0},{8,12},{12,8},{16,20},{20,16},{24,28},{28,24},{32,36},... | collective-permute-start | bytes 589832 | tf_op jit(solution)/shard_map/ppermute | solution.py:393
  97.8 1.0 collective-permute-done.7
  98.9 0.7 add_convert_fusion
  (5 shorter events, 0.0 us)
Async XLA Ops:
  7.2 79.0 %all-gather.3.cloned.1.call-start = ((), (), s32[]{:S(2)}) async-start(), calls=%async_computation.3 | async-start | bytes 5898240 | tf_op jit(solution)/shard_map/all_gather | solution.py:424
  7.2 5.1 %copy-start.2 = (bf16[768,768]{1,0:T(8,128)(2,1)S(1)}, bf16[768,768]{1,0:T(8,128)(2,1)}, u32[]{:S(2)}) copy-start(bf16[768,768]{1,0:T(8,128)(2,1)} %w_up) | copy-start | bytes 3538948
  7.2 5.1 %copy-start.3 = (bf16[768,768]{1,0:T(8,128)(2,1)S(1)}, bf16[768,768]{1,0:T(8,128)(2,1)}, u32[]{:S(2)}) copy-start(bf16[768,768]{1,0:T(8,128)(2,1)} %w_down) | copy-start | bytes 3538948
  12.3 1.2 %copy-start = (bf16[512,384]{1,0:T(8,128)(2,1)S(1)}, bf16[512,384]{1,0:T(8,128)(2,1)}, u32[]{:S(2)}) copy-start(bf16[512,384]{1,0:T(8,128)(2,1)} %get-tuple-element.31.own) | copy-start | bytes 1179652
  12.3 15.3 %copy-start.9 = (bf16[128,384]{1,0:T(8,128)(2,1)S(1)}, bf16[128,384]{1,0:T(8,128)(2,1)}, u32[]{:S(2)}) copy-start(bf16[128,384]{1,0:T(8,128)(2,1)} %get-tuple-element.32) | copy-start | bytes 294916
  12.3 24.1 %copy-start.7 = (s32[4]{0:T(128)S(1)}, s32[4]{0:T(128)}, u32[]{:S(2)}) copy-start(s32[4]{0:T(128)} %tiles.5) | copy-start | bytes 52
  12.3 24.1 %copy-start.8 = (bf16[512,256]{1,0:T(8,128)(2,1)S(1)}, bf16[512,256]{1,0:T(8,128)(2,1)}, u32[]{:S(2)}) copy-start(bf16[512,256]{1,0:T(8,128)(2,1)} %get-tuple-element.30.query) | copy-start | bytes 786436
  13.5 22.8 %collective-permute-start = (bf16[512,384]{1,0:T(8,128)(2,1)S(1)}, bf16[512,384]{1,0:T(8,128)(2,1)S(1)}, u32[]{:S(2)}, u32[]{:S(2)}) collective-permute-start(bf16[512,384]{1,0:T(8,128)(2,1)S(1)} %copy-done), channel_id=1, source_target_pairs={{0,8},{4,12},{8,0},{12,4},{16,24},{20,28},{24,16},{28,20},{32,40},... | collective-permute-start | bytes 1179656 | tf_op jit(solution)/shard_map/ppermute | solution.py:393
  17.6 18.1 %all-to-all-start = ((bf16[8,16,640]{2,1,0:T(8,128)(2,1)}), bf16[8,16,640]{2,1,0:T(8,128)(2,1)S(1)}, u32[]{:S(2)}, u32[]{:S(2)}) async-start(bf16[8,16,640]{2,1,0:T(8,128)(2,1)} %get-tuple-element.29), calls=%async_computation | async-start | bytes 327680 | tf_op jit(solution)/shard_map/all_to_all | solution.py:419
  27.6 12.0 %collective-permute-start.2 = (bf16[128,384]{1,0:T(8,128)(2,1)S(1)}, bf16[128,384]{1,0:T(8,128)(2,1)S(1)}, u32[]{:S(2)}, u32[]{:S(2)}) collective-permute-start(bf16[128,384]{1,0:T(8,128)(2,1)S(1)} %copy-done.9), channel_id=1, source_target_pairs={{0,24},{4,28},{8,16},{12,20},{16,8},{20,12},{24,0},{28,4},{32,56},... | collective-permute-start | bytes 294920 | tf_op jit(solution)/shard_map/ppermute | solution.py:393
  31.7 8.9 %collective-permute-start.1 = (bf16[128,384]{1,0:T(8,128)(2,1)S(1)}, bf16[128,384]{1,0:T(8,128)(2,1)S(1)}, u32[]{:S(2)}, u32[]{:S(2)}) collective-permute-start(bf16[128,384]{1,0:T(8,128)(2,1)S(1)} %copy-done.9), channel_id=1, source_target_pairs={{0,16},{4,20},{8,24},{12,28},{16,0},{20,4},{24,8},{28,12},{32,48},... | collective-permute-start | bytes 294920 | tf_op jit(solution)/shard_map/ppermute | solution.py:393
  35.7 3.9 %collective-permute-start.3 = (bf16[128,384]{1,0:T(8,128)(2,1)S(1)}, bf16[128,384]{1,0:T(8,128)(2,1)S(1)}, u32[]{:S(2)}, u32[]{:S(2)}) collective-permute-start(bf16[128,384]{1,0:T(8,128)(2,1)S(1)} %bitcast.6), channel_id=1, source_target_pairs={{0,0},{4,4},{56,8},{60,12},{48,16},{52,20},{40,24},{44,28},{32,32}... | collective-permute-start | bytes 294920 | tf_op jit(solution)/shard_map/ppermute | solution.py:428
  40.8 25.5 %copy-start.5 = (bf16[192,768]{1,0:T(8,128)(2,1)S(1)}, bf16[192,768]{1,0:T(8,128)(2,1)}, u32[]{:S(2)}) copy-start(bf16[192,768]{1,0:T(8,128)(2,1)} %w_out.1) | copy-start | bytes 884740
  40.8 25.5 %collective-permute-start.4 = (bf16[1280,384]{1,0:T(8,128)(2,1)S(1)}, bf16[1280,384]{1,0:T(8,128)(2,1)S(1)}, u32[]{:S(2)}, u32[]{:S(2)}) collective-permute-start(bf16[1280,384]{1,0:T(8,128)(2,1)S(1)} %pad_maximum_fusion), channel_id=1, source_target_pairs={{0,4},{4,0},{8,12},{12,8},{16,20},{20,16},{24,28},{28,24},{32,36},... | collective-permute-start | bytes 2949128 | tf_op jit(solution)/shard_map/ppermute | solution.py:393
  44.5 3.2 %collective-permute-start.5 = (bf16[128,384]{1,0:T(8,128)(2,1)S(1)}, bf16[128,384]{1,0:T(8,128)(2,1)S(1)}, u32[]{:S(2)}, u32[]{:S(2)}) collective-permute-start(bf16[128,384]{1,0:T(8,128)(2,1)S(1)} %collective-permute-done.3.here), channel_id=1, source_target_pairs={{0,4},{4,0},{8,12},{12,8},{16,20},{20,16},{24,28},{28,24},{32,36},... | collective-permute-start | bytes 294920 | tf_op jit(solution)/shard_map/ppermute | solution.py:393
  66.3 19.9 %copy-start.4 = (bf16[512,768]{1,0:T(8,128)(2,1)S(1)}, bf16[512,768]{1,0:T(8,128)(2,1)}, u32[]{:S(2)}) copy-start(bf16[512,768]{1,0:T(8,128)(2,1)} %tokens.3) | copy-start | bytes 2359300
  66.3 19.9 %copy-start.6 = (bf16[768]{0:T(1024)(128)(2,1)S(1)}, bf16[768]{0:T(1024)(128)(2,1)}, u32[]{:S(2)}) copy-start(bf16[768]{0:T(1024)(128)(2,1)} %gain.3) | copy-start | bytes 4612
  86.2 7.1 %copy-start.1 = (bf16[3072,768]{1,0:T(8,128)(2,1)S(1)}, bf16[3072,768]{1,0:T(8,128)(2,1)}, u32[]{:S(2)}) copy-start(bf16[3072,768]{1,0:T(8,128)(2,1)} %all-gather.3.cloned.1.call-done) | copy-start | bytes 14155780
  87.0 6.3 %collective-permute-start.6 = (bf16[128,768]{1,0:T(8,128)(2,1)S(1)}, bf16[128,768]{1,0:T(8,128)(2,1)S(1)}, u32[]{:S(2)}, u32[]{:S(2)}) collective-permute-start(bf16[128,768]{1,0:T(8,128)(2,1)S(1)} %get-tuple-element.49.own), channel_id=1, source_target_pairs={{0,4},{4,0},{8,12},{12,8},{16,20},{20,16},{24,28},{28,24},{32,36},... | collective-permute-start | bytes 589832 | tf_op jit(solution)/shard_map/ppermute | solution.py:393
  95.5 3.3 %collective-permute-start.7 = (bf16[128,768]{1,0:T(8,128)(2,1)S(1)}, bf16[128,768]{1,0:T(8,128)(2,1)S(1)}, u32[]{:S(2)}, u32[]{:S(2)}) collective-permute-start(bf16[128,768]{1,0:T(8,128)(2,1)S(1)} %get-tuple-element.52), channel_id=1, source_target_pairs={{0,4},{4,0},{8,12},{12,8},{16,20},{20,16},{24,28},{28,24},{32,36},... | collective-permute-start | bytes 589832 | tf_op jit(solution)/shard_map/ppermute | solution.py:393
Sparse Core Ops, SparseCore 0:
  13.6 63.4 all-gather.2

commit v15 on v14

--- a/solution.py
+++ b/solution.py
@@ -340,11 +340,22 @@
         parts[:, :, tile(index)] = shaped.astype(jnp.bfloat16)
 
 
-def weights_kernel(w_up, w_down, out):
+def weights_kernel(w_up, w_down, out, sems):
     start = pl.multiple_of((lax.axis_index("seq") & 1) * HALF, HALF)
-    out[:HALF, :HALF] = w_up[:HALF, pl.ds(start, HALF)]
-    out[:HALF, HALF:] = w_up[HALF:, pl.ds(start, HALF)]
-    out[HALF:, :] = w_down[pl.ds(start, HALF), :]
+    upper, lower = pl.ds(0, HALF), pl.ds(HALF, HALF)
+    parts = [
+        (w_up.at[upper, pl.ds(start, HALF)], out.at[upper, upper]),
+        (w_up.at[lower, pl.ds(start, HALF)], out.at[upper, lower]),
+        (w_down.at[pl.ds(start, HALF), :], out.at[lower, :]),
+    ]
+    copies = [
+        pltpu.make_async_copy(source, target, sems.at[index])
+        for index, (source, target) in enumerate(parts)
+    ]
+    for copy in copies:
+        copy.start()
+    for copy in copies:
+        copy.wait()
 
 
 def hidden_part(normed, weights):
@@ -405,6 +416,16 @@
         for core in range(2)
     ]
     w_query, w_key, w_value = w_query.T, w_key.T, w_value.T
+    (packed,) = call(
+        weights_kernel,
+        2,
+        [((2 * HALF, WIDTH), bf16)],
+        [(w_up, h), (w_down, h)],
+        [dma((3,))],
+        WHOLE_VMEM,
+    )
+    mine = lax.all_gather(packed, "mp", axis=0)
+    tokens, _ = lax.optimization_barrier((tokens, packed))
     query, own, mid, far = call(
         project_kernel,
         3,
@@ -419,9 +440,6 @@
     far_rows = lax.all_to_all(
         far, "seq", split_axis=0, concat_axis=0, tiled=True, axis_index_groups=columns
     )
-    w_up, w_down, _ = lax.optimization_barrier((w_up, w_down, far))
-    (packed,) = call(weights_kernel, 2, [((2 * HALF, WIDTH), bf16)], [(w_up, v), (w_down, v)])
-    mine = lax.all_gather(packed, "mp", axis=0)
     side = swap(own, 2)
 
     far_keys = far_rows[:, :, 256:].reshape(128, 384)

time: 107 us -> 111 us (1.037)
  local copies, waits for them, and re-layouts: 0.06 us -> 1.98 us
    unnamed x20 -> x18, local copies, waits for them, and re-layouts: 0.05 us -> 1.97 us
  transfers between devices with their start and end apart: 10 -> 10, of which waited for: 5 -> 4; matrix products, arithmetic and copies ran while one was open for 0% -> 0% of each run, Pallas kernels for 10% -> 14%
where the time goes in v15:
time: 111 us; the launch traced here: 110 us
  starting transfers between devices  35 us (32%)
  blocking collectives  32 us (29%)
  Pallas kernels  20.7 us (19%)
  between operations  14.2 us (13%)
  waiting for transfers between devices  5.32 us (5%)
  local copies, waits for them, and re-layouts  1.98 us (2%)
    ppermute x7, starting transfers between devices, swap(): lax.ppermute(value, 'seq', [(i, i ^ step) for i in range(lax.axis_size('s...  24.3 us
    pallas_call x7, Pallas kernels, call(): pl.pallas_call(kernel, out_shape=[jax.ShapeDtypeStruct(*out) for out in o...  20.7 us
    all_to_all x1, blocking collectives, local(): lax.all_to_all(parts, 'seq', split_axis=0, concat_axis=0, tiled=True, axi...  18.1 us
    all_to_all x1, blocking collectives, local(): terms = lax.all_to_all(terms, 'mp', split_axis=0, concat_axis=0, tiled=True)  13.9 us
    all_to_all x1, starting transfers between devices, local(): lax.all_to_all(far, 'seq', split_axis=0, concat_axis=0, tiled=True, axis_...  10 us
    ppermute x7, waiting for transfers between devices, swap(): lax.ppermute(value, 'seq', [(i, i ^ step) for i in range(lax.axis_size('s...  3.37 us
  transfers between devices with their start and end apart: 10, of which 4 were waited for; matrix products, arithmetic and copies ran while one was open for 0% of the time, Pallas kernels for 14%

profile of v15, /device:TPU:1, one launch (start us, length us, event | category | flops | bytes accessed | tf_op | source)
XLA Modules:
  0.0 110.0 jit_solution(10369228645808503187)
XLA Ops:
  7.2 0.0 all-gather.3.cloned.1.call-start
  7.2 2.3 %shard_map.121 = bf16[768,768]{1,0:T(8,128)(2,1)} custom-call(bf16[768,768]{1,0:T(8,128)(2,1)} %w_up.1, bf16[768,768]{1,0:T(8,128)(2,1)} %w_down.1), custom_call_target="tpu_custom_call" | custom-call | flops 2200000000 | bytes 2000000 | tf_op jit(solution)/shard_map/pallas_call | solution.py:390
  9.5 0.0 all-gather.3.cloned.1.call-update
  9.6 0.0 copy-start.6
  9.6 4.9 %shard_map.122 = (bf16[512,256]{1,0:T(8,128)(2,1)}, bf16[512,384]{1,0:T(8,128)(2,1)}, bf16[128,384]{1,0:T(8,128)(2,1)}, bf16[8,16,640]{2,1,0:T(8,128)(2,1)}) custom-call(bf16[512,768]{1,0:T(8,128)(2,1)} %tokens.1, bf16[768]{0:T(1024)(128)(2,1)} %gain.2, bf16[192,768]{1,0:T(8,128)(2,1)} %bitcast.7, bf16[192,768]{1,0:T(8,128)(2,1)} %bitcast.8, ...), custom_call_target="tpu_custom_call" | custom-call | flops 3300000000 | bytes 3000000 | tf_op jit(solution)/shard_map/pallas_call | solution.py:390
  14.5 4.0 %collective-permute-start = (bf16[512,384]{1,0:T(8,128)(2,1)}, bf16[512,384]{1,0:T(8,128)(2,1)S(1)}, u32[]{:S(2)}, u32[]{:S(2)}) collective-permute-start(bf16[512,384]{1,0:T(8,128)(2,1)} %get-tuple-element.31.own), channel_id=1, source_target_pairs={{0,8},{4,12},{8,0},{12,4},{16,24},{20,28},{24,16},{28,20},{32,40},... | collective-permute-start | bytes 1179656 | tf_op jit(solution)/shard_map/ppermute | solution.py:404
  18.5 10.0 %all-to-all-start = ((bf16[8,16,640]{2,1,0:T(8,128)(2,1)}), bf16[8,16,640]{2,1,0:T(8,128)(2,1)S(1)}, u32[]{:S(2)}, u32[]{:S(2)}) async-start(bf16[8,16,640]{2,1,0:T(8,128)(2,1)} %get-tuple-element.29), calls=%async_computation | async-start | bytes 327680 | tf_op jit(solution)/shard_map/all_to_all | solution.py:440
  28.6 4.2 %collective-permute-start.1 = (bf16[128,384]{1,0:T(8,128)(2,1)}, bf16[128,384]{1,0:T(8,128)(2,1)S(1)}, u32[]{:S(2)}, u32[]{:S(2)}) collective-permute-start(bf16[128,384]{1,0:T(8,128)(2,1)} %get-tuple-element.32), channel_id=1, source_target_pairs={{0,16},{4,20},{8,24},{12,28},{16,0},{20,4},{24,8},{28,12},{32,48},... | collective-permute-start | bytes 294920 | tf_op jit(solution)/shard_map/ppermute | solution.py:404
  32.8 1.9 %collective-permute-start.2 = (bf16[128,384]{1,0:T(8,128)(2,1)}, bf16[128,384]{1,0:T(8,128)(2,1)S(1)}, u32[]{:S(2)}, u32[]{:S(2)}) collective-permute-start(bf16[128,384]{1,0:T(8,128)(2,1)} %get-tuple-element.32), channel_id=1, source_target_pairs={{0,24},{4,28},{8,16},{12,20},{16,8},{20,12},{24,0},{28,4},{32,56},... | collective-permute-start | bytes 294920 | tf_op jit(solution)/shard_map/ppermute | solution.py:404
  34.7 1.9 %all-to-all-done.rows = bf16[8,16,640]{2,1,0:T(8,128)(2,1)S(1)} async-done(((bf16[8,16,640]{2,1,0:T(8,128)(2,1)}), bf16[8,16,640]{2,1,0:T(8,128)(2,1)S(1)}, u32[]{:S(2)}, u32[]{:S(2)}) %all-to-all-start) | async-done | bytes 163872 | tf_op jit(solution)/shard_map/all_to_all | solution.py:440
  36.6 0.7 collective-permute-start.3
  37.3 0.0 collective-permute-done.side
  37.3 0.0 copy-done.6
  37.3 0.0 copy-start
  37.3 1.0 copy-done
  38.3 0.0 copy-start.7
  38.3 0.9 copy-done.7
  39.3 0.0 copy-start.1
  39.3 3.2 %shard_map.123 = (f32[512,128]{1,0:T(8,128)S(1)}, f32[512,128]{1,0:T(8,128)S(1)}, f32[512,128]{1,0:T(8,128)S(1)}) custom-call(s32[4]{0:T(128)S(1)} %copy-done.6, bf16[512,256]{1,0:T(8,128)(2,1)S(1)} %copy-done.7, bf16[512,384]{1,0:T(8,128)(2,1)S(1)} %copy-done, bf16[512,384]{1,0:T(8,128)(2,1)S(1)} %collective-permute-done.side), custom_call_target="tpu_custom_call" | custom-call | flops 3300000000 | bytes 3000000 | tf_op jit(solution)/shard_map/pallas_call | solution.py:390
  42.5 0.0 collective-permute-done.3.here
  42.5 0.0 collective-permute-done.1.mid_a
  42.5 0.0 collective-permute-done.2.mid_b
  42.5 0.0 copy-done.1
  42.6 0.1 pad_maximum_fusion
  42.7 0.0 copy-start.4
  42.7 0.0 copy-start.8
  42.7 4.7 %collective-permute-start.4 = (bf16[1280,384]{1,0:T(8,128)(2,1)S(1)}, bf16[1280,384]{1,0:T(8,128)(2,1)S(1)}, u32[]{:S(2)}, u32[]{:S(2)}) collective-permute-start(bf16[1280,384]{1,0:T(8,128)(2,1)S(1)} %pad_maximum_fusion), channel_id=1, source_target_pairs={{0,4},{4,0},{8,12},{12,8},{16,20},{20,16},{24,28},{28,24},{32,36},... | collective-permute-start | bytes 2949128 | tf_op jit(solution)/shard_map/ppermute | solution.py:404
  47.4 1.9 %collective-permute-start.5 = (bf16[128,384]{1,0:T(8,128)(2,1)S(1)}, bf16[128,384]{1,0:T(8,128)(2,1)S(1)}, u32[]{:S(2)}, u32[]{:S(2)}) collective-permute-start(bf16[128,384]{1,0:T(8,128)(2,1)S(1)} %collective-permute-done.3.here), channel_id=1, source_target_pairs={{0,4},{4,0},{8,12},{12,8},{16,20},{20,16},{24,28},{28,24},{32,36},... | collective-permute-start | bytes 294920 | tf_op jit(solution)/shard_map/ppermute | solution.py:404
  49.3 1.3 %collective-permute-done.5.other = bf16[128,384]{1,0:T(8,128)(2,1)S(1)} collective-permute-done((bf16[128,384]{1,0:T(8,128)(2,1)S(1)}, bf16[128,384]{1,0:T(8,128)(2,1)S(1)}, u32[]{:S(2)}, u32[]{:S(2)}) %collective-permute-start.5) | collective-permute-done | bytes 98336 | tf_op jit(solution)/shard_map/ppermute | solution.py:404
  50.6 1.2 %shard_map.124 = bf16[8,16,256]{2,1,0:T(8,128)(2,1)S(1)} custom-call(s32[4]{0:T(128)S(1)} %copy-done.6, bf16[8,16,640]{2,1,0:T(8,128)(2,1)S(1)} %all-to-all-done.rows, bf16[128,384]{1,0:T(8,128)(2,1)S(1)} %collective-permute-done.3.here, bf16[128,384]{1,0:T(8,128)(2,1)S(1)} %collective-permute-done.5.other), custom_call_target="tpu_custom_call" | custom-call | flops 2200000000 | bytes 2000000 | tf_op jit(solution)/shard_map/pallas_call | solution.py:390
  51.8 18.1 %all_to_all.15.parts = bf16[8,16,256]{2,1,0:T(8,128)(2,1)S(1)} all-to-all(bf16[8,16,256]{2,1,0:T(8,128)(2,1)S(1)} %shard_map.124), channel_id=1, replica_groups={{0,64,128,192,256,320,384,448},{4,68,132,196,260,324,388,452},{8,72,136..., dimensions={0} | all-to-all | bytes 131072 | tf_op jit(solution)/shard_map/all_to_all | solution.py:461
  69.9 0.0 copy-start.3
  69.9 0.0 copy-start.5
  69.9 0.0 collective-permute-done.4.swapped
  69.9 0.0 copy-done.4
  69.9 0.0 copy-done.8
  69.9 5.9 %shard_map.125 = (bf16[4,128,768]{2,1,0:T(8,128)(2,1)S(1)}, bf16[16,192]{1,0:T(8,128)(2,1)}) custom-call(s32[4]{0:T(128)S(1)} %copy-done.6, bf16[512,256]{1,0:T(8,128)(2,1)S(1)} %copy-done.8, bf16[512,384]{1,0:T(8,128)(2,1)S(1)} %copy-done.1, bf16[512,384]{1,0:T(8,128)(2,1)S(1)} %collective-permute-done.side, ...), custom_call_target="tpu_custom_call" | custom-call | flops 7699999744 | bytes 7000000 | tf_op jit(solution)/shard_map/pallas_call | solution.py:390
  75.9 13.9 %all_to_all.16.terms = bf16[4,128,768]{2,1,0:T(8,128)(2,1)S(1)} all-to-all(bf16[4,128,768]{2,1,0:T(8,128)(2,1)S(1)} %get-tuple-element.43), channel_id=1, replica_groups=mesh['seq'=128,'mp'=4] {'mp'}, dimensions={0} | all-to-all | bytes 1572864 | tf_op jit(solution)/shard_map/all_to_all | solution.py:474
  89.8 0.0 copy-done.3
  89.8 0.0 copy-done.5
  89.8 0.8 shard_map.126
  90.6 5.2 %collective-permute-start.6 = (bf16[128,768]{1,0:T(8,128)(2,1)S(1)}, bf16[128,768]{1,0:T(8,128)(2,1)S(1)}, u32[]{:S(2)}, u32[]{:S(2)}) collective-permute-start(bf16[128,768]{1,0:T(8,128)(2,1)S(1)} %get-tuple-element.47.own), channel_id=1, source_target_pairs={{0,4},{4,0},{8,12},{12,8},{16,20},{20,16},{24,28},{28,24},{32,36},... | collective-permute-start | bytes 589832 | tf_op jit(solution)/shard_map/ppermute | solution.py:404
  95.8 1.0 collective-permute-done.6.other
  96.8 0.0 copy-done.2
  96.8 2.3 %shard_map.127 = (f32[128,768]{1,0:T(8,128)S(1)}, bf16[128,768]{1,0:T(8,128)(2,1)S(1)}) custom-call(bf16[128,768]{1,0:T(8,128)(2,1)S(1)} %get-tuple-element.47.own, bf16[128,768]{1,0:T(8,128)(2,1)S(1)} %collective-permute-done.6.other, bf16[4,768,768]{2,1,0:T(8,128)(2,1)S(1)} %bitcast.5), custom_call_target="tpu_custom_call" | custom-call | flops 4400000000 | bytes 4000000 | tf_op jit(solution)/shard_map/pallas_call | solution.py:390
  99.1 2.3 %collective-permute-start.7 = (bf16[128,768]{1,0:T(8,128)(2,1)S(1)}, bf16[128,768]{1,0:T(8,128)(2,1)S(1)}, u32[]{:S(2)}, u32[]{:S(2)}) collective-permute-start(bf16[128,768]{1,0:T(8,128)(2,1)S(1)} %get-tuple-element.50), channel_id=1, source_target_pairs={{0,4},{4,0},{8,12},{12,8},{16,20},{20,16},{24,28},{28,24},{32,36},... | collective-permute-start | bytes 589832 | tf_op jit(solution)/shard_map/ppermute | solution.py:404
  101.4 1.0 collective-permute-done.7
  102.4 0.7 add_convert_fusion
  (3 shorter events, 0.0 us)
Async XLA Ops:
  7.2 82.6 %all-gather.3.cloned.1.call-start = ((), (), s32[]{:S(2)}) async-start(), calls=%async_computation.3 | async-start | bytes 5898240 | tf_op jit(solution)/shard_map/all_gather | solution.py:427
  9.6 27.8 %copy-start.6 = (s32[4]{0:T(128)S(1)}, s32[4]{0:T(128)}, u32[]{:S(2)}) copy-start(s32[4]{0:T(128)} %tiles.5) | copy-start | bytes 52
  14.5 22.8 %collective-permute-start = (bf16[512,384]{1,0:T(8,128)(2,1)}, bf16[512,384]{1,0:T(8,128)(2,1)S(1)}, u32[]{:S(2)}, u32[]{:S(2)}) collective-permute-start(bf16[512,384]{1,0:T(8,128)(2,1)} %get-tuple-element.31.own), channel_id=1, source_target_pairs={{0,8},{4,12},{8,0},{12,4},{16,24},{20,28},{24,16},{28,20},{32,40},... | collective-permute-start | bytes 1179656 | tf_op jit(solution)/shard_map/ppermute | solution.py:404
  18.5 18.1 %all-to-all-start = ((bf16[8,16,640]{2,1,0:T(8,128)(2,1)}), bf16[8,16,640]{2,1,0:T(8,128)(2,1)S(1)}, u32[]{:S(2)}, u32[]{:S(2)}) async-start(bf16[8,16,640]{2,1,0:T(8,128)(2,1)} %get-tuple-element.29), calls=%async_computation | async-start | bytes 327680 | tf_op jit(solution)/shard_map/all_to_all | solution.py:440
  28.6 14.0 %collective-permute-start.1 = (bf16[128,384]{1,0:T(8,128)(2,1)}, bf16[128,384]{1,0:T(8,128)(2,1)S(1)}, u32[]{:S(2)}, u32[]{:S(2)}) collective-permute-start(bf16[128,384]{1,0:T(8,128)(2,1)} %get-tuple-element.32), channel_id=1, source_target_pairs={{0,16},{4,20},{8,24},{12,28},{16,0},{20,4},{24,8},{28,12},{32,48},... | collective-permute-start | bytes 294920 | tf_op jit(solution)/shard_map/ppermute | solution.py:404
  32.8 9.8 %collective-permute-start.2 = (bf16[128,384]{1,0:T(8,128)(2,1)}, bf16[128,384]{1,0:T(8,128)(2,1)S(1)}, u32[]{:S(2)}, u32[]{:S(2)}) collective-permute-start(bf16[128,384]{1,0:T(8,128)(2,1)} %get-tuple-element.32), channel_id=1, source_target_pairs={{0,24},{4,28},{8,16},{12,20},{16,8},{20,12},{24,0},{28,4},{32,56},... | collective-permute-start | bytes 294920 | tf_op jit(solution)/shard_map/ppermute | solution.py:404
  36.6 5.9 %collective-permute-start.3 = (bf16[128,384]{1,0:T(8,128)(2,1)S(1)}, bf16[128,384]{1,0:T(8,128)(2,1)S(1)}, u32[]{:S(2)}, u32[]{:S(2)}) collective-permute-start(bf16[128,384]{1,0:T(8,128)(2,1)S(1)} %bitcast.6), channel_id=1, source_target_pairs={{0,0},{4,4},{56,8},{60,12},{48,16},{52,20},{40,24},{44,28},{32,32}... | collective-permute-start | bytes 294920 | tf_op jit(solution)/shard_map/ppermute | solution.py:446
  37.3 1.0 copy-start
  38.3 0.9 copy-start.7
  39.3 3.3 %copy-start.1 = (bf16[512,384]{1,0:T(8,128)(2,1)S(1)}, bf16[512,384]{1,0:T(8,128)(2,1)}, u32[]{:S(2)}) copy-start(bf16[512,384]{1,0:T(8,128)(2,1)} %get-tuple-element.31.own) | copy-start | bytes 1179652
  42.7 27.3 %copy-start.4 = (bf16[192,768]{1,0:T(8,128)(2,1)S(1)}, bf16[192,768]{1,0:T(8,128)(2,1)}, u32[]{:S(2)}) copy-start(bf16[192,768]{1,0:T(8,128)(2,1)} %w_out.1) | copy-start | bytes 884740
  42.7 27.3 %copy-start.8 = (bf16[512,256]{1,0:T(8,128)(2,1)S(1)}, bf16[512,256]{1,0:T(8,128)(2,1)}, u32[]{:S(2)}) copy-start(bf16[512,256]{1,0:T(8,128)(2,1)} %get-tuple-element.30.query) | copy-start | bytes 786436
  42.7 27.2 %collective-permute-start.4 = (bf16[1280,384]{1,0:T(8,128)(2,1)S(1)}, bf16[1280,384]{1,0:T(8,128)(2,1)S(1)}, u32[]{:S(2)}, u32[]{:S(2)}) collective-permute-start(bf16[1280,384]{1,0:T(8,128)(2,1)S(1)} %pad_maximum_fusion), channel_id=1, source_target_pairs={{0,4},{4,0},{8,12},{12,8},{16,20},{20,16},{24,28},{28,24},{32,36},... | collective-permute-start | bytes 2949128 | tf_op jit(solution)/shard_map/ppermute | solution.py:404
  47.4 3.2 %collective-permute-start.5 = (bf16[128,384]{1,0:T(8,128)(2,1)S(1)}, bf16[128,384]{1,0:T(8,128)(2,1)S(1)}, u32[]{:S(2)}, u32[]{:S(2)}) collective-permute-start(bf16[128,384]{1,0:T(8,128)(2,1)S(1)} %collective-permute-done.3.here), channel_id=1, source_target_pairs={{0,4},{4,0},{8,12},{12,8},{16,20},{20,16},{24,28},{28,24},{32,36},... | collective-permute-start | bytes 294920 | tf_op jit(solution)/shard_map/ppermute | solution.py:404
  69.9 19.8 %copy-start.3 = (bf16[512,768]{1,0:T(8,128)(2,1)S(1)}, bf16[512,768]{1,0:T(8,128)(2,1)}, u32[]{:S(2)}) copy-start(bf16[512,768]{1,0:T(8,128)(2,1)} %tokens.1) | copy-start | bytes 2359300
  69.9 19.8 %copy-start.5 = (bf16[768]{0:T(1024)(128)(2,1)S(1)}, bf16[768]{0:T(1024)(128)(2,1)}, u32[]{:S(2)}) copy-start(bf16[768]{0:T(1024)(128)(2,1)} %gain.3) | copy-start | bytes 4612
  89.8 7.1 %copy-start.2 = (bf16[3072,768]{1,0:T(8,128)(2,1)S(1)}, bf16[3072,768]{1,0:T(8,128)(2,1)}, u32[]{:S(2)}) copy-start(bf16[3072,768]{1,0:T(8,128)(2,1)} %all-gather.3.cloned.1.call-done) | copy-start | bytes 14155780
  90.6 6.2 %collective-permute-start.6 = (bf16[128,768]{1,0:T(8,128)(2,1)S(1)}, bf16[128,768]{1,0:T(8,128)(2,1)S(1)}, u32[]{:S(2)}, u32[]{:S(2)}) collective-permute-start(bf16[128,768]{1,0:T(8,128)(2,1)S(1)} %get-tuple-element.47.own), channel_id=1, source_target_pairs={{0,4},{4,0},{8,12},{12,8},{16,20},{20,16},{24,28},{28,24},{32,36},... | collective-permute-start | bytes 589832 | tf_op jit(solution)/shard_map/ppermute | solution.py:404
  99.1 3.3 %collective-permute-start.7 = (bf16[128,768]{1,0:T(8,128)(2,1)S(1)}, bf16[128,768]{1,0:T(8,128)(2,1)S(1)}, u32[]{:S(2)}, u32[]{:S(2)}) collective-permute-start(bf16[128,768]{1,0:T(8,128)(2,1)S(1)} %get-tuple-element.50), channel_id=1, source_target_pairs={{0,4},{4,0},{8,12},{12,8},{16,20},{20,16},{24,28},{28,24},{32,36},... | collective-permute-start | bytes 589832 | tf_op jit(solution)/shard_map/ppermute | solution.py:404
Sparse Core Ops, SparseCore 0:
  10.1 63.4 all-gather.2
